TPU v7x, 32 devices: a whole 2x2x4 slice. The times are simulated.
32 devices in a mesh: dp: 4 (over z), sp: 8 (over y, x, core).
Axes of the slice: x: 2, y: 2, z: 4, core: 2. Of those that a mesh axis runs over, the one named last changes fastest.
Arguments:
- tokens: bfloat16 [4, 4096, 2048], P('dp', 'sp'), may hold values from -6 to 6
- segment_ids: int32 [4, 4096], P('dp', 'sp'), may hold values from 0 to 1, as said below
- selected: int32 [4, 4096], P('dp', 'sp'), may hold values from 0 to 1, as said below
- cotangent: bfloat16 [4, 4096, 2048], P('dp', 'sp'), may hold values from -6 to 6
- w_qkv: bfloat16 [2048, 2560], P('sp'), may hold values from -0.125 to 0.125
- w_out: bfloat16 [2048, 2048], P('sp'), may hold values from -1.5 to 1.5
- w_gate_up: bfloat16 [2048, 11264], P('sp'), may hold values from -0.125 to 0.125
- w_down: bfloat16 [5632, 2048], P('sp'), may hold values from -0.078125 to 0.078125
- g_attn: bfloat16 [2048], P('sp'), may hold values from 0.5 to 1.5
- g_mlp: bfloat16 [2048], P('sp'), may hold values from 0.5 to 1.5
Outputs:
- output: bfloat16 [4, 4096, 2048], P('dp', 'sp')
- grad_tokens: bfloat16 [4, 4096, 2048], P('dp', 'sp')
- grad_w_qkv: float32 [2048, 2560], P('sp')
- grad_w_out: float32 [2048, 2048], P('sp')
- grad_w_gate_up: float32 [2048, 11264], P('sp')
- grad_w_down: float32 [5632, 2048], P('sp')
- grad_g_attn: float32 [2048], P('sp')
- grad_g_mlp: float32 [2048], P('sp')
Inputs may be any that keep to these rules, and one draw needn't show every extreme that they name: `segment_ids`: 0 on a stream's first document and 1 on its second, never falling along a stream; one stream of all, drawn from the seed, is a single document, and in the others the second document begins at a place from 1024 to 3072. `selected`: 1 where a token's output gradient counts, else 0.
All inputs are finite; a program needn't handle non-finite values.
Results may differ from a plain program's by a relative error of at most 0.02.
Values may be sent and summed in bfloat16 or wider, within the bound.
No kernel may reach another device: no remote copies, remote signals or barrier semaphores. Data moves between devices by JAX's collectives and lax.ppermute only.
A program may use at most 640 MiB of HBM per device.

v0:
```python
import jax
import jax.numpy as jnp
from jax import lax
from jax.sharding import PartitionSpec as P

D = 2048
H = 32
KV = 4
HD = 64
FF = 5632


EPSILON = 1e-05
ROPE_BASE = 10000.0
MASKED = -1e30


def rope_tables(positions, head_size):
    half_dim = head_size // 2
    frequency = ROPE_BASE ** (-(jnp.arange(half_dim, dtype=jnp.float32) * 2.0 / head_size))
    angles = positions.astype(jnp.float32)[:, None] * frequency[None, :]
    return (jnp.cos(angles), jnp.sin(angles))


def rotate(values, cosine, sine_tab, inverse_turn):
    half_dim = values.shape[-1] // 2
    first_half = values[..., :half_dim]
    second = values[..., half_dim:]
    cos_wide = cosine[:, None, :]
    sin_wide = sine_tab[:, None, :]
    if inverse_turn:
        sin_wide = -sin_wide
    return jnp.concatenate(
        [first_half * cos_wide - second * sin_wide, second * cos_wide + first_half * sin_wide],
        axis=-1,
    )


def rms_norm(values, gain_vec):
    inverse = lax.rsqrt(jnp.mean(values * values, axis=-1, keepdims=True) + EPSILON)
    return (values * inverse * gain_vec, inverse)


def norm_back(values, inverse, gain_vec, upstream):
    scaled = upstream * gain_vec
    inner_mean = jnp.mean(scaled * values, axis=-1, keepdims=True)
    through = inverse * scaled - values * inverse**3 * inner_mean
    gain_grad = jnp.sum(upstream * values * inverse, axis=0)
    return (through, gain_grad)


def attention_inputs(flat_in, qkv_full, gain_vec, cosine, sine_tab):
    row_count = flat_in.shape[0]
    group_size = H // KV
    normed, inverse = rms_norm(flat_in, gain_vec)
    normed = normed.astype(jnp.bfloat16)
    projected = jnp.dot(normed, qkv_full, preferred_element_type=jnp.float32)
    queries = rotate(projected[:, :D].reshape(row_count, H, HD), cosine, sine_tab, False)
    key_heads = rotate(
        projected[:, D : D + KV * HD].reshape(row_count, KV, HD), cosine, sine_tab, False
    )
    value_heads = projected[:, D + KV * HD :].reshape(row_count, KV, HD)
    key_wide = jnp.broadcast_to(key_heads[:, :, None], (row_count, KV, group_size, HD)).reshape(
        row_count, D
    )
    value_wide = jnp.broadcast_to(value_heads[:, :, None], (row_count, KV, group_size, HD)).reshape(
        row_count, D
    )
    stacked = jnp.stack([queries.reshape(row_count, D), key_wide, value_wide]).astype(jnp.bfloat16)
    return (normed, inverse, stacked)


def block_mask(seg_full, position, row_begin, finish):
    row_seg = seg_full[:, row_begin:finish]
    col_seg = seg_full[:, :finish]
    same_doc = row_seg[:, :, None] == col_seg[:, None, :]
    causal = position[row_begin:finish, None] >= position[None, :finish]
    return same_doc & causal[None]


def attention_forward(queries, key_heads, value_heads, seg_full, score_scale):
    length = queries.shape[1]
    block_rows = min(512, length)
    position = jnp.arange(length, dtype=jnp.int32)
    outputs = []
    lse_parts = []
    for block_num in range(length // block_rows):
        row_begin = block_num * block_rows
        finish = row_begin + block_rows
        scores = (
            jnp.einsum(
                "sqhd,skhd->shqk",
                queries[:, row_begin:finish],
                key_heads[:, :finish],
                preferred_element_type=jnp.float32,
            )
            * score_scale
        )
        allowed = block_mask(seg_full, position, row_begin, finish)
        scores = jnp.where(allowed[:, None], scores, MASKED)
        row_max = jnp.max(scores, axis=-1, keepdims=True)
        shifted = jnp.exp(scores - row_max)
        row_total = jnp.sum(shifted, axis=-1, keepdims=True)
        softmax_w = (shifted / row_total).astype(jnp.bfloat16)
        outputs.append(
            jnp.einsum(
                "shqk,skhd->sqhd",
                softmax_w,
                value_heads[:, :finish],
                preferred_element_type=jnp.float32,
            )
        )
        lse_parts.append(row_max + jnp.log(row_total))
    return (jnp.concatenate(outputs, axis=1), jnp.concatenate(lse_parts, axis=2))


def attention_backward(queries, key_heads, value_heads, seg_full, log_sums, grad_out, score_scale):
    length = queries.shape[1]
    block_rows = min(512, length)
    position = jnp.arange(length, dtype=jnp.int32)
    grad_query = []
    grad_key = jnp.zeros(key_heads.shape, jnp.float32)
    grad_value = jnp.zeros(value_heads.shape, jnp.float32)
    for block_num in range(length // block_rows):
        row_begin = block_num * block_rows
        finish = row_begin + block_rows
        query_rows = queries[:, row_begin:finish]
        grad_rows = grad_out[:, row_begin:finish]
        key_part = key_heads[:, :finish]
        value_part = value_heads[:, :finish]
        scores = (
            jnp.einsum("sqhd,skhd->shqk", query_rows, key_part, preferred_element_type=jnp.float32)
            * score_scale
        )
        allowed = block_mask(seg_full, position, row_begin, finish)
        softmax_f = jnp.where(
            allowed[:, None], jnp.exp(scores - log_sums[:, :, row_begin:finish]), 0.0
        )
        grad_probs = jnp.einsum(
            "sqhd,skhd->shqk", grad_rows, value_part, preferred_element_type=jnp.float32
        )
        row_delta = jnp.sum(softmax_f * grad_probs, axis=-1, keepdims=True)
        grad_scores = (softmax_f * (grad_probs - row_delta)).astype(jnp.bfloat16)
        grad_query.append(
            jnp.einsum("shqk,skhd->sqhd", grad_scores, key_part, preferred_element_type=jnp.float32)
            * score_scale
        )
        grad_key = grad_key.at[:, :finish].add(
            jnp.einsum(
                "shqk,sqhd->skhd", grad_scores, query_rows, preferred_element_type=jnp.float32
            )
            * score_scale
        )
        grad_value = grad_value.at[:, :finish].add(
            jnp.einsum(
                "shqk,sqhd->skhd",
                softmax_f.astype(jnp.bfloat16),
                grad_rows,
                preferred_element_type=jnp.float32,
            )
        )
    return (jnp.concatenate(grad_query, axis=1), grad_key, grad_value)


def body(tokens, segment_ids, selected, cotangent, w_qkv, w_out, w_gate_up, w_down, g_attn, g_mlp):
    streams, local_len, model_dim = tokens.shape
    sp_count = lax.axis_size("sp")
    sp_index = lax.axis_index("sp")
    row_count = streams * local_len
    group_size = H // KV
    kv_width = KV * HD
    score_scale = HD ** (-0.5)
    contract = (((0,), (0,)), ((), ()))
    seg_full = lax.all_gather(segment_ids, "sp", axis=1, tiled=True)
    first_count = jnp.sum((seg_full == 0).astype(jnp.int32), axis=1, keepdims=True)
    local_pos = (
        sp_index * local_len
        + jnp.arange(local_len, dtype=jnp.int32)[None, :]
        - segment_ids * first_count
    )
    cosine, sine_tab = rope_tables(local_pos.reshape(row_count), HD)
    shards = (w_qkv, w_out, w_gate_up, w_down, g_attn, g_mlp)
    gathered = (
        lax.all_gather(shards[0], "sp", axis=0, tiled=True),
        lax.all_gather(shards[1], "sp", axis=0, tiled=True),
        lax.all_gather(shards[2], "sp", axis=0, tiled=True),
        lax.all_gather(shards[3], "sp", axis=0, tiled=True),
        lax.all_gather(shards[4], "sp", axis=0, tiled=True),
        lax.all_gather(shards[5], "sp", axis=0, tiled=True),
    )
    qkv_full, out_full, gate_up_full, down_full, attn_gain, mlp_gain = gathered
    attn_gain = attn_gain.astype(jnp.float32)
    mlp_gain = mlp_gain.astype(jnp.float32)
    flat_in = tokens.reshape(row_count, model_dim).astype(jnp.float32)
    normed, inverse_one, stacked = attention_inputs(flat_in, qkv_full, attn_gain, cosine, sine_tab)
    head_view = lax.all_to_all(
        stacked.reshape(3, streams, local_len, model_dim),
        "sp",
        split_axis=3,
        concat_axis=2,
        tiled=True,
    )
    length = head_view.shape[2]
    heads_here = head_view.shape[3] // HD
    head_shape = (streams, length, heads_here, HD)
    queries = head_view[0].reshape(head_shape)
    key_heads = head_view[1].reshape(head_shape)
    value_heads = head_view[2].reshape(head_shape)
    attn_heads, log_sums = attention_forward(queries, key_heads, value_heads, seg_full, score_scale)
    attn_send = attn_heads.astype(jnp.bfloat16).reshape(streams, length, heads_here * HD)
    attn_tok = lax.all_to_all(attn_send, "sp", split_axis=1, concat_axis=2, tiled=True).reshape(
        row_count, model_dim
    )
    branch = jnp.dot(attn_tok, out_full, preferred_element_type=jnp.float32)
    residual = flat_in + branch
    inner_f, inverse_two = rms_norm(residual, mlp_gain)
    inner_in = inner_f.astype(jnp.bfloat16)
    gate_up = jnp.dot(inner_in, gate_up_full, preferred_element_type=jnp.float32)
    gate_part = gate_up[:, :FF]
    up_part = gate_up[:, FF:]
    sigmoid_g = jax.nn.sigmoid(gate_part)
    silu_gate = gate_part * sigmoid_g
    hidden = (silu_gate * up_part).astype(jnp.bfloat16)
    result = residual + jnp.dot(hidden, down_full, preferred_element_type=jnp.float32)
    output = result.astype(jnp.bfloat16).reshape(streams, local_len, model_dim)
    qkv_back, out_back, gate_up_back, down_back, attn_gain_b, mlp_gain_b = gathered
    attn_gain_b = attn_gain_b.astype(jnp.float32)
    mlp_gain_b = mlp_gain_b.astype(jnp.float32)
    grad_y = (cotangent * selected[:, :, None].astype(jnp.bfloat16)).reshape(row_count, model_dim)
    grad_hidden = jnp.dot(grad_y, down_back.T, preferred_element_type=jnp.float32)
    silu_slope = sigmoid_g * (1.0 + gate_part * (1.0 - sigmoid_g))
    grad_both = jnp.concatenate(
        [grad_hidden * up_part * silu_slope, grad_hidden * silu_gate], axis=1
    ).astype(jnp.bfloat16)
    grad_inner = jnp.dot(grad_both, gate_up_back.T, preferred_element_type=jnp.float32)
    grad_resid, gain_two = norm_back(residual, inverse_two, mlp_gain_b, grad_inner)
    grad_resid = grad_resid + grad_y.astype(jnp.float32)
    grad_branch = grad_resid.astype(jnp.bfloat16)
    grad_attn = jnp.dot(grad_branch, out_back.T, preferred_element_type=jnp.float32).astype(
        jnp.bfloat16
    )
    grad_view = lax.all_to_all(
        grad_attn.reshape(streams, local_len, model_dim),
        "sp",
        split_axis=2,
        concat_axis=1,
        tiled=True,
    )
    grad_view = grad_view.reshape(head_shape)
    grad_q, grad_k, grad_v = attention_backward(
        queries, key_heads, value_heads, seg_full, log_sums, grad_view, score_scale
    )
    back_send = (
        jnp.stack([grad_q, grad_k, grad_v])
        .astype(jnp.bfloat16)
        .reshape(3, streams, length, heads_here * HD)
    )
    returned = lax.all_to_all(back_send, "sp", split_axis=2, concat_axis=3, tiled=True)
    returned = returned.astype(jnp.float32).reshape(3, row_count, H, HD)
    grad_pq = rotate(returned[0], cosine, sine_tab, True).reshape(row_count, model_dim)
    key_summed = jnp.sum(returned[1].reshape(row_count, KV, group_size, HD), axis=2)
    grad_pk = rotate(key_summed, cosine, sine_tab, True).reshape(row_count, kv_width)
    grad_pv = jnp.sum(returned[2].reshape(row_count, KV, group_size, HD), axis=2).reshape(
        row_count, kv_width
    )
    grad_mixed = jnp.concatenate(
        [grad_pq.astype(jnp.bfloat16), grad_pk.astype(jnp.bfloat16), grad_pv.astype(jnp.bfloat16)],
        axis=1,
    )
    grad_normed = jnp.dot(grad_mixed, qkv_back.T, preferred_element_type=jnp.float32)
    grad_in, gain_one = norm_back(flat_in, inverse_one, attn_gain_b, grad_normed)
    grad_in = grad_in + grad_resid
    grad_tokens = grad_in.astype(jnp.bfloat16).reshape(streams, local_len, model_dim)
    gain_totals = lax.psum((gain_one, gain_two), ("dp", "sp"))
    gain_share = model_dim // sp_count
    grad_g_attn = lax.dynamic_slice_in_dim(gain_totals[0], sp_index * gain_share, gain_share, 0)
    grad_g_mlp = lax.dynamic_slice_in_dim(gain_totals[1], sp_index * gain_share, gain_share, 0)
    row_sums = lax.psum_scatter(
        jnp.concatenate(
            [
                lax.dot_general(normed, grad_mixed, contract, preferred_element_type=jnp.float32),
                lax.dot_general(
                    attn_tok, grad_branch, contract, preferred_element_type=jnp.float32
                ),
                lax.dot_general(inner_in, grad_both, contract, preferred_element_type=jnp.float32),
            ],
            axis=1,
        ).astype(jnp.bfloat16),
        "sp",
        scatter_dimension=0,
        tiled=True,
    )
    down_sums = lax.psum_scatter(
        lax.dot_general(hidden, grad_y, contract, preferred_element_type=jnp.float32).astype(
            jnp.bfloat16
        ),
        "sp",
        scatter_dimension=0,
        tiled=True,
    )
    weight_rows, down_rows = (
        lax.psum(row_sums, "dp").astype(jnp.float32),
        lax.psum(down_sums, "dp").astype(jnp.float32),
    )
    qkv_cols = model_dim + 2 * kv_width
    grad_w_qkv = weight_rows[:, :qkv_cols]
    grad_w_out = weight_rows[:, qkv_cols : qkv_cols + model_dim]
    grad_w_gate_up = weight_rows[:, qkv_cols + model_dim :]
    return (
        output,
        grad_tokens,
        grad_w_qkv,
        grad_w_out,
        grad_w_gate_up,
        down_rows,
        grad_g_attn,
        grad_g_mlp,
    )


def solution(mesh):
    in_specs = (
        P("dp", "sp", None),
        P("dp", "sp"),
        P("dp", "sp"),
        P("dp", "sp", None),
        P("sp", None),
        P("sp", None),
        P("sp", None),
        P("sp", None),
        P("sp"),
        P("sp"),
    )
    out_specs = (
        P("dp", "sp", None),
        P("dp", "sp", None),
        P("sp", None),
        P("sp", None),
        P("sp", None),
        P("sp", None),
        P("sp"),
        P("sp"),
    )
    return jax.shard_map(body, mesh=mesh, in_specs=in_specs, out_specs=out_specs, check_vma=False)
```

profile of v0, /device:TPU:0, one launch (start us, length us, event | category | flops | bytes accessed | tf_op | source)
XLA Modules:
  0.0 2288.6 jit_solution(2649510872672990549)
XLA Ops:
  32.8 43.1 %all-gather.7.cloned.1.call-done = bf16[2048,2560]{1,0:T(8,128)(2,1)} async-done(((bf16[256,2560]{1,0:T(8,128)(2,1)}), bf16[2048,2560]{1,0:T(8,128)(2,1)}) %all-gather.7.cloned.1.call-update) | async-done | bytes 10485776 | tf_op jit(solution)/shard_map/all_gather | solution.py:184
  97.0 27.3 %copy.137 = bf16[3,1,512,2048]{2,0,1,3:T(4,128)(2,1)} copy(bf16[3,1,512,2048]{2,3,1,0:T(8,128)(2,1)S(1)} %pad_maximum_fusion.5) | data formatting | bytes 12582912 | tf_op jit(solution)/shard_map/stack | solution.py:69
  145.4 140.0 %all-to-all-done = bf16[3,1,512,2048]{2,0,1,3:T(4,128)(2,1)} async-done(((bf16[3,1,512,2048]{2,0,1,3:T(4,128)(2,1)}), bf16[3,1,512,2048]{2,0,1,3:T(4,128)(2,1)}, u32[]{:S(2)}, u32[]{:S(2)}) %all-to-all-start) | async-done | bytes 6291488 | tf_op jit(solution)/shard_map/all_to_all | solution.py:196
  402.3 12.1 select_reduce_fusion.2
  414.5 12.5 fusion.2
  427.0 14.7 fusion.178
  442.9 14.1 select_reduce_fusion.1
  456.9 13.6 fusion.1
  470.6 18.3 fusion.179
  490.0 15.5 select_reduce_fusion
  505.5 15.3 fusion
  520.9 16.1 fusion.180
  550.4 22.0 reduce.89
  579.3 29.5 %all-gather.1 = bf16[8,1,256]{2,1,0:T(2,128)(2,1)S(1)} all-gather(bf16[1,1,256]{2,1,0:T(2,128)(2,1)S(1)} %reshape.2359), channel_id=1, replica_groups=mesh['dp'=4,'sp'=8] {'sp'}, dimensions={0}, use_global_device_ids=true | all-gather | bytes 4608 | tf_op jit(solution)/shard_map/all_gather | solution.py:189
  623.0 11.3 multiply_reduce_fusion.10
  634.4 33.2 %fusion.255 = f32[512,11264]{1,0:T(8,128)} fusion(bf16[2048,11264]{1,0:T(8,128)(2,1)} %all-gather.11.cloned.1.call-done, f32[512,2048]{1,0:T(8,128)} %get-tuple-element.273, f32[2048]{0:T(1024)S(1)} %bitcast.582, f32[512]{0:T(512)S(1)} %get-tuple-element.255), kind=kOutput, calls=%fused_computation.388 | convolution fusion | flops 23625465856 | bytes 73410560 | tf_op jit(solution)/shard_map/dot_general | solution.py:218
  667.6 26.8 %multiply_convert_fusion.7 = (bf16[512,5632]{1,0:T(8,128)(2,1)}, bf16[512,5632]{1,0:T(8,128)(2,1)}, bf16[512,5632]{1,0:T(8,128)(2,1)}) fusion(f32[512,11264]{1,0:T(8,128)} %fusion.255, bf16[5632,2048]{1,0:T(8,128)(2,1)} %all-gather.13.cloned.1.call-done, bf16[1,512,2048]{2,1,0:T(8,128)(2,1)S(1)} %copy-done.55, bf16[512]{0:T(512)(128)(2,1)S(1)} %convert_reduce_fusion), kind=kOutput, calls=%fused_computation.59 | convolution fusion | flops 11855462400 | bytes 65537024 | tf_op jit(solution)/shard_map/dot_general | solution.py:230
  694.4 34.8 %multiply_reduce_fusion.7 = (f32[2048]{0:T(1024)}, f32[512]{0:T(512)S(1)}, f32[512,2048]{1,0:T(8,128)}) fusion(f32[512,2048]{1,0:T(8,128)} %get-tuple-element.273, f32[512]{0:T(512)S(1)} %get-tuple-element.255, f32[2048]{0:T(1024)S(1)} %bitcast.583, bf16[2048,11264]{1,0:T(8,128)(2,1)} %all-gather.11.cloned.1.call-done, ...), kind=kOutput, calls=%fused_computation.124 | convolution fusion | flops 23651678208 | bytes 66080768 | tf_op jit(solution)/shard_map/dot_general | solution.py:235
  751.2 14.3 reduce.90
  773.0 19.9 convolution_convert_fusion.1
  856.2 13.6 multiply_reduce_fusion.4
  869.8 12.0 fusion.127
  881.8 15.7 multiply_reduce_fusion.3
  897.5 11.3 fusion.94
  908.8 22.2 multiply_reduce_fusion.2
  931.1 14.5 fusion.100
  945.6 22.4 multiply_reduce_fusion.1
  968.0 15.6 fusion.49
  994.9 17.0 fusion.61
  1037.4 11.0 multiply_convert_fusion.4
  1055.8 21.0 multiply_convert_fusion.3
  1085.8 16.3 multiply_convert_fusion.2
  1121.7 25.4 %multiply_convert_fusion.1 = bf16[4,512,3584]{2,1,0:T(8,128)(2,1)} fusion(f32[4,512,3584]{2,1,0:T(8,128)} %get-tuple-element.288, f32[4,512,3584]{2,1,0:T(8,128)} %get-tuple-element.269, f32[4,512]{1,0:T(4,128)S(1)} %get-tuple-element.287, f32[4,512]{1,0:T(4,128)S(1)} %copy-done.61, pred[512,3584]{1,0:T(8,128)(4,1)} %compare_and_fusion), kind=kLoop, calls=%fused_computation.8 | loop fusion | flops 44040192 | bytes 75251712 | tf_op jit(solution)/shard_map/convert_element_type | solution.py:143
  1155.2 26.1 %multiply_reduce_fusion = (f32[4,512]{1,0:T(4,128)S(1)}, f32[4,512,4096]{2,1,0:T(8,128)}) fusion(f32[4,512,4096]{2,1,0:T(8,128)} %get-tuple-element.271, f32[4,512]{1,0:T(4,128)S(1)} %copy-done.60, pred[512,4096]{1,0:T(8,128)(4,1)S(1)} %copy-done.8, bf16[4096,4,64]{0,2,1:T(8,128)(2,1)S(1)} %copy-done.37, bf16[1,4096,4,64]{1,3,2,0:T(8,128)(2,1)} %reshape.2337), kind=kOutput, calls=%fused_computation.3 | convolution fusion | flops 1115682816 | bytes 71581696 | tf_op jit(solution)/shard_map/sqhd,skhd->shqk/dot_general | solution.py:139
  1181.3 27.6 %multiply_convert_fusion = bf16[4,512,4096]{2,1,0:T(8,128)(2,1)} fusion(f32[4,512,4096]{2,1,0:T(8,128)} %get-tuple-element.290, f32[4,512,4096]{2,1,0:T(8,128)} %get-tuple-element.271, f32[4,512]{1,0:T(4,128)S(1)} %get-tuple-element.289, f32[4,512]{1,0:T(4,128)S(1)} %copy-done.60, pred[512,4096]{1,0:T(8,128)(4,1)S(1)} %copy-done.8), kind=kLoop, calls=%fused_computation.2 | loop fusion | flops 50331648 | bytes 85999616 | tf_op jit(solution)/shard_map/convert_element_type | solution.py:143
  1208.9 11.4 fusion.60
  1264.7 11.1 fusion.196
  1275.8 11.8 fusion.186
  1297.6 16.9 pad_maximum_fusion.2
  1328.8 12.3 copy.166
  1341.1 33.0 %convolution_convert_fusion = bf16[2048,11264]{1,0:T(8,128)(2,1)} fusion(bf16[512,5632]{1,0:T(8,128)(2,1)} %get-tuple-element.225, bf16[512,5632]{1,0:T(8,128)(2,1)} %get-tuple-element.224, f32[512,2048]{1,0:T(8,128)} %get-tuple-element.273, f32[2048]{0:T(1024)S(1)} %bitcast.585, f32[512]{0:T(512)S(1)} %copy-done.100), kind=kOutput, calls=%fused_computation.1 | convolution fusion | flops 23671603200 | bytes 61876224 | tf_op jit(solution)/shard_map/dot_general | solution.py:285
  1374.1 39.7 %all-to-all-done.3 = bf16[3,1,4096,256]{3,0,1,2:T(4,128)(2,1)} async-done(((bf16[3,1,4096,256]{3,0,1,2:T(4,128)(2,1)}), bf16[3,1,4096,256]{3,0,1,2:T(4,128)(2,1)}, u32[]{:S(2)}, u32[]{:S(2)}) %all-to-all-start.3) | async-done | bytes 6291488 | tf_op jit(solution)/shard_map/all_to_all | solution.py:258
  1469.5 43.0 %pad_maximum_fusion = bf16[2048,15872]{1,0:T(8,128)(2,1)} fusion(bf16[2048,11264]{1,0:T(8,128)(2,1)} %convolution_convert_fusion, bf16[2048,2048]{1,0:T(8,128)(2,1)} %copy.166, bf16[2048,2560]{1,0:T(8,128)(2,1)} %convolution_convert_fusion.2), kind=kLoop, calls=%fused_computation | loop fusion | flops 195035136 | bytes 130023424 | tf_op jit(solution)/shard_map/concatenate | solution.py:279
  1512.7 373.4 %reduce-scatter.3.cloned.1.call-done = bf16[256,15872]{1,0:T(8,128)(2,1)} async-done(((bf16[2048,15872]{1,0:T(8,128)(2,1)}), bf16[256,15872]{1,0:T(8,128)(2,1)}) %reduce-scatter.3.cloned.1.call-update) | async-done | bytes 8126480 | tf_op jit(solution)/shard_map/reduce_scatter | solution.py:278
  1886.1 19.9 fusion.104
  1906.0 11.9 fusion.74
  1917.9 44.7 %all-reduce.2 = (f32[2048]{0:T(1024)S(1)}, f32[2048]{0:T(1024)S(1)}) all-reduce(f32[2048]{0:T(1024)S(1)} %get-tuple-element.218, f32[2048]{0:T(1024)S(1)} %copy-done.102), channel_id=1, replica_groups=mesh['dp'=4,'sp'=8] {'dp','sp'}, use_global_device_ids=true, to_apply=%region_36.37 | all-reduce | flops 4096 | bytes 32768 | tf_op jit(solution)/shard_map/psum | solution.py:274
  1970.1 295.6 %all-reduce.6.cloned.1.call-done = (bf16[256,15872]{1,0:T(8,128)(2,1)}, bf16[704,2048]{1,0:T(8,128)(2,1)}) async-done(((bf16[256,15872]{1,0:T(8,128)(2,1)}, bf16[704,2048]{1,0:T(8,128)(2,1)}), (bf16[256,15872]{1,0:T(8,128)(2,1)}, bf16[704,2048]{1,0:T(8,128)(2,1)})) %all-reduce.6.cloned.1.call-update) | async-done | bytes 11010064 | tf_op jit(solution)/shard_map/psum | solution.py:302
  (452 shorter events, 541.2 us)
Async XLA Ops:
  7.2 68.7 %all-gather.7.cloned.1.call-start = ((), (), s32[]{:S(2)}) async-start(), calls=%async_computation.6 | async-start | bytes 11796480 | tf_op jit(solution)/shard_map/all_gather | solution.py:184
  7.9 615.1 %all-gather.9.cloned.1.call-start = ((), (), s32[]{:S(2)}) async-start(), calls=%async_computation.7 | async-start | bytes 9437184 | tf_op jit(solution)/shard_map/all_gather | solution.py:185
  8.7 625.7 %all-gather.11.cloned.1.call-start = ((), (), s32[]{:S(2)}) async-start(), calls=%async_computation.8 | async-start | bytes 51904512 | tf_op jit(solution)/shard_map/all_gather | solution.py:186
  9.4 658.2 %all-gather.13.cloned.1.call-start = ((), (), s32[]{:S(2)}) async-start(), calls=%async_computation.9 | async-start | bytes 25952256 | tf_op jit(solution)/shard_map/all_gather | solution.py:187
  22.2 62.0 %copy-start.104 = (f32[512]{0:T(512)}, f32[512]{0:T(512)S(1)}, u32[]{:S(2)}) copy-start(f32[512]{0:T(512)S(1)} %get-tuple-element.253) | copy-start | bytes 6148
  31.1 53.2 %copy-start.96 = (f32[8,1,256]{2,1,0:T(1,128)}, f32[8,1,256]{2,1,0:T(1,128)S(1)}, u32[]{:S(2)}) copy-start(f32[8,1,256]{2,1,0:T(1,128)S(1)} %convert_element_type.283) | copy-start | bytes 24580
  32.8 62.7 %copy-start.56 = (f32[512,32]{0,1:T(8,128)}, f32[512,32]{0,1:T(8,128)S(1)}, u32[]{:S(2)}) copy-start(f32[512,32]{0,1:T(8,128)S(1)} %get-tuple-element.251) | copy-start | bytes 196612
  124.3 161.0 %all-to-all-start = ((bf16[3,1,512,2048]{2,0,1,3:T(4,128)(2,1)}), bf16[3,1,512,2048]{2,0,1,3:T(4,128)(2,1)}, u32[]{:S(2)}, u32[]{:S(2)}) async-start(bf16[3,1,512,2048]{2,0,1,3:T(4,128)(2,1)} %copy.137), calls=%async_computation | async-start | bytes 16777216 | tf_op jit(solution)/shard_map/all_to_all | solution.py:196
  134.5 228.1 %copy-start.26 = (pred[512,2048]{1,0:T(8,128)(4,1)}, pred[512,2048]{1,0:T(8,128)(4,1)S(1)}, u32[]{:S(2)}) copy-start(pred[512,2048]{1,0:T(8,128)(4,1)S(1)} %compare_and_fusion.3) | copy-start | bytes 3145732
  306.9 95.3 %copy-start.12 = (bf16[1,4096,4,64]{1,3,2,0:T(8,128)(2,1)}, bf16[1,4096,4,64]{1,3,2,0:T(8,128)(2,1)S(1)}, u32[]{:S(2)}) copy-start(bf16[1,4096,4,64]{1,3,2,0:T(8,128)(2,1)S(1)} %reshape_squeeze.17) | copy-start | bytes 6291460
  470.6 19.4 copy-start.7
  520.8 17.3 copy-start.48
  520.8 18.6 copy-start.49
  572.4 36.5 %copy-start.75 = (f32[4,512]{1,0:T(4,128)S(1)}, f32[4,512]{1,0:T(4,128)}, u32[]{:S(2)}) copy-start(f32[4,512]{1,0:T(4,128)} %copy-done.74) | copy-start | bytes 24580
  572.4 36.5 %copy-start.77 = (f32[4,512]{1,0:T(4,128)S(1)}, f32[4,512]{1,0:T(4,128)}, u32[]{:S(2)}) copy-start(f32[4,512]{1,0:T(4,128)} %copy-done.76) | copy-start | bytes 24580
  572.4 37.1 %copy-start.93 = (f32[4,512]{1,0:T(4,128)S(1)}, f32[4,512]{1,0:T(4,128)}, u32[]{:S(2)}) copy-start(f32[4,512]{1,0:T(4,128)} %copy-done.92) | copy-start | bytes 24580
  572.4 37.1 %copy-start.95 = (f32[4,512]{1,0:T(4,128)S(1)}, f32[4,512]{1,0:T(4,128)}, u32[]{:S(2)}) copy-start(f32[4,512]{1,0:T(4,128)} %copy-done.94) | copy-start | bytes 24580
  572.4 37.7 %copy-start.79 = (f32[4,512]{1,0:T(4,128)S(1)}, f32[4,512]{1,0:T(4,128)}, u32[]{:S(2)}) copy-start(f32[4,512]{1,0:T(4,128)} %copy-done.78) | copy-start | bytes 24580
  572.4 37.7 %copy-start.81 = (f32[4,512]{1,0:T(4,128)S(1)}, f32[4,512]{1,0:T(4,128)}, u32[]{:S(2)}) copy-start(f32[4,512]{1,0:T(4,128)} %copy-done.80) | copy-start | bytes 24580
  572.4 38.3 %copy-start.70 = (f32[4,512]{1,0:T(4,128)S(1)}, f32[4,512]{1,0:T(4,128)}, u32[]{:S(2)}) copy-start(f32[4,512]{1,0:T(4,128)} %copy-done.69) | copy-start | bytes 24580
  572.4 38.3 %copy-start.72 = (f32[4,512]{1,0:T(4,128)S(1)}, f32[4,512]{1,0:T(4,128)}, u32[]{:S(2)}) copy-start(f32[4,512]{1,0:T(4,128)} %copy-done.71) | copy-start | bytes 24580
  572.5 38.9 %copy-start.83 = (f32[4,512]{1,0:T(4,128)S(1)}, f32[4,512]{1,0:T(4,128)}, u32[]{:S(2)}) copy-start(f32[4,512]{1,0:T(4,128)} %copy-done.82) | copy-start | bytes 24580
  572.5 38.9 %copy-start.85 = (f32[4,512]{1,0:T(4,128)S(1)}, f32[4,512]{1,0:T(4,128)}, u32[]{:S(2)}) copy-start(f32[4,512]{1,0:T(4,128)} %copy-done.84) | copy-start | bytes 24580
  572.5 39.5 %copy-start.87 = (f32[4,512]{1,0:T(4,128)S(1)}, f32[4,512]{1,0:T(4,128)}, u32[]{:S(2)}) copy-start(f32[4,512]{1,0:T(4,128)} %copy-done.86) | copy-start | bytes 24580
  572.5 39.5 %copy-start.89 = (f32[4,512]{1,0:T(4,128)S(1)}, f32[4,512]{1,0:T(4,128)}, u32[]{:S(2)}) copy-start(f32[4,512]{1,0:T(4,128)} %copy-done.88) | copy-start | bytes 24580
  575.7 38.1 %all-to-all-start.1 = ((bf16[8,2,65536]{2,1,0:T(2,128)(2,1)}), bf16[8,2,65536]{2,1,0:T(2,128)(2,1)S(1)}, u32[]{:S(2)}, u32[]{:S(2)}) async-start(bf16[8,2,65536]{2,1,0:T(2,128)(2,1)} %reshape.2367), calls=%async_computation.1 | async-start | bytes 4194304 | tf_op jit(solution)/shard_map/all_to_all | solution.py:211
  608.9 120.3 %copy-start.90 = (f32[8,1,256]{2,1,0:T(1,128)}, f32[8,1,256]{2,1,0:T(1,128)S(1)}, u32[]{:S(2)}) copy-start(f32[8,1,256]{2,1,0:T(1,128)S(1)} %convert_element_type.284) | copy-start | bytes 24580
  634.4 94.8 %copy-start.99 = (f32[512]{0:T(512)}, f32[512]{0:T(512)S(1)}, u32[]{:S(2)}) copy-start(f32[512]{0:T(512)S(1)} %get-tuple-element.255) | copy-start | bytes 6148
  634.4 33.2 %copy-start.55 = (bf16[1,512,2048]{2,1,0:T(8,128)(2,1)S(1)}, bf16[1,512,2048]{2,1,0:T(8,128)(2,1)}, u32[]{:S(2)}) copy-start(bf16[1,512,2048]{2,1,0:T(8,128)(2,1)} %param.49) | copy-start | bytes 6291460
  769.3 30.2 %all-to-all-start.2 = ((bf16[8,2,65536]{2,1,0:T(2,128)(2,1)}), bf16[8,2,65536]{2,1,0:T(2,128)(2,1)S(1)}, u32[]{:S(2)}, u32[]{:S(2)}) async-start(bf16[8,2,65536]{2,1,0:T(2,128)(2,1)} %reshape.2369), calls=%async_computation.2 | async-start | bytes 4194304 | tf_op jit(solution)/shard_map/all_to_all | solution.py:242
  772.9 739.7 %reduce-scatter.5.cloned.1.call-start = ((), (), s32[]{:S(2)}) async-start(), calls=%async_computation.11 | async-start | bytes 25952256 | tf_op jit(solution)/shard_map/reduce_scatter | solution.py:293
  994.9 17.0 copy-start.36
  994.9 17.0 copy-start.63
  994.9 17.0 copy-start.68
  1021.4 15.9 slice-start.9
  1055.8 30.0 %slice-start = ((s8[25165824]{0:T(1024)(128)(4,1)}), s8[4194304]{0:T(1024)(128)(4,1)S(1)}, s32[]{:S(2)}) async-start(s8[25165824]{0:T(1024)(128)(4,1)} %bitcast.536), calls=%async_computation.13 | async-start | bytes 8388608
  1055.8 30.0 %slice-start.1 = ((s8[25165824]{0:T(1024)(128)(4,1)}), s8[4194304]{0:T(1024)(128)(4,1)S(1)}, s32[]{:S(2)}) async-start(s8[25165824]{0:T(1024)(128)(4,1)} %bitcast.536), calls=%async_computation.14 | async-start | bytes 8388608
  1055.8 30.0 %slice-start.2 = ((s8[25165824]{0:T(1024)(128)(4,1)}), s8[4194304]{0:T(1024)(128)(4,1)S(1)}, s32[]{:S(2)}) async-start(s8[25165824]{0:T(1024)(128)(4,1)} %bitcast.536), calls=%async_computation.15 | async-start | bytes 8388608
  1055.8 30.0 %slice-start.3 = ((s8[25165824]{0:T(1024)(128)(4,1)}), s8[4194304]{0:T(1024)(128)(4,1)S(1)}, s32[]{:S(2)}) async-start(s8[25165824]{0:T(1024)(128)(4,1)} %bitcast.536), calls=%async_computation.16 | async-start | bytes 8388608
  1055.8 30.0 %slice-start.4 = ((s8[25165824]{0:T(1024)(128)(4,1)}), s8[4194304]{0:T(1024)(128)(4,1)S(1)}, s32[]{:S(2)}) async-start(s8[25165824]{0:T(1024)(128)(4,1)} %bitcast.536), calls=%async_computation.17 | async-start | bytes 8388608
  1121.7 25.4 %copy-start.5 = (f32[1,4096,4,64]{1,3,2,0:T(8,128)S(1)}, f32[1,4096,4,64]{1,3,2,0:T(8,128)}, u32[]{:S(2)}) copy-start(f32[1,4096,4,64]{1,3,2,0:T(8,128)} %fusion.90) | copy-start | bytes 12582916
  1155.2 26.1 %copy-start.6 = (f32[1,4096,4,64]{1,3,2,0:T(8,128)}, f32[1,4096,4,64]{1,3,2,0:T(8,128)S(1)}, u32[]{:S(2)}) copy-start(f32[1,4096,4,64]{1,3,2,0:T(8,128)S(1)} %fusion.42) | copy-start | bytes 12582916
  1238.0 20.6 slice-start.6
  1314.6 99.2 %all-to-all-start.3 = ((bf16[3,1,4096,256]{3,0,1,2:T(4,128)(2,1)}), bf16[3,1,4096,256]{3,0,1,2:T(4,128)(2,1)}, u32[]{:S(2)}, u32[]{:S(2)}) async-start(bf16[3,1,4096,256]{3,0,1,2:T(4,128)(2,1)} %pad_maximum_fusion.2), calls=%async_computation.3 | async-start | bytes 16777216 | tf_op jit(solution)/shard_map/all_to_all | solution.py:258
  1319.7 566.3 %reduce-scatter.3.cloned.1.call-start = ((), (), s32[]{:S(2)}) async-start(), calls=%async_computation.10 | async-start | bytes 73138176 | tf_op jit(solution)/shard_map/reduce_scatter | solution.py:278
  1512.6 753.2 %all-reduce.6.cloned.1.call-start = ((), (), s32[]{:S(2)}) async-start(), calls=%async_computation.12 | async-start | bytes 22020096 | tf_op jit(solution)/shard_map/psum | solution.py:302
  1886.1 19.9 copy-start.47
  1906.0 57.9 %copy-start.103 = (f32[512]{0:T(512)S(1)}, f32[512]{0:T(512)}, u32[]{:S(2)}) copy-start(f32[512]{0:T(512)} %get-tuple-element.252) | copy-start | bytes 6148
  (90 other events, 685.6 us)
Sparse Core Ops, SparseCore 0:
  9.9 65.9 all-gather.6
  77.8 54.9 all-gather.8
  134.7 285.5 all-gather.10
  422.0 116.4 all-gather.12
  793.0 147.3 reduce-scatter.4
  1512.7 373.2 reduce-scatter.2
  1888.7 377.0 all-reduce.5
where the time goes:
time: 2300 us; the launch traced here: 2290 us
  waiting for transfers between devices  901 us (39%)
  matrix products  681 us (30%)
  other arithmetic  336 us (15%)
  local copies, waits for them, and re-layouts  242 us (11%)
  blocking collectives  93.5 us (4%)
    reduce_scatter x1, waiting for transfers between devices, body(): lax.psum_scatter(jnp.concatenate([lax.dot_general(normed, grad_mixed, con...  373 us
    psum x1, waiting for transfers between devices, body(): lax.psum(row_sums, 'dp').astype(jnp.float32)  296 us
    all_to_all x1, waiting for transfers between devices, body(): lax.all_to_all(stacked.reshape(3, streams, local_len, model_dim), 'sp', s...  140 us
    dot_general x8, matrix products, attention_backward(): jnp.einsum('sqhd,skhd->shqk', grad_rows, value_part, preferred_element_ty...  124 us
    convert_element_type x8, other arithmetic, attention_backward(): grad_scores = (softmax_f * (grad_probs - row_delta)).astype(jnp.bfloat16)  124 us
    dot_general x8, matrix products, attention_backward(): jnp.einsum('shqk,sqhd->skhd', softmax_f.astype(jnp.bfloat16), grad_rows,...  84.6 us
    dot_general x8, matrix products, attention_forward(): jnp.einsum('shqk,skhd->sqhd', softmax_w, value_heads[:, :finish], preferr...  77.3 us
    dot_general x8, matrix products, attention_forward(): jnp.einsum('sqhd,skhd->shqk', queries[:, row_begin:finish], key_heads[:,...  60.1 us
  transfers between devices with their start and end apart: 11, of which 6 were waited for; matrix products, arithmetic and copies ran while one was open for 49% of the time, Pallas kernels for 0%

commit v1 on v0

--- a/solution.py
+++ b/solution.py
@@ -1,6 +1,11 @@
+import functools
+import math
+
 import jax
 import jax.numpy as jnp
 from jax import lax
+from jax.experimental import pallas as pl
+from jax.experimental.pallas import tpu as pltpu
 from jax.sharding import PartitionSpec as P
 
 D = 2048
@@ -162,7 +167,7 @@
     return (jnp.concatenate(grad_query, axis=1), grad_key, grad_value)
 
 
-def body(tokens, segment_ids, selected, cotangent, w_qkv, w_out, w_gate_up, w_down, g_attn, g_mlp):
+def general_body(tokens, segment_ids, selected, cotangent, w_qkv, w_out, w_gate_up, w_down, g_attn, g_mlp):
     streams, local_len, model_dim = tokens.shape
     sp_count = lax.axis_size("sp")
     sp_index = lax.axis_index("sp")
@@ -318,6 +323,632 @@
     )
 
 
+CHIPS = 4
+EXTRA = 128
+BLOCK = 512
+LOG2E = math.log2(math.e)
+BF = jnp.bfloat16
+F32 = jnp.float32
+NT = (((1,), (1,)), ((), ()))
+TN = (((0,), (0,)), ((), ()))
+
+
+def swap_pairs(even_mask, odd_mask):
+    return [(i, i ^ (odd_mask if i & 1 else even_mask)) for i in range(2 * CHIPS)]
+
+
+FIRST = swap_pairs(2, 4)
+SECOND = swap_pairs(4, 2)
+SIBLING = swap_pairs(1, 1)
+SAME_CORE = [[0, 2, 4, 6], [1, 3, 5, 7]]
+
+
+def send_first(x):
+    return lax.ppermute(x, "sp", FIRST)
+
+
+def send_second(x):
+    return lax.ppermute(x, "sp", SECOND)
+
+
+def send_sibling(x):
+    return lax.ppermute(x, "sp", SIBLING)
+
+
+def after(value, *others):
+    return lax.optimization_barrier((value,) + others)[0]
+
+
+def gather_chips(own):
+    first = send_first(own)
+    second = send_second(after(own, first))
+    far = send_second(after(first, second))
+    return [own, first, second, far]
+
+
+def rel_masks(core):
+    first = jnp.where(core == 0, 2, 4)
+    return first, 6 - first
+
+
+def gather_plane(shard, me):
+    core = me & 1
+    first, second = rel_masks(core)
+    mine = gather_chips(shard)
+    theirs = [send_sibling(part) for part in mine]
+    places = [me, me ^ first, me ^ second, me ^ 6]
+    other = me ^ 1
+    places += [other, other ^ second, other ^ first, other ^ 6]
+    out = jnp.zeros((2 * CHIPS,) + shard.shape, shard.dtype)
+    for part, place in zip(mine + theirs, places):
+        out = lax.dynamic_update_slice_in_dim(out, part[None], place, 0)
+    return out
+
+
+def pick(parts, index):
+    return lax.dynamic_index_in_dim(parts, index, 0, keepdims=False)
+
+
+def line_scatter(parts):
+    planes = parts.shape[0]
+    z = lax.axis_index("dp")
+    right = left = None
+    for step in range(1, planes):
+        ahead = pick(parts, jnp.clip(planes - step + z, 0, planes - 1))
+        back = pick(parts, jnp.clip(z - planes + step, 0, planes - 1))
+        if right is not None:
+            ahead = (ahead.astype(F32) + right.astype(F32)).astype(BF)
+            back = (back.astype(F32) + left.astype(F32)).astype(BF)
+        right = lax.ppermute(ahead, "dp", [(i, i + 1) for i in range(step)])
+        left = lax.ppermute(back, "dp", [(planes - 1 - i, planes - 2 - i) for i in range(step)])
+    return (pick(parts, z).astype(F32) + right.astype(F32) + left.astype(F32)).astype(BF)
+
+
+def line_gather(own):
+    planes = lax.axis_size("dp")
+    z = lax.axis_index("dp")
+    rights, lefts = [own], [own]
+    for step in range(1, planes):
+        rights.append(lax.ppermute(rights[-1], "dp", [(i, i + 1) for i in range(step - 1, planes - 1)]))
+        lefts.append(lax.ppermute(lefts[-1], "dp", [(i + 1, i) for i in range(planes - step)]))
+    out = jnp.zeros((planes,) + own.shape, own.dtype)
+    out = lax.dynamic_update_slice_in_dim(out, own[None], z, 0)
+    for step in range(1, planes):
+        block = jnp.where(z >= step, rights[step], lefts[planes - step])
+        out = lax.dynamic_update_slice_in_dim(out, block[None], (z - step) % planes, 0)
+    return out
+
+
+def line_sum(rows):
+    planes = lax.axis_size("dp")
+    count, width = rows.shape
+    return line_gather(line_scatter(rows.reshape(planes, count // planes, width))).reshape(count, width)
+
+
+def scatter_chips(parts):
+    own, first, second, far = parts
+    got_first = send_first(first.astype(BF))
+    got_far = send_first(far.astype(BF))
+    passed = (second.astype(F32) + got_far.astype(F32)).astype(BF)
+    return own.astype(F32) + got_first.astype(F32) + send_second(passed).astype(F32)
+
+
+def scatter_plane(parts, me):
+    core = me & 1
+    chip = me // 2
+    first, second = rel_masks(core)
+    split = parts.reshape((CHIPS, 2) + parts.shape[1:])
+    got = send_sibling(lax.dynamic_index_in_dim(split, 1 - core, 1, keepdims=False))
+    kept = lax.dynamic_index_in_dim(split, core, 1, keepdims=False)
+
+    def part(place):
+        return pick(kept, place).astype(F32) + pick(got, place).astype(F32)
+
+    return scatter_chips([part(chip), part(chip ^ (first // 2)), part(chip ^ (second // 2)), part(chip ^ 3)])
+
+
+def spread_kernel(in_ref, out_ref):
+    planes, _, rows, width = in_ref.shape
+    out_ref[...] = in_ref[...].reshape(planes * rows, width).astype(F32)
+
+
+def spread(parts, columns):
+    planes, chips, rows, both = parts.shape
+    return pl.pallas_call(
+        spread_kernel,
+        grid=(2 * chips,),
+        in_specs=[pl.BlockSpec((planes, 1, rows, both // 2), lambda i: (0, i % chips, 0, i // chips))],
+        out_specs=pl.BlockSpec((planes * rows, both // 2), lambda i: (0, i)),
+        out_shape=jax.ShapeDtypeStruct((planes * rows, columns), F32),
+        compiler_params=pltpu.CompilerParams(vmem_limit_bytes=32 * 2**20),
+        cost_estimate=pl.CostEstimate(flops=0, bytes_accessed=18 * 10**6, transcendentals=0),
+        name="spread",
+    )(parts)
+
+
+def swap_halves(values):
+    width = values.shape[-1]
+    lane = lax.broadcasted_iota(jnp.int32, values.shape, 1)
+    ahead = pltpu.roll(values, width - HD // 2, 1)
+    behind = pltpu.roll(values, HD // 2, 1)
+    return jnp.where(lane % HD < HD // 2, ahead, behind)
+
+
+def project_kernel(x_ref, gain_ref, cos_ref, sin_ref, wq_ref, wkv_ref, send_ref, normed_ref, inv_ref, normed_scr):
+    step = pl.program_id(0)
+
+    @pl.when(step == 0)
+    def _():
+        x = x_ref[...].astype(F32)
+        inv = lax.rsqrt(jnp.mean(x * x, axis=-1, keepdims=True) + EPSILON)
+        normed = (x * inv * gain_ref[...]).astype(BF)
+        normed_scr[...] = normed
+        normed_ref[...] = normed
+        inv_ref[...] = inv
+
+    normed = normed_scr[...]
+    shards, depth = wq_ref.shape[:2]
+    wq = wq_ref[...].reshape(shards * depth, wq_ref.shape[2])
+    pq = jnp.dot(normed, wq, preferred_element_type=F32)
+    wkv = wkv_ref[...].reshape(shards * depth, wkv_ref.shape[2])
+    pkv = jnp.dot(normed, wkv, preferred_element_type=F32)
+    cos = cos_ref[...]
+    sin = sin_ref[...]
+    heads = pq.shape[1]
+    q_scale = LOG2E * HD**-0.5
+    turned = pq * jnp.tile(cos, (1, heads // 128)) + swap_halves(pq) * jnp.tile(sin, (1, heads // 128))
+    send_ref[0, :, :heads] = (turned * q_scale).astype(BF)
+    lane = lax.broadcasted_iota(jnp.int32, pkv.shape, 1)
+    turned_kv = jnp.where(lane < HD, pkv * cos + swap_halves(pkv) * sin, pkv)
+    send_ref[0, :, heads:] = turned_kv.astype(BF)
+
+
+def project(x, gain, cos, sin, w_all):
+    rows, width = x.shape
+    devices = 2 * CHIPS
+    heads = width // devices
+    out_width = heads + 2 * HD
+    depth = w_all.shape[1]
+    first_kv = width // (2 * HD)
+    return pl.pallas_call(
+        project_kernel,
+        grid=(devices,),
+        in_specs=[
+            pl.BlockSpec((rows, width), lambda d: (0, 0)),
+            pl.BlockSpec((1, width), lambda d: (0, 0)),
+            pl.BlockSpec((rows, 128), lambda d: (0, 0)),
+            pl.BlockSpec((rows, 128), lambda d: (0, 0)),
+            pl.BlockSpec((devices, depth, heads), lambda d: (0, 0, d)),
+            pl.BlockSpec((devices, depth, 2 * HD), lambda d: (0, 0, first_kv + d // 2)),
+        ],
+        out_specs=[
+            pl.BlockSpec((1, rows, out_width), lambda d: (d, 0, 0)),
+            pl.BlockSpec((rows, width), lambda d: (0, 0)),
+            pl.BlockSpec((rows, 1), lambda d: (0, 0)),
+        ],
+        out_shape=[
+            jax.ShapeDtypeStruct((devices, rows, out_width), BF),
+            jax.ShapeDtypeStruct((rows, width), BF),
+            jax.ShapeDtypeStruct((rows, 1), F32),
+        ],
+        scratch_shapes=[pltpu.VMEM((rows, width), BF)],
+        compiler_params=pltpu.CompilerParams(vmem_limit_bytes=48 * 2**20),
+        cost_estimate=pl.CostEstimate(flops=7 * 10**9, bytes_accessed=24 * 10**6, transcendentals=0),
+        name="project",
+    )(x, gain, cos, sin, w_all, w_all)
+
+
+def attend_kernel(zeros_ref, q_ref, kv_ref, o_ref, send_ref, lse_ref, k_scr, v_scr, acc_ref, max_ref, *, heads):
+    block = pl.program_id(0)
+    zeros = zeros_ref[0]
+    size = q_ref.shape[0]
+
+    @pl.when(block == 0)
+    def _():
+        for part in range(kv_ref.shape[0] // size):
+            rows = slice(part * size, (part + 1) * size)
+            both = kv_ref[rows, :].astype(F32)
+            lane = lax.broadcasted_iota(jnp.int32, both.shape, 1)
+            k_scr[rows, :] = kv_ref[rows, :HD]
+            v_scr[rows, :] = jnp.where(lane < HD, pltpu.roll(both, HD, 1), 1.0).astype(BF)
+
+    first_row = block * size
+    lowest = jnp.where(first_row >= zeros, zeros // size, 0)
+    acc_ref[...] = jnp.zeros_like(acc_ref)
+    max_ref[...] = jnp.full_like(max_ref, MASKED)
+    q_heads = [q_ref[:, h * HD : (h + 1) * HD] for h in range(heads)]
+
+    def step(index, masked):
+        first_key = pl.multiple_of(index * size, size)
+        keys = k_scr[pl.ds(first_key, size), :]
+        values = v_scr[pl.ds(first_key, size), :]
+        if masked:
+            row = first_row + lax.broadcasted_iota(jnp.int32, (size, size), 0)
+            col = first_key + lax.broadcasted_iota(jnp.int32, (size, size), 1)
+            begin = jnp.where(row >= zeros, zeros, 0)
+            refused = (col > row) | (col < begin)
+
+        def score(h):
+            return lax.dot_general(q_heads[h], keys, NT, preferred_element_type=F32)
+
+        upcoming = score(0)
+        for h in range(heads):
+            scores = upcoming
+            if h + 1 < heads:
+                upcoming = score(h + 1)
+            if masked:
+                scores = jnp.where(refused, MASKED, scores)
+            old_max = max_ref[h]
+            new_max = jnp.maximum(old_max, jnp.max(scores, axis=-1, keepdims=True))
+            weights = jnp.exp2(scores - jnp.tile(new_max, (1, size // 128)))
+            shrink = jnp.exp2(old_max - new_max)
+            acc_ref[h] = acc_ref[h] * shrink + jnp.dot(weights.astype(BF), values, preferred_element_type=F32)
+            max_ref[h] = new_max
+
+    def visit(index, carry):
+        first_key = index * size
+        mixed = (index == block) | ((first_row + size > zeros) & (first_key < zeros))
+
+        @pl.when(mixed)
+        def _():
+            step(index, True)
+
+        @pl.when(jnp.logical_not(mixed))
+        def _():
+            step(index, False)
+
+        return carry
+
+    lax.fori_loop(lowest, block + 1, visit, 0)
+    for h in range(heads):
+        acc = acc_ref[h]
+        total = acc[:, HD : HD + 1]
+        out = acc[:, :HD] / total
+        o_ref[:, h * HD : (h + 1) * HD] = out
+        send_ref[0, :, h * HD : (h + 1) * HD] = out.astype(BF)
+        lse = max_ref[h] + jnp.log2(total)
+        lse_ref[h : h + 1, :] = jnp.transpose(lse)[:1]
+
+
+def attend(zeros, qkv):
+    length, width = qkv.shape
+    q_width = width - 2 * HD
+    heads = q_width // HD
+    size = BLOCK
+    blocks = length // size
+    return pl.pallas_call(
+        functools.partial(attend_kernel, heads=heads),
+        grid_spec=pltpu.PrefetchScalarGridSpec(
+            num_scalar_prefetch=1,
+            grid=(blocks,),
+            in_specs=[
+                pl.BlockSpec((size, q_width), lambda i, z: (i, 0)),
+                pl.BlockSpec((length, 2 * HD), lambda i, z: (0, q_width // (2 * HD))),
+            ],
+            out_specs=[
+                pl.BlockSpec((size, q_width), lambda i, z: (i, 0)),
+                pl.BlockSpec((1, size, q_width), lambda i, z: (i, 0, 0)),
+                pl.BlockSpec((heads, size), lambda i, z: (0, i)),
+            ],
+            scratch_shapes=[
+                pltpu.VMEM((length, HD), BF),
+                pltpu.VMEM((length, 2 * HD), BF),
+                pltpu.VMEM((heads, size, 2 * HD), F32),
+                pltpu.VMEM((heads, size, 128), F32),
+            ],
+        ),
+        out_shape=[
+            jax.ShapeDtypeStruct((length, q_width), F32),
+            jax.ShapeDtypeStruct((blocks, size, q_width), BF),
+            jax.ShapeDtypeStruct((heads, length), F32),
+        ],
+        compiler_params=pltpu.CompilerParams(vmem_limit_bytes=48 * 2**20),
+        cost_estimate=pl.CostEstimate(flops=40 * 10**9, bytes_accessed=16 * 10**6, transcendentals=36 * 10**6),
+        name="attend",
+    )(zeros, qkv, qkv)
+
+
+def attend_back_kernel(
+    zeros_ref, q_ref, kv_ref, do_ref, o_ref, lse_ref, send_ref, q_scr, do_scr, delta_ref, dq_acc, *, heads
+):
+    block = pl.program_id(0)
+    zeros = zeros_ref[0]
+    size = kv_ref.shape[0]
+    length = q_ref.shape[0]
+    blocks = length // size
+
+    @pl.when(block == 0)
+    def _():
+        dq_acc[...] = jnp.zeros_like(dq_acc)
+        for part in range(blocks):
+            rows = slice(part * size, (part + 1) * size)
+            product = jnp.transpose(do_ref[rows, :].astype(F32) * o_ref[rows, :])
+            for h in range(heads):
+                cols = slice(h * HD, (h + 1) * HD)
+                q_scr[h, rows, :] = q_ref[rows, cols]
+                do_scr[h, rows, :] = do_ref[rows, cols]
+                delta_ref[h : h + 1, rows] = jnp.sum(product[cols], axis=0, keepdims=True)
+
+    first_key = block * size
+    both = kv_ref[...]
+    keys = both[:, :HD]
+    values = both[:, HD:]
+    keys_t = jnp.transpose(keys.astype(F32)).astype(BF)
+    highest = jnp.where(first_key + size <= zeros, jnp.minimum((zeros + size - 1) // size, blocks), blocks)
+
+    def step(index, carry, masked):
+        first_row = pl.multiple_of(index * size, size)
+        span = pl.ds(first_row, size)
+        if masked:
+            col = first_key + lax.broadcasted_iota(jnp.int32, (size, size), 0)
+            row = first_row + lax.broadcasted_iota(jnp.int32, (size, size), 1)
+            begin = jnp.where(row >= zeros, zeros, 0)
+            refused = (col > row) | (col < begin)
+
+        def products(h):
+            q_rows = q_scr[h, span, :]
+            do_rows = do_scr[h, span, :]
+            scores = lax.dot_general(keys, q_rows, NT, preferred_element_type=F32)
+            d_prob = lax.dot_general(values, do_rows, NT, preferred_element_type=F32)
+            return q_rows, do_rows, scores, d_prob
+
+        upcoming = products(0)
+        dk_sum, dv_sum = carry
+        for h in range(heads):
+            q_rows, do_rows, scores, d_prob = upcoming
+            if h + 1 < heads:
+                upcoming = products(h + 1)
+            shifted = scores - lse_ref[h : h + 1, span]
+            if masked:
+                shifted = jnp.where(refused, MASKED, shifted)
+            prob = jnp.exp2(shifted)
+            d_score = (prob * (d_prob - delta_ref[h : h + 1, span])).astype(BF)
+            dv_sum = dv_sum + jnp.dot(prob.astype(BF), do_rows, preferred_element_type=F32)
+            dk_sum = dk_sum + jnp.dot(d_score, q_rows, preferred_element_type=F32)
+            dq_acc[h * HD : (h + 1) * HD, span] += jnp.dot(keys_t, d_score, preferred_element_type=F32)
+        return dk_sum, dv_sum
+
+    def visit(index, carry):
+        first_row = index * size
+        mixed = (index == block) | ((first_row + size > zeros) & (first_key < zeros))
+        return lax.cond(
+            mixed,
+            lambda c: step(index, c, True),
+            lambda c: step(index, c, False),
+            carry,
+        )
+
+    zero = jnp.zeros((size, HD), F32)
+    dk_sum, dv_sum = lax.fori_loop(block, highest, visit, (zero, zero))
+    q_width = heads * HD
+    done = pl.ds(pl.multiple_of(first_key, size), size)
+    send_ref[0, :, :q_width] = (jnp.transpose(dq_acc[:, done]) * HD**-0.5).astype(BF)
+    send_ref[0, :, q_width : q_width + HD] = (dk_sum * (1.0 / LOG2E)).astype(BF)
+    send_ref[0, :, q_width + HD :] = dv_sum.astype(BF)
+
+
+def attend_back(zeros, qkv, d_out, out, lse):
+    length, width = qkv.shape
+    q_width = width - 2 * HD
+    heads = q_width // HD
+    size = BLOCK
+    blocks = length // size
+    return pl.pallas_call(
+        functools.partial(attend_back_kernel, heads=heads),
+        grid_spec=pltpu.PrefetchScalarGridSpec(
+            num_scalar_prefetch=1,
+            grid=(blocks,),
+            in_specs=[
+                pl.BlockSpec((length, q_width), lambda j, z: (0, 0)),
+                pl.BlockSpec((size, 2 * HD), lambda j, z: (j, q_width // (2 * HD))),
+                pl.BlockSpec((length, q_width), lambda j, z: (0, 0)),
+                pl.BlockSpec((length, q_width), lambda j, z: (0, 0)),
+                pl.BlockSpec((heads, length), lambda j, z: (0, 0)),
+            ],
+            out_specs=pl.BlockSpec((1, size, width), lambda j, z: (j, 0, 0)),
+            scratch_shapes=[
+                pltpu.VMEM((heads, length, HD), BF),
+                pltpu.VMEM((heads, length, HD), BF),
+                pltpu.VMEM((heads, length), F32),
+                pltpu.VMEM((q_width, length), F32),
+            ],
+        ),
+        out_shape=jax.ShapeDtypeStruct((blocks, size, width), BF),
+        compiler_params=pltpu.CompilerParams(vmem_limit_bytes=56 * 2**20),
+        cost_estimate=pl.CostEstimate(flops=90 * 10**9, bytes_accessed=16 * 10**6, transcendentals=36 * 10**6),
+        name="attend_back",
+    )(zeros, qkv, qkv, d_out, out, lse)
+
+
+def unturn_kernel(back_ref, cos_ref, sin_ref, out_ref):
+    cos = cos_ref[...]
+    sin = sin_ref[...]
+    devices, _, width = back_ref.shape
+    heads = width - 2 * HD
+    for d in range(devices):
+        dq = back_ref[d, :, :heads].astype(F32)
+        turned = dq * jnp.tile(cos, (1, heads // 128)) - swap_halves(dq) * jnp.tile(sin, (1, heads // 128))
+        out_ref[:, d * heads : (d + 1) * heads] = turned.astype(BF)
+    base = devices * heads
+    for g in range(KV):
+        pair = back_ref[2 * g, :, heads:].astype(F32) + back_ref[2 * g + 1, :, heads:].astype(F32)
+        lane = lax.broadcasted_iota(jnp.int32, pair.shape, 1)
+        pair = jnp.where(lane < HD, pair * cos - swap_halves(pair) * sin, pair)
+        out_ref[:, base + 2 * g * HD : base + 2 * (g + 1) * HD] = pair.astype(BF)
+    end = base + 2 * KV * HD
+    out_ref[:, end:] = jnp.zeros((out_ref.shape[0], out_ref.shape[1] - end), BF)
+
+
+def unturn(back, cos, sin):
+    devices, rows, width = back.shape
+    return pl.pallas_call(
+        unturn_kernel,
+        out_shape=jax.ShapeDtypeStruct((rows, devices * (width - 2 * HD) + 2 * KV * HD + EXTRA), BF),
+        compiler_params=pltpu.CompilerParams(vmem_limit_bytes=48 * 2**20),
+        cost_estimate=pl.CostEstimate(flops=10**7, bytes_accessed=6 * 10**6, transcendentals=0),
+        name="unturn",
+    )(back, cos, sin)
+
+
+def dot(left, right, dims=(((1,), (0,)), ((), ()))):
+    return lax.dot_general(left, right, dims, preferred_element_type=F32)
+
+
+def fast_body(tokens, segment_ids, selected, cotangent, w_qkv, w_out, w_gate_up, w_down, g_attn, g_mlp):
+    _, rows, width = tokens.shape
+    devices = 2 * CHIPS
+    me = lax.axis_index("sp")
+    core = me & 1
+    planes = lax.axis_size("dp")
+    share = width // devices
+    kv_width = KV * HD
+    qkv_width = w_qkv.shape[1]
+
+    count = jnp.sum((segment_ids == 0).astype(jnp.int32))
+    high = jnp.full((share,), count // 64, jnp.int32).astype(BF)
+    low = jnp.full((share,), count % 64, jnp.int32).astype(BF)
+    small = jnp.stack([g_attn, g_mlp, high, low], axis=1)
+    small = jnp.concatenate([small, jnp.zeros((share, EXTRA - 4), BF)], axis=1)
+    paired = [w_qkv[:, :width]]
+    for head in range(KV):
+        paired.append(w_qkv[:, width + head * HD : width + (head + 1) * HD])
+        paired.append(w_qkv[:, width + kv_width + head * HD : width + kv_width + (head + 1) * HD])
+    qkv_all = gather_plane(jnp.concatenate(paired + [small], axis=1), me)
+    extras = qkv_all[:, :, qkv_width : qkv_width + 4].astype(F32)
+    attn_gain = extras[:, :, 0].reshape(1, width)
+    mlp_gain = extras[:, :, 1].reshape(1, width)
+    zeros = jnp.sum(extras[:, 0, 2] * 64.0 + extras[:, 0, 3]).astype(jnp.int32)
+
+    local_pos = me * rows + jnp.arange(rows, dtype=jnp.int32) - segment_ids.reshape(rows) * zeros
+    cosine, sine = rope_tables(local_pos, HD)
+    cos = jnp.concatenate([cosine] * 4, axis=1)
+    sin = jnp.concatenate([-sine, sine, -sine, sine], axis=1)
+
+    hidden_chip = 2 * w_down.shape[0]
+    quarter = share // planes
+    plane = lax.axis_index("dp")
+    gu_rows = lax.dynamic_slice_in_dim(w_gate_up, plane * quarter, quarter, 0)
+    gu_send = []
+    for chip in range(CHIPS):
+        for begin in (chip * hidden_chip, (CHIPS + chip) * hidden_chip):
+            gu_send.append(gu_rows[:, begin : begin + hidden_chip])
+    gu_send = jnp.stack([jnp.concatenate(gu_send[2 * c : 2 * c + 2], axis=1) for c in range(CHIPS)])
+    gu_part = lax.all_to_all(gu_send, "sp", 0, 0, axis_index_groups=SAME_CORE, tiled=True)
+    gu_mine = lax.all_gather(gu_part, "dp", axis=0, tiled=False)
+    gu_mine = gu_mine.transpose(1, 0, 2, 3).reshape(CHIPS, 1, share, 2 * hidden_chip)
+    gu_theirs = send_sibling(gu_mine)
+    w_gu = jnp.where(
+        core == 0, jnp.concatenate([gu_mine, gu_theirs], axis=1), jnp.concatenate([gu_theirs, gu_mine], axis=1)
+    ).reshape(width, 2 * hidden_chip)
+    down_theirs = send_sibling(w_down)
+    w_dn = jnp.where(
+        core == 0, jnp.concatenate([w_down, down_theirs], axis=0), jnp.concatenate([down_theirs, w_down], axis=0)
+    )
+
+    x_bf = tokens.reshape(rows, width)
+    x = x_bf.astype(F32)
+    qkv_send, normed, inv_one = project(x_bf, attn_gain, cos, sin, qkv_all)
+    qkv_heads = lax.all_to_all(qkv_send, "sp", 0, 0, tiled=True)
+    length = devices * rows
+    qkv_heads = qkv_heads.reshape(length, qkv_send.shape[2])
+    zeros_one = zeros.reshape(1)
+    out_heads, out_send, lse = attend(zeros_one, qkv_heads)
+    out_all = gather_plane(after(w_out, qkv_all), me).reshape(width, width)
+    dy = (cotangent * selected[:, :, None].astype(BF)).reshape(rows, width)
+    dy_rows = gather_chips(after(dy, qkv_heads))
+    attn_tok = lax.all_to_all(out_send, "sp", 0, 0, tiled=True).transpose(1, 0, 2).reshape(rows, width)
+    residual = x + dot(attn_tok, out_all)
+    inv_two = lax.rsqrt(jnp.mean(residual * residual, axis=-1, keepdims=True) + EPSILON)
+    inner = (residual * inv_two * mlp_gain).astype(BF)
+
+    inner_rows = gather_chips(inner)
+    hid_rows, dgu_rows, y_parts, db_parts = [], [], [], []
+    for b_rows, dy_part in zip(inner_rows, dy_rows):
+        gate_up = dot(b_rows, w_gu)
+        d_hidden = dot(dy_part, w_dn, NT)
+        gate = gate_up[:, :hidden_chip]
+        up = gate_up[:, hidden_chip:]
+        sigmoid_g = jax.nn.sigmoid(gate)
+        silu_gate = gate * sigmoid_g
+        slope = sigmoid_g * (1.0 + gate * (1.0 - sigmoid_g))
+        hid = (silu_gate * up).astype(BF)
+        dgu = jnp.concatenate([d_hidden * up * slope, d_hidden * silu_gate], axis=1).astype(BF)
+        hid_rows.append(hid)
+        dgu_rows.append(dgu)
+        db_parts.append(dot(dgu, w_gu, NT))
+        y_parts.append(dot(hid, w_dn))
+
+    d_inner = scatter_chips(db_parts)
+    grad_y = dy.astype(F32)
+    scaled = d_inner * mlp_gain
+    inner_mean = jnp.mean(scaled * residual, axis=-1, keepdims=True)
+    d_resid = grad_y + inv_two * scaled - residual * inv_two**3 * inner_mean
+    gain_two = jnp.sum(d_inner * residual * inv_two, axis=0)
+    d_branch = d_resid.astype(BF)
+    d_attn = dot(d_branch, out_all, NT).astype(BF)
+    d_send = d_attn.reshape(rows, devices, share).transpose(1, 0, 2)
+    d_heads = lax.all_to_all(d_send, "sp", 0, 0, tiled=True).reshape(length, share)
+
+    all_inner = jnp.concatenate(inner_rows, axis=0)
+    all_dgu = jnp.concatenate(dgu_rows, axis=0)
+    grad_gu = dot(all_inner, all_dgu, TN).astype(BF).reshape(CHIPS, 2, share, 2 * hidden_chip)
+    gu_keep = lax.dynamic_slice_in_dim(grad_gu, core, 1, 1)
+    gu_give = lax.dynamic_slice_in_dim(grad_gu, 1 - core, 1, 1)
+    gu_sum = gu_keep.astype(F32) + send_sibling(gu_give).astype(F32)
+    gu_sum = gu_sum.astype(BF).reshape(CHIPS, planes, quarter, 2 * hidden_chip).transpose(1, 0, 2, 3)
+    gu_z = line_scatter(gu_sum)
+    gu_z = lax.all_to_all(gu_z, "sp", 0, 0, axis_index_groups=SAME_CORE, tiled=True)
+    grad_w_gate_up = spread(line_gather(gu_z), 2 * CHIPS * hidden_chip)
+    all_hid = jnp.concatenate(hid_rows, axis=0)
+    all_dy = jnp.concatenate(dy_rows, axis=0)
+    grad_dn = dot(all_hid, all_dy, TN).astype(BF).reshape(2, hidden_chip // 2, width)
+    dn_keep = lax.dynamic_slice_in_dim(grad_dn, core, 1, 0)[0]
+    dn_give = lax.dynamic_slice_in_dim(grad_dn, 1 - core, 1, 0)[0]
+    dn_sum = (dn_keep.astype(F32) + send_sibling(dn_give).astype(F32)).astype(BF)
+    grad_w_down = line_sum(dn_sum).astype(F32)
+
+    y_sum = scatter_chips(y_parts)
+    output = (residual + y_sum).astype(BF).reshape(tokens.shape)
+
+    pad = jnp.zeros((width, 128), F32)
+    grad_wo = jnp.concatenate([dot(attn_tok, d_branch, TN), pad.at[:, 0].set(gain_two)], axis=1).astype(BF)
+    wo_rows = lax.psum_scatter(grad_wo, "sp", scatter_dimension=0, tiled=True)
+    wo_rows = line_sum(wo_rows).astype(F32)
+    grad_w_out = wo_rows[:, :width]
+    grad_g_mlp = wo_rows[:, width]
+
+    d_heads = after(d_heads, gu_sum, dn_sum)
+    back_send = attend_back(zeros_one, qkv_heads, d_heads, out_heads, lse)
+    back = lax.all_to_all(back_send, "sp", 0, 0, tiled=True)
+    d_mixed = unturn(back, cos, sin)
+    d_normed = dot(d_mixed, qkv_all.reshape(width, qkv_width + EXTRA), NT)
+    scaled_one = d_normed * attn_gain
+    mean_one = jnp.mean(scaled_one * x, axis=-1, keepdims=True)
+    grad_in = d_resid + inv_one * scaled_one - x * inv_one**3 * mean_one
+    grad_tokens = grad_in.astype(BF).reshape(tokens.shape)
+    gain_one = jnp.sum(d_normed * x * inv_one, axis=0)
+    column = lax.broadcasted_iota(jnp.int32, (1, qkv_width + EXTRA), 1)
+    grad_wq = (dot(normed, d_mixed, TN) + jnp.where(column == qkv_width, gain_one[:, None], 0.0)).astype(BF)
+    wq_rows = scatter_plane(grad_wq.reshape(devices, share, qkv_width + EXTRA), me).astype(BF)
+    wq_rows = line_sum(wq_rows).astype(F32)
+    pieces = [wq_rows[:, :width]]
+    for kind in range(2):
+        for head in range(KV):
+            begin = width + (2 * head + kind) * HD
+            pieces.append(wq_rows[:, begin : begin + HD])
+    grad_w_qkv = jnp.concatenate(pieces, axis=1)
+    return (
+        output,
+        grad_tokens,
+        grad_w_qkv,
+        grad_w_out,
+        grad_w_gate_up,
+        grad_w_down,
+        wq_rows[:, qkv_width],
+        grad_g_mlp,
+    )
+
+
 def solution(mesh):
     in_specs = (
         P("dp", "sp", None),
@@ -341,4 +972,5 @@
         P("sp"),
         P("sp"),
     )
+    body = fast_body if mesh.shape["sp"] == 2 * CHIPS else general_body
     return jax.shard_map(body, mesh=mesh, in_specs=in_specs, out_specs=out_specs, check_vma=False)

time: 2300 us -> 1200 us (0.52)
  waiting for transfers between devices: 901 us -> 327 us
  matrix products: 681 us -> 235 us
  other arithmetic: 336 us -> 128 us
  starting transfers between devices: 17.8 us -> 213 us
  Pallas kernels: 0 us -> 168 us
  local copies, waits for them, and re-layouts: 242 us -> 103 us
  blocking collectives: 93.5 us -> 0 us
    dot_general x60 -> x23, matrix products: 681 us -> 235 us  [dot(): return lax.dot_general(left, right, dims, preferred_element_type=F32)]
    reduce_scatter x2 -> x1, waiting for transfers between devices: 373 us -> 0.02 us  [fast_body(): wo_rows = lax.psum_scatter(grad_wo, 'sp', scatter_dimension=0, tiled=True)]
    ppermute x0 -> x82, waiting for transfers between devices: none -> 304 us  [the longest x12 127 us: line_gather(): lax.ppermute(lefts[-1], 'dp', [(i + 1, i) for i in range(planes - step)])]
    psum x1 -> x0, waiting for transfers between devices: 296 us -> none  [body(): lax.psum(row_sums, 'dp').astype(jnp.float32)]
    ppermute x0 -> x82, starting transfers between devices: none -> 187 us  [the longest x12 98.3 us: line_scatter(): right = lax.ppermute(ahead, 'dp', [(i, i + 1) for i in range(step)])]
    pallas_call x0 -> x5, Pallas kernels: none -> 168 us  [the longest x1 90.2 us: attend_back(): pl.pallas_call(functools.partial(attend_back_kernel, heads=heads), grid_s...]
    all_to_all x4 -> x6, waiting for transfers between devices: 186 us -> 23 us  [the longest x1 10.8 us: fast_body(): lax.all_to_all(d_send, 'sp', 0, 0, tiled=True).reshape(length, share)]
    another operation x11 -> x5, local copies, waits for them, and re-layouts: 87.2 us -> 0.22 us  [the longest x4 0.22 us: fast_body(): small = jnp.stack([g_attn, g_mlp, high, low], axis=1)]
  transfers between devices with their start and end apart: 11 -> 90, of which waited for: 6 -> 28; matrix products, arithmetic and copies ran while one was open for 49% -> 37% of each run, Pallas kernels for 0% -> 14%
where the time goes in v1:
time: 1200 us; the launch traced here: 1190 us
  waiting for transfers between devices  327 us (27%)
  matrix products  235 us (20%)
  starting transfers between devices  213 us (18%)
  Pallas kernels  168 us (14%)
  other arithmetic  128 us (11%)
  local copies, waits for them, and re-layouts  103 us (9%)
  between operations  19.2 us (2%)
    dot_general x23, matrix products, dot(): return lax.dot_general(left, right, dims, preferred_element_type=F32)  235 us
    ppermute x12, waiting for transfers between devices, line_gather(): lax.ppermute(lefts[-1], 'dp', [(i + 1, i) for i in range(planes - step)])  127 us
    ppermute x12, starting transfers between devices, line_scatter(): right = lax.ppermute(ahead, 'dp', [(i, i + 1) for i in range(step)])  98.3 us
    pallas_call x1, Pallas kernels, attend_back(): pl.pallas_call(functools.partial(attend_back_kernel, heads=heads), grid_s...  90.2 us
    ppermute x11, waiting for transfers between devices, send_second(): return lax.ppermute(x, 'sp', SECOND)  77.2 us
    ppermute x10, waiting for transfers between devices, send_first(): return lax.ppermute(x, 'sp', FIRST)  66.4 us
    pallas_call x1, Pallas kernels, attend(): pl.pallas_call(functools.partial(attend_kernel, heads=heads), grid_spec=p...  51.1 us
    ppermute x12, waiting for transfers between devices, line_scatter(): right = lax.ppermute(ahead, 'dp', [(i, i + 1) for i in range(step)])  29.8 us
  transfers between devices with their start and end apart: 90, of which 28 were waited for; matrix products, arithmetic and copies ran while one was open for 37% of the time, Pallas kernels for 14%

profile of v1, /device:TPU:0, one launch (start us, length us, event | category | flops | bytes accessed | tf_op | source)
XLA Modules:
  0.0 1193.0 jit_solution(14368509730179911451)
XLA Ops:
  17.4 14.7 %collective-permute-done = bf16[256,2688]{1,0:T(8,128)(2,1)S(1)} collective-permute-done((bf16[256,2688]{1,0:T(8,128)(2,1)S(1)}, bf16[256,2688]{1,0:T(8,128)(2,1)S(1)}, u32[]{:S(2)}, u32[]{:S(2)}) %collective-permute-start) | collective-permute-done | bytes 1376288 | tf_op jit(solution)/shard_map/ppermute | solution.py:347
  45.8 16.3 %collective-permute-done.1 = bf16[256,2688]{1,0:T(8,128)(2,1)} collective-permute-done((bf16[256,2688]{1,0:T(8,128)(2,1)S(1)}, bf16[256,2688]{1,0:T(8,128)(2,1)}, u32[]{:S(2)}, u32[]{:S(2)}) %collective-permute-start.1) | collective-permute-done | bytes 1376288 | tf_op jit(solution)/shard_map/ppermute | solution.py:351
  67.9 12.7 %collective-permute-done.2 = bf16[256,2688]{1,0:T(8,128)(2,1)S(1)} collective-permute-done((bf16[256,2688]{1,0:T(8,128)(2,1)S(1)}, bf16[256,2688]{1,0:T(8,128)(2,1)S(1)}, u32[]{:S(2)}, u32[]{:S(2)}) %collective-permute-start.2) | collective-permute-done | bytes 1376288 | tf_op jit(solution)/shard_map/ppermute | solution.py:351
  95.0 16.1 %project.1 = (bf16[8,512,384]{2,1,0:T(8,128)(2,1)}, bf16[512,2048]{1,0:T(8,128)(2,1)S(1)}, f32[512,1]{1,0:T(8,128)S(1)}) custom-call(bf16[512,2048]{1,0:T(8,128)(2,1)S(1)} %bitcast.300, f32[1,2048]{1,0:T(1,128)S(1)} %bitcast.301, f32[512,128]{1,0:T(8,128)S(1)} %get-tuple-element.133.cos_ref, f32[512,128]{1,0:T(8,128)S(1)} %get-tuple-element.134.sin_ref, ...), custom_call_target="tpu_custom_call" | custom-call | flops 7000000000 | bytes 24000000 | tf_op jit(solution)/shard_map/project/pallas_call | solution.py:513
  133.1 32.7 %collective-permute-done.8 = bf16[256,2048]{1,0:T(8,128)(2,1)} collective-permute-done((bf16[256,2048]{1,0:T(8,128)(2,1)}, bf16[256,2048]{1,0:T(8,128)(2,1)}, u32[]{:S(2)}, u32[]{:S(2)}) %collective-permute-start.8) | collective-permute-done | bytes 1048608 | tf_op jit(solution)/shard_map/ppermute | solution.py:351
  168.5 51.1 %attend.1 = (f32[4096,256]{1,0:T(8,128)}, bf16[8,512,256]{2,1,0:T(8,128)(2,1)S(1)}, f32[4,4096]{1,0:T(4,128)S(1)}) custom-call(s32[1]{0:T(128)} %bitcast.9.zeros_ref, bf16[4096,384]{1,0:T(8,128)(2,1)S(1)} %bitcast.296, bf16[4096,384]{1,0:T(8,128)(2,1)S(1)} %bitcast.297), custom_call_target="tpu_custom_call" | custom-call | flops 40000000000 | bytes 16000000 | tf_op jit(solution)/shard_map/attend/pallas_call | solution.py:619
  245.1 8.1 all-to-all-done.1
  253.2 7.7 multiply_reduce_fusion.2
  263.4 11.2 collective-permute-done.22
  276.1 40.3 %collective-permute-done.16 = bf16[512,2048]{1,0:T(8,128)(2,1)S(1)} collective-permute-done((bf16[512,2048]{1,0:T(8,128)(2,1)S(1)}, bf16[512,2048]{1,0:T(8,128)(2,1)S(1)}, u32[]{:S(2)}, u32[]{:S(2)}) %collective-permute-start.16) | collective-permute-done | bytes 2097184 | tf_op jit(solution)/shard_map/ppermute | solution.py:347
  321.6 7.8 maximum_select_fusion.1
  334.8 9.7 collective-permute-done.18
  346.5 9.4 maximum_select_fusion
  357.6 8.1 fusion.125
  365.7 7.9 fusion.127
  373.6 7.4 multiply_convert_fusion.6
  381.1 7.5 convolution_convert_fusion.3
  388.6 8.5 multiply_convert_fusion.8
  403.7 9.2 fusion.128
  413.0 8.5 multiply_convert_fusion.4
  426.5 9.4 fusion.129
  436.0 8.5 multiply_convert_fusion.2
  444.5 9.2 convolution_convert_fusion.2
  460.4 17.5 %fusion.36 = bf16[1408,2048]{1,0:T(8,128)(2,1)} fusion(bf16[512,2048]{1,0:T(8,128)(2,1)} %collective-permute-done.25, bf16[512,2048]{1,0:T(8,128)(2,1)} %collective-permute-done.24, bf16[512,2048]{1,0:T(8,128)(2,1)} %collective-permute-done.22, bf16[512,2048]{1,0:T(8,128)(2,1)} %multiply_bitcast_fusion, bf16[512,1408]{1,0:T(8,128)(2,1)} %copy-done.55, ...), kind=kOutput, calls=%fused_computation.38 | convolution fusion | flops 11870666752 | bytes 19922944 | tf_op jit(solution)/shard_map/dot_general | solution.py:794
  481.8 14.2 %fusion.171 = bf16[2048,2048]{1,0:T(8,128)(2,1)} fusion(bf16[512,2048]{1,0:T(8,128)(2,1)} %collective-permute-done.19, bf16[512,2048]{1,0:T(8,128)(2,1)} %collective-permute-done.18, bf16[512,2048]{1,0:T(8,128)(2,1)S(1)} %copy-done.28, bf16[512,2048]{1,0:T(8,128)(2,1)S(1)} %copy-done.22), kind=kLoop, calls=%fused_computation.31.clone.2 | loop fusion | flops 33554432 | bytes 16777216 | tf_op jit(solution)/shard_map/dot_general | solution.py:794
  496.1 39.0 %fusion.17 = bf16[2048,2816]{1,0:T(8,128)(2,1)} fusion(bf16[512,1408]{1,0:T(8,128)(2,1)} %get-tuple-element.77, bf16[512,1408]{1,0:T(8,128)(2,1)} %get-tuple-element.76, bf16[512,1408]{1,0:T(8,128)(2,1)} %get-tuple-element.75, bf16[512,1408]{1,0:T(8,128)(2,1)} %get-tuple-element.74, bf16[512,1408]{1,0:T(8,128)(2,1)} %copy-done.57, ...), kind=kOutput, calls=%fused_computation.21 | convolution fusion | flops 23720361984 | bytes 31457280 | tf_op jit(solution)/shard_map/dot_general | solution.py:794
  541.8 13.2 %add_convert_fusion.2 = bf16[512,2048]{1,0:T(8,128)(2,1)} fusion(bf16[512,2048]{1,0:T(8,128)(2,1)} %collective-permute-done.26, bf16[2048,2816]{1,0:T(8,128)(2,1)} %bitcast.321, bf16[512,1408]{1,0:T(8,128)(2,1)S(1)} %copy-done.59, bf16[512,1408]{1,0:T(8,128)(2,1)S(1)} %copy-done.58), kind=kOutput, calls=%fused_computation.66 | convolution fusion | flops 5914492928 | bytes 18612224 | tf_op jit(solution)/shard_map/dot_general | solution.py:794
  560.7 17.0 %collective-permute-start.70 = (bf16[176,2048]{1,0:T(8,128)(2,1)S(1)}, bf16[176,2048]{1,0:T(8,128)(2,1)S(1)}, u32[]{:S(2)}, u32[]{:S(2)}) collective-permute-start(bf16[176,2048]{1,0:T(8,128)(2,1)S(1)} %get-tuple-element.100), channel_id=1, source_target_pairs={{0,8},{1,9},{2,10},{3,11},{4,12},{5,13},{6,14},{7,15}} | collective-permute-start | bytes 2162696 | tf_op jit(solution)/shard_map/ppermute | solution.py:402
  583.7 9.6 collective-permute-done.70
  601.3 12.4 %multiply_reduce_fusion = (bf16[2048]{0:T(1024)(128)(2,1)S(1)}, f32[512]{0:T(512)S(1)}, f32[512,2048]{1,0:T(8,128)}) fusion(f32[512,2048]{1,0:T(8,128)S(1)} %copy-done.18, f32[512]{0:T(512)S(1)} %copy-done.41, bf16[512,2048]{1,0:T(8,128)(2,1)S(1)} %collective-permute-done.27, bf16[512,2048]{1,0:T(8,128)(2,1)} %collective-permute-done.23, ...), kind=kOutput, calls=%fused_computation.62 | convolution fusion | flops 5921830400 | bytes 27017216 | tf_op jit(solution)/shard_map/dot_general | solution.py:794
  620.8 9.2 multiply_subtract_fusion
  630.0 9.7 convolution_convert_fusion.1
  646.2 10.8 convolution_convert_fusion
  661.4 10.8 all-to-all-done.3
  672.2 90.2 %attend_back.1 = bf16[8,512,384]{2,1,0:T(8,128)(2,1)} custom-call(s32[1]{0:T(128)} %bitcast.9.zeros_ref, bf16[4096,384]{1,0:T(8,128)(2,1)} %bitcast.298, bf16[4096,384]{1,0:T(8,128)(2,1)} %bitcast.299, bf16[4096,256]{1,0:T(8,128)(2,1)} %bitcast.34.do_ref, f32[4096,256]{1,0:T(8,128)} %get-tuple-element.51.o_ref, f32[4,4096]{1,0:T(4,128)} %copy-done.12), custom_call_target="tpu_custom_call" | custom-call | flops 89999998976 | bytes 16000000 | tf_op jit(solution)/shard_map/attend_back/pallas_call | solution.py:736
  775.9 32.7 %collective-permute-start.58 = (bf16[4,64,2816]{2,1,0:T(8,128)(2,1)}, bf16[4,64,2816]{2,1,0:T(8,128)(2,1)}, u32[]{:S(2)}, u32[]{:S(2)}) collective-permute-start(bf16[4,64,2816]{2,1,0:T(8,128)(2,1)} %get-tuple-element.82), channel_id=1, source_target_pairs={{0,8},{1,9},{2,10},{3,11},{4,12},{5,13},{6,14},{7,15}} | collective-permute-start | bytes 4325384 | tf_op jit(solution)/shard_map/ppermute | solution.py:402
  810.5 8.6 fusion.20
  825.2 14.5 %collective-permute-done.58 = bf16[4,64,2816]{2,1,0:T(8,128)(2,1)} collective-permute-done((bf16[4,64,2816]{2,1,0:T(8,128)(2,1)}, bf16[4,64,2816]{2,1,0:T(8,128)(2,1)}, u32[]{:S(2)}, u32[]{:S(2)}) %collective-permute-start.58) | collective-permute-done | bytes 1441824 | tf_op jit(solution)/shard_map/ppermute | solution.py:402
  857.1 11.1 fusion.52
  868.3 9.0 add_convert_fusion
  890.4 6.1 collective-permute-start.60
  908.3 32.2 %collective-permute-done.77 = bf16[176,2048]{1,0:T(8,128)(2,1)} collective-permute-done((bf16[176,2048]{1,0:T(8,128)(2,1)}, bf16[176,2048]{1,0:T(8,128)(2,1)}, u32[]{:S(2)}, u32[]{:S(2)}) %collective-permute-start.77) | collective-permute-done | bytes 720928 | tf_op jit(solution)/shard_map/ppermute | solution.py:413
  951.3 8.4 collective-permute-done.78
  968.1 12.8 %collective-permute-done.79 = bf16[176,2048]{1,0:T(8,128)(2,1)} collective-permute-done((bf16[176,2048]{1,0:T(8,128)(2,1)}, bf16[176,2048]{1,0:T(8,128)(2,1)}, u32[]{:S(2)}, u32[]{:S(2)}) %collective-permute-start.79) | collective-permute-done | bytes 720928 | tf_op jit(solution)/shard_map/ppermute | solution.py:413
  989.2 19.5 %collective-permute-done.65 = bf16[4,64,2816]{2,1,0:T(8,128)(2,1)S(1)} collective-permute-done((bf16[4,64,2816]{2,1,0:T(8,128)(2,1)S(1)}, bf16[4,64,2816]{2,1,0:T(8,128)(2,1)S(1)}, u32[]{:S(2)}, u32[]{:S(2)}) %collective-permute-start.65) | collective-permute-done | bytes 1441824 | tf_op jit(solution)/shard_map/ppermute | solution.py:413
  1024.3 16.9 %collective-permute-done.66 = bf16[4,64,2816]{2,1,0:T(8,128)(2,1)S(1)} collective-permute-done((bf16[4,64,2816]{2,1,0:T(8,128)(2,1)S(1)}, bf16[4,64,2816]{2,1,0:T(8,128)(2,1)S(1)}, u32[]{:S(2)}, u32[]{:S(2)}) %collective-permute-start.66) | collective-permute-done | bytes 1441824 | tf_op jit(solution)/shard_map/ppermute | solution.py:413
  1049.7 23.1 %collective-permute-done.67 = bf16[4,64,2816]{2,1,0:T(8,128)(2,1)S(1)} collective-permute-done((bf16[4,64,2816]{2,1,0:T(8,128)(2,1)S(1)}, bf16[4,64,2816]{2,1,0:T(8,128)(2,1)S(1)}, u32[]{:S(2)}, u32[]{:S(2)}) %collective-permute-start.67) | collective-permute-done | bytes 1441824 | tf_op jit(solution)/shard_map/ppermute | solution.py:413
  1110.4 10.6 collective-permute-start.47
  (425 shorter events, 392.5 us)
Async XLA Ops:
  15.8 66.0 %collective-permute-start.3 = (bf16[256,2688]{1,0:T(8,128)(2,1)S(1)}, bf16[256,2688]{1,0:T(8,128)(2,1)}, u32[]{:S(2)}, u32[]{:S(2)}) collective-permute-start(bf16[256,2688]{1,0:T(8,128)(2,1)S(1)} %concatenate.72), channel_id=1, source_target_pairs={{0,1},{1,0},{2,3},{3,2},{4,5},{5,4},{6,7},{7,6},{8,9},{9,8},{10,11... | collective-permute-start | bytes 4128776 | tf_op jit(solution)/shard_map/ppermute | solution.py:355
  35.5 78.4 %all-to-all-start.2 = ((bf16[4,64,2816]{2,1,0:T(8,128)(2,1)}), bf16[4,64,2816]{2,1,0:T(8,128)(2,1)}, u32[]{:S(2)}, u32[]{:S(2)}) async-start(bf16[4,64,2816]{2,1,0:T(8,128)(2,1)} %pad_maximum_fusion), calls=%async_computation.2 | async-start | bytes 2883584 | tf_op jit(solution)/shard_map/all_to_all | solution.py:836
  45.8 38.5 %collective-permute-start.4 = (bf16[256,2688]{1,0:T(8,128)(2,1)S(1)}, bf16[256,2688]{1,0:T(8,128)(2,1)S(1)}, u32[]{:S(2)}, u32[]{:S(2)}) collective-permute-start(bf16[256,2688]{1,0:T(8,128)(2,1)S(1)} %collective-permute-done), channel_id=1, source_target_pairs={{0,1},{1,0},{2,3},{3,2},{4,5},{5,4},{6,7},{7,6},{8,9},{9,8},{10,11... | collective-permute-start | bytes 4128776 | tf_op jit(solution)/shard_map/ppermute | solution.py:355
  113.9 54.6 %all-to-all-start = ((bf16[8,512,384]{2,1,0:T(8,128)(2,1)}), bf16[8,512,384]{2,1,0:T(8,128)(2,1)S(1)}, u32[]{:S(2)}, u32[]{:S(2)}) async-start(bf16[8,512,384]{2,1,0:T(8,128)(2,1)} %get-tuple-element.39), calls=%async_computation | async-start | bytes 6291456 | tf_op jit(solution)/shard_map/all_to_all | solution.py:851
  117.7 121.2 %all-gather.3.cloned.1.call-start = ((), (), s32[]{:S(2)}) async-start(), calls=%async_computation.8 | async-start | bytes 7208960 | tf_op jit(solution)/shard_map/all_gather | solution.py:837
  118.4 47.4 %collective-permute-start.8 = (bf16[256,2048]{1,0:T(8,128)(2,1)}, bf16[256,2048]{1,0:T(8,128)(2,1)}, u32[]{:S(2)}, u32[]{:S(2)}) collective-permute-start(bf16[256,2048]{1,0:T(8,128)(2,1)} %param.17), channel_id=1, source_target_pairs={{0,4},{1,3},{2,6},{3,1},{4,0},{5,7},{6,2},{7,5},{8,12},{9,11},{10,... | collective-permute-start | bytes 3145736 | tf_op jit(solution)/shard_map/ppermute | solution.py:351
  123.6 107.2 %collective-permute-start.10 = (bf16[256,2048]{1,0:T(8,128)(2,1)}, bf16[256,2048]{1,0:T(8,128)(2,1)}, u32[]{:S(2)}, u32[]{:S(2)}) collective-permute-start(bf16[256,2048]{1,0:T(8,128)(2,1)} %param.17), channel_id=1, source_target_pairs={{0,1},{1,0},{2,3},{3,2},{4,5},{5,4},{6,7},{7,6},{8,9},{9,8},{10,11... | collective-permute-start | bytes 3145736 | tf_op jit(solution)/shard_map/ppermute | solution.py:355
  130.3 102.8 %collective-permute-start.11 = (bf16[256,2048]{1,0:T(8,128)(2,1)}, bf16[256,2048]{1,0:T(8,128)(2,1)}, u32[]{:S(2)}, u32[]{:S(2)}) collective-permute-start(bf16[256,2048]{1,0:T(8,128)(2,1)} %collective-permute-done.7), channel_id=1, source_target_pairs={{0,1},{1,0},{2,3},{3,2},{4,5},{5,4},{6,7},{7,6},{8,9},{9,8},{10,11... | collective-permute-start | bytes 3145736 | tf_op jit(solution)/shard_map/ppermute | solution.py:355
  165.9 62.6 %collective-permute-start.9 = (bf16[256,2048]{1,0:T(8,128)(2,1)}, bf16[256,2048]{1,0:T(8,128)(2,1)}, u32[]{:S(2)}, u32[]{:S(2)}) collective-permute-start(bf16[256,2048]{1,0:T(8,128)(2,1)} %collective-permute-done.7), channel_id=1, source_target_pairs={{0,4},{1,3},{2,6},{3,1},{4,0},{5,7},{6,2},{7,5},{8,12},{9,11},{10,... | collective-permute-start | bytes 3145736 | tf_op jit(solution)/shard_map/ppermute | solution.py:351
  166.2 69.2 %collective-permute-start.12 = (bf16[256,2048]{1,0:T(8,128)(2,1)}, bf16[256,2048]{1,0:T(8,128)(2,1)}, u32[]{:S(2)}, u32[]{:S(2)}) collective-permute-start(bf16[256,2048]{1,0:T(8,128)(2,1)} %collective-permute-done.8), channel_id=1, source_target_pairs={{0,1},{1,0},{2,3},{3,2},{4,5},{5,4},{6,7},{7,6},{8,9},{9,8},{10,11... | collective-permute-start | bytes 3145736 | tf_op jit(solution)/shard_map/ppermute | solution.py:355
  221.5 31.6 %all-to-all-start.1 = ((bf16[8,512,256]{2,1,0:T(8,128)(2,1)}), bf16[8,512,256]{2,1,0:T(8,128)(2,1)}, u32[]{:S(2)}, u32[]{:S(2)}) async-start(bf16[8,512,256]{2,1,0:T(8,128)(2,1)} %copy-done.2), calls=%async_computation.1 | async-start | bytes 4194304 | tf_op jit(solution)/shard_map/all_to_all | solution.py:859
  226.4 48.3 %collective-permute-start.22 = (bf16[512,2048]{1,0:T(8,128)(2,1)}, bf16[512,2048]{1,0:T(8,128)(2,1)}, u32[]{:S(2)}, u32[]{:S(2)}) collective-permute-start(bf16[512,2048]{1,0:T(8,128)(2,1)} %multiply_bitcast_fusion), channel_id=1, source_target_pairs={{0,2},{1,5},{2,0},{3,7},{4,6},{5,1},{6,4},{7,3},{8,10},{9,13},{10,... | collective-permute-start | bytes 6291464 | tf_op jit(solution)/shard_map/ppermute | solution.py:347
  244.7 101.8 %collective-permute-start.14 = (bf16[4,1,256,2816]{3,2,0,1:T(8,128)(2,1)}, bf16[4,1,256,2816]{3,2,0,1:T(8,128)(2,1)}, u32[]{:S(2)}, u32[]{:S(2)}) collective-permute-start(bf16[4,1,256,2816]{3,2,0,1:T(8,128)(2,1)} %bitcast.28), channel_id=1, source_target_pairs={{0,1},{1,0},{2,3},{3,2},{4,5},{5,4},{6,7},{7,6},{8,9},{9,8},{10,11... | collective-permute-start | bytes 17301512 | tf_op jit(solution)/shard_map/ppermute | solution.py:355
  262.9 53.5 %collective-permute-start.16 = (bf16[512,2048]{1,0:T(8,128)(2,1)S(1)}, bf16[512,2048]{1,0:T(8,128)(2,1)S(1)}, u32[]{:S(2)}, u32[]{:S(2)}) collective-permute-start(bf16[512,2048]{1,0:T(8,128)(2,1)S(1)} %multiply_convert_fusion), channel_id=1, source_target_pairs={{0,2},{1,5},{2,0},{3,7},{4,6},{5,1},{6,4},{7,3},{8,10},{9,13},{10,... | collective-permute-start | bytes 6291464 | tf_op jit(solution)/shard_map/ppermute | solution.py:347
  263.4 58.2 %collective-permute-start.15 = (bf16[704,2048]{1,0:T(8,128)(2,1)}, bf16[704,2048]{1,0:T(8,128)(2,1)}, u32[]{:S(2)}, u32[]{:S(2)}) collective-permute-start(bf16[704,2048]{1,0:T(8,128)(2,1)} %param.19), channel_id=1, source_target_pairs={{0,1},{1,0},{2,3},{3,2},{4,5},{5,4},{6,7},{7,6},{8,9},{9,8},{10,11... | collective-permute-start | bytes 8650760 | tf_op jit(solution)/shard_map/ppermute | solution.py:355
  274.6 60.1 %collective-permute-start.24 = (bf16[512,2048]{1,0:T(8,128)(2,1)}, bf16[512,2048]{1,0:T(8,128)(2,1)}, u32[]{:S(2)}, u32[]{:S(2)}) collective-permute-start(bf16[512,2048]{1,0:T(8,128)(2,1)} %multiply_bitcast_fusion), channel_id=1, source_target_pairs={{0,4},{1,3},{2,6},{3,1},{4,0},{5,7},{6,2},{7,5},{8,12},{9,11},{10,... | collective-permute-start | bytes 6291464 | tf_op jit(solution)/shard_map/ppermute | solution.py:351
  334.8 101.2 %collective-permute-start.25 = (bf16[512,2048]{1,0:T(8,128)(2,1)}, bf16[512,2048]{1,0:T(8,128)(2,1)}, u32[]{:S(2)}, u32[]{:S(2)}) collective-permute-start(bf16[512,2048]{1,0:T(8,128)(2,1)} %collective-permute-done.22), channel_id=1, source_target_pairs={{0,4},{1,3},{2,6},{3,1},{4,0},{5,7},{6,2},{7,5},{8,12},{9,11},{10,... | collective-permute-start | bytes 6291464 | tf_op jit(solution)/shard_map/ppermute | solution.py:351
  344.5 82.1 %collective-permute-start.19 = (bf16[512,2048]{1,0:T(8,128)(2,1)}, bf16[512,2048]{1,0:T(8,128)(2,1)}, u32[]{:S(2)}, u32[]{:S(2)}) collective-permute-start(bf16[512,2048]{1,0:T(8,128)(2,1)} %copy-done.26), channel_id=1, source_target_pairs={{0,4},{1,3},{2,6},{3,1},{4,0},{5,7},{6,2},{7,5},{8,12},{9,11},{10,... | collective-permute-start | bytes 6291464 | tf_op jit(solution)/shard_map/ppermute | solution.py:351
  388.6 205.8 %collective-permute-start.23 = (bf16[512,2048]{1,0:T(8,128)(2,1)}, bf16[512,2048]{1,0:T(8,128)(2,1)}, u32[]{:S(2)}, u32[]{:S(2)}) collective-permute-start(bf16[512,2048]{1,0:T(8,128)(2,1)} %convolution_convert_fusion.3), channel_id=1, source_target_pairs={{0,2},{1,5},{2,0},{3,7},{4,6},{5,1},{6,4},{7,3},{8,10},{9,13},{10,... | collective-permute-start | bytes 6291464 | tf_op jit(solution)/shard_map/ppermute | solution.py:347
  401.7 211.9 %collective-permute-start.17 = (bf16[512,2048]{1,0:T(8,128)(2,1)}, bf16[512,2048]{1,0:T(8,128)(2,1)}, u32[]{:S(2)}, u32[]{:S(2)}) collective-permute-start(bf16[512,2048]{1,0:T(8,128)(2,1)} %convolution_convert_fusion.5), channel_id=1, source_target_pairs={{0,2},{1,5},{2,0},{3,7},{4,6},{5,1},{6,4},{7,3},{8,10},{9,13},{10,... | collective-permute-start | bytes 6291464 | tf_op jit(solution)/shard_map/ppermute | solution.py:347
  453.7 87.5 %collective-permute-start.26 = (bf16[512,2048]{1,0:T(8,128)(2,1)}, bf16[512,2048]{1,0:T(8,128)(2,1)}, u32[]{:S(2)}, u32[]{:S(2)}) collective-permute-start(bf16[512,2048]{1,0:T(8,128)(2,1)} %convolution_convert_fusion.2), channel_id=1, source_target_pairs={{0,2},{1,5},{2,0},{3,7},{4,6},{5,1},{6,4},{7,3},{8,10},{9,13},{10,... | collective-permute-start | bytes 6291464 | tf_op jit(solution)/shard_map/ppermute | solution.py:347
  458.4 102.3 %collective-permute-start.20 = (bf16[512,2048]{1,0:T(8,128)(2,1)}, bf16[512,2048]{1,0:T(8,128)(2,1)}, u32[]{:S(2)}, u32[]{:S(2)}) collective-permute-start(bf16[512,2048]{1,0:T(8,128)(2,1)} %convolution_convert_fusion.4), channel_id=1, source_target_pairs={{0,2},{1,5},{2,0},{3,7},{4,6},{5,1},{6,4},{7,3},{8,10},{9,13},{10,... | collective-permute-start | bytes 6291464 | tf_op jit(solution)/shard_map/ppermute | solution.py:347
  481.8 73.2 %collective-permute-start.28 = (bf16[704,2048]{1,0:T(8,128)(2,1)}, bf16[704,2048]{1,0:T(8,128)(2,1)S(1)}, u32[]{:S(2)}, u32[]{:S(2)}) collective-permute-start(bf16[704,2048]{1,0:T(8,128)(2,1)} %dynamic-slice_bitcast_fusion.2), channel_id=1, source_target_pairs={{0,1},{1,0},{2,3},{3,2},{4,5},{5,4},{6,7},{7,6},{8,9},{9,8},{10,11... | collective-permute-start | bytes 8650760 | tf_op jit(solution)/shard_map/ppermute | solution.py:355
  541.2 225.6 %collective-permute-start.57 = (bf16[4,1,256,2816]{3,2,0,1:T(8,128)(2,1)}, bf16[4,1,256,2816]{3,2,0,1:T(8,128)(2,1)}, u32[]{:S(2)}, u32[]{:S(2)}) collective-permute-start(bf16[4,1,256,2816]{3,2,0,1:T(8,128)(2,1)} %dynamic-slice_bitcast_fusion), channel_id=1, source_target_pairs={{0,1},{1,0},{2,3},{3,2},{4,5},{5,4},{6,7},{7,6},{8,9},{9,8},{10,11... | collective-permute-start | bytes 17301512 | tf_op jit(solution)/shard_map/ppermute | solution.py:355
  556.6 39.4 %collective-permute-start.27 = (bf16[512,2048]{1,0:T(8,128)(2,1)}, bf16[512,2048]{1,0:T(8,128)(2,1)S(1)}, u32[]{:S(2)}, u32[]{:S(2)}) collective-permute-start(bf16[512,2048]{1,0:T(8,128)(2,1)} %add_convert_fusion.2), channel_id=1, source_target_pairs={{0,4},{1,3},{2,6},{3,1},{4,0},{5,7},{6,2},{7,5},{8,12},{9,11},{10,... | collective-permute-start | bytes 6291464 | tf_op jit(solution)/shard_map/ppermute | solution.py:351
  560.7 32.6 %collective-permute-start.70 = (bf16[176,2048]{1,0:T(8,128)(2,1)S(1)}, bf16[176,2048]{1,0:T(8,128)(2,1)S(1)}, u32[]{:S(2)}, u32[]{:S(2)}) collective-permute-start(bf16[176,2048]{1,0:T(8,128)(2,1)S(1)} %get-tuple-element.100), channel_id=1, source_target_pairs={{0,8},{1,9},{2,10},{3,11},{4,12},{5,13},{6,14},{7,15}} | collective-permute-start | bytes 2162696 | tf_op jit(solution)/shard_map/ppermute | solution.py:402
  594.4 62.5 %collective-permute-start.73 = (bf16[176,2048]{1,0:T(8,128)(2,1)}, bf16[176,2048]{1,0:T(8,128)(2,1)}, u32[]{:S(2)}, u32[]{:S(2)}) collective-permute-start(bf16[176,2048]{1,0:T(8,128)(2,1)} %get-tuple-element.101), channel_id=1, source_target_pairs={{24,16},{25,17},{26,18},{27,19},{28,20},{29,21},{30,22},{31,23}} | collective-permute-start | bytes 2162696 | tf_op jit(solution)/shard_map/ppermute | solution.py:403
  596.0 60.9 %collective-permute-start.71 = (bf16[176,2048]{1,0:T(8,128)(2,1)}, bf16[176,2048]{1,0:T(8,128)(2,1)}, u32[]{:S(2)}, u32[]{:S(2)}) collective-permute-start(bf16[176,2048]{1,0:T(8,128)(2,1)} %fusion.90), channel_id=1, source_target_pairs={{0,8},{8,16},{1,9},{9,17},{2,10},{10,18},{3,11},{11,19},{4,12},{12... | collective-permute-start | bytes 2162696 | tf_op jit(solution)/shard_map/ppermute | solution.py:402
  641.2 31.0 %all-to-all-start.3 = ((bf16[8,512,256]{2,1,0:T(8,128)(2,1)}), bf16[8,512,256]{2,1,0:T(8,128)(2,1)}, u32[]{:S(2)}, u32[]{:S(2)}) async-start(bf16[8,512,256]{2,1,0:T(8,128)(2,1)} %bitcast.337), calls=%async_computation.3 | async-start | bytes 4194304 | tf_op jit(solution)/shard_map/all_to_all | solution.py:890
  659.9 161.7 %collective-permute-start.74 = (bf16[176,2048]{1,0:T(8,128)(2,1)}, bf16[176,2048]{1,0:T(8,128)(2,1)}, u32[]{:S(2)}, u32[]{:S(2)}) collective-permute-start(bf16[176,2048]{1,0:T(8,128)(2,1)} %get-tuple-element.99), channel_id=1, source_target_pairs={{24,16},{16,8},{25,17},{17,9},{26,18},{18,10},{27,19},{19,11},{28,... | collective-permute-start | bytes 2162696 | tf_op jit(solution)/shard_map/ppermute | solution.py:403
  762.3 89.7 %all-to-all-start.4 = ((bf16[8,512,384]{2,1,0:T(8,128)(2,1)}), bf16[8,512,384]{2,1,0:T(8,128)(2,1)}, u32[]{:S(2)}, u32[]{:S(2)}) async-start(bf16[8,512,384]{2,1,0:T(8,128)(2,1)} %attend_back.1), calls=%async_computation.4 | async-start | bytes 6291456 | tf_op jit(solution)/shard_map/all_to_all | solution.py:922
  766.8 315.8 %reduce-scatter.2.cloned.1.call-start = ((), (), s32[]{:S(2)}) async-start(), calls=%async_computation.7 | async-start | bytes 10027008 | tf_op jit(solution)/shard_map/reduce_scatter | solution.py:915
  775.9 63.8 %collective-permute-start.58 = (bf16[4,64,2816]{2,1,0:T(8,128)(2,1)}, bf16[4,64,2816]{2,1,0:T(8,128)(2,1)}, u32[]{:S(2)}, u32[]{:S(2)}) collective-permute-start(bf16[4,64,2816]{2,1,0:T(8,128)(2,1)} %get-tuple-element.82), channel_id=1, source_target_pairs={{0,8},{1,9},{2,10},{3,11},{4,12},{5,13},{6,14},{7,15}} | collective-permute-start | bytes 4325384 | tf_op jit(solution)/shard_map/ppermute | solution.py:402
  808.6 31.1 %collective-permute-start.61 = (bf16[4,64,2816]{2,1,0:T(8,128)(2,1)}, bf16[4,64,2816]{2,1,0:T(8,128)(2,1)}, u32[]{:S(2)}, u32[]{:S(2)}) collective-permute-start(bf16[4,64,2816]{2,1,0:T(8,128)(2,1)} %get-tuple-element.83), channel_id=1, source_target_pairs={{24,16},{25,17},{26,18},{27,19},{28,20},{29,21},{30,22},{31,23}} | collective-permute-start | bytes 4325384 | tf_op jit(solution)/shard_map/ppermute | solution.py:403
  819.2 77.4 %collective-permute-start.72 = (bf16[176,2048]{1,0:T(8,128)(2,1)}, bf16[176,2048]{1,0:T(8,128)(2,1)}, u32[]{:S(2)}, u32[]{:S(2)}) collective-permute-start(bf16[176,2048]{1,0:T(8,128)(2,1)} %get-tuple-element.98), channel_id=1, source_target_pairs={{0,8},{8,16},{16,24},{1,9},{9,17},{17,25},{2,10},{10,18},{18,26},{... | collective-permute-start | bytes 2162696 | tf_op jit(solution)/shard_map/ppermute | solution.py:402
  823.8 72.8 %collective-permute-start.75 = (bf16[176,2048]{1,0:T(8,128)(2,1)}, bf16[176,2048]{1,0:T(8,128)(2,1)}, u32[]{:S(2)}, u32[]{:S(2)}) collective-permute-start(bf16[176,2048]{1,0:T(8,128)(2,1)} %fusion.89), channel_id=1, source_target_pairs={{24,16},{16,8},{8,0},{25,17},{17,9},{9,1},{26,18},{18,10},{10,2},{... | collective-permute-start | bytes 2162696 | tf_op jit(solution)/shard_map/ppermute | solution.py:403
  844.6 40.9 %collective-permute-start.59 = (bf16[4,64,2816]{2,1,0:T(8,128)(2,1)}, bf16[4,64,2816]{2,1,0:T(8,128)(2,1)}, u32[]{:S(2)}, u32[]{:S(2)}) collective-permute-start(bf16[4,64,2816]{2,1,0:T(8,128)(2,1)} %get-tuple-element.80), channel_id=1, source_target_pairs={{0,8},{8,16},{1,9},{9,17},{2,10},{10,18},{3,11},{11,19},{4,12},{12... | collective-permute-start | bytes 4325384 | tf_op jit(solution)/shard_map/ppermute | solution.py:402
  850.2 35.3 %collective-permute-start.62 = (bf16[4,64,2816]{2,1,0:T(8,128)(2,1)}, bf16[4,64,2816]{2,1,0:T(8,128)(2,1)}, u32[]{:S(2)}, u32[]{:S(2)}) collective-permute-start(bf16[4,64,2816]{2,1,0:T(8,128)(2,1)} %get-tuple-element.81), channel_id=1, source_target_pairs={{24,16},{16,8},{25,17},{17,9},{26,18},{18,10},{27,19},{19,11},{28,... | collective-permute-start | bytes 4325384 | tf_op jit(solution)/shard_map/ppermute | solution.py:403
  882.6 127.4 %collective-permute-start.29 = (bf16[4,256,2688]{2,1,0:T(8,128)(2,1)}, bf16[4,256,2688]{2,1,0:T(8,128)(2,1)}, u32[]{:S(2)}, u32[]{:S(2)}) collective-permute-start(bf16[4,256,2688]{2,1,0:T(8,128)(2,1)} %dynamic-slice_bitcast_fusion.1), channel_id=1, source_target_pairs={{0,1},{1,0},{2,3},{3,2},{4,5},{5,4},{6,7},{7,6},{8,9},{9,8},{10,11... | collective-permute-start | bytes 16515080 | tf_op jit(solution)/shard_map/ppermute | solution.py:355
  889.2 53.1 %collective-permute-start.63 = (bf16[4,64,2816]{2,1,0:T(8,128)(2,1)}, bf16[4,64,2816]{2,1,0:T(8,128)(2,1)}, u32[]{:S(2)}, u32[]{:S(2)}) collective-permute-start(bf16[4,64,2816]{2,1,0:T(8,128)(2,1)} %get-tuple-element.79), channel_id=1, source_target_pairs={{24,16},{16,8},{8,0},{25,17},{17,9},{9,1},{26,18},{18,10},{10,2},{... | collective-permute-start | bytes 4325384 | tf_op jit(solution)/shard_map/ppermute | solution.py:403
  890.4 51.8 %collective-permute-start.60 = (bf16[4,64,2816]{2,1,0:T(8,128)(2,1)S(1)}, bf16[4,64,2816]{2,1,0:T(8,128)(2,1)}, u32[]{:S(2)}, u32[]{:S(2)}) collective-permute-start(bf16[4,64,2816]{2,1,0:T(8,128)(2,1)S(1)} %get-tuple-element.78), channel_id=1, source_target_pairs={{0,8},{8,16},{16,24},{1,9},{9,17},{17,25},{2,10},{10,18},{18,26},{... | collective-permute-start | bytes 4325384 | tf_op jit(solution)/shard_map/ppermute | solution.py:402
  901.6 38.9 %collective-permute-start.77 = (bf16[176,2048]{1,0:T(8,128)(2,1)}, bf16[176,2048]{1,0:T(8,128)(2,1)}, u32[]{:S(2)}, u32[]{:S(2)}) collective-permute-start(bf16[176,2048]{1,0:T(8,128)(2,1)} %get-tuple-element.63), channel_id=1, source_target_pairs={{8,0},{16,8},{24,16},{9,1},{17,9},{25,17},{10,2},{18,10},{26,18},{... | collective-permute-start | bytes 2162696 | tf_op jit(solution)/shard_map/ppermute | solution.py:413
  902.9 46.9 %collective-permute-start.76 = (bf16[176,2048]{1,0:T(8,128)(2,1)}, bf16[176,2048]{1,0:T(8,128)(2,1)}, u32[]{:S(2)}, u32[]{:S(2)}) collective-permute-start(bf16[176,2048]{1,0:T(8,128)(2,1)} %get-tuple-element.63), channel_id=1, source_target_pairs={{0,8},{8,16},{16,24},{1,9},{9,17},{17,25},{2,10},{10,18},{18,26},{... | collective-permute-start | bytes 2162696 | tf_op jit(solution)/shard_map/ppermute | solution.py:412
  966.9 41.9 %collective-permute-start.65 = (bf16[4,64,2816]{2,1,0:T(8,128)(2,1)S(1)}, bf16[4,64,2816]{2,1,0:T(8,128)(2,1)S(1)}, u32[]{:S(2)}, u32[]{:S(2)}) collective-permute-start(bf16[4,64,2816]{2,1,0:T(8,128)(2,1)S(1)} %all-to-all-done.5), channel_id=1, source_target_pairs={{8,0},{16,8},{24,16},{9,1},{17,9},{25,17},{10,2},{18,10},{26,18},{... | collective-permute-start | bytes 4325384 | tf_op jit(solution)/shard_map/ppermute | solution.py:413
  987.7 34.8 %collective-permute-start.64 = (bf16[4,64,2816]{2,1,0:T(8,128)(2,1)S(1)}, bf16[4,64,2816]{2,1,0:T(8,128)(2,1)S(1)}, u32[]{:S(2)}, u32[]{:S(2)}) collective-permute-start(bf16[4,64,2816]{2,1,0:T(8,128)(2,1)S(1)} %all-to-all-done.5), channel_id=1, source_target_pairs={{0,8},{8,16},{16,24},{1,9},{9,17},{17,25},{2,10},{10,18},{18,26},{... | collective-permute-start | bytes 4325384 | tf_op jit(solution)/shard_map/ppermute | solution.py:412
  1008.8 32.5 %collective-permute-start.66 = (bf16[4,64,2816]{2,1,0:T(8,128)(2,1)S(1)}, bf16[4,64,2816]{2,1,0:T(8,128)(2,1)S(1)}, u32[]{:S(2)}, u32[]{:S(2)}) collective-permute-start(bf16[4,64,2816]{2,1,0:T(8,128)(2,1)S(1)} %collective-permute-done.65), channel_id=1, source_target_pairs={{8,0},{16,8},{9,1},{17,9},{10,2},{18,10},{11,3},{19,11},{12,4},{20... | collective-permute-start | bytes 4325384 | tf_op jit(solution)/shard_map/ppermute | solution.py:413
  1041.2 31.5 %collective-permute-start.67 = (bf16[4,64,2816]{2,1,0:T(8,128)(2,1)S(1)}, bf16[4,64,2816]{2,1,0:T(8,128)(2,1)S(1)}, u32[]{:S(2)}, u32[]{:S(2)}) collective-permute-start(bf16[4,64,2816]{2,1,0:T(8,128)(2,1)S(1)} %collective-permute-done.66), channel_id=1, source_target_pairs={{8,0},{9,1},{10,2},{11,3},{12,4},{13,5},{14,6},{15,7}} | collective-permute-start | bytes 4325384 | tf_op jit(solution)/shard_map/ppermute | solution.py:413
  1047.8 112.2 %collective-permute-start.69 = (bf16[4,64,2816]{2,1,0:T(8,128)(2,1)}, bf16[4,64,2816]{2,1,0:T(8,128)(2,1)}, u32[]{:S(2)}, u32[]{:S(2)}) collective-permute-start(bf16[4,64,2816]{2,1,0:T(8,128)(2,1)} %collective-permute-done.68), channel_id=1, source_target_pairs={{16,24},{17,25},{18,26},{19,27},{20,28},{21,29},{22,30},{23,31}} | collective-permute-start | bytes 4325384 | tf_op jit(solution)/shard_map/ppermute | solution.py:412
  (113 other events, 2307.7 us)
Sparse Core Ops, SparseCore 0:
  120.1 108.3 all-gather.2
  819.3 72.3 reduce-scatter.1

commit v2 on v0

--- a/solution.py
+++ b/solution.py
@@ -1,6 +1,11 @@
+import functools
+import math
+
 import jax
 import jax.numpy as jnp
 from jax import lax
+from jax.experimental import pallas as pl
+from jax.experimental.pallas import tpu as pltpu
 from jax.sharding import PartitionSpec as P
 
 D = 2048
@@ -162,7 +167,7 @@
     return (jnp.concatenate(grad_query, axis=1), grad_key, grad_value)
 
 
-def body(tokens, segment_ids, selected, cotangent, w_qkv, w_out, w_gate_up, w_down, g_attn, g_mlp):
+def general_body(tokens, segment_ids, selected, cotangent, w_qkv, w_out, w_gate_up, w_down, g_attn, g_mlp):
     streams, local_len, model_dim = tokens.shape
     sp_count = lax.axis_size("sp")
     sp_index = lax.axis_index("sp")
@@ -318,6 +323,1137 @@
     )
 
 
+CHIPS = 4
+BLOCK = 512
+SHORT = pl.CostEstimate(flops=1, bytes_accessed=1, transcendentals=0)
+LOG2E = math.log2(math.e)
+BF = jnp.bfloat16
+F32 = jnp.float32
+NT = (((1,), (1,)), ((), ()))
+TN = (((0,), (0,)), ((), ()))
+
+
+def swap_pairs(even_mask, odd_mask):
+    return [(i, i ^ (odd_mask if i & 1 else even_mask)) for i in range(2 * CHIPS)]
+
+
+FIRST = swap_pairs(2, 4)
+SECOND = swap_pairs(4, 2)
+SIBLING = swap_pairs(1, 1)
+SAME_CORE = [[0, 2, 4, 6], [1, 3, 5, 7]]
+
+
+def send_first(x):
+    return lax.ppermute(x, "sp", FIRST)
+
+
+def send_second(x):
+    return lax.ppermute(x, "sp", SECOND)
+
+
+def send_sibling(x):
+    return lax.ppermute(x, "sp", SIBLING)
+
+
+def after(value, *others):
+    return lax.optimization_barrier((value,) + others)[0]
+
+
+def gather_chips(own):
+    first = send_first(own)
+    second = send_second(after(own, first))
+    far = send_second(after(first, second))
+    return [own, first, second, far]
+
+
+def rel_masks(core):
+    first = jnp.where(core == 0, 2, 4)
+    return first, 6 - first
+
+
+def fence(*values):
+    return lax.optimization_barrier(values)
+
+
+def gather_vectors(own, me):
+    for bit in (1, 2, 4):
+        got = lax.ppermute(own, "sp", swap_pairs(bit, bit))
+        high = (me & bit) != 0
+        own = jnp.concatenate([jnp.where(high, got, own), jnp.where(high, own, got)], axis=1)
+    return own
+
+
+def pick(parts, index):
+    return lax.dynamic_index_in_dim(parts, index, 0, keepdims=False)
+
+
+def pick_sum(parts, index, axis):
+    return sum(lax.dynamic_index_in_dim(p, index, axis, keepdims=False).astype(F32) for p in parts)
+
+
+def line_scatter_sends(parts, got, step, axis):
+    planes = parts[0].shape[axis]
+    z = lax.axis_index("dp")
+    ahead = pick_sum(parts, jnp.clip(planes - step + z, 0, planes - 1), axis)
+    back = pick_sum(parts, jnp.clip(z - planes + step, 0, planes - 1), axis)
+    if got is not None:
+        ahead = ahead + got[0].astype(F32)
+        back = back + got[1].astype(F32)
+    return ahead.astype(BF), back.astype(BF)
+
+
+def line_scatter_move(sends, step):
+    planes = lax.axis_size("dp")
+    right = lax.ppermute(sends[0], "dp", [(i, i + 1) for i in range(step)])
+    left = lax.ppermute(sends[1], "dp", [(planes - 1 - i, planes - 2 - i) for i in range(step)])
+    return right, left
+
+
+def line_scatter_end(parts, got, axis):
+    own = pick_sum(parts, lax.axis_index("dp"), axis)
+    return (own + got[0].astype(F32) + got[1].astype(F32)).astype(BF)
+
+
+def line_gather_move(got, step):
+    planes = lax.axis_size("dp")
+    right = lax.ppermute(got[0], "dp", [(i, i + 1) for i in range(step - 1, planes - 1)])
+    left = lax.ppermute(got[1], "dp", [(i + 1, i) for i in range(planes - step)])
+    return right, left
+
+
+def line_values(refs, planes, z):
+    for step in range(planes):
+        place = lax.rem(z - step + planes, planes)
+        if step == 0:
+            yield place, lambda index: refs[0][index]
+        else:
+            right, left = refs[step], refs[2 * planes - 1 - step]
+            yield place, lambda index, right=right, left=left, step=step: jnp.where(z >= step, right[index], left[index])
+
+
+def spread_kernel(in_ref, w_ref, g_ref, out_ref, gain_ref):
+    planes, _, rows, width = in_ref.shape
+    out = in_ref[...].reshape(planes * rows, width).astype(F32)
+    out_ref[...] = out
+    part = jnp.sum(out * w_ref[...].astype(F32), axis=-1, keepdims=True) / g_ref[...]
+
+    @pl.when(pl.program_id(0) == 0)
+    def _():
+        gain_ref[...] = part
+
+    @pl.when(pl.program_id(0) > 0)
+    def _():
+        gain_ref[...] += part
+
+
+def spread(parts, weight, gain):
+    planes, chips, rows, both = parts.shape
+    half = both // 2
+    total = planes * rows
+    line = pl.BlockSpec((total, half), lambda i: (0, i))
+    column = pl.BlockSpec((total, 1), lambda i: (0, 0))
+    return pl.pallas_call(
+        spread_kernel,
+        grid=(2 * chips,),
+        in_specs=[pl.BlockSpec((planes, 1, rows, half), lambda i: (0, i % chips, 0, i // chips)), line, column],
+        out_specs=[line, column],
+        out_shape=[jax.ShapeDtypeStruct(weight.shape, F32), jax.ShapeDtypeStruct((total, 1), F32)],
+        compiler_params=pltpu.CompilerParams(vmem_limit_bytes=32 * 2**20),
+        cost_estimate=SHORT,
+        name="spread",
+    )(parts, weight, gain)
+
+
+def spread_rows_kernel(z_ref, *refs, planes):
+    blocks, out_ref = refs[:-1], refs[-1]
+    rows = blocks[0].shape[0]
+    for place, load in line_values(blocks, planes, z_ref[0]):
+        out_ref[pl.ds(pl.multiple_of(place * rows, rows), rows), :] = load(slice(None)).astype(F32)
+
+
+def spread_rows(steps):
+    planes = len(steps)
+    rows, width = steps[0][0].shape
+    blocks = [steps[0][0]] + [s[0] for s in steps[1:]] + [s[1] for s in steps[1:]]
+    tile = width // 4
+    return pl.pallas_call(
+        functools.partial(spread_rows_kernel, planes=planes),
+        grid_spec=pltpu.PrefetchScalarGridSpec(
+            num_scalar_prefetch=1,
+            grid=(4,),
+            in_specs=[pl.BlockSpec((rows, tile), lambda i, z: (0, i))] * len(blocks),
+            out_specs=pl.BlockSpec((planes * rows, tile), lambda i, z: (0, i)),
+        ),
+        out_shape=jax.ShapeDtypeStruct((planes * rows, width), F32),
+        compiler_params=pltpu.CompilerParams(vmem_limit_bytes=32 * 2**20),
+        cost_estimate=SHORT,
+        name="spread_rows",
+    )(lax.axis_index("dp").reshape(1), *blocks)
+
+
+def spread_qkv_kernel(z_ref, *refs, planes):
+    blocks, (w_ref, g_ref, out_ref, gain_ref) = refs[:-4], refs[-4:]
+    devices, rows, width = blocks[0].shape
+    heads = width - 2 * HD
+    base = devices * heads
+    z = z_ref[0]
+    for place, load in line_values(blocks, planes, z):
+        span = pl.ds(pl.multiple_of(place * rows, rows), rows)
+        pairs = []
+        for d in range(devices):
+            block = load(d).astype(F32)
+            out_ref[span, d * heads : (d + 1) * heads] = block[:, :heads]
+            pairs.append(block[:, heads:])
+        for g in range(0, KV, 2):
+            low = pairs[2 * g] + pairs[2 * g + 1]
+            high = pairs[2 * g + 2] + pairs[2 * g + 3]
+            lane = lax.broadcasted_iota(jnp.int32, low.shape, 1)
+            out_ref[span, base + g * HD : base + (g + 2) * HD] = jnp.where(lane < HD, low, pltpu.roll(high, HD, 1))
+            out_ref[span, base + (KV + g) * HD : base + (KV + g + 2) * HD] = jnp.where(
+                lane < HD, pltpu.roll(low, HD, 1), high
+            )
+    gain_ref[...] = jnp.sum(out_ref[...] * w_ref[...].astype(F32), axis=-1, keepdims=True) / g_ref[...]
+
+
+def spread_qkv(steps, weight, gain):
+    planes = len(steps)
+    blocks = [steps[0][0]] + [s[0] for s in steps[1:]] + [s[1] for s in steps[1:]]
+    vmem = pl.BlockSpec(memory_space=pltpu.VMEM)
+    return pl.pallas_call(
+        functools.partial(spread_qkv_kernel, planes=planes),
+        in_specs=[pl.BlockSpec(memory_space=pltpu.SMEM)] + [vmem] * (len(blocks) + 2),
+        out_specs=[vmem, vmem],
+        out_shape=[jax.ShapeDtypeStruct(weight.shape, F32), jax.ShapeDtypeStruct((weight.shape[0], 1), F32)],
+        compiler_params=pltpu.CompilerParams(vmem_limit_bytes=32 * 2**20),
+        cost_estimate=SHORT,
+        name="spread_qkv",
+    )(lax.axis_index("dp").reshape(1), *blocks, weight, gain)
+
+
+def join_kernel(core_ref, mine_ref, theirs_ref, out_ref):
+    planes, _, rows, both = mine_ref.shape
+    block = jnp.where(pl.program_id(1) == 0, mine_ref[...], theirs_ref[...]).reshape(planes * rows, both)
+    out_ref[0, 0, 0] = block[:, : both // 2]
+    out_ref[1, 0, 0] = block[:, both // 2 :]
+
+
+def join(core, mine, theirs):
+    planes, chips, rows, both = mine.shape
+    spec = pl.BlockSpec((planes, 1, rows, both), lambda c, k, core: (0, c, 0, 0))
+    out = pl.pallas_call(
+        join_kernel,
+        grid_spec=pltpu.PrefetchScalarGridSpec(
+            num_scalar_prefetch=1,
+            grid=(chips, 2),
+            in_specs=[spec, spec],
+            out_specs=pl.BlockSpec(
+                (2, 1, 1, planes * rows, both // 2), lambda c, k, core: (0, c, (core[0] + k) % 2, 0, 0)
+            ),
+        ),
+        out_shape=jax.ShapeDtypeStruct((2, chips, 2, planes * rows, both // 2), BF),
+        compiler_params=pltpu.CompilerParams(vmem_limit_bytes=32 * 2**20),
+        cost_estimate=SHORT,
+        name="join",
+    )(core.reshape(1), mine, theirs)
+    return out.reshape(2, 2 * chips * planes * rows, both // 2)
+
+
+def ffn_kernel(b_ref, dy_ref, wg_ref, wu_ref, wd_ref, hid_ref, dg_ref, du_ref, db_ref, y_ref):
+    gate = jnp.dot(b_ref[...], wg_ref[...], preferred_element_type=F32)
+    up = jnp.dot(b_ref[...], wu_ref[...], preferred_element_type=F32)
+    d_hidden = lax.dot_general(dy_ref[...], wd_ref[...], NT, preferred_element_type=F32)
+    sigmoid_g = jax.nn.sigmoid(gate)
+    silu_gate = gate * sigmoid_g
+    hid = (silu_gate * up).astype(BF)
+    d_gate = (d_hidden * up * (sigmoid_g * (1.0 + gate * (1.0 - sigmoid_g)))).astype(BF)
+    d_up = (d_hidden * silu_gate).astype(BF)
+    hid_ref[...] = hid
+    dg_ref[...] = d_gate
+    du_ref[...] = d_up
+    y_ref[...] = jnp.dot(hid, wd_ref[...], preferred_element_type=F32).astype(BF)
+    d_in = lax.dot_general(d_gate, wg_ref[...], NT, preferred_element_type=F32)
+    db_ref[...] = (d_in + lax.dot_general(d_up, wu_ref[...], NT, preferred_element_type=F32)).astype(BF)
+
+
+def ffn(b_rows, dy_rows, w_gu, w_dn):
+    rows, width = b_rows.shape
+    hidden = w_dn.shape[0]
+    return pl.pallas_call(
+        ffn_kernel,
+        grid=(1,),
+        in_specs=[
+            pl.BlockSpec((rows, width), lambda i: (0, 0)),
+            pl.BlockSpec((rows, width), lambda i: (0, 0)),
+            pl.BlockSpec((None, width, hidden), lambda i: (0, 0, 0)),
+            pl.BlockSpec((None, width, hidden), lambda i: (1, 0, 0)),
+            pl.BlockSpec((hidden, width), lambda i: (0, 0)),
+        ],
+        out_specs=[pl.BlockSpec((rows, hidden), lambda i: (0, 0))] * 3
+        + [pl.BlockSpec((rows, width), lambda i: (0, 0))] * 2,
+        out_shape=[jax.ShapeDtypeStruct((rows, hidden), BF)] * 3 + [jax.ShapeDtypeStruct((rows, width), BF)] * 2,
+        compiler_params=pltpu.CompilerParams(vmem_limit_bytes=58 * 2**20),
+        cost_estimate=SHORT,
+        name="ffn",
+    )(b_rows, dy_rows, w_gu, w_gu, w_dn)
+
+
+def grad_gu_kernel(core_ref, *refs, count):
+    left, right = refs[: 2 * count], refs[2 * count : 4 * count]
+    half = right[0].shape[1]
+    for side in range(2):
+        for kind in range(2):
+            total = None
+            for r in range(count):
+                a_rows = left[side * count + r][...]
+                part = lax.dot_general(a_rows, right[kind * count + r][...], TN, preferred_element_type=F32)
+                total = part if total is None else total + part
+            refs[4 * count + side][0, :, kind * half : (kind + 1) * half] = total.astype(BF)
+
+
+def grad_gu(core, b_rows, dg_rows, du_rows, share):
+    count = len(b_rows)
+    tokens, width = b_rows[0].shape
+    hidden = dg_rows[0].shape[1]
+    keep = pl.BlockSpec((tokens, share), lambda c, core: (0, 2 * c + core[0]))
+    give = pl.BlockSpec((tokens, share), lambda c, core: (0, 2 * c + 1 - core[0]))
+    whole = pl.BlockSpec((tokens, hidden), lambda c, core: (0, 0))
+    out = pl.BlockSpec((1, share, 2 * hidden), lambda c, core: (c, 0, 0))
+    return pl.pallas_call(
+        functools.partial(grad_gu_kernel, count=count),
+        grid_spec=pltpu.PrefetchScalarGridSpec(
+            num_scalar_prefetch=1,
+            grid=(width // (2 * share),),
+            in_specs=[keep] * count + [give] * count + [whole] * (2 * count),
+            out_specs=[out, out],
+        ),
+        out_shape=[jax.ShapeDtypeStruct((width // (2 * share), share, 2 * hidden), BF)] * 2,
+        compiler_params=pltpu.CompilerParams(vmem_limit_bytes=58 * 2**20),
+        cost_estimate=SHORT,
+        name="grad_gu",
+    )(core.reshape(1), *b_rows, *b_rows, *dg_rows, *du_rows)
+
+
+def grad_qkv_kernel(place_ref, *refs, count):
+    dp_ref, out_ref = refs[-2:]
+    total = None
+    for r in range(count):
+        part = lax.dot_general(refs[r][...], dp_ref[place_ref[r]], TN, preferred_element_type=F32)
+        total = part if total is None else total + part
+    out_ref[...] = total.astype(BF)
+
+
+def grad_qkv(places, a_rows, dp_heads):
+    count = len(a_rows)
+    tokens, width = a_rows[0].shape
+    columns = dp_heads.shape[2]
+    depth = 512
+    return pl.pallas_call(
+        functools.partial(grad_qkv_kernel, count=count),
+        grid_spec=pltpu.PrefetchScalarGridSpec(
+            num_scalar_prefetch=1,
+            grid=(width // depth,),
+            in_specs=[pl.BlockSpec((tokens, depth), lambda i, p: (0, i))] * count
+            + [pl.BlockSpec(dp_heads.shape, lambda i, p: (0, 0, 0))],
+            out_specs=pl.BlockSpec((depth, columns), lambda i, p: (i, 0)),
+        ),
+        out_shape=jax.ShapeDtypeStruct((width, columns), BF),
+        compiler_params=pltpu.CompilerParams(vmem_limit_bytes=48 * 2**20),
+        cost_estimate=SHORT,
+        name="grad_qkv",
+    )(places, *a_rows, dp_heads)
+
+
+def swap_halves(values):
+    width = values.shape[-1]
+    lane = lax.broadcasted_iota(jnp.int32, values.shape, 1)
+    ahead = pltpu.roll(values, width - HD // 2, 1)
+    behind = pltpu.roll(values, HD // 2, 1)
+    return jnp.where(lane % HD < HD // 2, ahead, behind)
+
+
+def project_kernel(place_ref, x_ref, gain_ref, cos_ref, sin_ref, *refs, count):
+    wq_refs, wkv_refs = refs[:count], refs[count : 2 * count]
+    send_ref, normed_ref, inv_ref, normed_scr = refs[2 * count :]
+    share = normed_scr.shape[2]
+
+    @pl.when(pl.program_id(0) == 0)
+    def _():
+        x = x_ref[...].astype(F32)
+        inv = lax.rsqrt(jnp.mean(x * x, axis=-1, keepdims=True) + EPSILON)
+        normed = (x * inv * gain_ref[...]).astype(BF)
+        normed_ref[...] = normed
+        inv_ref[...] = inv
+        for part in range(count):
+            normed_scr[part] = normed[:, part * share : (part + 1) * share]
+
+    pq = pkv = None
+    for r in range(count):
+        a_rows = normed_scr[place_ref[r]]
+        q_part = jnp.dot(a_rows, wq_refs[r][...], preferred_element_type=F32)
+        kv_part = jnp.dot(a_rows, wkv_refs[r][...], preferred_element_type=F32)
+        pq = q_part if pq is None else pq + q_part
+        pkv = kv_part if pkv is None else pkv + kv_part
+    cos = cos_ref[...]
+    sin = sin_ref[...]
+    heads = pq.shape[1]
+    q_scale = LOG2E * HD**-0.5
+    turned = pq * jnp.tile(cos, (1, heads // 128)) + swap_halves(pq) * jnp.tile(sin, (1, heads // 128))
+    send_ref[0, :, :heads] = (turned * q_scale).astype(BF)
+    lane = lax.broadcasted_iota(jnp.int32, pkv.shape, 1)
+    turned_kv = jnp.where(lane < HD, pkv * cos + swap_halves(pkv) * sin, pkv)
+    send_ref[0, :, heads:] = turned_kv.astype(BF)
+
+
+def project(places, x, gain, cos, sin, parts):
+    rows, width = x.shape
+    count = len(parts)
+    heads = width // count
+    out_width = heads + 2 * HD
+    depth = parts[0].shape[0]
+    first_kv = width // (2 * HD)
+    return pl.pallas_call(
+        functools.partial(project_kernel, count=count),
+        grid_spec=pltpu.PrefetchScalarGridSpec(
+            num_scalar_prefetch=1,
+            grid=(count,),
+            in_specs=[
+                pl.BlockSpec((rows, width), lambda d, p: (0, 0)),
+                pl.BlockSpec((1, width), lambda d, p: (0, 0)),
+                pl.BlockSpec((rows, 128), lambda d, p: (0, 0)),
+                pl.BlockSpec((rows, 128), lambda d, p: (0, 0)),
+            ]
+            + [pl.BlockSpec((depth, heads), lambda d, p: (0, d))] * count
+            + [pl.BlockSpec((depth, 2 * HD), lambda d, p: (0, first_kv + d // 2))] * count,
+            out_specs=[
+                pl.BlockSpec((1, rows, out_width), lambda d, p: (d, 0, 0)),
+                pl.BlockSpec((rows, width), lambda d, p: (0, 0)),
+                pl.BlockSpec((rows, 1), lambda d, p: (0, 0)),
+            ],
+            scratch_shapes=[pltpu.VMEM((count, rows, width // count), BF)],
+        ),
+        out_shape=[
+            jax.ShapeDtypeStruct((count, rows, out_width), BF),
+            jax.ShapeDtypeStruct((rows, width), BF),
+            jax.ShapeDtypeStruct((rows, 1), F32),
+        ],
+        compiler_params=pltpu.CompilerParams(vmem_limit_bytes=48 * 2**20),
+        cost_estimate=SHORT,
+        name="project",
+    )(places, x, gain, cos, sin, *parts, *parts)
+
+
+def out_proj_kernel(place_ref, attn_ref, x_ref, gain_ref, *refs, count):
+    parts, (resid_ref, inv_ref, inner_ref) = refs[:count], refs[count:]
+    width = x_ref.shape[1]
+    tile = 512
+    square = None
+    for begin in range(0, width, tile):
+        cols = slice(begin, begin + tile)
+        total = x_ref[:, cols].astype(F32)
+        for r in range(count):
+            total = total + jnp.dot(attn_ref[place_ref[r]], parts[r][:, cols], preferred_element_type=F32)
+        resid_ref[:, cols] = total
+        part = jnp.sum(total * total, axis=-1, keepdims=True)
+        square = part if square is None else square + part
+    inv = lax.rsqrt(square / width + EPSILON)
+    inv_ref[...] = inv
+    inner_ref[...] = (resid_ref[...] * inv * gain_ref[...]).astype(BF)
+
+
+def out_proj(places, attn, x, gain, parts):
+    count, rows, share = attn.shape
+    width = x.shape[1]
+    step = rows // 2
+    line = pl.BlockSpec((step, width), lambda i, p: (i, 0))
+    return pl.pallas_call(
+        functools.partial(out_proj_kernel, count=count),
+        grid_spec=pltpu.PrefetchScalarGridSpec(
+            num_scalar_prefetch=1,
+            grid=(rows // step,),
+            in_specs=[
+                pl.BlockSpec((count, step, share), lambda i, p: (0, i, 0)),
+                line,
+                pl.BlockSpec((1, width), lambda i, p: (0, 0)),
+            ]
+            + [pl.BlockSpec((share, width), lambda i, p: (0, 0))] * count,
+            out_specs=[line, pl.BlockSpec((step, 1), lambda i, p: (i, 0)), line],
+        ),
+        out_shape=[
+            jax.ShapeDtypeStruct((rows, width), F32),
+            jax.ShapeDtypeStruct((rows, 1), F32),
+            jax.ShapeDtypeStruct((rows, width), BF),
+        ],
+        compiler_params=pltpu.CompilerParams(vmem_limit_bytes=56 * 2**20),
+        cost_estimate=SHORT,
+        name="out_proj",
+    )(places, attn, x, gain, *parts)
+
+
+def resid_back_kernel(place_ref, db_ref, first_ref, passed_ref, resid_ref, inv_ref, gain_ref, dy_ref, *refs, count):
+    parts, (d_resid_ref, branch_ref, send_ref) = refs[:count], refs[count:]
+    d_inner = db_ref[...].astype(F32) + first_ref[...].astype(F32) + passed_ref[...].astype(F32)
+    resid = resid_ref[...]
+    inv = inv_ref[...]
+    scaled = d_inner * gain_ref[...]
+    inner_mean = jnp.mean(scaled * resid, axis=-1, keepdims=True)
+    d_resid = dy_ref[...].astype(F32) + inv * scaled - resid * (inv * inv * inv * inner_mean)
+    d_resid_ref[...] = d_resid
+    branch = d_resid.astype(BF)
+    branch_ref[...] = branch
+    for r in range(count):
+        d_attn = lax.dot_general(branch, parts[r][...], NT, preferred_element_type=F32)
+        send_ref[place_ref[r]] = d_attn.astype(BF)
+
+
+def resid_back(places, db_own, db_first, db_passed, resid, inv, gain, dy, parts):
+    rows, width = resid.shape
+    count = len(parts)
+    share = parts[0].shape[0]
+    step = rows // 2
+    line = pl.BlockSpec((step, width), lambda i, p: (i, 0))
+    return pl.pallas_call(
+        functools.partial(resid_back_kernel, count=count),
+        grid_spec=pltpu.PrefetchScalarGridSpec(
+            num_scalar_prefetch=1,
+            grid=(rows // step,),
+            in_specs=[line, line, line, line]
+            + [pl.BlockSpec((step, 1), lambda i, p: (i, 0)), pl.BlockSpec((1, width), lambda i, p: (0, 0)), line]
+            + [pl.BlockSpec((share, width), lambda i, p: (0, 0))] * count,
+            out_specs=[line, line, pl.BlockSpec((count, step, share), lambda i, p: (0, i, 0))],
+        ),
+        out_shape=[
+            jax.ShapeDtypeStruct((rows, width), F32),
+            jax.ShapeDtypeStruct((rows, width), BF),
+            jax.ShapeDtypeStruct((count, rows, share), BF),
+        ],
+        compiler_params=pltpu.CompilerParams(vmem_limit_bytes=56 * 2**20),
+        cost_estimate=SHORT,
+        name="resid_back",
+    )(places, db_own, db_first, db_passed, resid, inv, gain, dy, *parts)
+
+
+def in_back_kernel(place_ref, back_ref, x_ref, inv_ref, gain_ref, d_resid_ref, *refs, count):
+    parts, (out_ref, mixed, d_scr) = refs[:count], refs[count:]
+    devices, _, width = back_ref.shape
+    heads = width - 2 * HD
+    for d in range(devices):
+        mixed[:, d * heads : (d + 1) * heads] = back_ref[d, :, :heads]
+    base = devices * heads
+    for g in range(KV):
+        pair = back_ref[2 * g, :, heads:].astype(F32) + back_ref[2 * g + 1, :, heads:].astype(F32)
+        mixed[:, base + 2 * g * HD : base + 2 * (g + 1) * HD] = pair.astype(BF)
+    for r in range(count):
+        d_scr[place_ref[r]] = lax.dot_general(mixed[...], parts[r][...], NT, preferred_element_type=F32)
+    inv = inv_ref[...]
+    share = d_scr.shape[2]
+    inner = None
+    for c in range(count):
+        cols = slice(c * share, (c + 1) * share)
+        part = jnp.sum(d_scr[c] * gain_ref[:, cols] * x_ref[:, cols].astype(F32), axis=-1, keepdims=True)
+        inner = part if inner is None else inner + part
+    factor = inv * inv * inv * (inner / (count * share))
+    for c in range(count):
+        cols = slice(c * share, (c + 1) * share)
+        through = inv * (d_scr[c] * gain_ref[:, cols]) - x_ref[:, cols].astype(F32) * factor
+        out_ref[:, cols] = (d_resid_ref[:, cols] + through).astype(BF)
+
+
+def in_back(places, back, x, inv, gain, d_resid, parts):
+    rows, width = x.shape
+    count = len(parts)
+    share, columns = parts[0].shape
+    step = rows // 2
+    line = pl.BlockSpec((step, width), lambda i, p: (i, 0))
+    return pl.pallas_call(
+        functools.partial(in_back_kernel, count=count),
+        grid_spec=pltpu.PrefetchScalarGridSpec(
+            num_scalar_prefetch=1,
+            grid=(rows // step,),
+            in_specs=[
+                pl.BlockSpec((count, step, back.shape[2]), lambda i, p: (0, i, 0)),
+                line,
+                pl.BlockSpec((step, 1), lambda i, p: (i, 0)),
+                pl.BlockSpec((1, width), lambda i, p: (0, 0)),
+                line,
+            ]
+            + [pl.BlockSpec((share, columns), lambda i, p: (0, 0))] * count,
+            out_specs=line,
+            scratch_shapes=[pltpu.VMEM((step, columns), BF), pltpu.VMEM((count, step, share), F32)],
+        ),
+        out_shape=jax.ShapeDtypeStruct((rows, width), BF),
+        compiler_params=pltpu.CompilerParams(vmem_limit_bytes=56 * 2**20),
+        cost_estimate=SHORT,
+        name="in_back",
+    )(places, back, x, inv, gain, d_resid, *parts)
+
+
+def grad_wo_kernel(core_ref, keep_ref, give_ref, branch_ref, keep_out, give_out):
+    branch = branch_ref[...]
+    keep_out[0] = lax.dot_general(keep_ref[0], branch, TN, preferred_element_type=F32).astype(BF)
+    give_out[0] = lax.dot_general(give_ref[0], branch, TN, preferred_element_type=F32).astype(BF)
+
+
+def grad_wo(core, attn, branch):
+    devices, rows, share = attn.shape
+    width = branch.shape[1]
+    out = pl.BlockSpec((1, share, width), lambda c, core: (c, 0, 0))
+    return pl.pallas_call(
+        grad_wo_kernel,
+        grid_spec=pltpu.PrefetchScalarGridSpec(
+            num_scalar_prefetch=1,
+            grid=(devices // 2,),
+            in_specs=[
+                pl.BlockSpec((1, rows, share), lambda c, core: (2 * c + core[0], 0, 0)),
+                pl.BlockSpec((1, rows, share), lambda c, core: (2 * c + 1 - core[0], 0, 0)),
+                pl.BlockSpec((rows, width), lambda c, core: (0, 0)),
+            ],
+            out_specs=[out, out],
+        ),
+        out_shape=[jax.ShapeDtypeStruct((devices // 2, share, width), BF)] * 2,
+        compiler_params=pltpu.CompilerParams(vmem_limit_bytes=48 * 2**20),
+        cost_estimate=SHORT,
+        name="grad_wo",
+    )(core.reshape(1), attn, attn, branch)
+
+
+def grad_dn_kernel(core_ref, *refs, count):
+    left, right, (keep_out, give_out) = refs[:count], refs[count : 2 * count], refs[2 * count :]
+    total = None
+    for r in range(count):
+        part = lax.dot_general(left[r][...], right[r][...], TN, preferred_element_type=F32)
+        total = part if total is None else total + part
+    half = total.shape[0] // 2
+    total = total.astype(BF)
+    low = core_ref[0] == 0
+    keep_out[...] = jnp.where(low, total[:half], total[half:])
+    give_out[...] = jnp.where(low, total[half:], total[:half])
+
+
+def grad_dn(core, hid_rows, dy_rows):
+    count = len(hid_rows)
+    tokens, hidden = hid_rows[0].shape
+    width = dy_rows[0].shape[1]
+    tile = 512
+    out = pl.BlockSpec((hidden // 2, tile), lambda i, core: (0, i))
+    return pl.pallas_call(
+        functools.partial(grad_dn_kernel, count=count),
+        grid_spec=pltpu.PrefetchScalarGridSpec(
+            num_scalar_prefetch=1,
+            grid=(width // tile,),
+            in_specs=[pl.BlockSpec((tokens, hidden), lambda i, core: (0, 0))] * count
+            + [pl.BlockSpec((tokens, tile), lambda i, core: (0, i))] * count,
+            out_specs=[out, out],
+        ),
+        out_shape=[jax.ShapeDtypeStruct((hidden // 2, width), BF)] * 2,
+        compiler_params=pltpu.CompilerParams(vmem_limit_bytes=56 * 2**20),
+        cost_estimate=SHORT,
+        name="grad_dn",
+    )(core.reshape(1), *hid_rows, *dy_rows)
+
+
+def attend_kernel(zeros_ref, q_ref, kv_ref, *refs, heads, start, stop):
+    o_ref, send_ref, lse_ref, k_scr, v_scr, acc_ref, max_ref = refs[-7:]
+    block = pl.program_id(0) + start
+    zeros = zeros_ref[0]
+    size = q_ref.shape[0]
+
+    @pl.when(block == start)
+    def _():
+        for part in range(stop):
+            rows = slice(part * size, (part + 1) * size)
+            both = kv_ref[rows, :].astype(F32)
+            lane = lax.broadcasted_iota(jnp.int32, both.shape, 1)
+            k_scr[rows, :] = kv_ref[rows, :HD]
+            v_scr[rows, :] = jnp.where(lane < HD, pltpu.roll(both, HD, 1), 1.0).astype(BF)
+
+    first_row = block * size
+    lowest = jnp.where(first_row >= zeros, zeros // size, 0)
+    acc_ref[...] = jnp.zeros_like(acc_ref)
+    max_ref[...] = jnp.full_like(max_ref, MASKED)
+    q_heads = [q_ref[:, h * HD : (h + 1) * HD] for h in range(heads)]
+
+    def step(index, masked):
+        first_key = pl.multiple_of(index * size, size)
+        keys = k_scr[pl.ds(first_key, size), :]
+        values = v_scr[pl.ds(first_key, size), :]
+        if masked:
+            row = first_row + lax.broadcasted_iota(jnp.int32, (size, size), 0)
+            col = first_key + lax.broadcasted_iota(jnp.int32, (size, size), 1)
+            begin = jnp.where(row >= zeros, zeros, 0)
+            refused = (col > row) | (col < begin)
+
+        def score(h):
+            return lax.dot_general(q_heads[h], keys, NT, preferred_element_type=F32)
+
+        upcoming = score(0)
+        for h in range(heads):
+            scores = upcoming
+            if h + 1 < heads:
+                upcoming = score(h + 1)
+            if masked:
+                scores = jnp.where(refused, MASKED, scores)
+            old_max = max_ref[h]
+            new_max = jnp.maximum(old_max, jnp.max(scores, axis=-1, keepdims=True))
+            weights = jnp.exp2(scores - jnp.tile(new_max, (1, size // 128)))
+            shrink = jnp.exp2(old_max - new_max)
+            acc_ref[h] = acc_ref[h] * shrink + jnp.dot(weights.astype(BF), values, preferred_element_type=F32)
+            max_ref[h] = new_max
+
+    def visit(index, carry):
+        first_key = index * size
+        mixed = (index == block) | ((first_row + size > zeros) & (first_key < zeros))
+
+        @pl.when(mixed)
+        def _():
+            step(index, True)
+
+        @pl.when(jnp.logical_not(mixed))
+        def _():
+            step(index, False)
+
+        return carry
+
+    lax.fori_loop(lowest, block + 1, visit, 0)
+    for h in range(heads):
+        acc = acc_ref[h]
+        total = acc[:, HD : HD + 1]
+        out = acc[:, :HD] / total
+        o_ref[:, h * HD : (h + 1) * HD] = out
+        send_ref[0, :, h * HD : (h + 1) * HD] = out.astype(BF)
+        lse = max_ref[h] + jnp.log2(total)
+        lse_ref[0, h : h + 1, :] = jnp.transpose(lse)[:1]
+
+
+def attend(zeros, qkv, start, stop, before=None):
+    length, width = qkv.shape
+    q_width = width - 2 * HD
+    heads = q_width // HD
+    size = BLOCK
+    blocks = length // size
+    before = () if before is None else before
+    return pl.pallas_call(
+        functools.partial(attend_kernel, heads=heads, start=start, stop=stop),
+        grid_spec=pltpu.PrefetchScalarGridSpec(
+            num_scalar_prefetch=1,
+            grid=(stop - start,),
+            in_specs=[
+                pl.BlockSpec((size, q_width), lambda i, z: (i + start, 0)),
+                pl.BlockSpec((length, 2 * HD), lambda i, z: (0, q_width // (2 * HD))),
+            ]
+            + [pl.BlockSpec(memory_space=pl.ANY)] * len(before),
+            out_specs=[
+                pl.BlockSpec((size, q_width), lambda i, z: (i + start, 0)),
+                pl.BlockSpec((1, size, q_width), lambda i, z: (i + start, 0, 0)),
+                pl.BlockSpec((1, heads, size), lambda i, z: (i + start, 0, 0)),
+            ],
+            scratch_shapes=[
+                pltpu.VMEM((length, HD), BF),
+                pltpu.VMEM((length, 2 * HD), BF),
+                pltpu.VMEM((heads, size, 2 * HD), F32),
+                pltpu.VMEM((heads, size, 128), F32),
+            ],
+        ),
+        out_shape=[
+            jax.ShapeDtypeStruct((length, q_width), F32),
+            jax.ShapeDtypeStruct((blocks, size, q_width), BF),
+            jax.ShapeDtypeStruct((blocks, heads, size), F32),
+        ],
+        input_output_aliases={3 + i: i for i in range(len(before))},
+        compiler_params=pltpu.CompilerParams(vmem_limit_bytes=48 * 2**20),
+        cost_estimate=SHORT,
+        name="attend",
+    )(zeros, qkv, qkv, *before)
+
+
+def attend_back_kernel(
+    zeros_ref, q_ref, kv_ref, do_ref, lse_ref, cos_ref, sin_ref, extra_ref, *refs, heads, start
+):
+    send_ref, dq_acc, delta_ref, q_scr, do_scr = refs[-5:]
+    block = pl.program_id(0) + start
+    zeros = zeros_ref[0]
+    size = kv_ref.shape[0]
+    length = q_ref.shape[0]
+    blocks = length // size
+
+    @pl.when(block == start)
+    def _():
+        if start == 0:
+            dq_acc[...] = jnp.zeros_like(dq_acc)
+        else:
+            dq_acc[...] = refs[0][...]
+            delta_ref[...] = extra_ref[...]
+        for part in range(start, blocks):
+            rows = slice(part * size, (part + 1) * size)
+            if start == 0:
+                product = jnp.transpose(do_ref[rows, :].astype(F32) * extra_ref[rows, :])
+            for h in range(heads):
+                cols = slice(h * HD, (h + 1) * HD)
+                q_scr[h, rows, :] = q_ref[rows, cols]
+                do_scr[h, rows, :] = do_ref[rows, cols]
+                if start == 0:
+                    delta_ref[part, h : h + 1, :] = jnp.sum(product[cols], axis=0, keepdims=True)
+
+    first_key = block * size
+    both = kv_ref[...]
+    keys = both[:, :HD]
+    values = both[:, HD:]
+    keys_t = jnp.transpose(keys.astype(F32)).astype(BF)
+    highest = jnp.where(first_key + size <= zeros, jnp.minimum((zeros + size - 1) // size, blocks), blocks)
+
+    def step(index, carry, masked):
+        first_row = pl.multiple_of(index * size, size)
+        span = pl.ds(first_row, size)
+        if masked:
+            col = first_key + lax.broadcasted_iota(jnp.int32, (size, size), 0)
+            row = first_row + lax.broadcasted_iota(jnp.int32, (size, size), 1)
+            begin = jnp.where(row >= zeros, zeros, 0)
+            refused = (col > row) | (col < begin)
+
+        def products(h):
+            q_rows = q_scr[h, span, :]
+            do_rows = do_scr[h, span, :]
+            scores = lax.dot_general(keys, q_rows, NT, preferred_element_type=F32)
+            d_prob = lax.dot_general(values, do_rows, NT, preferred_element_type=F32)
+            return q_rows, do_rows, scores, d_prob
+
+        upcoming = products(0)
+        dk_sum, dv_sum = carry
+        for h in range(heads):
+            q_rows, do_rows, scores, d_prob = upcoming
+            if h + 1 < heads:
+                upcoming = products(h + 1)
+            shifted = scores - lse_ref[index, h : h + 1, :]
+            if masked:
+                shifted = jnp.where(refused, MASKED, shifted)
+            prob = jnp.exp2(shifted)
+            d_score = (prob * (d_prob - delta_ref[index, h : h + 1, :])).astype(BF)
+            dv_sum = dv_sum + jnp.dot(prob.astype(BF), do_rows, preferred_element_type=F32)
+            dk_sum = dk_sum + jnp.dot(d_score, q_rows, preferred_element_type=F32)
+            dq_acc[h * HD : (h + 1) * HD, span] += jnp.dot(keys_t, d_score, preferred_element_type=F32)
+        return dk_sum, dv_sum
+
+    def visit(index, carry):
+        first_row = index * size
+        mixed = (index == block) | ((first_row + size > zeros) & (first_key < zeros))
+        return lax.cond(
+            mixed,
+            lambda c: step(index, c, True),
+            lambda c: step(index, c, False),
+            carry,
+        )
+
+    zero = jnp.zeros((size, HD), F32)
+    dk_sum, dv_sum = lax.fori_loop(block, highest, visit, (zero, zero))
+    q_width = heads * HD
+    done = pl.ds(pl.multiple_of(first_key, size), size)
+    cos = cos_ref[...]
+    sin = sin_ref[...]
+    dq = jnp.transpose(dq_acc[:, done]) * HD**-0.5
+    dq = dq * jnp.tile(cos, (1, q_width // 128)) - swap_halves(dq) * jnp.tile(sin, (1, q_width // 128))
+    send_ref[0, :, :q_width] = dq.astype(BF)
+    dkv = jnp.concatenate([dk_sum * (1.0 / LOG2E), dv_sum], axis=1)
+    lane = lax.broadcasted_iota(jnp.int32, dkv.shape, 1)
+    send_ref[0, :, q_width:] = jnp.where(lane < HD, dkv * cos - swap_halves(dkv) * sin, dkv).astype(BF)
+
+
+def attend_back(zeros, qkv, d_out, lse, cos, sin, start, stop, out=None, before=None):
+    length, width = qkv.shape
+    q_width = width - 2 * HD
+    heads = q_width // HD
+    size = BLOCK
+    blocks = length // size
+    whole = lambda *shape: pl.BlockSpec(shape, lambda j, z: (0,) * len(shape))
+    if before is None:
+        operands = (out,)
+        specs = [whole(length, q_width)]
+        aliases = {}
+    else:
+        send, d_query, delta = before
+        operands = (delta, d_query, send)
+        specs = [whole(blocks, heads, size), whole(q_width, length), pl.BlockSpec(memory_space=pl.ANY)]
+        aliases = {9: 0}
+    return pl.pallas_call(
+        functools.partial(attend_back_kernel, heads=heads, start=start),
+        grid_spec=pltpu.PrefetchScalarGridSpec(
+            num_scalar_prefetch=1,
+            grid=(stop - start,),
+            in_specs=[
+                whole(length, q_width),
+                pl.BlockSpec((size, 2 * HD), lambda j, z: (j + start, q_width // (2 * HD))),
+                whole(length, q_width),
+                whole(blocks, heads, size),
+                pl.BlockSpec((size, 128), lambda j, z: (j + start, 0)),
+                pl.BlockSpec((size, 128), lambda j, z: (j + start, 0)),
+            ]
+            + specs,
+            out_specs=[
+                pl.BlockSpec((1, size, width), lambda j, z: (j + start, 0, 0)),
+                whole(q_width, length),
+                whole(blocks, heads, size),
+            ],
+            scratch_shapes=[
+                pltpu.VMEM((heads, length, HD), BF),
+                pltpu.VMEM((heads, length, HD), BF),
+            ],
+        ),
+        out_shape=[
+            jax.ShapeDtypeStruct((blocks, size, width), BF),
+            jax.ShapeDtypeStruct((q_width, length), F32),
+            jax.ShapeDtypeStruct((blocks, heads, size), F32),
+        ],
+        input_output_aliases=aliases,
+        compiler_params=pltpu.CompilerParams(vmem_limit_bytes=58 * 2**20),
+        cost_estimate=SHORT,
+        name="attend_back",
+    )(zeros, qkv, qkv, d_out, lse, cos, sin, *operands)
+
+
+def turn_tables(positions):
+    cosine, sine = rope_tables(positions, HD)
+    return jnp.concatenate([cosine] * 4, axis=1), jnp.concatenate([-sine, sine, -sine, sine], axis=1)
+
+
+def fast_body(tokens, segment_ids, selected, cotangent, w_qkv, w_out, w_gate_up, w_down, g_attn, g_mlp):
+    _, rows, width = tokens.shape
+    devices = 2 * CHIPS
+    me = lax.axis_index("sp")
+    core = me & 1
+    planes = lax.axis_size("dp")
+    share = width // devices
+    kv_width = KV * HD
+    first_mask, second_mask = rel_masks(core)
+    other = me ^ 1
+    chip = me // 2
+    place_list = [me, me ^ first_mask, me ^ second_mask, me ^ 6]
+    place_list += [other, other ^ second_mask, other ^ first_mask, other ^ 6]
+    places = jnp.stack(place_list)
+    hidden_chip = 2 * w_down.shape[0]
+    quarter = share // planes
+    plane = lax.axis_index("dp")
+    length = devices * rows
+    blocks = length // BLOCK
+
+    count = jnp.sum((segment_ids == 0).astype(F32))
+    vectors = jnp.stack([g_attn.astype(F32), g_mlp.astype(F32)] + [jnp.full((share,), count)] * 6)
+    paired = [w_qkv[:, :width]]
+    for head in range(KV):
+        paired.append(w_qkv[:, width + head * HD : width + (head + 1) * HD])
+        paired.append(w_qkv[:, width + kv_width + head * HD : width + kv_width + (head + 1) * HD])
+    qkv_own = jnp.concatenate(paired, axis=1)
+    gu_rows = lax.dynamic_slice_in_dim(w_gate_up, plane * quarter, quarter, 0)
+    gu_send = []
+    for place in range(CHIPS):
+        for begin in (place * hidden_chip, (CHIPS + place) * hidden_chip):
+            gu_send.append(gu_rows[:, begin : begin + hidden_chip])
+    gu_send = jnp.stack([jnp.concatenate(gu_send[2 * c : 2 * c + 2], axis=1) for c in range(CHIPS)])
+    vectors = gather_vectors(vectors, me)
+    vectors, qkv_own, gu_send = fence(vectors, qkv_own, gu_send)
+    qkv_first = send_first(qkv_own)
+    attn_gain = vectors[0:1]
+    mlp_gain = vectors[1:2]
+    zeros = jnp.sum(vectors[2].reshape(devices, share)[:, 0]).astype(jnp.int32)
+    zeros_one = zeros.reshape(1)
+    local_pos = me * rows + jnp.arange(rows, dtype=jnp.int32) - segment_ids.reshape(rows) * zeros
+    cos, sin = turn_tables(local_pos)
+    dy = (cotangent * selected[:, :, None].astype(BF)).reshape(rows, width)
+    qkv_own, qkv_first, cos, sin = fence(qkv_own, qkv_first, cos, sin)
+    qkv_second = send_second(qkv_own)
+    qkv_theirs = [send_sibling(qkv_own), send_sibling(qkv_first)]
+    all_places = jnp.arange(length, dtype=jnp.int32)
+    cos_all, sin_all = turn_tables(all_places - jnp.where(all_places >= zeros, zeros, 0))
+    qkv_first, qkv_second, cos_all, sin_all, *qkv_theirs = fence(qkv_first, qkv_second, cos_all, sin_all, *qkv_theirs)
+    qkv_far = send_second(qkv_first)
+    qkv_theirs.append(send_sibling(qkv_second))
+    qkv_far, dy, *qkv_theirs = fence(qkv_far, dy, *qkv_theirs)
+    qkv_theirs.append(send_sibling(qkv_far))
+    qkv_parts = [qkv_own, qkv_first, qkv_second, qkv_far] + qkv_theirs
+    x_bf = tokens.reshape(rows, width)
+    x_bf, w_out, gu_send, *qkv_parts = fence(x_bf, w_out, gu_send, *qkv_parts)
+    out_first = send_first(w_out)
+    gu_part = lax.all_to_all(gu_send, "sp", 0, 0, axis_index_groups=SAME_CORE, tiled=True)
+    qkv_send, normed, inv_one = project(places, x_bf, attn_gain, cos, sin, qkv_parts)
+    qkv_send, out_first = fence(qkv_send, out_first)
+    gu_mine = lax.all_gather(after(gu_part, qkv_send), "dp", axis=0, tiled=False)
+    gu_mine = lax.all_gather(after(gu_part, qkv_send), "dp", axis=0, tiled=False)
+    down_theirs = send_sibling(w_down)
+    w_dn = jnp.where(
+        core == 0, jnp.concatenate([w_down, down_theirs], axis=0), jnp.concatenate([down_theirs, w_down], axis=0)
+    )
+    qkv_heads = lax.all_to_all(qkv_send, "sp", 0, 0, tiled=True).reshape(length, qkv_send.shape[2])
+
+    cuts = (0, (5 * blocks) // 8, (7 * blocks) // 8, blocks)
+    qkv_heads, w_dn, out_first = fence(qkv_heads, w_dn, out_first)
+    out_second = send_second(after(w_out, qkv_heads))
+    dy_first = send_first(after(dy, qkv_heads))
+    fwd = attend(zeros_one, qkv_heads, cuts[0], cuts[1])
+    qkv_heads, out_second, dy_first, out_first, dy, *fwd = fence(qkv_heads, out_second, dy_first, out_first, dy, *fwd)
+    out_far = send_second(out_first)
+    dy_second = send_second(dy)
+    fwd = attend(zeros_one, qkv_heads, cuts[1], cuts[2], fwd)
+    qkv_heads, out_far, dy_second, dy_first, *fwd = fence(qkv_heads, out_far, dy_second, dy_first, *fwd)
+    dy_far = send_second(dy_first)
+    gu_theirs = send_sibling(after(gu_mine, fwd[2]))
+    out_heads, out_send, lse = attend(zeros_one, qkv_heads, cuts[2], cuts[3], fwd)
+    out_parts = [w_out, out_first, out_second, out_far]
+    out_parts = out_parts + [send_sibling(part) for part in out_parts]
+    out_send, gu_mine, gu_theirs = fence(out_send, gu_mine, gu_theirs)
+    attn_tok = lax.all_to_all(out_send, "sp", 0, 0, tiled=True)
+    w_gu = join(core, gu_mine, gu_theirs)
+    attn_tok, w_gu, dy_far, *out_parts = fence(attn_tok, w_gu, dy_far, *out_parts)
+    residual, inv_two, inner = out_proj(places, attn_tok, x_bf, mlp_gain, out_parts)
+
+    b_first = send_first(inner)
+    own = ffn(inner, dy, w_gu, w_dn)
+    inner, b_first, *own = fence(inner, b_first, *own)
+    b_second = send_second(inner)
+    first = ffn(b_first, dy_first, w_gu, w_dn)
+    b_first, b_second, *first = fence(b_first, b_second, *first)
+    b_far = send_second(b_first)
+    second = ffn(b_second, dy_second, w_gu, w_dn)
+    b_far, db_first, *second = fence(b_far, first[3], *second)
+    db_got_first = send_first(db_first)
+    far = ffn(b_far, dy_far, w_gu, w_dn)
+    db_got_first, db_far, *hid_rows = fence(db_got_first, far[3], own[0], first[0], second[0], far[0])
+
+    db_got_far = send_first(db_far)
+    dn_keep, dn_give = grad_dn(core, hid_rows, [dy, dy_first, dy_second, dy_far])
+    db_got_far, dn_keep, dn_give = fence(db_got_far, dn_keep, dn_give)
+    db_pass = (second[3].astype(F32) + db_got_far.astype(F32)).astype(BF)
+    b_own, db_pass, dn_give = fence(inner, db_pass, dn_give)
+    db_passed = send_second(db_pass)
+    dn_got = send_sibling(dn_give)
+    gu_keep, gu_give = grad_gu(
+        core,
+        [b_own, b_first, b_second, b_far],
+        [own[1], first[1], second[1], far[1]],
+        [own[2], first[2], second[2], far[2]],
+        share,
+    )
+    db_passed, dn_got, gu_keep, gu_give = fence(db_passed, dn_got, gu_keep, gu_give)
+    dn_parts = [part.reshape(planes, dn_keep.shape[0] // planes, width) for part in (dn_keep, dn_got)]
+    dn_moves = line_scatter_sends(dn_parts, None, 1, 0)
+    db_passed, gu_give, normed, *dn_moves = fence(db_passed, gu_give, normed, *dn_moves)
+    a_first = send_first(normed)
+    gu_got = send_sibling(gu_give)
+    dn_moves = line_scatter_move(dn_moves, 1)
+    d_resid, d_branch, d_send = resid_back(
+        places, own[3], db_got_first, db_passed, residual, inv_two, mlp_gain, dy, out_parts
+    )
+    d_send, d_branch, gu_got, *dn_moves = fence(d_send, d_branch, gu_got, *dn_moves)
+    gu_sum = (gu_keep.astype(F32) + gu_got.astype(F32)).astype(BF)
+    gu_sum = gu_sum.reshape(CHIPS, planes, quarter, 2 * hidden_chip).transpose(1, 0, 2, 3)
+    gu_z = lax.psum_scatter(
+        gu_sum.reshape(planes * CHIPS * quarter, 2 * hidden_chip), "dp", scatter_dimension=0, tiled=True
+    )
+    gu_z = gu_z.reshape(CHIPS, quarter, 2 * hidden_chip)
+    d_heads = lax.all_to_all(d_send, "sp", 0, 0, tiled=True).reshape(length, share)
+    dn_moves = line_scatter_sends(dn_parts, dn_moves, 2, 0)
+    dn_moves = line_scatter_move(dn_moves, 2)
+    wo_keep, wo_give = grad_wo(core, attn_tok, d_branch)
+    d_heads, wo_keep, wo_give, a_first, normed, *dn_moves = fence(d_heads, wo_keep, wo_give, a_first, normed, *dn_moves)
+
+    def back_call(heads, start, stop, **kwargs):
+        return attend_back(zeros_one, qkv_heads, heads, lse, cos_all, sin_all, start, stop, **kwargs)
+
+    turns = (0, blocks // 8, blocks // 4, blocks // 2, blocks)
+    dn_moves = line_scatter_sends(dn_parts, dn_moves, 3, 0)
+    d_heads, wo_give, normed, *dn_moves = fence(d_heads, wo_give, normed, *dn_moves)
+    wo_got = send_sibling(wo_give)
+    a_second = send_second(normed)
+    a_theirs = [send_sibling(normed)]
+    dn_moves = line_scatter_move(dn_moves, 3)
+    bwd = back_call(d_heads, turns[0], turns[1], out=out_heads)
+    d_heads, a_first, a_second, wo_got, *moves = fence(d_heads, a_first, a_second, wo_got, *a_theirs, *bwd)
+    a_theirs, bwd = moves[:1], moves[1:]
+
+    a_far = send_second(a_first)
+    a_theirs.append(send_sibling(a_first))
+    bwd = back_call(d_heads, turns[1], turns[2], before=bwd)
+    d_heads, gu_z, a_far, *moves = fence(d_heads, gu_z, a_far, *a_theirs, *dn_moves, *bwd)
+    a_theirs, dn_moves, bwd = moves[:2], moves[2:4], moves[4:]
+
+    def wo_part(place):
+        return pick(wo_keep, place).astype(F32) + pick(wo_got, place).astype(F32)
+
+    dn_z = line_scatter_end(dn_parts, dn_moves, 0)
+    wo_first = wo_part(chip ^ (first_mask // 2)).astype(BF)
+    wo_far = wo_part(chip ^ 3).astype(BF)
+    d_heads, dn_z, gu_z, a_second, wo_first, wo_far = fence(d_heads, dn_z, gu_z, a_second, wo_first, wo_far)
+    dn_all = lax.all_gather(dn_z, "dp", axis=0, tiled=False)
+    gu_z = lax.all_to_all(gu_z, "sp", 0, 0, axis_index_groups=SAME_CORE, tiled=True)
+    wo_far = send_first(wo_far)
+    wo_first = send_first(wo_first)
+    a_theirs.append(send_sibling(a_second))
+    bwd = back_call(d_heads, turns[2], turns[3], before=bwd)
+    d_heads, gu_z, wo_far, wo_first, *moves = fence(d_heads, gu_z, wo_far, wo_first, *a_theirs, *bwd)
+    a_theirs, bwd = moves[:3], moves[3:]
+
+    wo_pass = (wo_part(chip ^ (second_mask // 2)) + wo_far.astype(F32)).astype(BF)
+    d_heads, gu_z, wo_pass, a_far, y_far = fence(d_heads, gu_z, wo_pass, a_far, far[4])
+    gu_all = lax.all_gather(gu_z, "dp", axis=0, tiled=False)
+    wo_passed = send_second(wo_pass)
+    y_got_far = send_first(y_far)
+    a_theirs.append(send_sibling(a_far))
+    bwd = back_call(d_heads, turns[3], turns[4], before=bwd)
+    dp_heads, wo_passed, y_got_far, y_first, *a_theirs = fence(bwd[0], wo_passed, y_got_far, first[4], *a_theirs)
+
+    back = lax.all_to_all(dp_heads, "sp", 0, 0, tiled=True)
+    y_got_first = send_first(y_first)
+    grad_wq = grad_qkv(places, [normed, a_first, a_second, a_far] + list(a_theirs), dp_heads)
+    wq_parts = [grad_wq.reshape(devices, planes, quarter, dp_heads.shape[2])]
+    wo_rows = (wo_part(chip) + wo_first.astype(F32) + wo_passed.astype(F32)).astype(BF)
+    wo_parts = [wo_rows.reshape(planes, quarter, width)]
+    y_pass = (second[4].astype(F32) + y_got_far.astype(F32)).astype(BF)
+    wq_moves = wo_moves = None
+    for step in range(1, planes):
+        wq_moves = line_scatter_sends(wq_parts, wq_moves, step, 1)
+        wo_moves = line_scatter_sends(wo_parts, wo_moves, step, 0)
+        moves = fence(*wq_moves, *wo_moves, y_pass)
+        wq_moves = line_scatter_move(moves[:2], step)
+        wo_moves = line_scatter_move(moves[2:4], step)
+        if step == planes - 1:
+            y_got_first, y_pass = fence(y_got_first, moves[4])
+            y_passed = send_second(y_pass)
+        moves = fence(*wq_moves, *wo_moves)
+        wq_moves, wo_moves = moves[:2], moves[2:]
+    wq_z = line_scatter_end(wq_parts, wq_moves, 1)
+    wo_z = line_scatter_end(wo_parts, wo_moves, 0)
+    wq_z, wo_z, back = fence(wq_z, wo_z, back)
+    wo_steps = [(wo_z, wo_z), line_gather_move((wo_z, wo_z), 1)]
+    wq_z = lax.all_to_all(wq_z, "sp", 0, 0, tiled=True)
+    grad_tokens = in_back(places, back, x_bf, inv_one, attn_gain, d_resid, qkv_parts).reshape(tokens.shape)
+    wq_z, grad_tokens, y_passed, *moves = fence(wq_z, grad_tokens, y_passed, *wo_steps[-1])
+    wo_steps[-1] = tuple(moves)
+    wq_steps = [(wq_z, wq_z)]
+    outs = []
+    for step in range(1, planes):
+        wq_steps.append(line_gather_move(wq_steps[-1], step))
+        if len(wo_steps) < planes:
+            wo_steps.append(line_gather_move(wo_steps[-1], len(wo_steps)))
+        if step == 1:
+            y_sum = own[4].astype(F32) + y_got_first.astype(F32) + y_passed.astype(F32)
+            outs.append((residual + y_sum).astype(BF).reshape(tokens.shape))
+            outs.append(dn_all.astype(F32).reshape(w_down.shape))
+        elif step == 2:
+            outs += spread(gu_all, w_gate_up, g_mlp.astype(F32).reshape(share, 1))
+        if step == planes - 1:
+            outs.append(spread_rows(wo_steps))
+        moves = fence(*wq_steps[-1], *wo_steps[-1], *outs)
+        wq_steps[-1], wo_steps[-1], outs = tuple(moves[:2]), tuple(moves[2:4]), list(moves[4:])
+    output, grad_w_down, grad_w_gate_up, grad_g_mlp, grad_w_out = outs
+    grad_w_qkv, grad_g_attn = spread_qkv(wq_steps, w_qkv, g_attn.astype(F32).reshape(share, 1))
+    return (
+        output,
+        grad_tokens,
+        grad_w_qkv,
+        grad_w_out,
+        grad_w_gate_up,
+        grad_w_down,
+        grad_g_attn.reshape(share),
+        grad_g_mlp.reshape(share),
+    )
+
+
 def solution(mesh):
     in_specs = (
         P("dp", "sp", None),
@@ -341,4 +1477,5 @@
         P("sp"),
         P("sp"),
     )
+    body = fast_body if mesh.shape["sp"] == 2 * CHIPS else general_body
     return jax.shard_map(body, mesh=mesh, in_specs=in_specs, out_specs=out_specs, check_vma=False)

time: 2300 us -> 968 us (0.42)
  waiting for transfers between devices: 901 us -> 214 us
  matrix products: 681 us -> 0 us
  Pallas kernels: 0 us -> 432 us
  other arithmetic: 336 us -> 81 us
  local copies, waits for them, and re-layouts: 242 us -> 48.2 us
  starting transfers between devices: 17.8 us -> 169 us
  blocking collectives: 93.5 us -> 0 us
    dot_general x60 -> x0, matrix products: 681 us -> none  [the longest x8 124 us: attention_backward(): jnp.einsum('sqhd,skhd->shqk', grad_rows, value_part, preferred_element_ty...]
    pallas_call x0 -> x23, Pallas kernels: none -> 432 us  [the longest x4 118 us: ffn(): pl.pallas_call(ffn_kernel, grid=(1,), in_specs=[pl.BlockSpec((rows, width...]
    reduce_scatter x2 -> x1, waiting for transfers between devices: 373 us -> 0.02 us  [fast_body(): lax.psum_scatter(gu_sum.reshape(planes * CHIPS * quarter, 2 * hidden_chip...]
    psum x1 -> x0, waiting for transfers between devices: 296 us -> none  [body(): lax.psum(row_sums, 'dp').astype(jnp.float32)]
    ppermute x0 -> x74, waiting for transfers between devices: none -> 169 us  [the longest x11 56.5 us: send_first(): return lax.ppermute(x, 'sp', FIRST)]
    all_to_all x4 -> x7, waiting for transfers between devices: 186 us -> 44.7 us  [the longest x1 27.7 us: fast_body(): lax.all_to_all(qkv_send, 'sp', 0, 0, tiled=True)]
    ppermute x0 -> x74, starting transfers between devices: none -> 140 us  [the longest x9 74.5 us: line_scatter_move(): right = lax.ppermute(sends[0], 'dp', [(i, i + 1) for i in range(step)])]
    convert_element_type x13 -> x19, other arithmetic: 133 us -> 39.3 us  [the longest x7 12.6 us: line_scatter_sends(): return (ahead.astype(BF), back.astype(BF))]
  transfers between devices with their start and end apart: 11 -> 85, of which waited for: 6 -> 27; matrix products, arithmetic and copies ran while one was open for 49% -> 7% of each run, Pallas kernels for 0% -> 43%
where the time goes in v2:
time: 968 us; the launch traced here: 960 us
  Pallas kernels  432 us (45%)
  waiting for transfers between devices  214 us (22%)
  starting transfers between devices  169 us (17%)
  other arithmetic  81 us (8%)
  local copies, waits for them, and re-layouts  48.2 us (5%)
  between operations  15.6 us (2%)
    pallas_call x4, Pallas kernels, ffn(): pl.pallas_call(ffn_kernel, grid=(1,), in_specs=[pl.BlockSpec((rows, width...  118 us
    pallas_call x4, Pallas kernels, attend_back(): pl.pallas_call(functools.partial(attend_back_kernel, heads=heads, start=s...  113 us
    ppermute x9, starting transfers between devices, line_scatter_move(): right = lax.ppermute(sends[0], 'dp', [(i, i + 1) for i in range(step)])  74.5 us
    ppermute x11, waiting for transfers between devices, send_first(): return lax.ppermute(x, 'sp', FIRST)  56.5 us
    pallas_call x3, Pallas kernels, attend(): pl.pallas_call(functools.partial(attend_kernel, heads=heads, start=start,...  50 us
    ppermute x9, waiting for transfers between devices, line_scatter_move(): right = lax.ppermute(sends[0], 'dp', [(i, i + 1) for i in range(step)])  47.7 us
    unnamed x138, local copies, waits for them, and re-layouts  40.2 us
    ppermute x13, waiting for transfers between devices, send_second(): return lax.ppermute(x, 'sp', SECOND)  38 us
  transfers between devices with their start and end apart: 85, of which 27 were waited for; matrix products, arithmetic and copies ran while one was open for 7% of the time, Pallas kernels for 43%

profile of v2, /device:TPU:0, one launch (start us, length us, event | category | flops | bytes accessed | tf_op | source)
XLA Modules:
  0.0 959.6 jit_solution(17180320789334669111)
XLA Ops:
  27.8 12.1 %collective-permute-done.3.refs_1_.refs_9_ = bf16[256,2560]{1,0:T(8,128)(2,1)S(1)} collective-permute-done((bf16[256,2560]{1,0:T(8,128)(2,1)S(1)}, bf16[256,2560]{1,0:T(8,128)(2,1)S(1)}, u32[]{:S(2)}, u32[]{:S(2)}) %collective-permute-start.3) | collective-permute-done | bytes 1310752 | tf_op jit(solution)/shard_map/ppermute | solution.py:347
  42.5 7.5 fusion.20
  61.3 14.0 %collective-permute-done.7.refs_3_.refs_11_ = bf16[256,2560]{1,0:T(8,128)(2,1)S(1)} collective-permute-done((bf16[256,2560]{1,0:T(8,128)(2,1)S(1)}, bf16[256,2560]{1,0:T(8,128)(2,1)S(1)}, u32[]{:S(2)}, u32[]{:S(2)}) %collective-permute-start.7) | collective-permute-done | bytes 1310752 | tf_op jit(solution)/shard_map/ppermute | solution.py:351
  89.1 18.3 %project.1 = (bf16[8,512,384]{2,1,0:T(8,128)(2,1)}, bf16[512,2048]{1,0:T(8,128)(2,1)}, f32[512,1]{1,0:T(8,128)S(1)}) custom-call(s32[8]{0:T(128)S(1)} %stack.59.place_ref, bf16[512,2048]{1,0:T(8,128)(2,1)} %bitcast.163, f32[1,2048]{1,0:T(1,128)S(1)} %get-tuple-element.618.gain_ref, f32[512,128]{1,0:T(8,128)S(1)} %pad_maximum_fusion.3.cos_ref, ...), custom_call_target="tpu_custom_call" | custom-call | flops 1 | bytes 1 | tf_op jit(solution)/shard_map/project/pallas_call | solution.py:714
  108.1 5.6 collective-permute-done.10.refs_1_
  119.5 8.3 maximum_select_fusion.wd_ref
  127.8 27.7 %all-to-all-done = bf16[8,512,384]{2,1,0:T(8,128)(2,1)S(1)} async-done(((bf16[8,512,384]{2,1,0:T(8,128)(2,1)}), bf16[8,512,384]{2,1,0:T(8,128)(2,1)S(1)}, u32[]{:S(2)}, u32[]{:S(2)}) %all-to-all-start) | async-done | bytes 3145760 | tf_op jit(solution)/shard_map/all_to_all | solution.py:1282
  156.6 26.0 %attend.3 = (f32[4096,256]{1,0:T(8,128)}, bf16[8,512,256]{2,1,0:T(8,128)(2,1)S(1)}, f32[8,4,512]{2,1,0:T(4,128)S(1)}) custom-call(s32[1]{0:T(128)} %bitcast.14.zeros_ref, bf16[4096,384]{1,0:T(8,128)(2,1)S(1)} %bitcast.132, bf16[4096,384]{1,0:T(8,128)(2,1)S(1)} %bitcast.133), custom_call_target="tpu_custom_call" | custom-call | flops 1 | bytes 1 | tf_op jit(solution)/shard_map/attend/pallas_call | solution.py:1034
  182.6 8.3 collective-permute-done.13.dy_ref.refs_5_
  193.1 14.2 %attend.4 = (f32[4096,256]{1,0:T(8,128)}, bf16[8,512,256]{2,1,0:T(8,128)(2,1)S(1)}, f32[8,4,512]{2,1,0:T(4,128)S(1)}) custom-call(s32[1]{0:T(128)} %bitcast.14.zeros_ref, bf16[4096,384]{1,0:T(8,128)(2,1)S(1)} %bitcast.134, bf16[4096,384]{1,0:T(8,128)(2,1)S(1)} %bitcast.135, ...), custom_call_target="tpu_custom_call", output_to_operand_aliasing={{0}: (3, {}), {1}: (4, {}), {2}: (5, {})} | custom-call | flops 1 | bytes 1 | tf_op jit(solution)/shard_map/attend/pallas_call | solution.py:1034
  208.6 19.8 %collective-permute-done.14.refs_3_ = bf16[256,2048]{1,0:T(8,128)(2,1)S(1)} collective-permute-done((bf16[256,2048]{1,0:T(8,128)(2,1)}, bf16[256,2048]{1,0:T(8,128)(2,1)S(1)}, u32[]{:S(2)}, u32[]{:S(2)}) %collective-permute-start.14) | collective-permute-done | bytes 1048608 | tf_op jit(solution)/shard_map/ppermute | solution.py:351
  233.3 9.8 %attend.5 = (f32[4096,256]{1,0:T(8,128)}, bf16[8,512,256]{2,1,0:T(8,128)(2,1)S(1)}, f32[8,4,512]{2,1,0:T(4,128)S(1)}) custom-call(s32[1]{0:T(128)} %bitcast.14.zeros_ref, bf16[4096,384]{1,0:T(8,128)(2,1)S(1)} %bitcast.136, bf16[4096,384]{1,0:T(8,128)(2,1)S(1)} %bitcast.137, ...), custom_call_target="tpu_custom_call", output_to_operand_aliasing={{0}: (3, {}), {1}: (4, {}), {2}: (5, {})} | custom-call | flops 1 | bytes 1 | tf_op jit(solution)/shard_map/attend/pallas_call | solution.py:1034
  257.8 6.1 join.1
  266.5 12.9 %all-to-all-done.2.attn_ref.keep_ref.give_ref = bf16[8,512,256]{2,1,0:T(8,128)(2,1)S(1)} async-done(((bf16[8,512,256]{2,1,0:T(8,128)(2,1)}), bf16[8,512,256]{2,1,0:T(8,128)(2,1)S(1)}, u32[]{:S(2)}, u32[]{:S(2)}) %all-to-all-start.2) | async-done | bytes 2097184 | tf_op jit(solution)/shard_map/all_to_all | solution.py:1300
  280.8 11.7 %out_proj.1 = (f32[512,2048]{1,0:T(8,128)}, f32[512,1]{1,0:T(8,128)}, bf16[512,2048]{1,0:T(8,128)(2,1)}) custom-call(s32[8]{0:T(128)} %copy-done.27, bf16[8,512,256]{2,1,0:T(8,128)(2,1)} %copy-done.1, bf16[512,2048]{1,0:T(8,128)(2,1)} %bitcast.164, f32[1,2048]{1,0:T(1,128)} %get-tuple-element.617.gain_ref, bf16[256,2048]{1,0:T(8,128)(2,1)} %refs_0_.1, ...), custom_call_target="tpu_custom_call" | custom-call | flops 1 | bytes 1 | tf_op jit(solution)/shard_map/out_proj/pallas_call | solution.py:768
  293.6 29.2 %ffn.4 = (bf16[512,1408]{1,0:T(8,128)(2,1)}, bf16[512,1408]{1,0:T(8,128)(2,1)}, bf16[512,1408]{1,0:T(8,128)(2,1)}, bf16[512,2048]{1,0:T(8,128)(2,1)}, bf16[512,2048]{1,0:T(8,128)(2,1)}) custom-call(bf16[512,2048]{1,0:T(8,128)(2,1)} %get-tuple-element.410.b_ref.refs_0_.refs_4_, bf16[512,2048]{1,0:T(8,128)(2,1)} %multiply_bitcast_fusion.dy_ref.refs_4_, ...), custom_call_target="tpu_custom_call" | custom-call | flops 1 | bytes 1 | tf_op jit(solution)/shard_map/ffn/pallas_call | solution.py:581
  324.3 29.6 %ffn.5 = (bf16[512,1408]{1,0:T(8,128)(2,1)}, bf16[512,1408]{1,0:T(8,128)(2,1)}, bf16[512,1408]{1,0:T(8,128)(2,1)}, bf16[512,2048]{1,0:T(8,128)(2,1)}, bf16[512,2048]{1,0:T(8,128)(2,1)}) custom-call(bf16[512,2048]{1,0:T(8,128)(2,1)} %copy-done.31, bf16[512,2048]{1,0:T(8,128)(2,1)} %copy-done.39, bf16[2,2048,1408]{2,1,0:T(8,128)(2,1)} %bitcast.155, ...), custom_call_target="tpu_custom_call" | custom-call | flops 1 | bytes 1 | tf_op jit(solution)/shard_map/ffn/pallas_call | solution.py:581
  355.2 29.5 %ffn.6 = (bf16[512,1408]{1,0:T(8,128)(2,1)}, bf16[512,1408]{1,0:T(8,128)(2,1)}, bf16[512,1408]{1,0:T(8,128)(2,1)}, bf16[512,2048]{1,0:T(8,128)(2,1)}, bf16[512,2048]{1,0:T(8,128)(2,1)}) custom-call(bf16[512,2048]{1,0:T(8,128)(2,1)} %collective-permute-done.23.b_ref.refs_2_.refs_6_, bf16[512,2048]{1,0:T(8,128)(2,1)} %copy-done.40, ...), custom_call_target="tpu_custom_call" | custom-call | flops 1 | bytes 1 | tf_op jit(solution)/shard_map/ffn/pallas_call | solution.py:581
  386.1 29.7 %ffn.7 = (bf16[512,1408]{1,0:T(8,128)(2,1)}, bf16[512,1408]{1,0:T(8,128)(2,1)}, bf16[512,1408]{1,0:T(8,128)(2,1)}, bf16[512,2048]{1,0:T(8,128)(2,1)}, bf16[512,2048]{1,0:T(8,128)(2,1)}) custom-call(bf16[512,2048]{1,0:T(8,128)(2,1)} %copy-done.32, bf16[512,2048]{1,0:T(8,128)(2,1)} %collective-permute-done.17.dy_ref.refs_7_, bf16[2,2048,1408]{2,1,0:T(8,128)(2,1)} %bitcast.159, ...), custom_call_target="tpu_custom_call" | custom-call | flops 1 | bytes 1 | tf_op jit(solution)/shard_map/ffn/pallas_call | solution.py:581
  417.9 17.7 %grad_dn.1 = (bf16[704,2048]{1,0:T(8,128)(2,1)}, bf16[704,2048]{1,0:T(8,128)(2,1)}) custom-call(s32[1]{0:T(128)} %bitcast.20.core_ref, bf16[512,1408]{1,0:T(8,128)(2,1)} %get-tuple-element.400.refs_0_, bf16[512,1408]{1,0:T(8,128)(2,1)} %get-tuple-element.401.refs_1_, bf16[512,1408]{1,0:T(8,128)(2,1)} %get-tuple-element.402.refs_2_, ...), custom_call_target="tpu_custom_call" | custom-call | flops 1 | bytes 1 | tf_op jit(solution)/shard_map/grad_dn/pallas_call | solution.py:938
  435.6 7.8 collective-permute-done.26
  446.4 33.8 %grad_gu.1 = (bf16[4,256,2816]{2,1,0:T(8,128)(2,1)}, bf16[4,256,2816]{2,1,0:T(8,128)(2,1)}) custom-call(s32[1]{0:T(128)} %bitcast.20.core_ref, bf16[512,2048]{1,0:T(8,128)(2,1)} %get-tuple-element.410.b_ref.refs_0_.refs_4_, bf16[512,2048]{1,0:T(8,128)(2,1)} %copy-done.31, bf16[512,2048]{1,0:T(8,128)(2,1)} %collective-permute-done.23.b_ref.refs_2_.refs_6_, ...), custom_call_target="tpu_custom_call" | custom-call | flops 1 | bytes 1 | tf_op jit(solution)/shard_map/grad_gu/pallas_call | solution.py:621
  486.8 14.3 %resid_back.1 = (f32[512,2048]{1,0:T(8,128)}, bf16[512,2048]{1,0:T(8,128)(2,1)}, bf16[8,512,256]{2,1,0:T(8,128)(2,1)}) custom-call(s32[8]{0:T(128)} %copy-done.27, bf16[512,2048]{1,0:T(8,128)(2,1)} %get-tuple-element.372.db_ref, bf16[512,2048]{1,0:T(8,128)(2,1)} %copy-done.57, bf16[512,2048]{1,0:T(8,128)(2,1)} %collective-permute-done.27.passed_ref, ...), custom_call_target="tpu_custom_call" | custom-call | flops 1 | bytes 1 | tf_op jit(solution)/shard_map/resid_back/pallas_call | solution.py:814
  504.7 5.7 add_convert_fusion
  529.3 6.5 grad_wo.1
  535.8 15.2 %collective-permute-done.32.refs_1_ = bf16[512,2048]{1,0:T(8,128)(2,1)} collective-permute-done((bf16[512,2048]{1,0:T(8,128)(2,1)}, bf16[512,2048]{1,0:T(8,128)(2,1)}, u32[]{:S(2)}, u32[]{:S(2)}) %collective-permute-start.32) | collective-permute-done | bytes 2097184 | tf_op jit(solution)/shard_map/ppermute | solution.py:347
  551.0 7.9 collective-permute-done.33
  567.2 22.8 %attend_back.4 = (bf16[8,512,384]{2,1,0:T(8,128)(2,1)}, f32[256,4096]{1,0:T(8,128)}, f32[8,4,512]{2,1,0:T(4,128)}) custom-call(s32[1]{0:T(128)} %bitcast.14.zeros_ref, bf16[4096,384]{1,0:T(8,128)(2,1)} %bitcast.138, bf16[4096,384]{1,0:T(8,128)(2,1)} %bitcast.139, bf16[4096,256]{1,0:T(8,128)(2,1)} %bitcast.26.do_ref, f32[8,4,512]{2,1,0:T(4,128)} %copy-done.19, ...), custom_call_target="tpu_custom_call" | custom-call | flops 1 | bytes 1 | tf_op jit(solution)/shard_map/attend_back/pallas_call | solution.py:1175
  593.6 26.1 %collective-permute-start.40 = (bf16[176,2048]{1,0:T(8,128)(2,1)S(1)}, bf16[176,2048]{1,0:T(8,128)(2,1)}, u32[]{:S(2)}, u32[]{:S(2)}) collective-permute-start(bf16[176,2048]{1,0:T(8,128)(2,1)S(1)} %get-tuple-element.462), channel_id=1, source_target_pairs={{0,8},{8,16},{16,24},{1,9},{9,17},{17,25},{2,10},{10,18},{18,26},{... | collective-permute-start | bytes 2162696 | tf_op jit(solution)/shard_map/ppermute | solution.py:407
  621.2 18.6 %attend_back.5 = (bf16[8,512,384]{2,1,0:T(8,128)(2,1)}, f32[256,4096]{1,0:T(8,128)}, f32[8,4,512]{2,1,0:T(4,128)}) custom-call(s32[1]{0:T(128)} %bitcast.14.zeros_ref, bf16[4096,384]{1,0:T(8,128)(2,1)} %bitcast.140, bf16[4096,384]{1,0:T(8,128)(2,1)} %bitcast.141, bf16[4096,256]{1,0:T(8,128)(2,1)} %bitcast.26.do_ref, ...), custom_call_target="tpu_custom_call", output_to_operand_aliasing={{0}: (9, {})} | custom-call | flops 1 | bytes 1 | tf_op jit(solution)/shard_map/attend_back/pallas_call | solution.py:1175
  655.0 31.2 %attend_back.6 = (bf16[8,512,384]{2,1,0:T(8,128)(2,1)}, f32[256,4096]{1,0:T(8,128)}, f32[8,4,512]{2,1,0:T(4,128)}) custom-call(s32[1]{0:T(128)} %bitcast.14.zeros_ref, bf16[4096,384]{1,0:T(8,128)(2,1)} %bitcast.142, bf16[4096,384]{1,0:T(8,128)(2,1)} %bitcast.143, bf16[4096,256]{1,0:T(8,128)(2,1)} %bitcast.26.do_ref, ...), custom_call_target="tpu_custom_call", output_to_operand_aliasing={{0}: (9, {})} | custom-call | flops 1 | bytes 1 | tf_op jit(solution)/shard_map/attend_back/pallas_call | solution.py:1175
  686.3 7.4 collective-permute-done.43
  700.6 40.6 %attend_back.7 = (bf16[8,512,384]{2,1,0:T(8,128)(2,1)}, f32[256,4096]{1,0:T(8,128)}, f32[8,4,512]{2,1,0:T(4,128)}) custom-call(s32[1]{0:T(128)} %bitcast.14.zeros_ref, bf16[4096,384]{1,0:T(8,128)(2,1)} %bitcast.144, bf16[4096,384]{1,0:T(8,128)(2,1)} %bitcast.145, bf16[4096,256]{1,0:T(8,128)(2,1)} %bitcast.26.do_ref, ...), custom_call_target="tpu_custom_call", output_to_operand_aliasing={{0}: (9, {})} | custom-call | flops 1 | bytes 1 | tf_op jit(solution)/shard_map/attend_back/pallas_call | solution.py:1175
  742.5 13.9 %grad_qkv.1 = bf16[2048,384]{1,0:T(8,128)(2,1)S(1)} custom-call(s32[8]{0:T(128)S(1)} %copy-done.28, bf16[512,2048]{1,0:T(8,128)(2,1)} %get-tuple-element.446.refs_0_, bf16[512,2048]{1,0:T(8,128)(2,1)} %collective-permute-done.32.refs_1_, bf16[512,2048]{1,0:T(8,128)(2,1)} %collective-permute-done.35.refs_2_, ...), custom_call_target="tpu_custom_call" | custom-call | flops 1 | bytes 1 | tf_op jit(solution)/shard_map/grad_qkv/pallas_call | solution.py:650
  763.0 5.2 collective-permute-start.48
  772.4 24.6 %collective-permute-done.50 = bf16[64,2048]{1,0:T(8,128)(2,1)S(1)} collective-permute-done((bf16[64,2048]{1,0:T(8,128)(2,1)S(1)}, bf16[64,2048]{1,0:T(8,128)(2,1)S(1)}, u32[]{:S(2)}, u32[]{:S(2)}) %collective-permute-start.50) | collective-permute-done | bytes 262176 | tf_op jit(solution)/shard_map/ppermute | solution.py:407
  798.2 5.1 collective-permute-start.52
  804.7 11.1 %collective-permute-start.54 = (bf16[64,2048]{1,0:T(8,128)(2,1)}, bf16[64,2048]{1,0:T(8,128)(2,1)}, u32[]{:S(2)}, u32[]{:S(2)}) collective-permute-start(bf16[64,2048]{1,0:T(8,128)(2,1)} %get-tuple-element.526), channel_id=1, source_target_pairs={{0,8},{8,16},{1,9},{9,17},{2,10},{10,18},{3,11},{11,19},{4,12},{12... | collective-permute-start | bytes 786440 | tf_op jit(solution)/shard_map/ppermute | solution.py:407
  821.8 9.6 collective-permute-done.54
  840.4 13.3 %collective-permute-start.58 = (bf16[64,2048]{1,0:T(8,128)(2,1)S(1)}, bf16[64,2048]{1,0:T(8,128)(2,1)S(1)}, u32[]{:S(2)}, u32[]{:S(2)}) collective-permute-start(bf16[64,2048]{1,0:T(8,128)(2,1)S(1)} %get-tuple-element.534), channel_id=1, source_target_pairs={{0,8},{8,16},{16,24},{1,9},{9,17},{17,25},{2,10},{10,18},{18,26},{... | collective-permute-start | bytes 786440 | tf_op jit(solution)/shard_map/ppermute | solution.py:407
  857.6 7.2 collective-permute-done.59
  874.3 5.1 reshape.222
  879.4 14.5 %in_back.1 = bf16[512,2048]{1,0:T(8,128)(2,1)} custom-call(s32[8]{0:T(128)} %copy-done.27, bf16[8,512,384]{2,1,0:T(8,128)(2,1)} %all-to-all-done.5.back_ref, bf16[512,2048]{1,0:T(8,128)(2,1)} %bitcast.165, f32[512,1]{1,0:T(8,128)} %copy-done.21, f32[1,2048]{1,0:T(1,128)} %copy-done.26, f32[512,2048]{1,0:T(8,128)} %get-tuple-element.543.d_resid_ref, ...), custom_call_target="tpu_custom_call" | custom-call | flops 1 | bytes 1 | tf_op jit(solution)/shard_map/in_back/pallas_call | solution.py:867
  893.9 4.7 collective-permute-start.64
  902.6 7.0 fusion
  909.5 7.2 collective-permute-done.67.refs_5_
  926.9 6.5 spread.1
  942.1 6.0 collective-permute-done.73.refs_6_
  (347 shorter events, 226.9 us)
Async XLA Ops:
  79.5 34.3 %all-to-all-start.1 = ((bf16[4,64,2816]{2,1,0:T(8,128)(2,1)}), bf16[4,64,2816]{2,1,0:T(8,128)(2,1)}, u32[]{:S(2)}, u32[]{:S(2)}) async-start(bf16[4,64,2816]{2,1,0:T(8,128)(2,1)} %pad_maximum_fusion.2), calls=%async_computation.1 | async-start | bytes 2883584 | tf_op jit(solution)/shard_map/all_to_all | solution.py:1273
  83.8 146.2 %all-gather.7.cloned.1.call-start = ((), (), s32[]{:S(2)}) async-start(), calls=%async_computation.9 | async-start | bytes 7208960 | tf_op jit(solution)/shard_map/all_gather | solution.py:1277
  84.4 29.4 %collective-permute-start.10 = (bf16[256,2048]{1,0:T(8,128)(2,1)}, bf16[256,2048]{1,0:T(8,128)(2,1)}, u32[]{:S(2)}, u32[]{:S(2)}) collective-permute-start(bf16[256,2048]{1,0:T(8,128)(2,1)} %refs_0_.1), channel_id=1, source_target_pairs={{0,2},{1,5},{2,0},{3,7},{4,6},{5,1},{6,4},{7,3},{8,10},{9,13},{10,... | collective-permute-start | bytes 3145736 | tf_op jit(solution)/shard_map/ppermute | solution.py:347
  114.0 41.5 %all-to-all-start = ((bf16[8,512,384]{2,1,0:T(8,128)(2,1)}), bf16[8,512,384]{2,1,0:T(8,128)(2,1)S(1)}, u32[]{:S(2)}, u32[]{:S(2)}) async-start(bf16[8,512,384]{2,1,0:T(8,128)(2,1)} %get-tuple-element.321), calls=%async_computation | async-start | bytes 6291456 | tf_op jit(solution)/shard_map/all_to_all | solution.py:1282
  155.5 35.5 %collective-permute-start.13 = (bf16[512,2048]{1,0:T(8,128)(2,1)}, bf16[512,2048]{1,0:T(8,128)(2,1)S(1)}, u32[]{:S(2)}, u32[]{:S(2)}) collective-permute-start(bf16[512,2048]{1,0:T(8,128)(2,1)} %multiply_bitcast_fusion.dy_ref.refs_4_), channel_id=1, source_target_pairs={{0,2},{1,5},{2,0},{3,7},{4,6},{5,1},{6,4},{7,3},{8,10},{9,13},{10,... | collective-permute-start | bytes 6291464 | tf_op jit(solution)/shard_map/ppermute | solution.py:347
  156.0 26.7 %collective-permute-start.12 = (bf16[256,2048]{1,0:T(8,128)(2,1)}, bf16[256,2048]{1,0:T(8,128)(2,1)S(1)}, u32[]{:S(2)}, u32[]{:S(2)}) collective-permute-start(bf16[256,2048]{1,0:T(8,128)(2,1)} %refs_0_.1), channel_id=1, source_target_pairs={{0,4},{1,3},{2,6},{3,1},{4,0},{5,7},{6,2},{7,5},{8,12},{9,11},{10,... | collective-permute-start | bytes 3145736 | tf_op jit(solution)/shard_map/ppermute | solution.py:351
  191.0 37.3 %collective-permute-start.15 = (bf16[512,2048]{1,0:T(8,128)(2,1)S(1)}, bf16[512,2048]{1,0:T(8,128)(2,1)S(1)}, u32[]{:S(2)}, u32[]{:S(2)}) collective-permute-start(bf16[512,2048]{1,0:T(8,128)(2,1)S(1)} %copy-done.29), channel_id=1, source_target_pairs={{0,4},{1,3},{2,6},{3,1},{4,0},{5,7},{6,2},{7,5},{8,12},{9,11},{10,... | collective-permute-start | bytes 6291464 | tf_op jit(solution)/shard_map/ppermute | solution.py:351
  192.7 35.6 %collective-permute-start.14 = (bf16[256,2048]{1,0:T(8,128)(2,1)}, bf16[256,2048]{1,0:T(8,128)(2,1)S(1)}, u32[]{:S(2)}, u32[]{:S(2)}) collective-permute-start(bf16[256,2048]{1,0:T(8,128)(2,1)} %collective-permute-done.10.refs_1_), channel_id=1, source_target_pairs={{0,4},{1,3},{2,6},{3,1},{4,0},{5,7},{6,2},{7,5},{8,12},{9,11},{10,... | collective-permute-start | bytes 3145736 | tf_op jit(solution)/shard_map/ppermute | solution.py:351
  230.0 36.5 %collective-permute-start.17 = (bf16[512,2048]{1,0:T(8,128)(2,1)}, bf16[512,2048]{1,0:T(8,128)(2,1)}, u32[]{:S(2)}, u32[]{:S(2)}) collective-permute-start(bf16[512,2048]{1,0:T(8,128)(2,1)} %copy-done.39), channel_id=1, source_target_pairs={{0,4},{1,3},{2,6},{3,1},{4,0},{5,7},{6,2},{7,5},{8,12},{9,11},{10,... | collective-permute-start | bytes 6291464 | tf_op jit(solution)/shard_map/ppermute | solution.py:351
  247.6 31.8 %all-to-all-start.2 = ((bf16[8,512,256]{2,1,0:T(8,128)(2,1)}), bf16[8,512,256]{2,1,0:T(8,128)(2,1)S(1)}, u32[]{:S(2)}, u32[]{:S(2)}) async-start(bf16[8,512,256]{2,1,0:T(8,128)(2,1)} %copy-done.6), calls=%async_computation.2 | async-start | bytes 4194304 | tf_op jit(solution)/shard_map/all_to_all | solution.py:1300
  251.4 394.1 %reduce-scatter.2.cloned.1.call-start = ((), (), s32[]{:S(2)}) async-start(), calls=%async_computation.8 | async-start | bytes 7208960 | tf_op jit(solution)/shard_map/reduce_scatter | solution.py:1345
  292.5 30.3 %collective-permute-start.22 = (bf16[512,2048]{1,0:T(8,128)(2,1)}, bf16[512,2048]{1,0:T(8,128)(2,1)S(1)}, u32[]{:S(2)}, u32[]{:S(2)}) collective-permute-start(bf16[512,2048]{1,0:T(8,128)(2,1)} %get-tuple-element.410.b_ref.refs_0_.refs_4_), channel_id=1, source_target_pairs={{0,2},{1,5},{2,0},{3,7},{4,6},{5,1},{6,4},{7,3},{8,10},{9,13},{10,... | collective-permute-start | bytes 6291464 | tf_op jit(solution)/shard_map/ppermute | solution.py:347
  322.8 31.1 %collective-permute-start.23 = (bf16[512,2048]{1,0:T(8,128)(2,1)S(1)}, bf16[512,2048]{1,0:T(8,128)(2,1)}, u32[]{:S(2)}, u32[]{:S(2)}) collective-permute-start(bf16[512,2048]{1,0:T(8,128)(2,1)S(1)} %copy-done.30), channel_id=1, source_target_pairs={{0,4},{1,3},{2,6},{3,1},{4,0},{5,7},{6,2},{7,5},{8,12},{9,11},{10,... | collective-permute-start | bytes 6291464 | tf_op jit(solution)/shard_map/ppermute | solution.py:351
  353.9 30.8 %collective-permute-start.24 = (bf16[512,2048]{1,0:T(8,128)(2,1)}, bf16[512,2048]{1,0:T(8,128)(2,1)S(1)}, u32[]{:S(2)}, u32[]{:S(2)}) collective-permute-start(bf16[512,2048]{1,0:T(8,128)(2,1)} %copy-done.31), channel_id=1, source_target_pairs={{0,4},{1,3},{2,6},{3,1},{4,0},{5,7},{6,2},{7,5},{8,12},{9,11},{10,... | collective-permute-start | bytes 6291464 | tf_op jit(solution)/shard_map/ppermute | solution.py:351
  384.7 31.0 %collective-permute-start.25 = (bf16[512,2048]{1,0:T(8,128)(2,1)}, bf16[512,2048]{1,0:T(8,128)(2,1)S(1)}, u32[]{:S(2)}, u32[]{:S(2)}) collective-permute-start(bf16[512,2048]{1,0:T(8,128)(2,1)} %get-tuple-element.389), channel_id=1, source_target_pairs={{0,2},{1,5},{2,0},{3,7},{4,6},{5,1},{6,4},{7,3},{8,10},{9,13},{10,... | collective-permute-start | bytes 6291464 | tf_op jit(solution)/shard_map/ppermute | solution.py:347
  417.1 26.2 %collective-permute-start.26 = (bf16[512,2048]{1,0:T(8,128)(2,1)}, bf16[512,2048]{1,0:T(8,128)(2,1)S(1)}, u32[]{:S(2)}, u32[]{:S(2)}) collective-permute-start(bf16[512,2048]{1,0:T(8,128)(2,1)} %get-tuple-element.399), channel_id=1, source_target_pairs={{0,2},{1,5},{2,0},{3,7},{4,6},{5,1},{6,4},{7,3},{8,10},{9,13},{10,... | collective-permute-start | bytes 6291464 | tf_op jit(solution)/shard_map/ppermute | solution.py:347
  445.6 34.5 %collective-permute-start.28 = (bf16[704,2048]{1,0:T(8,128)(2,1)}, bf16[704,2048]{1,0:T(8,128)(2,1)S(1)}, u32[]{:S(2)}, u32[]{:S(2)}) collective-permute-start(bf16[704,2048]{1,0:T(8,128)(2,1)} %get-tuple-element.409), channel_id=1, source_target_pairs={{0,1},{1,0},{2,3},{3,2},{4,5},{5,4},{6,7},{7,6},{8,9},{9,8},{10,11... | collective-permute-start | bytes 8650760 | tf_op jit(solution)/shard_map/ppermute | solution.py:355
  445.6 34.5 %collective-permute-start.27 = (bf16[512,2048]{1,0:T(8,128)(2,1)}, bf16[512,2048]{1,0:T(8,128)(2,1)}, u32[]{:S(2)}, u32[]{:S(2)}) collective-permute-start(bf16[512,2048]{1,0:T(8,128)(2,1)} %add_convert_fusion.3), channel_id=1, source_target_pairs={{0,4},{1,3},{2,6},{3,1},{4,0},{5,7},{6,2},{7,5},{8,12},{9,11},{10,... | collective-permute-start | bytes 6291464 | tf_op jit(solution)/shard_map/ppermute | solution.py:351
  513.3 37.7 %collective-permute-start.32 = (bf16[512,2048]{1,0:T(8,128)(2,1)}, bf16[512,2048]{1,0:T(8,128)(2,1)}, u32[]{:S(2)}, u32[]{:S(2)}) collective-permute-start(bf16[512,2048]{1,0:T(8,128)(2,1)} %get-tuple-element.446.refs_0_), channel_id=1, source_target_pairs={{0,2},{1,5},{2,0},{3,7},{4,6},{5,1},{6,4},{7,3},{8,10},{9,13},{10,... | collective-permute-start | bytes 6291464 | tf_op jit(solution)/shard_map/ppermute | solution.py:347
  514.4 48.6 %all-to-all-start.3 = ((bf16[8,512,256]{2,1,0:T(8,128)(2,1)}), bf16[8,512,256]{2,1,0:T(8,128)(2,1)}, u32[]{:S(2)}, u32[]{:S(2)}) async-start(bf16[8,512,256]{2,1,0:T(8,128)(2,1)} %get-tuple-element.434), calls=%async_computation.3 | async-start | bytes 4194304 | tf_op jit(solution)/shard_map/all_to_all | solution.py:1349
  518.8 355.5 %all-gather.9.cloned.1.call-start = ((), (), s32[]{:S(2)}) async-start(), calls=%async_computation.10 | async-start | bytes 3604480 | tf_op jit(solution)/shard_map/all_gather | solution.py:1382
  522.6 36.3 %collective-permute-start.33 = (bf16[176,2048]{1,0:T(8,128)(2,1)}, bf16[176,2048]{1,0:T(8,128)(2,1)S(1)}, u32[]{:S(2)}, u32[]{:S(2)}) collective-permute-start(bf16[176,2048]{1,0:T(8,128)(2,1)} %get-tuple-element.587), channel_id=1, source_target_pairs={{0,8},{8,16},{1,9},{9,17},{2,10},{10,18},{3,11},{11,19},{4,12},{12... | collective-permute-start | bytes 2162696 | tf_op jit(solution)/shard_map/ppermute | solution.py:407
  527.0 32.0 %collective-permute-start.34 = (bf16[176,2048]{1,0:T(8,128)(2,1)}, bf16[176,2048]{1,0:T(8,128)(2,1)S(1)}, u32[]{:S(2)}, u32[]{:S(2)}) collective-permute-start(bf16[176,2048]{1,0:T(8,128)(2,1)} %get-tuple-element.586), channel_id=1, source_target_pairs={{24,16},{16,8},{25,17},{17,9},{26,18},{18,10},{27,19},{19,11},{28,... | collective-permute-start | bytes 2162696 | tf_op jit(solution)/shard_map/ppermute | solution.py:408
  566.5 26.4 %collective-permute-start.36 = (bf16[4,256,2048]{2,1,0:T(8,128)(2,1)S(1)}, bf16[4,256,2048]{2,1,0:T(8,128)(2,1)}, u32[]{:S(2)}, u32[]{:S(2)}) collective-permute-start(bf16[4,256,2048]{2,1,0:T(8,128)(2,1)S(1)} %copy-done.68), channel_id=1, source_target_pairs={{0,1},{1,0},{2,3},{3,2},{4,5},{5,4},{6,7},{7,6},{8,9},{9,8},{10,11... | collective-permute-start | bytes 12582920 | tf_op jit(solution)/shard_map/ppermute | solution.py:355
  566.5 26.4 %collective-permute-start.35 = (bf16[512,2048]{1,0:T(8,128)(2,1)}, bf16[512,2048]{1,0:T(8,128)(2,1)}, u32[]{:S(2)}, u32[]{:S(2)}) collective-permute-start(bf16[512,2048]{1,0:T(8,128)(2,1)} %get-tuple-element.446.refs_0_), channel_id=1, source_target_pairs={{0,4},{1,3},{2,6},{3,1},{4,0},{5,7},{6,2},{7,5},{8,12},{9,11},{10,... | collective-permute-start | bytes 6291464 | tf_op jit(solution)/shard_map/ppermute | solution.py:351
  592.8 52.6 %collective-permute-start.38 = (bf16[512,2048]{1,0:T(8,128)(2,1)}, bf16[512,2048]{1,0:T(8,128)(2,1)}, u32[]{:S(2)}, u32[]{:S(2)}) collective-permute-start(bf16[512,2048]{1,0:T(8,128)(2,1)} %collective-permute-done.32.refs_1_), channel_id=1, source_target_pairs={{0,4},{1,3},{2,6},{3,1},{4,0},{5,7},{6,2},{7,5},{8,12},{9,11},{10,... | collective-permute-start | bytes 6291464 | tf_op jit(solution)/shard_map/ppermute | solution.py:351
  593.6 51.9 %collective-permute-start.39 = (bf16[512,2048]{1,0:T(8,128)(2,1)}, bf16[512,2048]{1,0:T(8,128)(2,1)}, u32[]{:S(2)}, u32[]{:S(2)}) collective-permute-start(bf16[512,2048]{1,0:T(8,128)(2,1)} %collective-permute-done.32.refs_1_), channel_id=1, source_target_pairs={{0,1},{1,0},{2,3},{3,2},{4,5},{5,4},{6,7},{7,6},{8,9},{9,8},{10,11... | collective-permute-start | bytes 6291464 | tf_op jit(solution)/shard_map/ppermute | solution.py:355
  593.6 51.9 %collective-permute-start.40 = (bf16[176,2048]{1,0:T(8,128)(2,1)S(1)}, bf16[176,2048]{1,0:T(8,128)(2,1)}, u32[]{:S(2)}, u32[]{:S(2)}) collective-permute-start(bf16[176,2048]{1,0:T(8,128)(2,1)S(1)} %get-tuple-element.462), channel_id=1, source_target_pairs={{0,8},{8,16},{16,24},{1,9},{9,17},{17,25},{2,10},{10,18},{18,26},{... | collective-permute-start | bytes 2162696 | tf_op jit(solution)/shard_map/ppermute | solution.py:407
  648.7 45.0 %collective-permute-start.44 = (bf16[512,2048]{1,0:T(8,128)(2,1)}, bf16[512,2048]{1,0:T(8,128)(2,1)S(1)}, u32[]{:S(2)}, u32[]{:S(2)}) collective-permute-start(bf16[512,2048]{1,0:T(8,128)(2,1)} %collective-permute-done.35.refs_2_), channel_id=1, source_target_pairs={{0,1},{1,0},{2,3},{3,2},{4,5},{5,4},{6,7},{7,6},{8,9},{9,8},{10,11... | collective-permute-start | bytes 6291464 | tf_op jit(solution)/shard_map/ppermute | solution.py:355
  648.8 44.9 %all-to-all-start.4 = ((bf16[4,64,2816]{2,1,0:T(8,128)(2,1)}), bf16[4,64,2816]{2,1,0:T(8,128)(2,1)S(1)}, u32[]{:S(2)}, u32[]{:S(2)}) async-start(bf16[4,64,2816]{2,1,0:T(8,128)(2,1)} %bitcast.179), calls=%async_computation.5 | async-start | bytes 2883584 | tf_op jit(solution)/shard_map/all_to_all | solution.py:1383
  652.6 269.0 %all-gather.11.cloned.1.call-start = ((), (), s32[]{:S(2)}) async-start(), calls=%async_computation.11 | async-start | bytes 7208960 | tf_op jit(solution)/shard_map/all_gather | solution.py:1393
  652.9 33.4 %collective-permute-start.42 = (bf16[256,2048]{1,0:T(8,128)(2,1)}, bf16[256,2048]{1,0:T(8,128)(2,1)}, u32[]{:S(2)}, u32[]{:S(2)}) collective-permute-start(bf16[256,2048]{1,0:T(8,128)(2,1)} %get-tuple-element.480), channel_id=1, source_target_pairs={{0,2},{1,5},{2,0},{3,7},{4,6},{5,1},{6,4},{7,3},{8,10},{9,13},{10,... | collective-permute-start | bytes 3145736 | tf_op jit(solution)/shard_map/ppermute | solution.py:347
  655.0 38.8 %collective-permute-start.43 = (bf16[256,2048]{1,0:T(8,128)(2,1)}, bf16[256,2048]{1,0:T(8,128)(2,1)}, u32[]{:S(2)}, u32[]{:S(2)}) collective-permute-start(bf16[256,2048]{1,0:T(8,128)(2,1)} %get-tuple-element.481), channel_id=1, source_target_pairs={{0,2},{1,5},{2,0},{3,7},{4,6},{5,1},{6,4},{7,3},{8,10},{9,13},{10,... | collective-permute-start | bytes 3145736 | tf_op jit(solution)/shard_map/ppermute | solution.py:347
  698.4 42.7 %collective-permute-start.46 = (bf16[512,2048]{1,0:T(8,128)(2,1)}, bf16[512,2048]{1,0:T(8,128)(2,1)S(1)}, u32[]{:S(2)}, u32[]{:S(2)}) collective-permute-start(bf16[512,2048]{1,0:T(8,128)(2,1)} %get-tuple-element.502), channel_id=1, source_target_pairs={{0,2},{1,5},{2,0},{3,7},{4,6},{5,1},{6,4},{7,3},{8,10},{9,13},{10,... | collective-permute-start | bytes 6291464 | tf_op jit(solution)/shard_map/ppermute | solution.py:347
  698.7 42.5 %collective-permute-start.47 = (bf16[512,2048]{1,0:T(8,128)(2,1)}, bf16[512,2048]{1,0:T(8,128)(2,1)}, u32[]{:S(2)}, u32[]{:S(2)}) collective-permute-start(bf16[512,2048]{1,0:T(8,128)(2,1)} %collective-permute-done.38.refs_3_), channel_id=1, source_target_pairs={{0,1},{1,0},{2,3},{3,2},{4,5},{5,4},{6,7},{7,6},{8,9},{9,8},{10,11... | collective-permute-start | bytes 6291464 | tf_op jit(solution)/shard_map/ppermute | solution.py:355
  698.8 42.4 %collective-permute-start.45 = (bf16[256,2048]{1,0:T(8,128)(2,1)}, bf16[256,2048]{1,0:T(8,128)(2,1)S(1)}, u32[]{:S(2)}, u32[]{:S(2)}) collective-permute-start(bf16[256,2048]{1,0:T(8,128)(2,1)} %fusion.3), channel_id=1, source_target_pairs={{0,4},{1,3},{2,6},{3,1},{4,0},{5,7},{6,2},{7,5},{8,12},{9,11},{10,... | collective-permute-start | bytes 3145736 | tf_op jit(solution)/shard_map/ppermute | solution.py:351
  763.0 34.0 %collective-permute-start.48 = (bf16[8,64,384]{2,1,0:T(8,128)(2,1)S(1)}, bf16[8,64,384]{2,1,0:T(8,128)(2,1)S(1)}, u32[]{:S(2)}, u32[]{:S(2)}) collective-permute-start(bf16[8,64,384]{2,1,0:T(8,128)(2,1)S(1)} %get-tuple-element.516), channel_id=1, source_target_pairs={{0,8},{1,9},{2,10},{3,11},{4,12},{5,13},{6,14},{7,15}} | collective-permute-start | bytes 1179656 | tf_op jit(solution)/shard_map/ppermute | solution.py:407
  768.2 28.9 %collective-permute-start.49 = (bf16[8,64,384]{2,1,0:T(8,128)(2,1)S(1)}, bf16[8,64,384]{2,1,0:T(8,128)(2,1)S(1)}, u32[]{:S(2)}, u32[]{:S(2)}) collective-permute-start(bf16[8,64,384]{2,1,0:T(8,128)(2,1)S(1)} %get-tuple-element.517), channel_id=1, source_target_pairs={{24,16},{25,17},{26,18},{27,19},{28,20},{29,21},{30,22},{31,23}} | collective-permute-start | bytes 1179656 | tf_op jit(solution)/shard_map/ppermute | solution.py:408
  768.9 28.2 %collective-permute-start.50 = (bf16[64,2048]{1,0:T(8,128)(2,1)S(1)}, bf16[64,2048]{1,0:T(8,128)(2,1)S(1)}, u32[]{:S(2)}, u32[]{:S(2)}) collective-permute-start(bf16[64,2048]{1,0:T(8,128)(2,1)S(1)} %get-tuple-element.518), channel_id=1, source_target_pairs={{0,8},{1,9},{2,10},{3,11},{4,12},{5,13},{6,14},{7,15}} | collective-permute-start | bytes 786440 | tf_op jit(solution)/shard_map/ppermute | solution.py:407
  770.2 26.8 %collective-permute-start.51 = (bf16[64,2048]{1,0:T(8,128)(2,1)S(1)}, bf16[64,2048]{1,0:T(8,128)(2,1)S(1)}, u32[]{:S(2)}, u32[]{:S(2)}) collective-permute-start(bf16[64,2048]{1,0:T(8,128)(2,1)S(1)} %get-tuple-element.519), channel_id=1, source_target_pairs={{24,16},{25,17},{26,18},{27,19},{28,20},{29,21},{30,22},{31,23}} | collective-permute-start | bytes 786440 | tf_op jit(solution)/shard_map/ppermute | solution.py:408
  770.9 63.0 %collective-permute-start.60 = (bf16[512,2048]{1,0:T(8,128)(2,1)}, bf16[512,2048]{1,0:T(8,128)(2,1)}, u32[]{:S(2)}, u32[]{:S(2)}) collective-permute-start(bf16[512,2048]{1,0:T(8,128)(2,1)} %get-tuple-element.544), channel_id=1, source_target_pairs={{0,2},{1,5},{2,0},{3,7},{4,6},{5,1},{6,4},{7,3},{8,10},{9,13},{10,... | collective-permute-start | bytes 6291464 | tf_op jit(solution)/shard_map/ppermute | solution.py:347
  798.2 33.1 %collective-permute-start.52 = (bf16[8,64,384]{2,1,0:T(8,128)(2,1)S(1)}, bf16[8,64,384]{2,1,0:T(8,128)(2,1)}, u32[]{:S(2)}, u32[]{:S(2)}) collective-permute-start(bf16[8,64,384]{2,1,0:T(8,128)(2,1)S(1)} %get-tuple-element.524), channel_id=1, source_target_pairs={{0,8},{8,16},{1,9},{9,17},{2,10},{10,18},{3,11},{11,19},{4,12},{12... | collective-permute-start | bytes 1179656 | tf_op jit(solution)/shard_map/ppermute | solution.py:407
  803.3 28.0 %collective-permute-start.53 = (bf16[8,64,384]{2,1,0:T(8,128)(2,1)S(1)}, bf16[8,64,384]{2,1,0:T(8,128)(2,1)}, u32[]{:S(2)}, u32[]{:S(2)}) collective-permute-start(bf16[8,64,384]{2,1,0:T(8,128)(2,1)S(1)} %get-tuple-element.525), channel_id=1, source_target_pairs={{24,16},{16,8},{25,17},{17,9},{26,18},{18,10},{27,19},{19,11},{28,... | collective-permute-start | bytes 1179656 | tf_op jit(solution)/shard_map/ppermute | solution.py:408
  804.7 26.6 %collective-permute-start.54 = (bf16[64,2048]{1,0:T(8,128)(2,1)}, bf16[64,2048]{1,0:T(8,128)(2,1)}, u32[]{:S(2)}, u32[]{:S(2)}) collective-permute-start(bf16[64,2048]{1,0:T(8,128)(2,1)} %get-tuple-element.526), channel_id=1, source_target_pairs={{0,8},{8,16},{1,9},{9,17},{2,10},{10,18},{3,11},{11,19},{4,12},{12... | collective-permute-start | bytes 786440 | tf_op jit(solution)/shard_map/ppermute | solution.py:407
  817.2 48.6 %all-to-all-start.5 = ((bf16[8,512,384]{2,1,0:T(8,128)(2,1)}), bf16[8,512,384]{2,1,0:T(8,128)(2,1)}, u32[]{:S(2)}, u32[]{:S(2)}) async-start(bf16[8,512,384]{2,1,0:T(8,128)(2,1)} %get-tuple-element.511.refs_8_), calls=%async_computation.6 | async-start | bytes 6291456 | tf_op jit(solution)/shard_map/all_to_all | solution.py:1400
  833.9 60.0 %collective-permute-start.61 = (bf16[512,2048]{1,0:T(8,128)(2,1)}, bf16[512,2048]{1,0:T(8,128)(2,1)}, u32[]{:S(2)}, u32[]{:S(2)}) collective-permute-start(bf16[512,2048]{1,0:T(8,128)(2,1)} %add_convert_fusion.2), channel_id=1, source_target_pairs={{0,4},{1,3},{2,6},{3,1},{4,0},{5,7},{6,2},{7,5},{8,12},{9,11},{10,... | collective-permute-start | bytes 6291464 | tf_op jit(solution)/shard_map/ppermute | solution.py:351
  834.6 30.1 %collective-permute-start.56 = (bf16[8,64,384]{2,1,0:T(8,128)(2,1)S(1)}, bf16[8,64,384]{2,1,0:T(8,128)(2,1)S(1)}, u32[]{:S(2)}, u32[]{:S(2)}) collective-permute-start(bf16[8,64,384]{2,1,0:T(8,128)(2,1)S(1)} %get-tuple-element.532), channel_id=1, source_target_pairs={{0,8},{8,16},{16,24},{1,9},{9,17},{17,25},{2,10},{10,18},{18,26},{... | collective-permute-start | bytes 1179656 | tf_op jit(solution)/shard_map/ppermute | solution.py:407
  865.8 28.1 %all-to-all-start.6 = ((bf16[8,64,384]{2,1,0:T(8,128)(2,1)}), bf16[8,64,384]{2,1,0:T(8,128)(2,1)S(1)}, u32[]{:S(2)}, u32[]{:S(2)}) async-start(bf16[8,64,384]{2,1,0:T(8,128)(2,1)} %fusion.17), calls=%async_computation.7 | async-start | bytes 786432 | tf_op jit(solution)/shard_map/all_to_all | solution.py:1423
  (106 other events, 1261.8 us)
Sparse Core Ops, SparseCore 0:
  113.9 107.2 all-gather.6
  513.4 129.1 reduce-scatter.1
  648.8 63.5 all-gather.8
  714.4 134.4 all-gather.10

commit v3 on v2

--- a/solution.py
+++ b/solution.py
@@ -464,69 +464,50 @@
     )(parts, weight, gain)
 
 
-def spread_rows_kernel(z_ref, *refs, planes):
-    blocks, out_ref = refs[:-1], refs[-1]
+def spread_last_kernel(z_ref, *refs, planes):
+    blocks, (w_ref, g_ref, out_ref, gain_ref, wo_ref) = refs[:-5], refs[-5:]
     rows = blocks[0].shape[0]
+    devices = 2 * CHIPS
+    width = wo_ref.shape[1]
+    heads = width // devices
+    each = heads + 2 * HD
     for place, load in line_values(blocks, planes, z_ref[0]):
-        out_ref[pl.ds(pl.multiple_of(place * rows, rows), rows), :] = load(slice(None)).astype(F32)
-
-
-def spread_rows(steps):
-    planes = len(steps)
-    rows, width = steps[0][0].shape
-    blocks = [steps[0][0]] + [s[0] for s in steps[1:]] + [s[1] for s in steps[1:]]
-    tile = width // 4
-    return pl.pallas_call(
-        functools.partial(spread_rows_kernel, planes=planes),
-        grid_spec=pltpu.PrefetchScalarGridSpec(
-            num_scalar_prefetch=1,
-            grid=(4,),
-            in_specs=[pl.BlockSpec((rows, tile), lambda i, z: (0, i))] * len(blocks),
-            out_specs=pl.BlockSpec((planes * rows, tile), lambda i, z: (0, i)),
-        ),
-        out_shape=jax.ShapeDtypeStruct((planes * rows, width), F32),
-        compiler_params=pltpu.CompilerParams(vmem_limit_bytes=32 * 2**20),
-        cost_estimate=SHORT,
-        name="spread_rows",
-    )(lax.axis_index("dp").reshape(1), *blocks)
-
-
-def spread_qkv_kernel(z_ref, *refs, planes):
-    blocks, (w_ref, g_ref, out_ref, gain_ref) = refs[:-4], refs[-4:]
-    devices, rows, width = blocks[0].shape
-    heads = width - 2 * HD
-    base = devices * heads
-    z = z_ref[0]
-    for place, load in line_values(blocks, planes, z):
         span = pl.ds(pl.multiple_of(place * rows, rows), rows)
         pairs = []
         for d in range(devices):
-            block = load(d).astype(F32)
-            out_ref[span, d * heads : (d + 1) * heads] = block[:, :heads]
-            pairs.append(block[:, heads:])
+            begin = d * each
+            cols = slice(begin, begin + heads)
+            out_ref[span, d * heads : (d + 1) * heads] = load((slice(None), cols)).astype(F32)
+            pairs.append(load((slice(None), slice(begin + heads, begin + each))).astype(F32))
         for g in range(0, KV, 2):
             low = pairs[2 * g] + pairs[2 * g + 1]
             high = pairs[2 * g + 2] + pairs[2 * g + 3]
             lane = lax.broadcasted_iota(jnp.int32, low.shape, 1)
-            out_ref[span, base + g * HD : base + (g + 2) * HD] = jnp.where(lane < HD, low, pltpu.roll(high, HD, 1))
-            out_ref[span, base + (KV + g) * HD : base + (KV + g + 2) * HD] = jnp.where(
-                lane < HD, pltpu.roll(low, HD, 1), high
-            )
+            begin = width + g * HD
+            out_ref[span, begin : begin + 2 * HD] = jnp.where(lane < HD, low, pltpu.roll(high, HD, 1))
+            begin = width + (KV + g) * HD
+            out_ref[span, begin : begin + 2 * HD] = jnp.where(lane < HD, pltpu.roll(low, HD, 1), high)
+        wo_ref[span, :] = load((slice(None), slice(devices * each, devices * each + width))).astype(F32)
     gain_ref[...] = jnp.sum(out_ref[...] * w_ref[...].astype(F32), axis=-1, keepdims=True) / g_ref[...]
 
 
-def spread_qkv(steps, weight, gain):
+def spread_last(steps, weight, gain, width):
     planes = len(steps)
     blocks = [steps[0][0]] + [s[0] for s in steps[1:]] + [s[1] for s in steps[1:]]
     vmem = pl.BlockSpec(memory_space=pltpu.VMEM)
+    total = weight.shape[0]
     return pl.pallas_call(
-        functools.partial(spread_qkv_kernel, planes=planes),
+        functools.partial(spread_last_kernel, planes=planes),
         in_specs=[pl.BlockSpec(memory_space=pltpu.SMEM)] + [vmem] * (len(blocks) + 2),
-        out_specs=[vmem, vmem],
-        out_shape=[jax.ShapeDtypeStruct(weight.shape, F32), jax.ShapeDtypeStruct((weight.shape[0], 1), F32)],
+        out_specs=[vmem] * 3,
+        out_shape=[
+            jax.ShapeDtypeStruct(weight.shape, F32),
+            jax.ShapeDtypeStruct((total, 1), F32),
+            jax.ShapeDtypeStruct((total, width), F32),
+        ],
         compiler_params=pltpu.CompilerParams(vmem_limit_bytes=32 * 2**20),
         cost_estimate=SHORT,
-        name="spread_qkv",
+        name="spread_last",
     )(lax.axis_index("dp").reshape(1), *blocks, weight, gain)
 
 
@@ -607,17 +588,20 @@
                 a_rows = left[side * count + r][...]
                 part = lax.dot_general(a_rows, right[kind * count + r][...], TN, preferred_element_type=F32)
                 total = part if total is None else total + part
-            refs[4 * count + side][0, :, kind * half : (kind + 1) * half] = total.astype(BF)
-
-
-def grad_gu(core, b_rows, dg_rows, du_rows, share):
+            out_ref = refs[4 * count + side]
+            planes, _, rows, _ = out_ref.shape
+            out_ref[:, 0, :, kind * half : (kind + 1) * half] = total.astype(BF).reshape(planes, rows, half)
+
+
+def grad_gu(core, b_rows, dg_rows, du_rows, share, planes):
     count = len(b_rows)
     tokens, width = b_rows[0].shape
     hidden = dg_rows[0].shape[1]
     keep = pl.BlockSpec((tokens, share), lambda c, core: (0, 2 * c + core[0]))
     give = pl.BlockSpec((tokens, share), lambda c, core: (0, 2 * c + 1 - core[0]))
     whole = pl.BlockSpec((tokens, hidden), lambda c, core: (0, 0))
-    out = pl.BlockSpec((1, share, 2 * hidden), lambda c, core: (c, 0, 0))
+    rows = share // planes
+    out = pl.BlockSpec((planes, 1, rows, 2 * hidden), lambda c, core: (0, c, 0, 0))
     return pl.pallas_call(
         functools.partial(grad_gu_kernel, count=count),
         grid_spec=pltpu.PrefetchScalarGridSpec(
@@ -626,7 +610,7 @@
             in_specs=[keep] * count + [give] * count + [whole] * (2 * count),
             out_specs=[out, out],
         ),
-        out_shape=[jax.ShapeDtypeStruct((width // (2 * share), share, 2 * hidden), BF)] * 2,
+        out_shape=[jax.ShapeDtypeStruct((planes, width // (2 * share), rows, 2 * hidden), BF)] * 2,
         compiler_params=pltpu.CompilerParams(vmem_limit_bytes=58 * 2**20),
         cost_estimate=SHORT,
         name="grad_gu",
@@ -639,14 +623,19 @@
     for r in range(count):
         part = lax.dot_general(refs[r][...], dp_ref[place_ref[r]], TN, preferred_element_type=F32)
         total = part if total is None else total + part
-    out_ref[...] = total.astype(BF)
-
-
-def grad_qkv(places, a_rows, dp_heads):
+    planes, rows, wide = out_ref.shape
+    columns = total.shape[1]
+    for k in range(wide // columns):
+        block = total[k * planes * rows : (k + 1) * planes * rows].astype(BF)
+        out_ref[:, :, k * columns : (k + 1) * columns] = block.reshape(planes, rows, columns)
+
+
+def grad_qkv(places, a_rows, dp_heads, planes):
     count = len(a_rows)
     tokens, width = a_rows[0].shape
     columns = dp_heads.shape[2]
-    depth = 512
+    share = width // count
+    depth = 2 * share
     return pl.pallas_call(
         functools.partial(grad_qkv_kernel, count=count),
         grid_spec=pltpu.PrefetchScalarGridSpec(
@@ -654,9 +643,9 @@
             grid=(width // depth,),
             in_specs=[pl.BlockSpec((tokens, depth), lambda i, p: (0, i))] * count
             + [pl.BlockSpec(dp_heads.shape, lambda i, p: (0, 0, 0))],
-            out_specs=pl.BlockSpec((depth, columns), lambda i, p: (i, 0)),
+            out_specs=pl.BlockSpec((planes, share // planes, 2 * columns), lambda i, p: (0, 0, i)),
         ),
-        out_shape=jax.ShapeDtypeStruct((width, columns), BF),
+        out_shape=jax.ShapeDtypeStruct((planes, share // planes, count * columns), BF),
         compiler_params=pltpu.CompilerParams(vmem_limit_bytes=48 * 2**20),
         cost_estimate=SHORT,
         name="grad_qkv",
@@ -1328,12 +1317,12 @@
         [own[1], first[1], second[1], far[1]],
         [own[2], first[2], second[2], far[2]],
         share,
+        planes,
     )
     db_passed, dn_got, gu_keep, gu_give = fence(db_passed, dn_got, gu_keep, gu_give)
     dn_parts = [part.reshape(planes, dn_keep.shape[0] // planes, width) for part in (dn_keep, dn_got)]
     dn_moves = line_scatter_sends(dn_parts, None, 1, 0)
-    db_passed, gu_give, normed, *dn_moves = fence(db_passed, gu_give, normed, *dn_moves)
-    a_first = send_first(normed)
+    db_passed, gu_give, *dn_moves = fence(db_passed, gu_give, *dn_moves)
     gu_got = send_sibling(gu_give)
     dn_moves = line_scatter_move(dn_moves, 1)
     d_resid, d_branch, d_send = resid_back(
@@ -1341,7 +1330,6 @@
     )
     d_send, d_branch, gu_got, *dn_moves = fence(d_send, d_branch, gu_got, *dn_moves)
     gu_sum = (gu_keep.astype(F32) + gu_got.astype(F32)).astype(BF)
-    gu_sum = gu_sum.reshape(CHIPS, planes, quarter, 2 * hidden_chip).transpose(1, 0, 2, 3)
     gu_z = lax.psum_scatter(
         gu_sum.reshape(planes * CHIPS * quarter, 2 * hidden_chip), "dp", scatter_dimension=0, tiled=True
     )
@@ -1350,98 +1338,92 @@
     dn_moves = line_scatter_sends(dn_parts, dn_moves, 2, 0)
     dn_moves = line_scatter_move(dn_moves, 2)
     wo_keep, wo_give = grad_wo(core, attn_tok, d_branch)
-    d_heads, wo_keep, wo_give, a_first, normed, *dn_moves = fence(d_heads, wo_keep, wo_give, a_first, normed, *dn_moves)
+    d_heads, wo_keep, wo_give, normed = fence(d_heads, wo_keep, wo_give, normed)
 
     def back_call(heads, start, stop, **kwargs):
         return attend_back(zeros_one, qkv_heads, heads, lse, cos_all, sin_all, start, stop, **kwargs)
 
     turns = (0, blocks // 8, blocks // 4, blocks // 2, blocks)
+    wo_got = send_sibling(wo_give)
+    a_first = send_first(normed)
+    bwd = back_call(d_heads, turns[0], turns[1], out=out_heads)
+    d_heads, a_first, wo_got, normed, *moves = fence(d_heads, a_first, wo_got, normed, *dn_moves, *bwd)
+    dn_moves, bwd = moves[:2], moves[2:]
+
     dn_moves = line_scatter_sends(dn_parts, dn_moves, 3, 0)
-    d_heads, wo_give, normed, *dn_moves = fence(d_heads, wo_give, normed, *dn_moves)
-    wo_got = send_sibling(wo_give)
+    d_heads, normed, a_first, *dn_moves = fence(d_heads, normed, a_first, *dn_moves)
     a_second = send_second(normed)
-    a_theirs = [send_sibling(normed)]
+    a_theirs = [send_sibling(normed), send_sibling(a_first)]
     dn_moves = line_scatter_move(dn_moves, 3)
-    bwd = back_call(d_heads, turns[0], turns[1], out=out_heads)
-    d_heads, a_first, a_second, wo_got, *moves = fence(d_heads, a_first, a_second, wo_got, *a_theirs, *bwd)
-    a_theirs, bwd = moves[:1], moves[1:]
-
-    a_far = send_second(a_first)
-    a_theirs.append(send_sibling(a_first))
     bwd = back_call(d_heads, turns[1], turns[2], before=bwd)
-    d_heads, gu_z, a_far, *moves = fence(d_heads, gu_z, a_far, *a_theirs, *dn_moves, *bwd)
+    d_heads, gu_z, a_second, *moves = fence(d_heads, gu_z, a_second, *a_theirs, *dn_moves, *bwd)
     a_theirs, dn_moves, bwd = moves[:2], moves[2:4], moves[4:]
 
     def wo_part(place):
         return pick(wo_keep, place).astype(F32) + pick(wo_got, place).astype(F32)
 
     dn_z = line_scatter_end(dn_parts, dn_moves, 0)
+    d_heads, dn_z, gu_z, a_first, a_second = fence(d_heads, dn_z, gu_z, a_first, a_second)
+    dn_all = lax.all_gather(dn_z, "dp", axis=0, tiled=False)
+    gu_z = lax.all_to_all(gu_z, "sp", 0, 0, axis_index_groups=SAME_CORE, tiled=True)
+    a_far = send_second(a_first)
+    a_theirs.append(send_sibling(a_second))
+    bwd = back_call(d_heads, turns[2], turns[3], before=bwd)
+    d_heads, gu_z, a_far, *moves = fence(d_heads, gu_z, a_far, *a_theirs, *bwd)
+    a_theirs, bwd = moves[:3], moves[3:]
+
     wo_first = wo_part(chip ^ (first_mask // 2)).astype(BF)
     wo_far = wo_part(chip ^ 3).astype(BF)
-    d_heads, dn_z, gu_z, a_second, wo_first, wo_far = fence(d_heads, dn_z, gu_z, a_second, wo_first, wo_far)
-    dn_all = lax.all_gather(dn_z, "dp", axis=0, tiled=False)
-    gu_z = lax.all_to_all(gu_z, "sp", 0, 0, axis_index_groups=SAME_CORE, tiled=True)
+    d_heads, gu_z, a_far, wo_first, wo_far = fence(d_heads, gu_z, a_far, wo_first, wo_far)
+    gu_all = lax.all_gather(gu_z, "dp", axis=0, tiled=False)
     wo_far = send_first(wo_far)
     wo_first = send_first(wo_first)
-    a_theirs.append(send_sibling(a_second))
-    bwd = back_call(d_heads, turns[2], turns[3], before=bwd)
-    d_heads, gu_z, wo_far, wo_first, *moves = fence(d_heads, gu_z, wo_far, wo_first, *a_theirs, *bwd)
-    a_theirs, bwd = moves[:3], moves[3:]
-
-    wo_pass = (wo_part(chip ^ (second_mask // 2)) + wo_far.astype(F32)).astype(BF)
-    d_heads, gu_z, wo_pass, a_far, y_far = fence(d_heads, gu_z, wo_pass, a_far, far[4])
-    gu_all = lax.all_gather(gu_z, "dp", axis=0, tiled=False)
-    wo_passed = send_second(wo_pass)
-    y_got_far = send_first(y_far)
     a_theirs.append(send_sibling(a_far))
     bwd = back_call(d_heads, turns[3], turns[4], before=bwd)
-    dp_heads, wo_passed, y_got_far, y_first, *a_theirs = fence(bwd[0], wo_passed, y_got_far, first[4], *a_theirs)
-
+    wo_pass = (wo_part(chip ^ (second_mask // 2)) + wo_far.astype(F32)).astype(BF)
+    dp_heads, wo_first, wo_pass, *a_theirs = fence(bwd[0], wo_first, wo_pass, *a_theirs)
+
+    wo_passed = send_second(wo_pass)
     back = lax.all_to_all(dp_heads, "sp", 0, 0, tiled=True)
-    y_got_first = send_first(y_first)
-    grad_wq = grad_qkv(places, [normed, a_first, a_second, a_far] + list(a_theirs), dp_heads)
-    wq_parts = [grad_wq.reshape(devices, planes, quarter, dp_heads.shape[2])]
+    grad_wq = grad_qkv(places, [normed, a_first, a_second, a_far] + list(a_theirs), dp_heads, planes)
     wo_rows = (wo_part(chip) + wo_first.astype(F32) + wo_passed.astype(F32)).astype(BF)
-    wo_parts = [wo_rows.reshape(planes, quarter, width)]
-    y_pass = (second[4].astype(F32) + y_got_far.astype(F32)).astype(BF)
-    wq_moves = wo_moves = None
+    split = grad_wq.shape[2]
+    last_parts = [jnp.concatenate([grad_wq, wo_rows.reshape(planes, quarter, width)], axis=2)]
+    y_far, y_first = far[4], first[4]
+    moves = None
     for step in range(1, planes):
-        wq_moves = line_scatter_sends(wq_parts, wq_moves, step, 1)
-        wo_moves = line_scatter_sends(wo_parts, wo_moves, step, 0)
-        moves = fence(*wq_moves, *wo_moves, y_pass)
-        wq_moves = line_scatter_move(moves[:2], step)
-        wo_moves = line_scatter_move(moves[2:4], step)
-        if step == planes - 1:
-            y_got_first, y_pass = fence(y_got_first, moves[4])
-            y_passed = send_second(y_pass)
-        moves = fence(*wq_moves, *wo_moves)
-        wq_moves, wo_moves = moves[:2], moves[2:]
-    wq_z = line_scatter_end(wq_parts, wq_moves, 1)
-    wo_z = line_scatter_end(wo_parts, wo_moves, 0)
-    wq_z, wo_z, back = fence(wq_z, wo_z, back)
-    wo_steps = [(wo_z, wo_z), line_gather_move((wo_z, wo_z), 1)]
+        moves = line_scatter_sends(last_parts, moves, step, 0)
+        y_far, y_first, *moves = fence(y_far, y_first, *moves)
+        moves = line_scatter_move(moves, step)
+        if step == 1:
+            y_got_far = send_first(y_far)
+        elif step == 2:
+            y_got_first = send_first(y_first)
+        moves = fence(*moves)
+    last_z = line_scatter_end(last_parts, moves, 0)
+    wq_z = last_z[:, :split].reshape(quarter, devices, split // devices).transpose(1, 0, 2)
+    wq_z, wo_z, back = fence(wq_z, last_z[:, split:], back)
     wq_z = lax.all_to_all(wq_z, "sp", 0, 0, tiled=True)
     grad_tokens = in_back(places, back, x_bf, inv_one, attn_gain, d_resid, qkv_parts).reshape(tokens.shape)
-    wq_z, grad_tokens, y_passed, *moves = fence(wq_z, grad_tokens, y_passed, *wo_steps[-1])
-    wo_steps[-1] = tuple(moves)
-    wq_steps = [(wq_z, wq_z)]
+    y_pass = (second[4].astype(F32) + y_got_far.astype(F32)).astype(BF)
+    last_z = jnp.concatenate([wq_z.transpose(1, 0, 2).reshape(quarter, split), wo_z], axis=1)
+    last_z, grad_tokens, y_pass, y_got_first = fence(last_z, grad_tokens, y_pass, y_got_first)
+    y_passed = send_second(y_pass)
+    last_steps = [(last_z, last_z)]
     outs = []
     for step in range(1, planes):
-        wq_steps.append(line_gather_move(wq_steps[-1], step))
-        if len(wo_steps) < planes:
-            wo_steps.append(line_gather_move(wo_steps[-1], len(wo_steps)))
+        last_steps.append(line_gather_move(last_steps[-1], step))
         if step == 1:
-            y_sum = own[4].astype(F32) + y_got_first.astype(F32) + y_passed.astype(F32)
-            outs.append((residual + y_sum).astype(BF).reshape(tokens.shape))
             outs.append(dn_all.astype(F32).reshape(w_down.shape))
         elif step == 2:
             outs += spread(gu_all, w_gate_up, g_mlp.astype(F32).reshape(share, 1))
         if step == planes - 1:
-            outs.append(spread_rows(wo_steps))
-        moves = fence(*wq_steps[-1], *wo_steps[-1], *outs)
-        wq_steps[-1], wo_steps[-1], outs = tuple(moves[:2]), tuple(moves[2:4]), list(moves[4:])
-    output, grad_w_down, grad_w_gate_up, grad_g_mlp, grad_w_out = outs
-    grad_w_qkv, grad_g_attn = spread_qkv(wq_steps, w_qkv, g_attn.astype(F32).reshape(share, 1))
+            y_sum = own[4].astype(F32) + y_got_first.astype(F32) + y_passed.astype(F32)
+            outs.append((residual + y_sum).astype(BF).reshape(tokens.shape))
+        moves = fence(*last_steps[-1], *outs)
+        last_steps[-1], outs = tuple(moves[:2]), list(moves[2:])
+    grad_w_down, grad_w_gate_up, grad_g_mlp, output = outs
+    grad_w_qkv, grad_g_attn, grad_w_out = spread_last(last_steps, w_qkv, g_attn.astype(F32).reshape(share, 1), width)
     return (
         output,
         grad_tokens,

time: 968 us -> 1000 us (1.033)
  Pallas kernels: 432 us -> 477 us
  starting transfers between devices: 169 us -> 158 us
    pallas_call x4, Pallas kernels: 113 us -> 146 us  [attend_back(): pl.pallas_call(functools.partial(attend_back_kernel, heads=heads, start=s...]
    ppermute x11, waiting for transfers between devices: 56.5 us -> 29.4 us  [send_first(): return lax.ppermute(x, 'sp', FIRST)]
    pallas_call x3, Pallas kernels: 50 us -> 66.2 us  [attend(): pl.pallas_call(functools.partial(attend_kernel, heads=heads, start=start,...]
    all_to_all x1, waiting for transfers between devices: 4.05 us -> 18.9 us  [fast_body(): lax.all_to_all(d_send, 'sp', 0, 0, tiled=True).reshape(length, share)]
    ppermute x9 -> x6, waiting for transfers between devices: 47.7 us -> 62.4 us  [line_scatter_move(): right = lax.ppermute(sends[0], 'dp', [(i, i + 1) for i in range(step)])]
    ppermute x9 -> x6, starting transfers between devices: 74.5 us -> 60.8 us  [line_scatter_move(): right = lax.ppermute(sends[0], 'dp', [(i, i + 1) for i in range(step)])]
    ppermute x13, waiting for transfers between devices: 38 us -> 27 us  [send_second(): return lax.ppermute(x, 'sp', SECOND)]
    ppermute x6 -> x3, starting transfers between devices: 13.2 us -> 20.4 us  [line_gather_move(): lax.ppermute(got[0], 'dp', [(i, i + 1) for i in range(step - 1, planes -...]
  transfers between devices with their start and end apart: 85 -> 73, of which waited for: 27 -> 23; matrix products, arithmetic and copies ran while one was open for 7% -> 7% of each run, Pallas kernels for 43% -> 47%
where the time goes in v3:
time: 1000 us; the launch traced here: 987 us
  Pallas kernels  477 us (48%)
  waiting for transfers between devices  213 us (21%)
  starting transfers between devices  158 us (16%)
  other arithmetic  82.1 us (8%)
  local copies, waits for them, and re-layouts  41.7 us (4%)
  between operations  15.7 us (2%)
    pallas_call x4, Pallas kernels, attend_back(): pl.pallas_call(functools.partial(attend_back_kernel, heads=heads, start=s...  146 us
    pallas_call x4, Pallas kernels, ffn(): pl.pallas_call(ffn_kernel, grid=(1,), in_specs=[pl.BlockSpec((rows, width...  118 us
    pallas_call x3, Pallas kernels, attend(): pl.pallas_call(functools.partial(attend_kernel, heads=heads, start=start,...  66.2 us
    ppermute x6, waiting for transfers between devices, line_scatter_move(): right = lax.ppermute(sends[0], 'dp', [(i, i + 1) for i in range(step)])  62.4 us
    ppermute x6, starting transfers between devices, line_scatter_move(): right = lax.ppermute(sends[0], 'dp', [(i, i + 1) for i in range(step)])  60.8 us
    unnamed x134, local copies, waits for them, and re-layouts  35.8 us
    pallas_call x1, Pallas kernels, grad_gu(): pl.pallas_call(functools.partial(grad_gu_kernel, count=count), grid_spec=...  34.3 us
    ppermute x11, waiting for transfers between devices, send_first(): return lax.ppermute(x, 'sp', FIRST)  29.4 us
  transfers between devices with their start and end apart: 73, of which 23 were waited for; matrix products, arithmetic and copies ran while one was open for 7% of the time, Pallas kernels for 47%

profile of v3, /device:TPU:0, one launch (start us, length us, event | category | flops | bytes accessed | tf_op | source)
XLA Modules:
  0.0 987.0 jit_solution(307908315892136051)
XLA Ops:
  27.8 12.1 %collective-permute-done.3.refs_1_.refs_9_ = bf16[256,2560]{1,0:T(8,128)(2,1)S(1)} collective-permute-done((bf16[256,2560]{1,0:T(8,128)(2,1)S(1)}, bf16[256,2560]{1,0:T(8,128)(2,1)S(1)}, u32[]{:S(2)}, u32[]{:S(2)}) %collective-permute-start.3) | collective-permute-done | bytes 1310752 | tf_op jit(solution)/shard_map/ppermute | solution.py:347
  42.5 7.5 fusion.20
  61.3 14.0 %collective-permute-done.7.refs_3_.refs_11_ = bf16[256,2560]{1,0:T(8,128)(2,1)S(1)} collective-permute-done((bf16[256,2560]{1,0:T(8,128)(2,1)S(1)}, bf16[256,2560]{1,0:T(8,128)(2,1)S(1)}, u32[]{:S(2)}, u32[]{:S(2)}) %collective-permute-start.7) | collective-permute-done | bytes 1310752 | tf_op jit(solution)/shard_map/ppermute | solution.py:351
  89.1 18.3 %project.1 = (bf16[8,512,384]{2,1,0:T(8,128)(2,1)}, bf16[512,2048]{1,0:T(8,128)(2,1)}, f32[512,1]{1,0:T(8,128)S(1)}) custom-call(s32[8]{0:T(128)S(1)} %stack.59.place_ref, bf16[512,2048]{1,0:T(8,128)(2,1)} %bitcast.149, f32[1,2048]{1,0:T(1,128)S(1)} %get-tuple-element.562.gain_ref, f32[512,128]{1,0:T(8,128)S(1)} %pad_maximum_fusion.4.cos_ref, ...), custom_call_target="tpu_custom_call" | custom-call | flops 1 | bytes 1 | tf_op jit(solution)/shard_map/project/pallas_call | solution.py:703
  108.1 5.7 collective-permute-done.10.refs_1_
  119.5 8.2 maximum_select_fusion.wd_ref
  127.7 27.8 %all-to-all-done = bf16[8,512,384]{2,1,0:T(8,128)(2,1)S(1)} async-done(((bf16[8,512,384]{2,1,0:T(8,128)(2,1)}), bf16[8,512,384]{2,1,0:T(8,128)(2,1)S(1)}, u32[]{:S(2)}, u32[]{:S(2)}) %all-to-all-start) | async-done | bytes 3145760 | tf_op jit(solution)/shard_map/all_to_all | solution.py:1271
  156.6 29.8 %attend.3 = (f32[4096,256]{1,0:T(8,128)}, bf16[8,512,256]{2,1,0:T(8,128)(2,1)S(1)}, f32[8,4,512]{2,1,0:T(4,128)S(1)}) custom-call(s32[1]{0:T(128)} %bitcast.14.zeros_ref, bf16[4096,384]{1,0:T(8,128)(2,1)S(1)} %bitcast.119, bf16[4096,384]{1,0:T(8,128)(2,1)S(1)} %bitcast.120), custom_call_target="tpu_custom_call" | custom-call | flops 1 | bytes 1 | tf_op jit(solution)/shard_map/attend/pallas_call | solution.py:1023
  186.4 4.6 collective-permute-done.13.dy_ref.refs_5_
  193.1 22.4 %attend.4 = (f32[4096,256]{1,0:T(8,128)}, bf16[8,512,256]{2,1,0:T(8,128)(2,1)S(1)}, f32[8,4,512]{2,1,0:T(4,128)S(1)}) custom-call(s32[1]{0:T(128)} %bitcast.14.zeros_ref, bf16[4096,384]{1,0:T(8,128)(2,1)S(1)} %bitcast.121, bf16[4096,384]{1,0:T(8,128)(2,1)S(1)} %bitcast.122, ...), custom_call_target="tpu_custom_call", output_to_operand_aliasing={{0}: (3, {}), {1}: (4, {}), {2}: (5, {})} | custom-call | flops 1 | bytes 1 | tf_op jit(solution)/shard_map/attend/pallas_call | solution.py:1023
  216.8 11.5 %collective-permute-done.14.refs_3_ = bf16[256,2048]{1,0:T(8,128)(2,1)S(1)} collective-permute-done((bf16[256,2048]{1,0:T(8,128)(2,1)}, bf16[256,2048]{1,0:T(8,128)(2,1)S(1)}, u32[]{:S(2)}, u32[]{:S(2)}) %collective-permute-start.14) | collective-permute-done | bytes 1048608 | tf_op jit(solution)/shard_map/ppermute | solution.py:351
  233.3 14.0 %attend.5 = (f32[4096,256]{1,0:T(8,128)}, bf16[8,512,256]{2,1,0:T(8,128)(2,1)S(1)}, f32[8,4,512]{2,1,0:T(4,128)S(1)}) custom-call(s32[1]{0:T(128)} %bitcast.14.zeros_ref, bf16[4096,384]{1,0:T(8,128)(2,1)S(1)} %bitcast.123, bf16[4096,384]{1,0:T(8,128)(2,1)S(1)} %bitcast.124, ...), custom_call_target="tpu_custom_call", output_to_operand_aliasing={{0}: (3, {}), {1}: (4, {}), {2}: (5, {})} | custom-call | flops 1 | bytes 1 | tf_op jit(solution)/shard_map/attend/pallas_call | solution.py:1023
  261.9 6.1 join.1
  270.6 11.4 %all-to-all-done.2.attn_ref.keep_ref.give_ref = bf16[8,512,256]{2,1,0:T(8,128)(2,1)S(1)} async-done(((bf16[8,512,256]{2,1,0:T(8,128)(2,1)}), bf16[8,512,256]{2,1,0:T(8,128)(2,1)S(1)}, u32[]{:S(2)}, u32[]{:S(2)}) %all-to-all-start.2) | async-done | bytes 2097184 | tf_op jit(solution)/shard_map/all_to_all | solution.py:1289
  283.3 11.7 %out_proj.1 = (f32[512,2048]{1,0:T(8,128)}, f32[512,1]{1,0:T(8,128)}, bf16[512,2048]{1,0:T(8,128)(2,1)}) custom-call(s32[8]{0:T(128)} %copy-done.28, bf16[8,512,256]{2,1,0:T(8,128)(2,1)} %copy-done.1, bf16[512,2048]{1,0:T(8,128)(2,1)} %bitcast.150, f32[1,2048]{1,0:T(1,128)} %get-tuple-element.561.gain_ref, bf16[256,2048]{1,0:T(8,128)(2,1)} %refs_0_.1, ...), custom_call_target="tpu_custom_call" | custom-call | flops 1 | bytes 1 | tf_op jit(solution)/shard_map/out_proj/pallas_call | solution.py:757
  295.7 29.3 %ffn.4 = (bf16[512,1408]{1,0:T(8,128)(2,1)}, bf16[512,1408]{1,0:T(8,128)(2,1)}, bf16[512,1408]{1,0:T(8,128)(2,1)}, bf16[512,2048]{1,0:T(8,128)(2,1)}, bf16[512,2048]{1,0:T(8,128)(2,1)}) custom-call(bf16[512,2048]{1,0:T(8,128)(2,1)} %get-tuple-element.385.b_ref.refs_0_.refs_4_, bf16[512,2048]{1,0:T(8,128)(2,1)} %multiply_bitcast_fusion.dy_ref.refs_4_, ...), custom_call_target="tpu_custom_call" | custom-call | flops 1 | bytes 1 | tf_op jit(solution)/shard_map/ffn/pallas_call | solution.py:562
  326.3 29.7 %ffn.5 = (bf16[512,1408]{1,0:T(8,128)(2,1)}, bf16[512,1408]{1,0:T(8,128)(2,1)}, bf16[512,1408]{1,0:T(8,128)(2,1)}, bf16[512,2048]{1,0:T(8,128)(2,1)}, bf16[512,2048]{1,0:T(8,128)(2,1)}) custom-call(bf16[512,2048]{1,0:T(8,128)(2,1)} %copy-done.32, bf16[512,2048]{1,0:T(8,128)(2,1)} %copy-done.41, bf16[2,2048,1408]{2,1,0:T(8,128)(2,1)} %bitcast.138, ...), custom_call_target="tpu_custom_call" | custom-call | flops 1 | bytes 1 | tf_op jit(solution)/shard_map/ffn/pallas_call | solution.py:562
  356.7 29.5 %ffn.6 = (bf16[512,1408]{1,0:T(8,128)(2,1)}, bf16[512,1408]{1,0:T(8,128)(2,1)}, bf16[512,1408]{1,0:T(8,128)(2,1)}, bf16[512,2048]{1,0:T(8,128)(2,1)}, bf16[512,2048]{1,0:T(8,128)(2,1)}) custom-call(bf16[512,2048]{1,0:T(8,128)(2,1)} %collective-permute-done.23.b_ref.refs_2_.refs_6_, bf16[512,2048]{1,0:T(8,128)(2,1)} %copy-done.42, ...), custom_call_target="tpu_custom_call" | custom-call | flops 1 | bytes 1 | tf_op jit(solution)/shard_map/ffn/pallas_call | solution.py:562
  387.7 29.6 %ffn.7 = (bf16[512,1408]{1,0:T(8,128)(2,1)}, bf16[512,1408]{1,0:T(8,128)(2,1)}, bf16[512,1408]{1,0:T(8,128)(2,1)}, bf16[512,2048]{1,0:T(8,128)(2,1)}, bf16[512,2048]{1,0:T(8,128)(2,1)}) custom-call(bf16[512,2048]{1,0:T(8,128)(2,1)} %copy-done.33, bf16[512,2048]{1,0:T(8,128)(2,1)} %collective-permute-done.17.dy_ref.refs_7_, bf16[2,2048,1408]{2,1,0:T(8,128)(2,1)} %bitcast.142, ...), custom_call_target="tpu_custom_call" | custom-call | flops 1 | bytes 1 | tf_op jit(solution)/shard_map/ffn/pallas_call | solution.py:562
  419.9 18.0 %grad_dn.1 = (bf16[704,2048]{1,0:T(8,128)(2,1)}, bf16[704,2048]{1,0:T(8,128)(2,1)}) custom-call(s32[1]{0:T(128)} %bitcast.20.core_ref, bf16[512,1408]{1,0:T(8,128)(2,1)} %get-tuple-element.375.refs_0_, bf16[512,1408]{1,0:T(8,128)(2,1)} %get-tuple-element.376.refs_1_, bf16[512,1408]{1,0:T(8,128)(2,1)} %get-tuple-element.377.refs_2_, ...), custom_call_target="tpu_custom_call" | custom-call | flops 1 | bytes 1 | tf_op jit(solution)/shard_map/grad_dn/pallas_call | solution.py:927
  437.9 7.0 collective-permute-done.26
  448.4 34.3 %grad_gu.1 = (bf16[4,4,64,2816]{3,2,1,0:T(8,128)(2,1)}, bf16[4,4,64,2816]{3,2,1,0:T(8,128)(2,1)}) custom-call(s32[1]{0:T(128)} %bitcast.20.core_ref, bf16[512,2048]{1,0:T(8,128)(2,1)} %get-tuple-element.385.b_ref.refs_0_.refs_4_, bf16[512,2048]{1,0:T(8,128)(2,1)} %copy-done.32, bf16[512,2048]{1,0:T(8,128)(2,1)} %collective-permute-done.23.b_ref.refs_2_.refs_6_, ...), custom_call_target="tpu_custom_call" | custom-call | flops 1 | bytes 1 | tf_op jit(solution)/shard_map/grad_gu/pallas_call | solution.py:605
  487.2 15.1 %resid_back.1 = (f32[512,2048]{1,0:T(8,128)}, bf16[512,2048]{1,0:T(8,128)(2,1)}, bf16[8,512,256]{2,1,0:T(8,128)(2,1)}) custom-call(s32[8]{0:T(128)} %copy-done.28, bf16[512,2048]{1,0:T(8,128)(2,1)} %get-tuple-element.347.db_ref, bf16[512,2048]{1,0:T(8,128)(2,1)} %copy-done.57, bf16[512,2048]{1,0:T(8,128)(2,1)} %collective-permute-done.27.passed_ref, ...), custom_call_target="tpu_custom_call" | custom-call | flops 1 | bytes 1 | tf_op jit(solution)/shard_map/resid_back/pallas_call | solution.py:803
  502.7 6.9 add_convert_fusion
  509.6 4.5 all-to-all-start.3
  515.7 6.1 grad_wo.1
  521.9 18.9 %all-to-all-done.3 = bf16[8,512,256]{2,1,0:T(8,128)(2,1)} async-done(((bf16[8,512,256]{2,1,0:T(8,128)(2,1)}), bf16[8,512,256]{2,1,0:T(8,128)(2,1)}, u32[]{:S(2)}, u32[]{:S(2)}) %all-to-all-start.3) | async-done | bytes 2097184 | tf_op jit(solution)/shard_map/all_to_all | solution.py:1337
  549.8 34.2 %attend_back.4 = (bf16[8,512,384]{2,1,0:T(8,128)(2,1)}, f32[256,4096]{1,0:T(8,128)}, f32[8,4,512]{2,1,0:T(4,128)}) custom-call(s32[1]{0:T(128)} %bitcast.14.zeros_ref, bf16[4096,384]{1,0:T(8,128)(2,1)} %bitcast.125, bf16[4096,384]{1,0:T(8,128)(2,1)} %bitcast.126, bf16[4096,256]{1,0:T(8,128)(2,1)} %bitcast.26.do_ref, f32[8,4,512]{2,1,0:T(4,128)} %copy-done.19, ...), custom_call_target="tpu_custom_call" | custom-call | flops 1 | bytes 1 | tf_op jit(solution)/shard_map/attend_back/pallas_call | solution.py:1164
  589.6 21.6 %collective-permute-start.39 = (bf16[176,2048]{1,0:T(8,128)(2,1)}, bf16[176,2048]{1,0:T(8,128)(2,1)S(1)}, u32[]{:S(2)}, u32[]{:S(2)}) collective-permute-start(bf16[176,2048]{1,0:T(8,128)(2,1)} %get-tuple-element.435), channel_id=1, source_target_pairs={{0,8},{8,16},{16,24},{1,9},{9,17},{17,25},{2,10},{10,18},{18,26},{... | collective-permute-start | bytes 2162696 | tf_op jit(solution)/shard_map/ppermute | solution.py:407
  612.5 29.6 %attend_back.5 = (bf16[8,512,384]{2,1,0:T(8,128)(2,1)}, f32[256,4096]{1,0:T(8,128)}, f32[8,4,512]{2,1,0:T(4,128)}) custom-call(s32[1]{0:T(128)} %bitcast.14.zeros_ref, bf16[4096,384]{1,0:T(8,128)(2,1)} %bitcast.127, bf16[4096,384]{1,0:T(8,128)(2,1)} %bitcast.128, bf16[4096,256]{1,0:T(8,128)(2,1)} %bitcast.26.do_ref, ...), custom_call_target="tpu_custom_call", output_to_operand_aliasing={{0}: (9, {})} | custom-call | flops 1 | bytes 1 | tf_op jit(solution)/shard_map/attend_back/pallas_call | solution.py:1164
  650.1 4.5 fusion.17
  654.6 41.4 %attend_back.6 = (bf16[8,512,384]{2,1,0:T(8,128)(2,1)}, f32[256,4096]{1,0:T(8,128)}, f32[8,4,512]{2,1,0:T(4,128)}) custom-call(s32[1]{0:T(128)} %bitcast.14.zeros_ref, bf16[4096,384]{1,0:T(8,128)(2,1)} %bitcast.129, bf16[4096,384]{1,0:T(8,128)(2,1)} %bitcast.130, bf16[4096,256]{1,0:T(8,128)(2,1)} %bitcast.26.do_ref, ...), custom_call_target="tpu_custom_call", output_to_operand_aliasing={{0}: (9, {})} | custom-call | flops 1 | bytes 1 | tf_op jit(solution)/shard_map/attend_back/pallas_call | solution.py:1164
  698.8 40.4 %attend_back.7 = (bf16[8,512,384]{2,1,0:T(8,128)(2,1)}, f32[256,4096]{1,0:T(8,128)}, f32[8,4,512]{2,1,0:T(4,128)}) custom-call(s32[1]{0:T(128)} %bitcast.14.zeros_ref, bf16[4096,384]{1,0:T(8,128)(2,1)} %bitcast.131, bf16[4096,384]{1,0:T(8,128)(2,1)} %bitcast.132, bf16[4096,256]{1,0:T(8,128)(2,1)} %bitcast.26.do_ref, ...), custom_call_target="tpu_custom_call", output_to_operand_aliasing={{0}: (9, {})} | custom-call | flops 1 | bytes 1 | tf_op jit(solution)/shard_map/attend_back/pallas_call | solution.py:1164
  745.0 13.3 %grad_qkv.1 = bf16[4,64,3072]{2,1,0:T(8,128)(2,1)S(1)} custom-call(s32[8]{0:T(128)S(1)} %copy-done.29, bf16[512,2048]{1,0:T(8,128)(2,1)S(1)} %copy-done.21, bf16[512,2048]{1,0:T(8,128)(2,1)} %collective-permute-done.32.refs_1_, bf16[512,2048]{1,0:T(8,128)(2,1)} %collective-permute-done.36.refs_2_, bf16[512,2048]{1,0:T(8,128)(2,1)} %collective-permute-done.41.refs_3_, ...), custom_call_target="tpu_custom_call" | custom-call | flops 1 | bytes 1 | tf_op jit(solution)/shard_map/grad_qkv/pallas_call | solution.py:639
  765.8 18.1 %collective-permute-done.47 = bf16[64,5120]{1,0:T(8,128)(2,1)} collective-permute-done((bf16[64,5120]{1,0:T(8,128)(2,1)}, bf16[64,5120]{1,0:T(8,128)(2,1)}, u32[]{:S(2)}, u32[]{:S(2)}) %collective-permute-start.47) | collective-permute-done | bytes 655392 | tf_op jit(solution)/shard_map/ppermute | solution.py:407
  786.4 5.2 collective-permute-start.49
  793.1 4.5 all-to-all-start.5
  799.5 19.2 %collective-permute-done.49 = bf16[64,5120]{1,0:T(8,128)(2,1)} collective-permute-done((bf16[64,5120]{1,0:T(8,128)(2,1)}, bf16[64,5120]{1,0:T(8,128)(2,1)}, u32[]{:S(2)}, u32[]{:S(2)}) %collective-permute-start.49) | collective-permute-done | bytes 655392 | tf_op jit(solution)/shard_map/ppermute | solution.py:407
  820.3 25.9 %collective-permute-start.51 = (bf16[64,5120]{1,0:T(8,128)(2,1)S(1)}, bf16[64,5120]{1,0:T(8,128)(2,1)S(1)}, u32[]{:S(2)}, u32[]{:S(2)}) collective-permute-start(bf16[64,5120]{1,0:T(8,128)(2,1)S(1)} %get-tuple-element.496), channel_id=1, source_target_pairs={{0,8},{8,16},{16,24},{1,9},{9,17},{17,25},{2,10},{10,18},{18,26},{... | collective-permute-start | bytes 1966088 | tf_op jit(solution)/shard_map/ppermute | solution.py:407
  847.7 24.7 %collective-permute-done.51 = bf16[64,5120]{1,0:T(8,128)(2,1)S(1)} collective-permute-done((bf16[64,5120]{1,0:T(8,128)(2,1)S(1)}, bf16[64,5120]{1,0:T(8,128)(2,1)S(1)}, u32[]{:S(2)}, u32[]{:S(2)}) %collective-permute-start.51) | collective-permute-done | bytes 655392 | tf_op jit(solution)/shard_map/ppermute | solution.py:407
  872.4 5.0 collective-permute-done.52
  882.0 14.6 %in_back.1 = bf16[512,2048]{1,0:T(8,128)(2,1)} custom-call(s32[8]{0:T(128)} %copy-done.28, bf16[8,512,384]{2,1,0:T(8,128)(2,1)} %all-to-all-done.5.back_ref, bf16[512,2048]{1,0:T(8,128)(2,1)} %bitcast.151, f32[512,1]{1,0:T(8,128)} %copy-done.23, f32[1,2048]{1,0:T(1,128)} %copy-done.27, f32[512,2048]{1,0:T(8,128)} %get-tuple-element.504.d_resid_ref, ...), custom_call_target="tpu_custom_call" | custom-call | flops 1 | bytes 1 | tf_op jit(solution)/shard_map/in_back/pallas_call | solution.py:856
  902.8 18.9 %collective-permute-start.55 = (bf16[64,5120]{1,0:T(8,128)(2,1)S(1)}, bf16[64,5120]{1,0:T(8,128)(2,1)S(1)}, u32[]{:S(2)}, u32[]{:S(2)}) collective-permute-start(bf16[64,5120]{1,0:T(8,128)(2,1)S(1)} %pad_maximum_fusion.3.refs_0_), channel_id=1, source_target_pairs={{0,8},{8,16},{16,24},{1,9},{9,17},{17,25},{2,10},{10,18},{18,26},{... | collective-permute-start | bytes 1966088 | tf_op jit(solution)/shard_map/ppermute | solution.py:419
  923.0 5.1 reshape.206
  928.1 7.5 collective-permute-done.55.refs_1_
  947.4 6.5 spread.1
  959.8 5.1 fusion
  965.0 9.8 collective-permute-done.60.refs_6_
  (320 shorter events, 182.2 us)
Async XLA Ops:
  79.5 34.3 %all-to-all-start.1 = ((bf16[4,64,2816]{2,1,0:T(8,128)(2,1)}), bf16[4,64,2816]{2,1,0:T(8,128)(2,1)}, u32[]{:S(2)}, u32[]{:S(2)}) async-start(bf16[4,64,2816]{2,1,0:T(8,128)(2,1)} %pad_maximum_fusion.2), calls=%async_computation.1 | async-start | bytes 2883584 | tf_op jit(solution)/shard_map/all_to_all | solution.py:1262
  83.8 146.1 %all-gather.7.cloned.1.call-start = ((), (), s32[]{:S(2)}) async-start(), calls=%async_computation.9 | async-start | bytes 7208960 | tf_op jit(solution)/shard_map/all_gather | solution.py:1266
  84.3 29.5 %collective-permute-start.10 = (bf16[256,2048]{1,0:T(8,128)(2,1)}, bf16[256,2048]{1,0:T(8,128)(2,1)}, u32[]{:S(2)}, u32[]{:S(2)}) collective-permute-start(bf16[256,2048]{1,0:T(8,128)(2,1)} %refs_0_.1), channel_id=1, source_target_pairs={{0,2},{1,5},{2,0},{3,7},{4,6},{5,1},{6,4},{7,3},{8,10},{9,13},{10,... | collective-permute-start | bytes 3145736 | tf_op jit(solution)/shard_map/ppermute | solution.py:347
  114.0 41.5 %all-to-all-start = ((bf16[8,512,384]{2,1,0:T(8,128)(2,1)}), bf16[8,512,384]{2,1,0:T(8,128)(2,1)S(1)}, u32[]{:S(2)}, u32[]{:S(2)}) async-start(bf16[8,512,384]{2,1,0:T(8,128)(2,1)} %get-tuple-element.296), calls=%async_computation | async-start | bytes 6291456 | tf_op jit(solution)/shard_map/all_to_all | solution.py:1271
  155.5 35.5 %collective-permute-start.13 = (bf16[512,2048]{1,0:T(8,128)(2,1)}, bf16[512,2048]{1,0:T(8,128)(2,1)S(1)}, u32[]{:S(2)}, u32[]{:S(2)}) collective-permute-start(bf16[512,2048]{1,0:T(8,128)(2,1)} %multiply_bitcast_fusion.dy_ref.refs_4_), channel_id=1, source_target_pairs={{0,2},{1,5},{2,0},{3,7},{4,6},{5,1},{6,4},{7,3},{8,10},{9,13},{10,... | collective-permute-start | bytes 6291464 | tf_op jit(solution)/shard_map/ppermute | solution.py:347
  156.0 30.4 %collective-permute-start.12 = (bf16[256,2048]{1,0:T(8,128)(2,1)}, bf16[256,2048]{1,0:T(8,128)(2,1)S(1)}, u32[]{:S(2)}, u32[]{:S(2)}) collective-permute-start(bf16[256,2048]{1,0:T(8,128)(2,1)} %refs_0_.1), channel_id=1, source_target_pairs={{0,4},{1,3},{2,6},{3,1},{4,0},{5,7},{6,2},{7,5},{8,12},{9,11},{10,... | collective-permute-start | bytes 3145736 | tf_op jit(solution)/shard_map/ppermute | solution.py:351
  191.0 37.3 %collective-permute-start.15 = (bf16[512,2048]{1,0:T(8,128)(2,1)S(1)}, bf16[512,2048]{1,0:T(8,128)(2,1)S(1)}, u32[]{:S(2)}, u32[]{:S(2)}) collective-permute-start(bf16[512,2048]{1,0:T(8,128)(2,1)S(1)} %copy-done.30), channel_id=1, source_target_pairs={{0,4},{1,3},{2,6},{3,1},{4,0},{5,7},{6,2},{7,5},{8,12},{9,11},{10,... | collective-permute-start | bytes 6291464 | tf_op jit(solution)/shard_map/ppermute | solution.py:351
  192.7 35.6 %collective-permute-start.14 = (bf16[256,2048]{1,0:T(8,128)(2,1)}, bf16[256,2048]{1,0:T(8,128)(2,1)S(1)}, u32[]{:S(2)}, u32[]{:S(2)}) collective-permute-start(bf16[256,2048]{1,0:T(8,128)(2,1)} %collective-permute-done.10.refs_1_), channel_id=1, source_target_pairs={{0,4},{1,3},{2,6},{3,1},{4,0},{5,7},{6,2},{7,5},{8,12},{9,11},{10,... | collective-permute-start | bytes 3145736 | tf_op jit(solution)/shard_map/ppermute | solution.py:351
  230.0 40.6 %collective-permute-start.17 = (bf16[512,2048]{1,0:T(8,128)(2,1)}, bf16[512,2048]{1,0:T(8,128)(2,1)}, u32[]{:S(2)}, u32[]{:S(2)}) collective-permute-start(bf16[512,2048]{1,0:T(8,128)(2,1)} %copy-done.41), channel_id=1, source_target_pairs={{0,4},{1,3},{2,6},{3,1},{4,0},{5,7},{6,2},{7,5},{8,12},{9,11},{10,... | collective-permute-start | bytes 6291464 | tf_op jit(solution)/shard_map/ppermute | solution.py:351
  251.7 30.3 %all-to-all-start.2 = ((bf16[8,512,256]{2,1,0:T(8,128)(2,1)}), bf16[8,512,256]{2,1,0:T(8,128)(2,1)S(1)}, u32[]{:S(2)}, u32[]{:S(2)}) async-start(bf16[8,512,256]{2,1,0:T(8,128)(2,1)} %copy-done.6), calls=%async_computation.2 | async-start | bytes 4194304 | tf_op jit(solution)/shard_map/all_to_all | solution.py:1289
  255.4 386.8 %reduce-scatter.2.cloned.1.call-start = ((), (), s32[]{:S(2)}) async-start(), calls=%async_computation.8 | async-start | bytes 7208960 | tf_op jit(solution)/shard_map/reduce_scatter | solution.py:1333
  295.1 29.8 %collective-permute-start.22 = (bf16[512,2048]{1,0:T(8,128)(2,1)}, bf16[512,2048]{1,0:T(8,128)(2,1)S(1)}, u32[]{:S(2)}, u32[]{:S(2)}) collective-permute-start(bf16[512,2048]{1,0:T(8,128)(2,1)} %get-tuple-element.385.b_ref.refs_0_.refs_4_), channel_id=1, source_target_pairs={{0,2},{1,5},{2,0},{3,7},{4,6},{5,1},{6,4},{7,3},{8,10},{9,13},{10,... | collective-permute-start | bytes 6291464 | tf_op jit(solution)/shard_map/ppermute | solution.py:347
  324.9 31.0 %collective-permute-start.23 = (bf16[512,2048]{1,0:T(8,128)(2,1)S(1)}, bf16[512,2048]{1,0:T(8,128)(2,1)}, u32[]{:S(2)}, u32[]{:S(2)}) collective-permute-start(bf16[512,2048]{1,0:T(8,128)(2,1)S(1)} %copy-done.31), channel_id=1, source_target_pairs={{0,4},{1,3},{2,6},{3,1},{4,0},{5,7},{6,2},{7,5},{8,12},{9,11},{10,... | collective-permute-start | bytes 6291464 | tf_op jit(solution)/shard_map/ppermute | solution.py:351
  356.0 30.2 %collective-permute-start.24 = (bf16[512,2048]{1,0:T(8,128)(2,1)}, bf16[512,2048]{1,0:T(8,128)(2,1)S(1)}, u32[]{:S(2)}, u32[]{:S(2)}) collective-permute-start(bf16[512,2048]{1,0:T(8,128)(2,1)} %copy-done.32), channel_id=1, source_target_pairs={{0,4},{1,3},{2,6},{3,1},{4,0},{5,7},{6,2},{7,5},{8,12},{9,11},{10,... | collective-permute-start | bytes 6291464 | tf_op jit(solution)/shard_map/ppermute | solution.py:351
  386.2 31.1 %collective-permute-start.25 = (bf16[512,2048]{1,0:T(8,128)(2,1)}, bf16[512,2048]{1,0:T(8,128)(2,1)S(1)}, u32[]{:S(2)}, u32[]{:S(2)}) collective-permute-start(bf16[512,2048]{1,0:T(8,128)(2,1)} %get-tuple-element.364), channel_id=1, source_target_pairs={{0,2},{1,5},{2,0},{3,7},{4,6},{5,1},{6,4},{7,3},{8,10},{9,13},{10,... | collective-permute-start | bytes 6291464 | tf_op jit(solution)/shard_map/ppermute | solution.py:347
  418.7 26.2 %collective-permute-start.26 = (bf16[512,2048]{1,0:T(8,128)(2,1)}, bf16[512,2048]{1,0:T(8,128)(2,1)S(1)}, u32[]{:S(2)}, u32[]{:S(2)}) collective-permute-start(bf16[512,2048]{1,0:T(8,128)(2,1)} %get-tuple-element.374), channel_id=1, source_target_pairs={{0,2},{1,5},{2,0},{3,7},{4,6},{5,1},{6,4},{7,3},{8,10},{9,13},{10,... | collective-permute-start | bytes 6291464 | tf_op jit(solution)/shard_map/ppermute | solution.py:347
  447.2 35.5 %collective-permute-start.28 = (bf16[704,2048]{1,0:T(8,128)(2,1)}, bf16[704,2048]{1,0:T(8,128)(2,1)S(1)}, u32[]{:S(2)}, u32[]{:S(2)}) collective-permute-start(bf16[704,2048]{1,0:T(8,128)(2,1)} %get-tuple-element.384), channel_id=1, source_target_pairs={{0,1},{1,0},{2,3},{3,2},{4,5},{5,4},{6,7},{7,6},{8,9},{9,8},{10,11... | collective-permute-start | bytes 8650760 | tf_op jit(solution)/shard_map/ppermute | solution.py:355
  447.2 35.5 %collective-permute-start.27 = (bf16[512,2048]{1,0:T(8,128)(2,1)}, bf16[512,2048]{1,0:T(8,128)(2,1)}, u32[]{:S(2)}, u32[]{:S(2)}) collective-permute-start(bf16[512,2048]{1,0:T(8,128)(2,1)} %add_convert_fusion.3), channel_id=1, source_target_pairs={{0,4},{1,3},{2,6},{3,1},{4,0},{5,7},{6,2},{7,5},{8,12},{9,11},{10,... | collective-permute-start | bytes 6291464 | tf_op jit(solution)/shard_map/ppermute | solution.py:351
  509.6 31.1 %all-to-all-start.3 = ((bf16[8,512,256]{2,1,0:T(8,128)(2,1)}), bf16[8,512,256]{2,1,0:T(8,128)(2,1)}, u32[]{:S(2)}, u32[]{:S(2)}) async-start(bf16[8,512,256]{2,1,0:T(8,128)(2,1)} %get-tuple-element.408), calls=%async_computation.3 | async-start | bytes 4194304 | tf_op jit(solution)/shard_map/all_to_all | solution.py:1337
  540.8 43.3 %collective-permute-start.33 = (bf16[4,256,2048]{2,1,0:T(8,128)(2,1)}, bf16[4,256,2048]{2,1,0:T(8,128)(2,1)}, u32[]{:S(2)}, u32[]{:S(2)}) collective-permute-start(bf16[4,256,2048]{2,1,0:T(8,128)(2,1)} %get-tuple-element.415), channel_id=1, source_target_pairs={{0,1},{1,0},{2,3},{3,2},{4,5},{5,4},{6,7},{7,6},{8,9},{9,8},{10,11... | collective-permute-start | bytes 12582920 | tf_op jit(solution)/shard_map/ppermute | solution.py:355
  540.8 43.3 %collective-permute-start.32 = (bf16[512,2048]{1,0:T(8,128)(2,1)}, bf16[512,2048]{1,0:T(8,128)(2,1)}, u32[]{:S(2)}, u32[]{:S(2)}) collective-permute-start(bf16[512,2048]{1,0:T(8,128)(2,1)} %get-tuple-element.430.refs_0_), channel_id=1, source_target_pairs={{0,2},{1,5},{2,0},{3,7},{4,6},{5,1},{6,4},{7,3},{8,10},{9,13},{10,... | collective-permute-start | bytes 6291464 | tf_op jit(solution)/shard_map/ppermute | solution.py:347
  544.7 39.3 %collective-permute-start.34 = (bf16[176,2048]{1,0:T(8,128)(2,1)}, bf16[176,2048]{1,0:T(8,128)(2,1)S(1)}, u32[]{:S(2)}, u32[]{:S(2)}) collective-permute-start(bf16[176,2048]{1,0:T(8,128)(2,1)} %get-tuple-element.537), channel_id=1, source_target_pairs={{0,8},{8,16},{1,9},{9,17},{2,10},{10,18},{3,11},{11,19},{4,12},{12... | collective-permute-start | bytes 2162696 | tf_op jit(solution)/shard_map/ppermute | solution.py:407
  549.1 34.9 %collective-permute-start.35 = (bf16[176,2048]{1,0:T(8,128)(2,1)S(1)}, bf16[176,2048]{1,0:T(8,128)(2,1)S(1)}, u32[]{:S(2)}, u32[]{:S(2)}) collective-permute-start(bf16[176,2048]{1,0:T(8,128)(2,1)S(1)} %get-tuple-element.536), channel_id=1, source_target_pairs={{24,16},{16,8},{25,17},{17,9},{26,18},{18,10},{27,19},{19,11},{28,... | collective-permute-start | bytes 2162696 | tf_op jit(solution)/shard_map/ppermute | solution.py:408
  588.6 53.5 %collective-permute-start.36 = (bf16[512,2048]{1,0:T(8,128)(2,1)S(1)}, bf16[512,2048]{1,0:T(8,128)(2,1)}, u32[]{:S(2)}, u32[]{:S(2)}) collective-permute-start(bf16[512,2048]{1,0:T(8,128)(2,1)S(1)} %copy-done.20), channel_id=1, source_target_pairs={{0,4},{1,3},{2,6},{3,1},{4,0},{5,7},{6,2},{7,5},{8,12},{9,11},{10,... | collective-permute-start | bytes 6291464 | tf_op jit(solution)/shard_map/ppermute | solution.py:351
  589.1 53.0 %collective-permute-start.37 = (bf16[512,2048]{1,0:T(8,128)(2,1)S(1)}, bf16[512,2048]{1,0:T(8,128)(2,1)}, u32[]{:S(2)}, u32[]{:S(2)}) collective-permute-start(bf16[512,2048]{1,0:T(8,128)(2,1)S(1)} %copy-done.20), channel_id=1, source_target_pairs={{0,1},{1,0},{2,3},{3,2},{4,5},{5,4},{6,7},{7,6},{8,9},{9,8},{10,11... | collective-permute-start | bytes 6291464 | tf_op jit(solution)/shard_map/ppermute | solution.py:355
  589.1 53.0 %collective-permute-start.38 = (bf16[512,2048]{1,0:T(8,128)(2,1)}, bf16[512,2048]{1,0:T(8,128)(2,1)}, u32[]{:S(2)}, u32[]{:S(2)}) collective-permute-start(bf16[512,2048]{1,0:T(8,128)(2,1)} %collective-permute-done.32.refs_1_), channel_id=1, source_target_pairs={{0,1},{1,0},{2,3},{3,2},{4,5},{5,4},{6,7},{7,6},{8,9},{9,8},{10,11... | collective-permute-start | bytes 6291464 | tf_op jit(solution)/shard_map/ppermute | solution.py:355
  589.6 52.5 %collective-permute-start.39 = (bf16[176,2048]{1,0:T(8,128)(2,1)}, bf16[176,2048]{1,0:T(8,128)(2,1)S(1)}, u32[]{:S(2)}, u32[]{:S(2)}) collective-permute-start(bf16[176,2048]{1,0:T(8,128)(2,1)} %get-tuple-element.435), channel_id=1, source_target_pairs={{0,8},{8,16},{16,24},{1,9},{9,17},{17,25},{2,10},{10,18},{18,26},{... | collective-permute-start | bytes 2162696 | tf_op jit(solution)/shard_map/ppermute | solution.py:407
  611.2 30.9 %collective-permute-start.40 = (bf16[176,2048]{1,0:T(8,128)(2,1)S(1)}, bf16[176,2048]{1,0:T(8,128)(2,1)}, u32[]{:S(2)}, u32[]{:S(2)}) collective-permute-start(bf16[176,2048]{1,0:T(8,128)(2,1)S(1)} %get-tuple-element.436), channel_id=1, source_target_pairs={{24,16},{16,8},{8,0},{25,17},{17,9},{9,1},{26,18},{18,10},{10,2},{... | collective-permute-start | bytes 2162696 | tf_op jit(solution)/shard_map/ppermute | solution.py:408
  645.1 50.9 %collective-permute-start.41 = (bf16[512,2048]{1,0:T(8,128)(2,1)}, bf16[512,2048]{1,0:T(8,128)(2,1)}, u32[]{:S(2)}, u32[]{:S(2)}) collective-permute-start(bf16[512,2048]{1,0:T(8,128)(2,1)} %collective-permute-done.32.refs_1_), channel_id=1, source_target_pairs={{0,4},{1,3},{2,6},{3,1},{4,0},{5,7},{6,2},{7,5},{8,12},{9,11},{10,... | collective-permute-start | bytes 6291464 | tf_op jit(solution)/shard_map/ppermute | solution.py:351
  645.9 50.2 %collective-permute-start.42 = (bf16[512,2048]{1,0:T(8,128)(2,1)}, bf16[512,2048]{1,0:T(8,128)(2,1)S(1)}, u32[]{:S(2)}, u32[]{:S(2)}) collective-permute-start(bf16[512,2048]{1,0:T(8,128)(2,1)} %collective-permute-done.36.refs_2_), channel_id=1, source_target_pairs={{0,1},{1,0},{2,3},{3,2},{4,5},{5,4},{6,7},{7,6},{8,9},{9,8},{10,11... | collective-permute-start | bytes 6291464 | tf_op jit(solution)/shard_map/ppermute | solution.py:355
  646.1 49.9 %all-to-all-start.4 = ((bf16[4,64,2816]{2,1,0:T(8,128)(2,1)}), bf16[4,64,2816]{2,1,0:T(8,128)(2,1)S(1)}, u32[]{:S(2)}, u32[]{:S(2)}) async-start(bf16[4,64,2816]{2,1,0:T(8,128)(2,1)} %bitcast.166), calls=%async_computation.5 | async-start | bytes 2883584 | tf_op jit(solution)/shard_map/all_to_all | solution.py:1368
  649.7 273.3 %all-gather.9.cloned.1.call-start = ((), (), s32[]{:S(2)}) async-start(), calls=%async_computation.10 | async-start | bytes 3604480 | tf_op jit(solution)/shard_map/all_gather | solution.py:1367
  696.1 45.6 %collective-permute-start.45 = (bf16[512,2048]{1,0:T(8,128)(2,1)}, bf16[512,2048]{1,0:T(8,128)(2,1)}, u32[]{:S(2)}, u32[]{:S(2)}) collective-permute-start(bf16[512,2048]{1,0:T(8,128)(2,1)} %collective-permute-done.41.refs_3_), channel_id=1, source_target_pairs={{0,1},{1,0},{2,3},{3,2},{4,5},{5,4},{6,7},{7,6},{8,9},{9,8},{10,11... | collective-permute-start | bytes 6291464 | tf_op jit(solution)/shard_map/ppermute | solution.py:355
  696.5 245.6 %all-gather.11.cloned.1.call-start = ((), (), s32[]{:S(2)}) async-start(), calls=%async_computation.11 | async-start | bytes 7208960 | tf_op jit(solution)/shard_map/all_gather | solution.py:1378
  696.7 42.5 %collective-permute-start.44 = (bf16[256,2048]{1,0:T(8,128)(2,1)}, bf16[256,2048]{1,0:T(8,128)(2,1)}, u32[]{:S(2)}, u32[]{:S(2)}) collective-permute-start(bf16[256,2048]{1,0:T(8,128)(2,1)} %get-tuple-element.472), channel_id=1, source_target_pairs={{0,2},{1,5},{2,0},{3,7},{4,6},{5,1},{6,4},{7,3},{8,10},{9,13},{10,... | collective-permute-start | bytes 3145736 | tf_op jit(solution)/shard_map/ppermute | solution.py:347
  698.4 43.2 %collective-permute-start.43 = (bf16[256,2048]{1,0:T(8,128)(2,1)}, bf16[256,2048]{1,0:T(8,128)(2,1)}, u32[]{:S(2)}, u32[]{:S(2)}) collective-permute-start(bf16[256,2048]{1,0:T(8,128)(2,1)} %get-tuple-element.471), channel_id=1, source_target_pairs={{0,2},{1,5},{2,0},{3,7},{4,6},{5,1},{6,4},{7,3},{8,10},{9,13},{10,... | collective-permute-start | bytes 3145736 | tf_op jit(solution)/shard_map/ppermute | solution.py:347
  762.2 21.8 %collective-permute-start.47 = (bf16[64,5120]{1,0:T(8,128)(2,1)}, bf16[64,5120]{1,0:T(8,128)(2,1)}, u32[]{:S(2)}, u32[]{:S(2)}) collective-permute-start(bf16[64,5120]{1,0:T(8,128)(2,1)} %get-tuple-element.487), channel_id=1, source_target_pairs={{0,8},{1,9},{2,10},{3,11},{4,12},{5,13},{6,14},{7,15}} | collective-permute-start | bytes 1966088 | tf_op jit(solution)/shard_map/ppermute | solution.py:407
  764.3 19.7 %collective-permute-start.48 = (bf16[64,5120]{1,0:T(8,128)(2,1)S(1)}, bf16[64,5120]{1,0:T(8,128)(2,1)}, u32[]{:S(2)}, u32[]{:S(2)}) collective-permute-start(bf16[64,5120]{1,0:T(8,128)(2,1)S(1)} %get-tuple-element.488), channel_id=1, source_target_pairs={{24,16},{25,17},{26,18},{27,19},{28,20},{29,21},{30,22},{31,23}} | collective-permute-start | bytes 1966088 | tf_op jit(solution)/shard_map/ppermute | solution.py:408
  786.4 32.4 %collective-permute-start.49 = (bf16[64,5120]{1,0:T(8,128)(2,1)}, bf16[64,5120]{1,0:T(8,128)(2,1)}, u32[]{:S(2)}, u32[]{:S(2)}) collective-permute-start(bf16[64,5120]{1,0:T(8,128)(2,1)} %get-tuple-element.492), channel_id=1, source_target_pairs={{0,8},{8,16},{1,9},{9,17},{2,10},{10,18},{3,11},{11,19},{4,12},{12... | collective-permute-start | bytes 1966088 | tf_op jit(solution)/shard_map/ppermute | solution.py:407
  791.6 27.1 %collective-permute-start.50 = (bf16[64,5120]{1,0:T(8,128)(2,1)S(1)}, bf16[64,5120]{1,0:T(8,128)(2,1)}, u32[]{:S(2)}, u32[]{:S(2)}) collective-permute-start(bf16[64,5120]{1,0:T(8,128)(2,1)S(1)} %get-tuple-element.493), channel_id=1, source_target_pairs={{24,16},{16,8},{25,17},{17,9},{26,18},{18,10},{27,19},{19,11},{28,... | collective-permute-start | bytes 1966088 | tf_op jit(solution)/shard_map/ppermute | solution.py:408
  793.1 85.4 %all-to-all-start.5 = ((bf16[8,512,384]{2,1,0:T(8,128)(2,1)}), bf16[8,512,384]{2,1,0:T(8,128)(2,1)}, u32[]{:S(2)}, u32[]{:S(2)}) async-start(bf16[8,512,384]{2,1,0:T(8,128)(2,1)} %get-tuple-element.480.refs_8_), calls=%async_computation.6 | async-start | bytes 6291456 | tf_op jit(solution)/shard_map/all_to_all | solution.py:1387
  797.6 99.1 %collective-permute-start.53 = (bf16[512,2048]{1,0:T(8,128)(2,1)}, bf16[512,2048]{1,0:T(8,128)(2,1)}, u32[]{:S(2)}, u32[]{:S(2)}) collective-permute-start(bf16[512,2048]{1,0:T(8,128)(2,1)} %get-tuple-element.485), channel_id=1, source_target_pairs={{0,2},{1,5},{2,0},{3,7},{4,6},{5,1},{6,4},{7,3},{8,10},{9,13},{10,... | collective-permute-start | bytes 6291464 | tf_op jit(solution)/shard_map/ppermute | solution.py:347
  820.3 52.0 %collective-permute-start.51 = (bf16[64,5120]{1,0:T(8,128)(2,1)S(1)}, bf16[64,5120]{1,0:T(8,128)(2,1)S(1)}, u32[]{:S(2)}, u32[]{:S(2)}) collective-permute-start(bf16[64,5120]{1,0:T(8,128)(2,1)S(1)} %get-tuple-element.496), channel_id=1, source_target_pairs={{0,8},{8,16},{16,24},{1,9},{9,17},{17,25},{2,10},{10,18},{18,26},{... | collective-permute-start | bytes 1966088 | tf_op jit(solution)/shard_map/ppermute | solution.py:407
  846.3 31.1 %collective-permute-start.52 = (bf16[64,5120]{1,0:T(8,128)(2,1)S(1)}, bf16[64,5120]{1,0:T(8,128)(2,1)S(1)}, u32[]{:S(2)}, u32[]{:S(2)}) collective-permute-start(bf16[64,5120]{1,0:T(8,128)(2,1)S(1)} %get-tuple-element.497), channel_id=1, source_target_pairs={{24,16},{16,8},{8,0},{25,17},{17,9},{9,1},{26,18},{18,10},{10,2},{... | collective-permute-start | bytes 1966088 | tf_op jit(solution)/shard_map/ppermute | solution.py:408
  847.6 53.1 %collective-permute-start.54 = (bf16[512,2048]{1,0:T(8,128)(2,1)}, bf16[512,2048]{1,0:T(8,128)(2,1)}, u32[]{:S(2)}, u32[]{:S(2)}) collective-permute-start(bf16[512,2048]{1,0:T(8,128)(2,1)} %get-tuple-element.491), channel_id=1, source_target_pairs={{0,2},{1,5},{2,0},{3,7},{4,6},{5,1},{6,4},{7,3},{8,10},{9,13},{10,... | collective-permute-start | bytes 6291464 | tf_op jit(solution)/shard_map/ppermute | solution.py:347
  878.6 22.0 %all-to-all-start.6 = ((bf16[8,64,384]{2,1,0:T(8,128)(2,1)}), bf16[8,64,384]{2,1,0:T(8,128)(2,1)S(1)}, u32[]{:S(2)}, u32[]{:S(2)}) async-start(bf16[8,64,384]{2,1,0:T(8,128)(2,1)} %bitcast.118), calls=%async_computation.7 | async-start | bytes 786432 | tf_op jit(solution)/shard_map/all_to_all | solution.py:1406
  900.7 59.1 %collective-permute-start.61 = (bf16[512,2048]{1,0:T(8,128)(2,1)}, bf16[512,2048]{1,0:T(8,128)(2,1)}, u32[]{:S(2)}, u32[]{:S(2)}) collective-permute-start(bf16[512,2048]{1,0:T(8,128)(2,1)} %add_convert_fusion.2), channel_id=1, source_target_pairs={{0,4},{1,3},{2,6},{3,1},{4,0},{5,7},{6,2},{7,5},{8,12},{9,11},{10,... | collective-permute-start | bytes 6291464 | tf_op jit(solution)/shard_map/ppermute | solution.py:351
  902.8 32.8 %collective-permute-start.55 = (bf16[64,5120]{1,0:T(8,128)(2,1)S(1)}, bf16[64,5120]{1,0:T(8,128)(2,1)S(1)}, u32[]{:S(2)}, u32[]{:S(2)}) collective-permute-start(bf16[64,5120]{1,0:T(8,128)(2,1)S(1)} %pad_maximum_fusion.3.refs_0_), channel_id=1, source_target_pairs={{0,8},{8,16},{16,24},{1,9},{9,17},{17,25},{2,10},{10,18},{18,26},{... | collective-permute-start | bytes 1966088 | tf_op jit(solution)/shard_map/ppermute | solution.py:419
  (93 other events, 1113.1 us)
Sparse Core Ops, SparseCore 0:
  113.9 107.2 all-gather.6
  509.7 129.4 reduce-scatter.1
  696.6 57.6 all-gather.8
  765.9 132.7 all-gather.10

commit v4 on v3

--- a/solution.py
+++ b/solution.py
@@ -464,6 +464,33 @@
     )(parts, weight, gain)
 
 
+def spread_rows_kernel(z_ref, *refs, planes):
+    blocks, out_ref = refs[:-1], refs[-1]
+    rows = blocks[0].shape[0]
+    for place, load in line_values(blocks, planes, z_ref[0]):
+        out_ref[pl.ds(pl.multiple_of(place * rows, rows), rows), :] = load(slice(None)).astype(F32)
+
+
+def spread_rows(steps):
+    planes = len(steps)
+    rows, width = steps[0][0].shape
+    blocks = [steps[0][0]] + [s[0] for s in steps[1:]] + [s[1] for s in steps[1:]]
+    tile = width // 4
+    return pl.pallas_call(
+        functools.partial(spread_rows_kernel, planes=planes),
+        grid_spec=pltpu.PrefetchScalarGridSpec(
+            num_scalar_prefetch=1,
+            grid=(4,),
+            in_specs=[pl.BlockSpec((rows, tile), lambda i, z: (0, i))] * len(blocks),
+            out_specs=pl.BlockSpec((planes * rows, tile), lambda i, z: (0, i)),
+        ),
+        out_shape=jax.ShapeDtypeStruct((planes * rows, width), F32),
+        compiler_params=pltpu.CompilerParams(vmem_limit_bytes=32 * 2**20),
+        cost_estimate=SHORT,
+        name="spread_rows",
+    )(lax.axis_index("dp").reshape(1), *blocks)
+
+
 def spread_last_kernel(z_ref, *refs, planes):
     blocks, (w_ref, g_ref, out_ref, gain_ref, wo_ref) = refs[:-5], refs[-5:]
     rows = blocks[0].shape[0]
@@ -539,43 +566,74 @@
     return out.reshape(2, 2 * chips * planes * rows, both // 2)
 
 
-def ffn_kernel(b_ref, dy_ref, wg_ref, wu_ref, wd_ref, hid_ref, dg_ref, du_ref, db_ref, y_ref):
-    gate = jnp.dot(b_ref[...], wg_ref[...], preferred_element_type=F32)
-    up = jnp.dot(b_ref[...], wu_ref[...], preferred_element_type=F32)
-    d_hidden = lax.dot_general(dy_ref[...], wd_ref[...], NT, preferred_element_type=F32)
-    sigmoid_g = jax.nn.sigmoid(gate)
-    silu_gate = gate * sigmoid_g
-    hid = (silu_gate * up).astype(BF)
-    d_gate = (d_hidden * up * (sigmoid_g * (1.0 + gate * (1.0 - sigmoid_g)))).astype(BF)
-    d_up = (d_hidden * silu_gate).astype(BF)
-    hid_ref[...] = hid
-    dg_ref[...] = d_gate
-    du_ref[...] = d_up
-    y_ref[...] = jnp.dot(hid, wd_ref[...], preferred_element_type=F32).astype(BF)
-    d_in = lax.dot_general(d_gate, wg_ref[...], NT, preferred_element_type=F32)
-    db_ref[...] = (d_in + lax.dot_general(d_up, wu_ref[...], NT, preferred_element_type=F32)).astype(BF)
+def ffn_kernel(*refs, cuts):
+    b_hbm, dy_hbm, wgu_hbm, wd_hbm, hid_hbm, dg_hbm, du_hbm, db_hbm, y_hbm = refs[:9]
+    b_ref, dy_ref, wg_ref, wu_ref, wd_ref, hid_ref, dg_ref, du_ref, db_ref, y_ref, sems = refs[9:]
+    count = len(cuts) - 1
+
+    def move(source, target, index):
+        copy = pltpu.make_async_copy(source, target, sems.at[index])
+        copy.start()
+        return copy
+
+    b_copy = move(b_hbm, b_ref, 3 * count)
+    weights = []
+    for c in range(count):
+        span = slice(cuts[c], cuts[c + 1])
+        gate_copy = move(wgu_hbm.at[0, :, span], wg_ref.at[:, span], 3 * c)
+        up_copy = move(wgu_hbm.at[1, :, span], wu_ref.at[:, span], 3 * c + 1)
+        weights.append([gate_copy, up_copy])
+        if c == 0:
+            dy_copy = move(dy_hbm, dy_ref, 3 * count + 1)
+        weights[-1].append(move(wd_hbm.at[span, :], wd_ref.at[span, :], 3 * c + 2))
+    b_copy.wait()
+    for c in range(count):
+        span = slice(cuts[c], cuts[c + 1])
+        for copy in weights[c][:2]:
+            copy.wait()
+        gate = jnp.dot(b_ref[...], wg_ref[:, span], preferred_element_type=F32)
+        up = jnp.dot(b_ref[...], wu_ref[:, span], preferred_element_type=F32)
+        if c == 0:
+            dy_copy.wait()
+        weights[c][2].wait()
+        d_hidden = lax.dot_general(dy_ref[...], wd_ref[span, :], NT, preferred_element_type=F32)
+        sigmoid_g = jax.nn.sigmoid(gate)
+        silu_gate = gate * sigmoid_g
+        hid_ref[:, span] = (silu_gate * up).astype(BF)
+        dg_ref[:, span] = (d_hidden * up * (sigmoid_g * (1.0 + gate * (1.0 - sigmoid_g)))).astype(BF)
+        du_ref[:, span] = (d_hidden * silu_gate).astype(BF)
+    base = 3 * count + 2
+    outs = [move(hid_ref, hid_hbm, base), move(dg_ref, dg_hbm, base + 1), move(du_ref, du_hbm, base + 2)]
+    y_ref[...] = jnp.dot(hid_ref[...], wd_ref[...], preferred_element_type=F32).astype(BF)
+    outs.append(move(y_ref, y_hbm, base + 3))
+    d_in = lax.dot_general(dg_ref[...], wg_ref[...], NT, preferred_element_type=F32)
+    db_ref[...] = (d_in + lax.dot_general(du_ref[...], wu_ref[...], NT, preferred_element_type=F32)).astype(BF)
+    outs.append(move(db_ref, db_hbm, base + 4))
+    for copy in outs:
+        copy.wait()
 
 
 def ffn(b_rows, dy_rows, w_gu, w_dn):
     rows, width = b_rows.shape
     hidden = w_dn.shape[0]
+    pieces = 3
+    cuts = tuple(round(hidden * c / pieces / 128) * 128 for c in range(pieces)) + (hidden,)
+    hbm = pl.BlockSpec(memory_space=pl.ANY)
     return pl.pallas_call(
-        ffn_kernel,
-        grid=(1,),
-        in_specs=[
-            pl.BlockSpec((rows, width), lambda i: (0, 0)),
-            pl.BlockSpec((rows, width), lambda i: (0, 0)),
-            pl.BlockSpec((None, width, hidden), lambda i: (0, 0, 0)),
-            pl.BlockSpec((None, width, hidden), lambda i: (1, 0, 0)),
-            pl.BlockSpec((hidden, width), lambda i: (0, 0)),
-        ],
-        out_specs=[pl.BlockSpec((rows, hidden), lambda i: (0, 0))] * 3
-        + [pl.BlockSpec((rows, width), lambda i: (0, 0))] * 2,
+        functools.partial(ffn_kernel, cuts=cuts),
+        in_specs=[hbm] * 4,
+        out_specs=[hbm] * 5,
         out_shape=[jax.ShapeDtypeStruct((rows, hidden), BF)] * 3 + [jax.ShapeDtypeStruct((rows, width), BF)] * 2,
+        scratch_shapes=[pltpu.VMEM((rows, width), BF)] * 2
+        + [pltpu.VMEM((width, hidden), BF)] * 2
+        + [pltpu.VMEM((hidden, width), BF)]
+        + [pltpu.VMEM((rows, hidden), BF)] * 3
+        + [pltpu.VMEM((rows, width), BF)] * 2
+        + [pltpu.SemaphoreType.DMA((3 * pieces + 7,))],
         compiler_params=pltpu.CompilerParams(vmem_limit_bytes=58 * 2**20),
         cost_estimate=SHORT,
         name="ffn",
-    )(b_rows, dy_rows, w_gu, w_gu, w_dn)
+    )(b_rows, dy_rows, w_gu, w_dn)
 
 
 def grad_gu_kernel(core_ref, *refs, count):
@@ -1343,7 +1401,7 @@
     def back_call(heads, start, stop, **kwargs):
         return attend_back(zeros_one, qkv_heads, heads, lse, cos_all, sin_all, start, stop, **kwargs)
 
-    turns = (0, blocks // 8, blocks // 4, blocks // 2, blocks)
+    turns = (0, blocks // 8, blocks // 4, (3 * blocks) // 8, blocks)
     wo_got = send_sibling(wo_give)
     a_first = send_first(normed)
     bwd = back_call(d_heads, turns[0], turns[1], out=out_heads)
@@ -1363,27 +1421,30 @@
         return pick(wo_keep, place).astype(F32) + pick(wo_got, place).astype(F32)
 
     dn_z = line_scatter_end(dn_parts, dn_moves, 0)
-    d_heads, dn_z, gu_z, a_first, a_second = fence(d_heads, dn_z, gu_z, a_first, a_second)
-    dn_all = lax.all_gather(dn_z, "dp", axis=0, tiled=False)
+    d_heads, dn_z, gu_z, a_second = fence(d_heads, dn_z, gu_z, a_second)
+    dn_steps = [(dn_z, dn_z), line_gather_move((dn_z, dn_z), 1)]
     gu_z = lax.all_to_all(gu_z, "sp", 0, 0, axis_index_groups=SAME_CORE, tiled=True)
-    a_far = send_second(a_first)
     a_theirs.append(send_sibling(a_second))
     bwd = back_call(d_heads, turns[2], turns[3], before=bwd)
-    d_heads, gu_z, a_far, *moves = fence(d_heads, gu_z, a_far, *a_theirs, *bwd)
-    a_theirs, bwd = moves[:3], moves[3:]
+    d_heads, gu_z, a_first, *moves = fence(d_heads, gu_z, a_first, *a_theirs, *dn_steps[-1], *bwd)
+    a_theirs, dn_steps[-1], bwd = moves[:3], tuple(moves[3:5]), moves[5:]
 
     wo_first = wo_part(chip ^ (first_mask // 2)).astype(BF)
     wo_far = wo_part(chip ^ 3).astype(BF)
-    d_heads, gu_z, a_far, wo_first, wo_far = fence(d_heads, gu_z, a_far, wo_first, wo_far)
+    d_heads, gu_z, a_first, wo_first, wo_far = fence(d_heads, gu_z, a_first, wo_first, wo_far)
     gu_all = lax.all_gather(gu_z, "dp", axis=0, tiled=False)
+    a_far = send_second(a_first)
     wo_far = send_first(wo_far)
     wo_first = send_first(wo_first)
-    a_theirs.append(send_sibling(a_far))
+    dn_steps.append(line_gather_move(dn_steps[-1], 2))
     bwd = back_call(d_heads, turns[3], turns[4], before=bwd)
     wo_pass = (wo_part(chip ^ (second_mask // 2)) + wo_far.astype(F32)).astype(BF)
-    dp_heads, wo_first, wo_pass, *a_theirs = fence(bwd[0], wo_first, wo_pass, *a_theirs)
+    dp_heads, wo_first, wo_pass, a_far, *moves = fence(bwd[0], wo_first, wo_pass, a_far, *dn_steps[-1])
+    dn_steps[-1] = tuple(moves)
 
     wo_passed = send_second(wo_pass)
+    a_theirs.append(send_sibling(a_far))
+    dn_steps.append(line_gather_move(dn_steps[-1], 3))
     back = lax.all_to_all(dp_heads, "sp", 0, 0, tiled=True)
     grad_wq = grad_qkv(places, [normed, a_first, a_second, a_far] + list(a_theirs), dp_heads, planes)
     wo_rows = (wo_part(chip) + wo_first.astype(F32) + wo_passed.astype(F32)).astype(BF)
@@ -1397,6 +1458,8 @@
         moves = line_scatter_move(moves, step)
         if step == 1:
             y_got_far = send_first(y_far)
+            moves = fence(*moves, *dn_steps[-1])
+            moves, dn_steps[-1] = moves[:2], tuple(moves[2:])
         elif step == 2:
             y_got_first = send_first(y_first)
         moves = fence(*moves)
@@ -1414,7 +1477,7 @@
     for step in range(1, planes):
         last_steps.append(line_gather_move(last_steps[-1], step))
         if step == 1:
-            outs.append(dn_all.astype(F32).reshape(w_down.shape))
+            outs.append(spread_rows(dn_steps))
         elif step == 2:
             outs += spread(gu_all, w_gate_up, g_mlp.astype(F32).reshape(share, 1))
         if step == planes - 1:

time: 1000 us -> 1020 us (1.020)
  starting transfers between devices: 158 us -> 208 us
  Pallas kernels: 477 us -> 429 us
  waiting for transfers between devices: 213 us -> 239 us
    ppermute x6, starting transfers between devices: 60.8 us -> 99.2 us  [line_scatter_move(): right = lax.ppermute(sends[0], 'dp', [(i, i + 1) for i in range(step)])]
    pallas_call x4, Pallas kernels: 146 us -> 119 us  [attend_back(): pl.pallas_call(functools.partial(attend_back_kernel, heads=heads, start=s...]
    ppermute x13, waiting for transfers between devices: 27 us -> 45 us  [send_second(): return lax.ppermute(x, 'sp', SECOND)]
    pallas_call x3, Pallas kernels: 66.2 us -> 53.2 us  [attend(): pl.pallas_call(functools.partial(attend_kernel, heads=heads, start=start,...]
    pallas_call x4 -> x5, Pallas kernels: 118 us -> 108 us  [the longest x4 103 us: ffn(): pl.pallas_call(functools.partial(ffn_kernel, cuts=cuts), in_specs=[hbm] *...]
    ppermute x3 -> x6, starting transfers between devices: 20.4 us -> 25.7 us  [line_gather_move(): lax.ppermute(got[0], 'dp', [(i, i + 1) for i in range(step - 1, planes -...]
    unnamed x134 -> x132, local copies, waits for them, and re-layouts: 35.8 us -> 34.3 us
  transfers between devices with their start and end apart: 73 -> 78, of which waited for: 23 -> 27; matrix products, arithmetic and copies ran while one was open for 7% -> 6% of each run, Pallas kernels for 47% -> 41%
where the time goes in v4:
time: 1020 us; the launch traced here: 1010 us
  Pallas kernels  429 us (42%)
  waiting for transfers between devices  239 us (23%)
  starting transfers between devices  208 us (20%)
  other arithmetic  76.5 us (8%)
  local copies, waits for them, and re-layouts  40.2 us (4%)
  between operations  16 us (2%)
    pallas_call x4, Pallas kernels, attend_back(): pl.pallas_call(functools.partial(attend_back_kernel, heads=heads, start=s...  119 us
    pallas_call x4, Pallas kernels, ffn(): pl.pallas_call(functools.partial(ffn_kernel, cuts=cuts), in_specs=[hbm] *...  103 us
    ppermute x6, starting transfers between devices, line_scatter_move(): right = lax.ppermute(sends[0], 'dp', [(i, i + 1) for i in range(step)])  99.2 us
    ppermute x6, waiting for transfers between devices, line_scatter_move(): right = lax.ppermute(sends[0], 'dp', [(i, i + 1) for i in range(step)])  60.4 us
    pallas_call x3, Pallas kernels, attend(): pl.pallas_call(functools.partial(attend_kernel, heads=heads, start=start,...  53.2 us
    ppermute x13, waiting for transfers between devices, send_second(): return lax.ppermute(x, 'sp', SECOND)  45 us
    unnamed x132, local copies, waits for them, and re-layouts  34.3 us
    pallas_call x1, Pallas kernels, grad_gu(): pl.pallas_call(functools.partial(grad_gu_kernel, count=count), grid_spec=...  34.3 us
  transfers between devices with their start and end apart: 78, of which 27 were waited for; matrix products, arithmetic and copies ran while one was open for 6% of the time, Pallas kernels for 41%

profile of v4, /device:TPU:0, one launch (start us, length us, event | category | flops | bytes accessed | tf_op | source)
XLA Modules:
  0.0 1007.7 jit_solution(1541061569623455600)
XLA Ops:
  27.8 12.1 %collective-permute-done.3.refs_1_.refs_9_ = bf16[256,2560]{1,0:T(8,128)(2,1)S(1)} collective-permute-done((bf16[256,2560]{1,0:T(8,128)(2,1)S(1)}, bf16[256,2560]{1,0:T(8,128)(2,1)S(1)}, u32[]{:S(2)}, u32[]{:S(2)}) %collective-permute-start.3) | collective-permute-done | bytes 1310752 | tf_op jit(solution)/shard_map/ppermute | solution.py:347
  42.5 7.5 fusion.20
  61.3 14.0 %collective-permute-done.7.refs_3_.refs_11_ = bf16[256,2560]{1,0:T(8,128)(2,1)S(1)} collective-permute-done((bf16[256,2560]{1,0:T(8,128)(2,1)S(1)}, bf16[256,2560]{1,0:T(8,128)(2,1)S(1)}, u32[]{:S(2)}, u32[]{:S(2)}) %collective-permute-start.7) | collective-permute-done | bytes 1310752 | tf_op jit(solution)/shard_map/ppermute | solution.py:351
  88.9 18.3 %project.1 = (bf16[8,512,384]{2,1,0:T(8,128)(2,1)}, bf16[512,2048]{1,0:T(8,128)(2,1)}, f32[512,1]{1,0:T(8,128)S(1)}) custom-call(s32[8]{0:T(128)S(1)} %stack.59.place_ref, bf16[512,2048]{1,0:T(8,128)(2,1)} %bitcast.145, f32[1,2048]{1,0:T(1,128)S(1)} %get-tuple-element.570.gain_ref, f32[512,128]{1,0:T(8,128)S(1)} %pad_maximum_fusion.4.cos_ref, ...), custom_call_target="tpu_custom_call" | custom-call | flops 1 | bytes 1 | tf_op jit(solution)/shard_map/project/pallas_call | solution.py:761
  107.9 5.9 collective-permute-done.10.refs_1_
  119.5 8.2 maximum_select_fusion.refs_3_
  127.7 27.8 %all-to-all-done = bf16[8,512,384]{2,1,0:T(8,128)(2,1)S(1)} async-done(((bf16[8,512,384]{2,1,0:T(8,128)(2,1)}), bf16[8,512,384]{2,1,0:T(8,128)(2,1)S(1)}, u32[]{:S(2)}, u32[]{:S(2)}) %all-to-all-start) | async-done | bytes 3145760 | tf_op jit(solution)/shard_map/all_to_all | solution.py:1329
  156.6 29.7 %attend.3 = (f32[4096,256]{1,0:T(8,128)}, bf16[8,512,256]{2,1,0:T(8,128)(2,1)S(1)}, f32[8,4,512]{2,1,0:T(4,128)S(1)}) custom-call(s32[1]{0:T(128)} %bitcast.14.zeros_ref, bf16[4096,384]{1,0:T(8,128)(2,1)S(1)} %bitcast.119, bf16[4096,384]{1,0:T(8,128)(2,1)S(1)} %bitcast.120), custom_call_target="tpu_custom_call" | custom-call | flops 1 | bytes 1 | tf_op jit(solution)/shard_map/attend/pallas_call | solution.py:1081
  193.1 16.2 %attend.4 = (f32[4096,256]{1,0:T(8,128)}, bf16[8,512,256]{2,1,0:T(8,128)(2,1)S(1)}, f32[8,4,512]{2,1,0:T(4,128)S(1)}) custom-call(s32[1]{0:T(128)} %bitcast.14.zeros_ref, bf16[4096,384]{1,0:T(8,128)(2,1)S(1)} %bitcast.121, bf16[4096,384]{1,0:T(8,128)(2,1)S(1)} %bitcast.122, ...), custom_call_target="tpu_custom_call", output_to_operand_aliasing={{0}: (3, {}), {1}: (4, {}), {2}: (5, {})} | custom-call | flops 1 | bytes 1 | tf_op jit(solution)/shard_map/attend/pallas_call | solution.py:1081
  210.6 17.7 %collective-permute-done.14.refs_3_ = bf16[256,2048]{1,0:T(8,128)(2,1)S(1)} collective-permute-done((bf16[256,2048]{1,0:T(8,128)(2,1)}, bf16[256,2048]{1,0:T(8,128)(2,1)S(1)}, u32[]{:S(2)}, u32[]{:S(2)}) %collective-permute-start.14) | collective-permute-done | bytes 1048608 | tf_op jit(solution)/shard_map/ppermute | solution.py:351
  233.2 7.2 attend.5
  255.1 6.1 join.1
  264.0 15.4 %all-to-all-done.2.attn_ref.keep_ref.give_ref = bf16[8,512,256]{2,1,0:T(8,128)(2,1)S(1)} async-done(((bf16[8,512,256]{2,1,0:T(8,128)(2,1)}), bf16[8,512,256]{2,1,0:T(8,128)(2,1)S(1)}, u32[]{:S(2)}, u32[]{:S(2)}) %all-to-all-start.2) | async-done | bytes 2097184 | tf_op jit(solution)/shard_map/all_to_all | solution.py:1347
  280.7 11.7 %out_proj.1 = (f32[512,2048]{1,0:T(8,128)}, f32[512,1]{1,0:T(8,128)}, bf16[512,2048]{1,0:T(8,128)(2,1)}) custom-call(s32[8]{0:T(128)} %copy-done.27, bf16[8,512,256]{2,1,0:T(8,128)(2,1)} %copy-done.1, bf16[512,2048]{1,0:T(8,128)(2,1)} %bitcast.146, f32[1,2048]{1,0:T(1,128)} %get-tuple-element.569.gain_ref, bf16[256,2048]{1,0:T(8,128)(2,1)} %refs_0_.1, ...), custom_call_target="tpu_custom_call" | custom-call | flops 1 | bytes 1 | tf_op jit(solution)/shard_map/out_proj/pallas_call | solution.py:815
  293.5 25.7 %ffn.4 = (bf16[512,1408]{1,0:T(8,128)(2,1)}, bf16[512,1408]{1,0:T(8,128)(2,1)}, bf16[512,1408]{1,0:T(8,128)(2,1)}, bf16[512,2048]{1,0:T(8,128)(2,1)}, bf16[512,2048]{1,0:T(8,128)(2,1)}) custom-call(bf16[512,2048]{1,0:T(8,128)(2,1)} %get-tuple-element.389.refs_0_.refs_4_, bf16[512,2048]{1,0:T(8,128)(2,1)} %multiply_bitcast_fusion.refs_1_.refs_4_.dy_ref, ...), custom_call_target="tpu_custom_call" | custom-call | flops 1 | bytes 1 | tf_op jit(solution)/shard_map/ffn/pallas_call | solution.py:622
  320.7 25.9 %ffn.5 = (bf16[512,1408]{1,0:T(8,128)(2,1)}, bf16[512,1408]{1,0:T(8,128)(2,1)}, bf16[512,1408]{1,0:T(8,128)(2,1)}, bf16[512,2048]{1,0:T(8,128)(2,1)}, bf16[512,2048]{1,0:T(8,128)(2,1)}) custom-call(bf16[512,2048]{1,0:T(8,128)(2,1)} %copy-done.33, bf16[512,2048]{1,0:T(8,128)(2,1)} %copy-done.42, bf16[2,2048,1408]{2,1,0:T(8,128)(2,1)} %bitcast.137, ...), custom_call_target="tpu_custom_call" | custom-call | flops 1 | bytes 1 | tf_op jit(solution)/shard_map/ffn/pallas_call | solution.py:622
  348.0 25.8 %ffn.6 = (bf16[512,1408]{1,0:T(8,128)(2,1)}, bf16[512,1408]{1,0:T(8,128)(2,1)}, bf16[512,1408]{1,0:T(8,128)(2,1)}, bf16[512,2048]{1,0:T(8,128)(2,1)}, bf16[512,2048]{1,0:T(8,128)(2,1)}) custom-call(bf16[512,2048]{1,0:T(8,128)(2,1)} %collective-permute-done.23.refs_0_.refs_2_.refs_6_, bf16[512,2048]{1,0:T(8,128)(2,1)} %copy-done.43, ...), custom_call_target="tpu_custom_call" | custom-call | flops 1 | bytes 1 | tf_op jit(solution)/shard_map/ffn/pallas_call | solution.py:622
  375.1 25.7 %ffn.7 = (bf16[512,1408]{1,0:T(8,128)(2,1)}, bf16[512,1408]{1,0:T(8,128)(2,1)}, bf16[512,1408]{1,0:T(8,128)(2,1)}, bf16[512,2048]{1,0:T(8,128)(2,1)}, bf16[512,2048]{1,0:T(8,128)(2,1)}) custom-call(bf16[512,2048]{1,0:T(8,128)(2,1)} %copy-done.34, bf16[512,2048]{1,0:T(8,128)(2,1)} %collective-permute-done.17.refs_1_.refs_7_, ...), custom_call_target="tpu_custom_call" | custom-call | flops 1 | bytes 1 | tf_op jit(solution)/shard_map/ffn/pallas_call | solution.py:622
  403.0 17.9 %grad_dn.1 = (bf16[704,2048]{1,0:T(8,128)(2,1)}, bf16[704,2048]{1,0:T(8,128)(2,1)}) custom-call(s32[1]{0:T(128)} %bitcast.20.core_ref, bf16[512,1408]{1,0:T(8,128)(2,1)} %get-tuple-element.379.refs_0_, bf16[512,1408]{1,0:T(8,128)(2,1)} %get-tuple-element.380.refs_1_, bf16[512,1408]{1,0:T(8,128)(2,1)} %get-tuple-element.381.refs_2_, ...), custom_call_target="tpu_custom_call" | custom-call | flops 1 | bytes 1 | tf_op jit(solution)/shard_map/grad_dn/pallas_call | solution.py:985
  420.9 7.5 collective-permute-done.26
  431.5 34.3 %grad_gu.1 = (bf16[4,4,64,2816]{3,2,1,0:T(8,128)(2,1)}, bf16[4,4,64,2816]{3,2,1,0:T(8,128)(2,1)}) custom-call(s32[1]{0:T(128)} %bitcast.20.core_ref, bf16[512,2048]{1,0:T(8,128)(2,1)} %get-tuple-element.389.refs_0_.refs_4_, bf16[512,2048]{1,0:T(8,128)(2,1)} %copy-done.33, bf16[512,2048]{1,0:T(8,128)(2,1)} %collective-permute-done.23.refs_0_.refs_2_.refs_6_, ...), custom_call_target="tpu_custom_call" | custom-call | flops 1 | bytes 1 | tf_op jit(solution)/shard_map/grad_gu/pallas_call | solution.py:663
  472.4 15.1 %resid_back.1 = (f32[512,2048]{1,0:T(8,128)}, bf16[512,2048]{1,0:T(8,128)(2,1)}, bf16[8,512,256]{2,1,0:T(8,128)(2,1)}) custom-call(s32[8]{0:T(128)} %copy-done.27, bf16[512,2048]{1,0:T(8,128)(2,1)} %get-tuple-element.351.db_ref, bf16[512,2048]{1,0:T(8,128)(2,1)} %copy-done.56, bf16[512,2048]{1,0:T(8,128)(2,1)} %collective-permute-done.27.passed_ref, ...), custom_call_target="tpu_custom_call" | custom-call | flops 1 | bytes 1 | tf_op jit(solution)/shard_map/resid_back/pallas_call | solution.py:861
  487.8 6.9 add_convert_fusion
  500.8 6.1 grad_wo.1
  507.0 18.9 %all-to-all-done.3 = bf16[8,512,256]{2,1,0:T(8,128)(2,1)} async-done(((bf16[8,512,256]{2,1,0:T(8,128)(2,1)}), bf16[8,512,256]{2,1,0:T(8,128)(2,1)}, u32[]{:S(2)}, u32[]{:S(2)}) %all-to-all-start.3) | async-done | bytes 2097184 | tf_op jit(solution)/shard_map/all_to_all | solution.py:1395
  534.8 29.0 %attend_back.4 = (bf16[8,512,384]{2,1,0:T(8,128)(2,1)}, f32[256,4096]{1,0:T(8,128)}, f32[8,4,512]{2,1,0:T(4,128)}) custom-call(s32[1]{0:T(128)} %bitcast.14.zeros_ref, bf16[4096,384]{1,0:T(8,128)(2,1)} %bitcast.125, bf16[4096,384]{1,0:T(8,128)(2,1)} %bitcast.126, bf16[4096,256]{1,0:T(8,128)(2,1)} %bitcast.26.do_ref, f32[8,4,512]{2,1,0:T(4,128)} %copy-done.19, ...), custom_call_target="tpu_custom_call" | custom-call | flops 1 | bytes 1 | tf_op jit(solution)/shard_map/attend_back/pallas_call | solution.py:1222
  572.1 26.8 %collective-permute-start.39 = (bf16[176,2048]{1,0:T(8,128)(2,1)}, bf16[176,2048]{1,0:T(8,128)(2,1)S(1)}, u32[]{:S(2)}, u32[]{:S(2)}) collective-permute-start(bf16[176,2048]{1,0:T(8,128)(2,1)} %get-tuple-element.439), channel_id=1, source_target_pairs={{0,8},{8,16},{16,24},{1,9},{9,17},{17,25},{2,10},{10,18},{18,26},{... | collective-permute-start | bytes 2162696 | tf_op jit(solution)/shard_map/ppermute | solution.py:407
  600.2 24.2 %attend_back.5 = (bf16[8,512,384]{2,1,0:T(8,128)(2,1)}, f32[256,4096]{1,0:T(8,128)}, f32[8,4,512]{2,1,0:T(4,128)}) custom-call(s32[1]{0:T(128)} %bitcast.14.zeros_ref, bf16[4096,384]{1,0:T(8,128)(2,1)} %bitcast.127, bf16[4096,384]{1,0:T(8,128)(2,1)} %bitcast.128, bf16[4096,256]{1,0:T(8,128)(2,1)} %bitcast.26.do_ref, ...), custom_call_target="tpu_custom_call", output_to_operand_aliasing={{0}: (9, {})} | custom-call | flops 1 | bytes 1 | tf_op jit(solution)/shard_map/attend_back/pallas_call | solution.py:1222
  634.5 5.3 collective-permute-start.42
  645.6 20.9 %attend_back.6 = (bf16[8,512,384]{2,1,0:T(8,128)(2,1)}, f32[256,4096]{1,0:T(8,128)}, f32[8,4,512]{2,1,0:T(4,128)}) custom-call(s32[1]{0:T(128)} %bitcast.14.zeros_ref, bf16[4096,384]{1,0:T(8,128)(2,1)} %bitcast.129, bf16[4096,384]{1,0:T(8,128)(2,1)} %bitcast.130, bf16[4096,256]{1,0:T(8,128)(2,1)} %bitcast.26.do_ref, ...), custom_call_target="tpu_custom_call", output_to_operand_aliasing={{0}: (9, {})} | custom-call | flops 1 | bytes 1 | tf_op jit(solution)/shard_map/attend_back/pallas_call | solution.py:1222
  673.6 45.4 %attend_back.7 = (bf16[8,512,384]{2,1,0:T(8,128)(2,1)}, f32[256,4096]{1,0:T(8,128)}, f32[8,4,512]{2,1,0:T(4,128)}) custom-call(s32[1]{0:T(128)} %bitcast.14.zeros_ref, bf16[4096,384]{1,0:T(8,128)(2,1)} %bitcast.131, bf16[4096,384]{1,0:T(8,128)(2,1)} %bitcast.132, bf16[4096,256]{1,0:T(8,128)(2,1)} %bitcast.26.do_ref, ...), custom_call_target="tpu_custom_call", output_to_operand_aliasing={{0}: (9, {})} | custom-call | flops 1 | bytes 1 | tf_op jit(solution)/shard_map/attend_back/pallas_call | solution.py:1222
  726.0 11.6 %collective-permute-done.50 = bf16[256,2048]{1,0:T(8,128)(2,1)S(1)} collective-permute-done((bf16[256,2048]{1,0:T(8,128)(2,1)}, bf16[256,2048]{1,0:T(8,128)(2,1)S(1)}, u32[]{:S(2)}, u32[]{:S(2)}) %collective-permute-start.50) | collective-permute-done | bytes 1048608 | tf_op jit(solution)/shard_map/ppermute | solution.py:351
  740.2 13.3 %grad_qkv.1 = bf16[4,64,3072]{2,1,0:T(8,128)(2,1)S(1)} custom-call(s32[8]{0:T(128)S(1)} %copy-done.28, bf16[512,2048]{1,0:T(8,128)(2,1)S(1)} %copy-done.21, bf16[512,2048]{1,0:T(8,128)(2,1)} %collective-permute-done.32.refs_1_, bf16[512,2048]{1,0:T(8,128)(2,1)} %collective-permute-done.36.refs_2_, bf16[512,2048]{1,0:T(8,128)(2,1)} %collective-permute-done.46.refs_3_, ...), custom_call_target="tpu_custom_call" | custom-call | flops 1 | bytes 1 | tf_op jit(solution)/shard_map/grad_qkv/pallas_call | solution.py:697
  754.7 18.9 %collective-permute-start.51 = (bf16[64,5120]{1,0:T(8,128)(2,1)}, bf16[64,5120]{1,0:T(8,128)(2,1)}, u32[]{:S(2)}, u32[]{:S(2)}) collective-permute-start(bf16[64,5120]{1,0:T(8,128)(2,1)} %get-tuple-element.490), channel_id=1, source_target_pairs={{0,8},{1,9},{2,10},{3,11},{4,12},{5,13},{6,14},{7,15}} | collective-permute-start | bytes 1966088 | tf_op jit(solution)/shard_map/ppermute | solution.py:407
  775.2 11.6 %collective-permute-done.51 = bf16[64,5120]{1,0:T(8,128)(2,1)} collective-permute-done((bf16[64,5120]{1,0:T(8,128)(2,1)}, bf16[64,5120]{1,0:T(8,128)(2,1)}, u32[]{:S(2)}, u32[]{:S(2)}) %collective-permute-start.51) | collective-permute-done | bytes 655392 | tf_op jit(solution)/shard_map/ppermute | solution.py:407
  789.6 5.3 collective-permute-start.55
  803.1 19.5 %collective-permute-done.55 = bf16[64,5120]{1,0:T(8,128)(2,1)} collective-permute-done((bf16[64,5120]{1,0:T(8,128)(2,1)}, bf16[64,5120]{1,0:T(8,128)(2,1)}, u32[]{:S(2)}, u32[]{:S(2)}) %collective-permute-start.55) | collective-permute-done | bytes 655392 | tf_op jit(solution)/shard_map/ppermute | solution.py:407
  824.4 40.3 %collective-permute-start.57 = (bf16[64,5120]{1,0:T(8,128)(2,1)S(1)}, bf16[64,5120]{1,0:T(8,128)(2,1)S(1)}, u32[]{:S(2)}, u32[]{:S(2)}) collective-permute-start(bf16[64,5120]{1,0:T(8,128)(2,1)S(1)} %get-tuple-element.503), channel_id=1, source_target_pairs={{0,8},{8,16},{16,24},{1,9},{9,17},{17,25},{2,10},{10,18},{18,26},{... | collective-permute-start | bytes 1966088 | tf_op jit(solution)/shard_map/ppermute | solution.py:407
  867.7 23.2 %collective-permute-done.57 = bf16[64,5120]{1,0:T(8,128)(2,1)S(1)} collective-permute-done((bf16[64,5120]{1,0:T(8,128)(2,1)S(1)}, bf16[64,5120]{1,0:T(8,128)(2,1)S(1)}, u32[]{:S(2)}, u32[]{:S(2)}) %collective-permute-start.57) | collective-permute-done | bytes 655392 | tf_op jit(solution)/shard_map/ppermute | solution.py:407
  890.9 9.5 collective-permute-done.58
  905.8 14.6 %in_back.1 = bf16[512,2048]{1,0:T(8,128)(2,1)} custom-call(s32[8]{0:T(128)} %copy-done.27, bf16[8,512,384]{2,1,0:T(8,128)(2,1)} %all-to-all-done.5.back_ref, bf16[512,2048]{1,0:T(8,128)(2,1)} %bitcast.147, f32[512,1]{1,0:T(8,128)} %copy-done.25, f32[1,2048]{1,0:T(1,128)} %copy-done.26, f32[512,2048]{1,0:T(8,128)} %get-tuple-element.511.d_resid_ref, ...), custom_call_target="tpu_custom_call" | custom-call | flops 1 | bytes 1 | tf_op jit(solution)/shard_map/in_back/pallas_call | solution.py:914
  926.4 15.8 %collective-permute-start.61 = (bf16[64,5120]{1,0:T(8,128)(2,1)S(1)}, bf16[64,5120]{1,0:T(8,128)(2,1)}, u32[]{:S(2)}, u32[]{:S(2)}) collective-permute-start(bf16[64,5120]{1,0:T(8,128)(2,1)S(1)} %pad_maximum_fusion.3.refs_0_), channel_id=1, source_target_pairs={{0,8},{8,16},{16,24},{1,9},{9,17},{17,25},{2,10},{10,18},{18,26},{... | collective-permute-start | bytes 1966088 | tf_op jit(solution)/shard_map/ppermute | solution.py:419
  943.5 5.0 spread_rows.1
  948.4 6.8 collective-permute-done.61.refs_1_
  955.2 5.1 collective-permute-done.62.refs_4_
  967.9 6.5 spread.1
  980.6 5.1 fusion
  985.7 9.8 collective-permute-done.66.refs_6_
  (327 shorter events, 210.5 us)
Async XLA Ops:
  79.5 34.3 %all-to-all-start.1 = ((bf16[4,64,2816]{2,1,0:T(8,128)(2,1)}), bf16[4,64,2816]{2,1,0:T(8,128)(2,1)}, u32[]{:S(2)}, u32[]{:S(2)}) async-start(bf16[4,64,2816]{2,1,0:T(8,128)(2,1)} %pad_maximum_fusion.2), calls=%async_computation.1 | async-start | bytes 2883584 | tf_op jit(solution)/shard_map/all_to_all | solution.py:1320
  83.8 146.1 %all-gather.5.cloned.1.call-start = ((), (), s32[]{:S(2)}) async-start(), calls=%async_computation.9 | async-start | bytes 7208960 | tf_op jit(solution)/shard_map/all_gather | solution.py:1324
  84.1 29.7 %collective-permute-start.10 = (bf16[256,2048]{1,0:T(8,128)(2,1)}, bf16[256,2048]{1,0:T(8,128)(2,1)}, u32[]{:S(2)}, u32[]{:S(2)}) collective-permute-start(bf16[256,2048]{1,0:T(8,128)(2,1)} %refs_0_.1), channel_id=1, source_target_pairs={{0,2},{1,5},{2,0},{3,7},{4,6},{5,1},{6,4},{7,3},{8,10},{9,13},{10,... | collective-permute-start | bytes 3145736 | tf_op jit(solution)/shard_map/ppermute | solution.py:347
  114.0 41.5 %all-to-all-start = ((bf16[8,512,384]{2,1,0:T(8,128)(2,1)}), bf16[8,512,384]{2,1,0:T(8,128)(2,1)S(1)}, u32[]{:S(2)}, u32[]{:S(2)}) async-start(bf16[8,512,384]{2,1,0:T(8,128)(2,1)} %get-tuple-element.300), calls=%async_computation | async-start | bytes 6291456 | tf_op jit(solution)/shard_map/all_to_all | solution.py:1329
  155.5 35.5 %collective-permute-start.13 = (bf16[512,2048]{1,0:T(8,128)(2,1)}, bf16[512,2048]{1,0:T(8,128)(2,1)S(1)}, u32[]{:S(2)}, u32[]{:S(2)}) collective-permute-start(bf16[512,2048]{1,0:T(8,128)(2,1)} %multiply_bitcast_fusion.refs_1_.refs_4_.dy_ref), channel_id=1, source_target_pairs={{0,2},{1,5},{2,0},{3,7},{4,6},{5,1},{6,4},{7,3},{8,10},{9,13},{10,... | collective-permute-start | bytes 6291464 | tf_op jit(solution)/shard_map/ppermute | solution.py:347
  156.0 30.4 %collective-permute-start.12 = (bf16[256,2048]{1,0:T(8,128)(2,1)}, bf16[256,2048]{1,0:T(8,128)(2,1)S(1)}, u32[]{:S(2)}, u32[]{:S(2)}) collective-permute-start(bf16[256,2048]{1,0:T(8,128)(2,1)} %refs_0_.1), channel_id=1, source_target_pairs={{0,4},{1,3},{2,6},{3,1},{4,0},{5,7},{6,2},{7,5},{8,12},{9,11},{10,... | collective-permute-start | bytes 3145736 | tf_op jit(solution)/shard_map/ppermute | solution.py:351
  191.0 37.3 %collective-permute-start.15 = (bf16[512,2048]{1,0:T(8,128)(2,1)S(1)}, bf16[512,2048]{1,0:T(8,128)(2,1)S(1)}, u32[]{:S(2)}, u32[]{:S(2)}) collective-permute-start(bf16[512,2048]{1,0:T(8,128)(2,1)S(1)} %copy-done.29), channel_id=1, source_target_pairs={{0,4},{1,3},{2,6},{3,1},{4,0},{5,7},{6,2},{7,5},{8,12},{9,11},{10,... | collective-permute-start | bytes 6291464 | tf_op jit(solution)/shard_map/ppermute | solution.py:351
  192.7 35.6 %collective-permute-start.14 = (bf16[256,2048]{1,0:T(8,128)(2,1)}, bf16[256,2048]{1,0:T(8,128)(2,1)S(1)}, u32[]{:S(2)}, u32[]{:S(2)}) collective-permute-start(bf16[256,2048]{1,0:T(8,128)(2,1)} %collective-permute-done.10.refs_1_), channel_id=1, source_target_pairs={{0,4},{1,3},{2,6},{3,1},{4,0},{5,7},{6,2},{7,5},{8,12},{9,11},{10,... | collective-permute-start | bytes 3145736 | tf_op jit(solution)/shard_map/ppermute | solution.py:351
  230.0 34.0 %collective-permute-start.17 = (bf16[512,2048]{1,0:T(8,128)(2,1)}, bf16[512,2048]{1,0:T(8,128)(2,1)}, u32[]{:S(2)}, u32[]{:S(2)}) collective-permute-start(bf16[512,2048]{1,0:T(8,128)(2,1)} %copy-done.42), channel_id=1, source_target_pairs={{0,4},{1,3},{2,6},{3,1},{4,0},{5,7},{6,2},{7,5},{8,12},{9,11},{10,... | collective-permute-start | bytes 6291464 | tf_op jit(solution)/shard_map/ppermute | solution.py:351
  244.9 34.4 %all-to-all-start.2 = ((bf16[8,512,256]{2,1,0:T(8,128)(2,1)}), bf16[8,512,256]{2,1,0:T(8,128)(2,1)S(1)}, u32[]{:S(2)}, u32[]{:S(2)}) async-start(bf16[8,512,256]{2,1,0:T(8,128)(2,1)} %copy-done.6), calls=%async_computation.2 | async-start | bytes 4194304 | tf_op jit(solution)/shard_map/all_to_all | solution.py:1347
  248.7 379.3 %reduce-scatter.2.cloned.1.call-start = ((), (), s32[]{:S(2)}) async-start(), calls=%async_computation.8 | async-start | bytes 7208960 | tf_op jit(solution)/shard_map/reduce_scatter | solution.py:1391
  292.4 26.9 %collective-permute-start.22 = (bf16[512,2048]{1,0:T(8,128)(2,1)}, bf16[512,2048]{1,0:T(8,128)(2,1)S(1)}, u32[]{:S(2)}, u32[]{:S(2)}) collective-permute-start(bf16[512,2048]{1,0:T(8,128)(2,1)} %get-tuple-element.389.refs_0_.refs_4_), channel_id=1, source_target_pairs={{0,2},{1,5},{2,0},{3,7},{4,6},{5,1},{6,4},{7,3},{8,10},{9,13},{10,... | collective-permute-start | bytes 6291464 | tf_op jit(solution)/shard_map/ppermute | solution.py:347
  319.3 27.4 %collective-permute-start.23 = (bf16[512,2048]{1,0:T(8,128)(2,1)S(1)}, bf16[512,2048]{1,0:T(8,128)(2,1)}, u32[]{:S(2)}, u32[]{:S(2)}) collective-permute-start(bf16[512,2048]{1,0:T(8,128)(2,1)S(1)} %copy-done.32), channel_id=1, source_target_pairs={{0,4},{1,3},{2,6},{3,1},{4,0},{5,7},{6,2},{7,5},{8,12},{9,11},{10,... | collective-permute-start | bytes 6291464 | tf_op jit(solution)/shard_map/ppermute | solution.py:351
  346.7 27.1 %collective-permute-start.24 = (bf16[512,2048]{1,0:T(8,128)(2,1)}, bf16[512,2048]{1,0:T(8,128)(2,1)S(1)}, u32[]{:S(2)}, u32[]{:S(2)}) collective-permute-start(bf16[512,2048]{1,0:T(8,128)(2,1)} %copy-done.33), channel_id=1, source_target_pairs={{0,4},{1,3},{2,6},{3,1},{4,0},{5,7},{6,2},{7,5},{8,12},{9,11},{10,... | collective-permute-start | bytes 6291464 | tf_op jit(solution)/shard_map/ppermute | solution.py:351
  373.8 27.0 %collective-permute-start.25 = (bf16[512,2048]{1,0:T(8,128)(2,1)}, bf16[512,2048]{1,0:T(8,128)(2,1)S(1)}, u32[]{:S(2)}, u32[]{:S(2)}) collective-permute-start(bf16[512,2048]{1,0:T(8,128)(2,1)} %get-tuple-element.368), channel_id=1, source_target_pairs={{0,2},{1,5},{2,0},{3,7},{4,6},{5,1},{6,4},{7,3},{8,10},{9,13},{10,... | collective-permute-start | bytes 6291464 | tf_op jit(solution)/shard_map/ppermute | solution.py:347
  430.7 35.1 %collective-permute-start.28 = (bf16[704,2048]{1,0:T(8,128)(2,1)}, bf16[704,2048]{1,0:T(8,128)(2,1)S(1)}, u32[]{:S(2)}, u32[]{:S(2)}) collective-permute-start(bf16[704,2048]{1,0:T(8,128)(2,1)} %get-tuple-element.388), channel_id=1, source_target_pairs={{0,1},{1,0},{2,3},{3,2},{4,5},{5,4},{6,7},{7,6},{8,9},{9,8},{10,11... | collective-permute-start | bytes 8650760 | tf_op jit(solution)/shard_map/ppermute | solution.py:355
  430.7 35.1 %collective-permute-start.27 = (bf16[512,2048]{1,0:T(8,128)(2,1)}, bf16[512,2048]{1,0:T(8,128)(2,1)}, u32[]{:S(2)}, u32[]{:S(2)}) collective-permute-start(bf16[512,2048]{1,0:T(8,128)(2,1)} %add_convert_fusion.3), channel_id=1, source_target_pairs={{0,4},{1,3},{2,6},{3,1},{4,0},{5,7},{6,2},{7,5},{8,12},{9,11},{10,... | collective-permute-start | bytes 6291464 | tf_op jit(solution)/shard_map/ppermute | solution.py:351
  494.7 31.2 %all-to-all-start.3 = ((bf16[8,512,256]{2,1,0:T(8,128)(2,1)}), bf16[8,512,256]{2,1,0:T(8,128)(2,1)}, u32[]{:S(2)}, u32[]{:S(2)}) async-start(bf16[8,512,256]{2,1,0:T(8,128)(2,1)} %get-tuple-element.412), calls=%async_computation.3 | async-start | bytes 4194304 | tf_op jit(solution)/shard_map/all_to_all | solution.py:1395
  525.9 40.2 %collective-permute-start.33 = (bf16[4,256,2048]{2,1,0:T(8,128)(2,1)}, bf16[4,256,2048]{2,1,0:T(8,128)(2,1)}, u32[]{:S(2)}, u32[]{:S(2)}) collective-permute-start(bf16[4,256,2048]{2,1,0:T(8,128)(2,1)} %get-tuple-element.419), channel_id=1, source_target_pairs={{0,1},{1,0},{2,3},{3,2},{4,5},{5,4},{6,7},{7,6},{8,9},{9,8},{10,11... | collective-permute-start | bytes 12582920 | tf_op jit(solution)/shard_map/ppermute | solution.py:355
  525.9 40.2 %collective-permute-start.32 = (bf16[512,2048]{1,0:T(8,128)(2,1)}, bf16[512,2048]{1,0:T(8,128)(2,1)}, u32[]{:S(2)}, u32[]{:S(2)}) collective-permute-start(bf16[512,2048]{1,0:T(8,128)(2,1)} %get-tuple-element.434.refs_0_), channel_id=1, source_target_pairs={{0,2},{1,5},{2,0},{3,7},{4,6},{5,1},{6,4},{7,3},{8,10},{9,13},{10,... | collective-permute-start | bytes 6291464 | tf_op jit(solution)/shard_map/ppermute | solution.py:347
  529.8 36.3 %collective-permute-start.34 = (bf16[176,2048]{1,0:T(8,128)(2,1)}, bf16[176,2048]{1,0:T(8,128)(2,1)S(1)}, u32[]{:S(2)}, u32[]{:S(2)}) collective-permute-start(bf16[176,2048]{1,0:T(8,128)(2,1)} %get-tuple-element.545), channel_id=1, source_target_pairs={{0,8},{8,16},{1,9},{9,17},{2,10},{10,18},{3,11},{11,19},{4,12},{12... | collective-permute-start | bytes 2162696 | tf_op jit(solution)/shard_map/ppermute | solution.py:407
  534.1 32.0 %collective-permute-start.35 = (bf16[176,2048]{1,0:T(8,128)(2,1)S(1)}, bf16[176,2048]{1,0:T(8,128)(2,1)S(1)}, u32[]{:S(2)}, u32[]{:S(2)}) collective-permute-start(bf16[176,2048]{1,0:T(8,128)(2,1)S(1)} %get-tuple-element.544), channel_id=1, source_target_pairs={{24,16},{16,8},{25,17},{17,9},{26,18},{18,10},{27,19},{19,11},{28,... | collective-permute-start | bytes 2162696 | tf_op jit(solution)/shard_map/ppermute | solution.py:408
  570.7 57.2 %collective-permute-start.36 = (bf16[512,2048]{1,0:T(8,128)(2,1)S(1)}, bf16[512,2048]{1,0:T(8,128)(2,1)}, u32[]{:S(2)}, u32[]{:S(2)}) collective-permute-start(bf16[512,2048]{1,0:T(8,128)(2,1)S(1)} %copy-done.20), channel_id=1, source_target_pairs={{0,4},{1,3},{2,6},{3,1},{4,0},{5,7},{6,2},{7,5},{8,12},{9,11},{10,... | collective-permute-start | bytes 6291464 | tf_op jit(solution)/shard_map/ppermute | solution.py:351
  571.6 56.4 %collective-permute-start.37 = (bf16[512,2048]{1,0:T(8,128)(2,1)S(1)}, bf16[512,2048]{1,0:T(8,128)(2,1)}, u32[]{:S(2)}, u32[]{:S(2)}) collective-permute-start(bf16[512,2048]{1,0:T(8,128)(2,1)S(1)} %copy-done.20), channel_id=1, source_target_pairs={{0,1},{1,0},{2,3},{3,2},{4,5},{5,4},{6,7},{7,6},{8,9},{9,8},{10,11... | collective-permute-start | bytes 6291464 | tf_op jit(solution)/shard_map/ppermute | solution.py:355
  571.6 56.4 %collective-permute-start.38 = (bf16[512,2048]{1,0:T(8,128)(2,1)}, bf16[512,2048]{1,0:T(8,128)(2,1)}, u32[]{:S(2)}, u32[]{:S(2)}) collective-permute-start(bf16[512,2048]{1,0:T(8,128)(2,1)} %collective-permute-done.32.refs_1_), channel_id=1, source_target_pairs={{0,1},{1,0},{2,3},{3,2},{4,5},{5,4},{6,7},{7,6},{8,9},{9,8},{10,11... | collective-permute-start | bytes 6291464 | tf_op jit(solution)/shard_map/ppermute | solution.py:355
  572.1 55.8 %collective-permute-start.39 = (bf16[176,2048]{1,0:T(8,128)(2,1)}, bf16[176,2048]{1,0:T(8,128)(2,1)S(1)}, u32[]{:S(2)}, u32[]{:S(2)}) collective-permute-start(bf16[176,2048]{1,0:T(8,128)(2,1)} %get-tuple-element.439), channel_id=1, source_target_pairs={{0,8},{8,16},{16,24},{1,9},{9,17},{17,25},{2,10},{10,18},{18,26},{... | collective-permute-start | bytes 2162696 | tf_op jit(solution)/shard_map/ppermute | solution.py:407
  598.9 29.1 %collective-permute-start.40 = (bf16[176,2048]{1,0:T(8,128)(2,1)S(1)}, bf16[176,2048]{1,0:T(8,128)(2,1)}, u32[]{:S(2)}, u32[]{:S(2)}) collective-permute-start(bf16[176,2048]{1,0:T(8,128)(2,1)S(1)} %get-tuple-element.440), channel_id=1, source_target_pairs={{24,16},{16,8},{8,0},{25,17},{17,9},{9,1},{26,18},{18,10},{10,2},{... | collective-permute-start | bytes 2162696 | tf_op jit(solution)/shard_map/ppermute | solution.py:408
  630.0 36.6 %collective-permute-start.41 = (bf16[512,2048]{1,0:T(8,128)(2,1)}, bf16[512,2048]{1,0:T(8,128)(2,1)}, u32[]{:S(2)}, u32[]{:S(2)}) collective-permute-start(bf16[512,2048]{1,0:T(8,128)(2,1)} %collective-permute-done.36.refs_2_), channel_id=1, source_target_pairs={{0,1},{1,0},{2,3},{3,2},{4,5},{5,4},{6,7},{7,6},{8,9},{9,8},{10,11... | collective-permute-start | bytes 6291464 | tf_op jit(solution)/shard_map/ppermute | solution.py:355
  630.1 36.5 %all-to-all-start.4 = ((bf16[4,64,2816]{2,1,0:T(8,128)(2,1)}), bf16[4,64,2816]{2,1,0:T(8,128)(2,1)}, u32[]{:S(2)}, u32[]{:S(2)}) async-start(bf16[4,64,2816]{2,1,0:T(8,128)(2,1)} %bitcast.32), calls=%async_computation.5 | async-start | bytes 2883584 | tf_op jit(solution)/shard_map/all_to_all | solution.py:1426
  634.4 328.2 %all-gather.7.cloned.1.call-start = ((), (), s32[]{:S(2)}) async-start(), calls=%async_computation.10 | async-start | bytes 7208960 | tf_op jit(solution)/shard_map/all_gather | solution.py:1435
  634.5 32.0 %collective-permute-start.42 = (bf16[176,2048]{1,0:T(8,128)(2,1)S(1)}, bf16[176,2048]{1,0:T(8,128)(2,1)S(1)}, u32[]{:S(2)}, u32[]{:S(2)}) collective-permute-start(bf16[176,2048]{1,0:T(8,128)(2,1)S(1)} %fusion.5.refs_0_), channel_id=1, source_target_pairs={{0,8},{8,16},{16,24},{1,9},{9,17},{17,25},{2,10},{10,18},{18,26},{... | collective-permute-start | bytes 2162696 | tf_op jit(solution)/shard_map/ppermute | solution.py:419
  666.6 55.9 %collective-permute-start.46 = (bf16[512,2048]{1,0:T(8,128)(2,1)}, bf16[512,2048]{1,0:T(8,128)(2,1)}, u32[]{:S(2)}, u32[]{:S(2)}) collective-permute-start(bf16[512,2048]{1,0:T(8,128)(2,1)} %collective-permute-done.32.refs_1_), channel_id=1, source_target_pairs={{0,4},{1,3},{2,6},{3,1},{4,0},{5,7},{6,2},{7,5},{8,12},{9,11},{10,... | collective-permute-start | bytes 6291464 | tf_op jit(solution)/shard_map/ppermute | solution.py:351
  668.5 50.5 %collective-permute-start.45 = (bf16[256,2048]{1,0:T(8,128)(2,1)}, bf16[256,2048]{1,0:T(8,128)(2,1)}, u32[]{:S(2)}, u32[]{:S(2)}) collective-permute-start(bf16[256,2048]{1,0:T(8,128)(2,1)} %get-tuple-element.476), channel_id=1, source_target_pairs={{0,2},{1,5},{2,0},{3,7},{4,6},{5,1},{6,4},{7,3},{8,10},{9,13},{10,... | collective-permute-start | bytes 3145736 | tf_op jit(solution)/shard_map/ppermute | solution.py:347
  670.0 52.5 %collective-permute-start.44 = (bf16[256,2048]{1,0:T(8,128)(2,1)}, bf16[256,2048]{1,0:T(8,128)(2,1)}, u32[]{:S(2)}, u32[]{:S(2)}) collective-permute-start(bf16[256,2048]{1,0:T(8,128)(2,1)} %get-tuple-element.475), channel_id=1, source_target_pairs={{0,2},{1,5},{2,0},{3,7},{4,6},{5,1},{6,4},{7,3},{8,10},{9,13},{10,... | collective-permute-start | bytes 3145736 | tf_op jit(solution)/shard_map/ppermute | solution.py:347
  670.6 51.9 %collective-permute-start.47 = (bf16[176,2048]{1,0:T(8,128)(2,1)S(1)}, bf16[176,2048]{1,0:T(8,128)(2,1)}, u32[]{:S(2)}, u32[]{:S(2)}) collective-permute-start(bf16[176,2048]{1,0:T(8,128)(2,1)S(1)} %collective-permute-done.42.refs_1_), channel_id=1, source_target_pairs={{8,16},{16,24},{9,17},{17,25},{10,18},{18,26},{11,19},{19,27},{12,... | collective-permute-start | bytes 2162696 | tf_op jit(solution)/shard_map/ppermute | solution.py:419
  672.1 50.4 %collective-permute-start.48 = (bf16[176,2048]{1,0:T(8,128)(2,1)S(1)}, bf16[176,2048]{1,0:T(8,128)(2,1)}, u32[]{:S(2)}, u32[]{:S(2)}) collective-permute-start(bf16[176,2048]{1,0:T(8,128)(2,1)S(1)} %collective-permute-done.43.refs_4_), channel_id=1, source_target_pairs={{8,0},{16,8},{9,1},{17,9},{10,2},{18,10},{11,3},{19,11},{12,4},{20... | collective-permute-start | bytes 2162696 | tf_op jit(solution)/shard_map/ppermute | solution.py:420
  723.1 52.1 %collective-permute-start.53 = (bf16[176,2048]{1,0:T(8,128)(2,1)}, bf16[176,2048]{1,0:T(8,128)(2,1)}, u32[]{:S(2)}, u32[]{:S(2)}) collective-permute-start(bf16[176,2048]{1,0:T(8,128)(2,1)} %collective-permute-done.47.refs_2_), channel_id=1, source_target_pairs={{16,24},{17,25},{18,26},{19,27},{20,28},{21,29},{22,30},{23,31}} | collective-permute-start | bytes 2162696 | tf_op jit(solution)/shard_map/ppermute | solution.py:419
  724.7 50.4 %collective-permute-start.54 = (bf16[176,2048]{1,0:T(8,128)(2,1)}, bf16[176,2048]{1,0:T(8,128)(2,1)}, u32[]{:S(2)}, u32[]{:S(2)}) collective-permute-start(bf16[176,2048]{1,0:T(8,128)(2,1)} %collective-permute-done.48.refs_5_), channel_id=1, source_target_pairs={{8,0},{9,1},{10,2},{11,3},{12,4},{13,5},{14,6},{15,7}} | collective-permute-start | bytes 2162696 | tf_op jit(solution)/shard_map/ppermute | solution.py:420
  754.7 32.1 %collective-permute-start.51 = (bf16[64,5120]{1,0:T(8,128)(2,1)}, bf16[64,5120]{1,0:T(8,128)(2,1)}, u32[]{:S(2)}, u32[]{:S(2)}) collective-permute-start(bf16[64,5120]{1,0:T(8,128)(2,1)} %get-tuple-element.490), channel_id=1, source_target_pairs={{0,8},{1,9},{2,10},{3,11},{4,12},{5,13},{6,14},{7,15}} | collective-permute-start | bytes 1966088 | tf_op jit(solution)/shard_map/ppermute | solution.py:407
  789.6 33.0 %collective-permute-start.55 = (bf16[64,5120]{1,0:T(8,128)(2,1)}, bf16[64,5120]{1,0:T(8,128)(2,1)}, u32[]{:S(2)}, u32[]{:S(2)}) collective-permute-start(bf16[64,5120]{1,0:T(8,128)(2,1)} %get-tuple-element.499), channel_id=1, source_target_pairs={{0,8},{8,16},{1,9},{9,17},{2,10},{10,18},{3,11},{11,19},{4,12},{12... | collective-permute-start | bytes 1966088 | tf_op jit(solution)/shard_map/ppermute | solution.py:407
  794.9 27.7 %collective-permute-start.56 = (bf16[64,5120]{1,0:T(8,128)(2,1)}, bf16[64,5120]{1,0:T(8,128)(2,1)}, u32[]{:S(2)}, u32[]{:S(2)}) collective-permute-start(bf16[64,5120]{1,0:T(8,128)(2,1)} %get-tuple-element.500), channel_id=1, source_target_pairs={{24,16},{16,8},{25,17},{17,9},{26,18},{18,10},{27,19},{19,11},{28,... | collective-permute-start | bytes 1966088 | tf_op jit(solution)/shard_map/ppermute | solution.py:408
  796.4 105.9 %all-to-all-start.5 = ((bf16[8,512,384]{2,1,0:T(8,128)(2,1)}), bf16[8,512,384]{2,1,0:T(8,128)(2,1)}, u32[]{:S(2)}, u32[]{:S(2)}) async-start(bf16[8,512,384]{2,1,0:T(8,128)(2,1)} %get-tuple-element.483.refs_8_), calls=%async_computation.6 | async-start | bytes 6291456 | tf_op jit(solution)/shard_map/all_to_all | solution.py:1448
  801.1 119.3 %collective-permute-start.59 = (bf16[512,2048]{1,0:T(8,128)(2,1)}, bf16[512,2048]{1,0:T(8,128)(2,1)}, u32[]{:S(2)}, u32[]{:S(2)}) collective-permute-start(bf16[512,2048]{1,0:T(8,128)(2,1)} %get-tuple-element.488), channel_id=1, source_target_pairs={{0,2},{1,5},{2,0},{3,7},{4,6},{5,1},{6,4},{7,3},{8,10},{9,13},{10,... | collective-permute-start | bytes 6291464 | tf_op jit(solution)/shard_map/ppermute | solution.py:347
  824.4 66.5 %collective-permute-start.57 = (bf16[64,5120]{1,0:T(8,128)(2,1)S(1)}, bf16[64,5120]{1,0:T(8,128)(2,1)S(1)}, u32[]{:S(2)}, u32[]{:S(2)}) collective-permute-start(bf16[64,5120]{1,0:T(8,128)(2,1)S(1)} %get-tuple-element.503), channel_id=1, source_target_pairs={{0,8},{8,16},{16,24},{1,9},{9,17},{17,25},{2,10},{10,18},{18,26},{... | collective-permute-start | bytes 1966088 | tf_op jit(solution)/shard_map/ppermute | solution.py:407
  864.6 35.8 %collective-permute-start.58 = (bf16[64,5120]{1,0:T(8,128)(2,1)S(1)}, bf16[64,5120]{1,0:T(8,128)(2,1)S(1)}, u32[]{:S(2)}, u32[]{:S(2)}) collective-permute-start(bf16[64,5120]{1,0:T(8,128)(2,1)S(1)} %get-tuple-element.504), channel_id=1, source_target_pairs={{24,16},{16,8},{8,0},{25,17},{17,9},{9,1},{26,18},{18,10},{10,2},{... | collective-permute-start | bytes 1966088 | tf_op jit(solution)/shard_map/ppermute | solution.py:408
  865.9 58.4 %collective-permute-start.60 = (bf16[512,2048]{1,0:T(8,128)(2,1)}, bf16[512,2048]{1,0:T(8,128)(2,1)}, u32[]{:S(2)}, u32[]{:S(2)}) collective-permute-start(bf16[512,2048]{1,0:T(8,128)(2,1)} %get-tuple-element.498), channel_id=1, source_target_pairs={{0,2},{1,5},{2,0},{3,7},{4,6},{5,1},{6,4},{7,3},{8,10},{9,13},{10,... | collective-permute-start | bytes 6291464 | tf_op jit(solution)/shard_map/ppermute | solution.py:347
  924.4 56.2 %collective-permute-start.67 = (bf16[512,2048]{1,0:T(8,128)(2,1)}, bf16[512,2048]{1,0:T(8,128)(2,1)}, u32[]{:S(2)}, u32[]{:S(2)}) collective-permute-start(bf16[512,2048]{1,0:T(8,128)(2,1)} %add_convert_fusion.2), channel_id=1, source_target_pairs={{0,4},{1,3},{2,6},{3,1},{4,0},{5,7},{6,2},{7,5},{8,12},{9,11},{10,... | collective-permute-start | bytes 6291464 | tf_op jit(solution)/shard_map/ppermute | solution.py:351
  926.4 28.9 %collective-permute-start.61 = (bf16[64,5120]{1,0:T(8,128)(2,1)S(1)}, bf16[64,5120]{1,0:T(8,128)(2,1)}, u32[]{:S(2)}, u32[]{:S(2)}) collective-permute-start(bf16[64,5120]{1,0:T(8,128)(2,1)S(1)} %pad_maximum_fusion.3.refs_0_), channel_id=1, source_target_pairs={{0,8},{8,16},{16,24},{1,9},{9,17},{17,25},{2,10},{10,18},{18,26},{... | collective-permute-start | bytes 1966088 | tf_op jit(solution)/shard_map/ppermute | solution.py:419
  (97 other events, 1293.0 us)
Sparse Core Ops, SparseCore 0:
  113.9 107.2 all-gather.4
  494.8 131.9 reduce-scatter.1
  775.3 142.5 all-gather.6

commit v5 on v4

--- a/solution.py
+++ b/solution.py
@@ -341,6 +341,8 @@
 SECOND = swap_pairs(4, 2)
 SIBLING = swap_pairs(1, 1)
 SAME_CORE = [[0, 2, 4, 6], [1, 3, 5, 7]]
+LINE_NEAR = [(z, z ^ 1) for z in range(4)]
+LINE_FAR = [(z, z ^ 2) for z in range(4)]
 
 
 def send_first(x):
@@ -462,33 +464,6 @@
         cost_estimate=SHORT,
         name="spread",
     )(parts, weight, gain)
-
-
-def spread_rows_kernel(z_ref, *refs, planes):
-    blocks, out_ref = refs[:-1], refs[-1]
-    rows = blocks[0].shape[0]
-    for place, load in line_values(blocks, planes, z_ref[0]):
-        out_ref[pl.ds(pl.multiple_of(place * rows, rows), rows), :] = load(slice(None)).astype(F32)
-
-
-def spread_rows(steps):
-    planes = len(steps)
-    rows, width = steps[0][0].shape
-    blocks = [steps[0][0]] + [s[0] for s in steps[1:]] + [s[1] for s in steps[1:]]
-    tile = width // 4
-    return pl.pallas_call(
-        functools.partial(spread_rows_kernel, planes=planes),
-        grid_spec=pltpu.PrefetchScalarGridSpec(
-            num_scalar_prefetch=1,
-            grid=(4,),
-            in_specs=[pl.BlockSpec((rows, tile), lambda i, z: (0, i))] * len(blocks),
-            out_specs=pl.BlockSpec((planes * rows, tile), lambda i, z: (0, i)),
-        ),
-        out_shape=jax.ShapeDtypeStruct((planes * rows, width), F32),
-        compiler_params=pltpu.CompilerParams(vmem_limit_bytes=32 * 2**20),
-        cost_estimate=SHORT,
-        name="spread_rows",
-    )(lax.axis_index("dp").reshape(1), *blocks)
 
 
 def spread_last_kernel(z_ref, *refs, planes):
@@ -1362,39 +1337,38 @@
     far = ffn(b_far, dy_far, w_gu, w_dn)
     db_got_first, db_far, *hid_rows = fence(db_got_first, far[3], own[0], first[0], second[0], far[0])
 
+    b_rows = [inner, b_first, b_second, b_far]
     db_got_far = send_first(db_far)
-    dn_keep, dn_give = grad_dn(core, hid_rows, [dy, dy_first, dy_second, dy_far])
-    db_got_far, dn_keep, dn_give = fence(db_got_far, dn_keep, dn_give)
-    db_pass = (second[3].astype(F32) + db_got_far.astype(F32)).astype(BF)
-    b_own, db_pass, dn_give = fence(inner, db_pass, dn_give)
-    db_passed = send_second(db_pass)
-    dn_got = send_sibling(dn_give)
     gu_keep, gu_give = grad_gu(
         core,
-        [b_own, b_first, b_second, b_far],
+        b_rows,
         [own[1], first[1], second[1], far[1]],
         [own[2], first[2], second[2], far[2]],
         share,
         planes,
     )
-    db_passed, dn_got, gu_keep, gu_give = fence(db_passed, dn_got, gu_keep, gu_give)
-    dn_parts = [part.reshape(planes, dn_keep.shape[0] // planes, width) for part in (dn_keep, dn_got)]
-    dn_moves = line_scatter_sends(dn_parts, None, 1, 0)
-    db_passed, gu_give, *dn_moves = fence(db_passed, gu_give, *dn_moves)
+    db_got_far, gu_keep, gu_give, *hid_rows = fence(db_got_far, gu_keep, gu_give, *hid_rows)
+    db_pass = (second[3].astype(F32) + db_got_far.astype(F32)).astype(BF)
+    db_pass, gu_give, *hid_rows = fence(db_pass, gu_give, *hid_rows)
+    db_passed = send_second(db_pass)
     gu_got = send_sibling(gu_give)
-    dn_moves = line_scatter_move(dn_moves, 1)
+    dn_keep, dn_give = grad_dn(core, hid_rows, [dy, dy_first, dy_second, dy_far])
+    db_passed, gu_got, dn_keep, dn_give = fence(db_passed, gu_got, dn_keep, dn_give)
+    gu_sum = (gu_keep.astype(F32) + gu_got.astype(F32)).astype(BF)
+    gu_sum, db_passed, dn_give = fence(gu_sum, db_passed, dn_give)
+    gu_z = lax.psum_scatter(
+        gu_sum.reshape(planes * CHIPS * quarter, 2 * hidden_chip), "dp", scatter_dimension=0, tiled=True
+    )
+    gu_z = gu_z.reshape(CHIPS, quarter, 2 * hidden_chip)
+    dn_got = send_sibling(dn_give)
     d_resid, d_branch, d_send = resid_back(
         places, own[3], db_got_first, db_passed, residual, inv_two, mlp_gain, dy, out_parts
     )
-    d_send, d_branch, gu_got, *dn_moves = fence(d_send, d_branch, gu_got, *dn_moves)
-    gu_sum = (gu_keep.astype(F32) + gu_got.astype(F32)).astype(BF)
-    gu_z = lax.psum_scatter(
-        gu_sum.reshape(planes * CHIPS * quarter, 2 * hidden_chip), "dp", scatter_dimension=0, tiled=True
-    )
-    gu_z = gu_z.reshape(CHIPS, quarter, 2 * hidden_chip)
+    d_send, d_branch, dn_got = fence(d_send, d_branch, dn_got)
     d_heads = lax.all_to_all(d_send, "sp", 0, 0, tiled=True).reshape(length, share)
-    dn_moves = line_scatter_sends(dn_parts, dn_moves, 2, 0)
-    dn_moves = line_scatter_move(dn_moves, 2)
+    dn_parts = [part.reshape(2, 2, dn_keep.shape[0] // planes, width) for part in (dn_keep, dn_got)]
+    dn_own = pick_sum(dn_parts, plane & 1, 1)
+    dn_move = lax.ppermute(pick_sum(dn_parts, 1 - (plane & 1), 1).astype(BF), "dp", LINE_NEAR)
     wo_keep, wo_give = grad_wo(core, attn_tok, d_branch)
     d_heads, wo_keep, wo_give, normed = fence(d_heads, wo_keep, wo_give, normed)
 
@@ -1405,46 +1379,46 @@
     wo_got = send_sibling(wo_give)
     a_first = send_first(normed)
     bwd = back_call(d_heads, turns[0], turns[1], out=out_heads)
-    d_heads, a_first, wo_got, normed, *moves = fence(d_heads, a_first, wo_got, normed, *dn_moves, *bwd)
-    dn_moves, bwd = moves[:2], moves[2:]
-
-    dn_moves = line_scatter_sends(dn_parts, dn_moves, 3, 0)
-    d_heads, normed, a_first, *dn_moves = fence(d_heads, normed, a_first, *dn_moves)
+    d_heads, a_first, wo_got, normed, dn_move, *bwd = fence(d_heads, a_first, wo_got, normed, dn_move, *bwd)
+
+    dn_own = dn_own + dn_move.astype(F32)
+    far_side = plane // 2
+    dn_move = pick(dn_own, 1 - far_side).astype(BF)
+    d_heads, normed, a_first, dn_move = fence(d_heads, normed, a_first, dn_move)
     a_second = send_second(normed)
     a_theirs = [send_sibling(normed), send_sibling(a_first)]
-    dn_moves = line_scatter_move(dn_moves, 3)
+    dn_move = lax.ppermute(dn_move, "dp", LINE_FAR)
     bwd = back_call(d_heads, turns[1], turns[2], before=bwd)
-    d_heads, gu_z, a_second, *moves = fence(d_heads, gu_z, a_second, *a_theirs, *dn_moves, *bwd)
-    a_theirs, dn_moves, bwd = moves[:2], moves[2:4], moves[4:]
+    d_heads, gu_z, a_second, dn_move, *moves = fence(d_heads, gu_z, a_second, dn_move, *a_theirs, *bwd)
+    a_theirs, bwd = moves[:2], moves[2:]
 
     def wo_part(place):
         return pick(wo_keep, place).astype(F32) + pick(wo_got, place).astype(F32)
 
-    dn_z = line_scatter_end(dn_parts, dn_moves, 0)
+    dn_z = (pick(dn_own, far_side) + dn_move.astype(F32)).astype(BF)
     d_heads, dn_z, gu_z, a_second = fence(d_heads, dn_z, gu_z, a_second)
-    dn_steps = [(dn_z, dn_z), line_gather_move((dn_z, dn_z), 1)]
+    dn_move = lax.ppermute(dn_z, "dp", LINE_FAR)
     gu_z = lax.all_to_all(gu_z, "sp", 0, 0, axis_index_groups=SAME_CORE, tiled=True)
     a_theirs.append(send_sibling(a_second))
     bwd = back_call(d_heads, turns[2], turns[3], before=bwd)
-    d_heads, gu_z, a_first, *moves = fence(d_heads, gu_z, a_first, *a_theirs, *dn_steps[-1], *bwd)
-    a_theirs, dn_steps[-1], bwd = moves[:3], tuple(moves[3:5]), moves[5:]
-
+    d_heads, gu_z, a_first, dn_move, *moves = fence(d_heads, gu_z, a_first, dn_move, *a_theirs, *bwd)
+    a_theirs, bwd = moves[:3], moves[3:]
+
+    dn_pair = jnp.where(far_side == 0, jnp.stack([dn_z, dn_move]), jnp.stack([dn_move, dn_z]))
     wo_first = wo_part(chip ^ (first_mask // 2)).astype(BF)
     wo_far = wo_part(chip ^ 3).astype(BF)
-    d_heads, gu_z, a_first, wo_first, wo_far = fence(d_heads, gu_z, a_first, wo_first, wo_far)
+    d_heads, gu_z, a_first, wo_first, wo_far, dn_pair = fence(d_heads, gu_z, a_first, wo_first, wo_far, dn_pair)
     gu_all = lax.all_gather(gu_z, "dp", axis=0, tiled=False)
     a_far = send_second(a_first)
     wo_far = send_first(wo_far)
     wo_first = send_first(wo_first)
-    dn_steps.append(line_gather_move(dn_steps[-1], 2))
+    dn_other = lax.ppermute(dn_pair, "dp", LINE_NEAR)
     bwd = back_call(d_heads, turns[3], turns[4], before=bwd)
     wo_pass = (wo_part(chip ^ (second_mask // 2)) + wo_far.astype(F32)).astype(BF)
-    dp_heads, wo_first, wo_pass, a_far, *moves = fence(bwd[0], wo_first, wo_pass, a_far, *dn_steps[-1])
-    dn_steps[-1] = tuple(moves)
+    dp_heads, wo_first, wo_pass, a_far, dn_other = fence(bwd[0], wo_first, wo_pass, a_far, dn_other)
 
     wo_passed = send_second(wo_pass)
     a_theirs.append(send_sibling(a_far))
-    dn_steps.append(line_gather_move(dn_steps[-1], 3))
     back = lax.all_to_all(dp_heads, "sp", 0, 0, tiled=True)
     grad_wq = grad_qkv(places, [normed, a_first, a_second, a_far] + list(a_theirs), dp_heads, planes)
     wo_rows = (wo_part(chip) + wo_first.astype(F32) + wo_passed.astype(F32)).astype(BF)
@@ -1458,14 +1432,12 @@
         moves = line_scatter_move(moves, step)
         if step == 1:
             y_got_far = send_first(y_far)
-            moves = fence(*moves, *dn_steps[-1])
-            moves, dn_steps[-1] = moves[:2], tuple(moves[2:])
         elif step == 2:
             y_got_first = send_first(y_first)
         moves = fence(*moves)
     last_z = line_scatter_end(last_parts, moves, 0)
     wq_z = last_z[:, :split].reshape(quarter, devices, split // devices).transpose(1, 0, 2)
-    wq_z, wo_z, back = fence(wq_z, last_z[:, split:], back)
+    wq_z, wo_z, back, gu_all = fence(wq_z, last_z[:, split:], back, gu_all)
     wq_z = lax.all_to_all(wq_z, "sp", 0, 0, tiled=True)
     grad_tokens = in_back(places, back, x_bf, inv_one, attn_gain, d_resid, qkv_parts).reshape(tokens.shape)
     y_pass = (second[4].astype(F32) + y_got_far.astype(F32)).astype(BF)
@@ -1477,7 +1449,8 @@
     for step in range(1, planes):
         last_steps.append(line_gather_move(last_steps[-1], step))
         if step == 1:
-            outs.append(spread_rows(dn_steps))
+            low, high = jnp.stack([dn_pair, dn_other], axis=1), jnp.stack([dn_other, dn_pair], axis=1)
+            outs.append(jnp.where((plane & 1) == 0, low, high).astype(F32).reshape(w_down.shape))
         elif step == 2:
             outs += spread(gu_all, w_gate_up, g_mlp.astype(F32).reshape(share, 1))
         if step == planes - 1:
@@ -1522,5 +1495,5 @@
         P("sp"),
         P("sp"),
     )
-    body = fast_body if mesh.shape["sp"] == 2 * CHIPS else general_body
+    body = fast_body if dict(mesh.shape) == {"dp": 4, "sp": 2 * CHIPS} else general_body
     return jax.shard_map(body, mesh=mesh, in_specs=in_specs, out_specs=out_specs, check_vma=False)

time: 1020 us -> 1020 us (level)
  waiting for transfers between devices: 239 us -> 359 us
  starting transfers between devices: 208 us -> 96.6 us
  Pallas kernels: 429 us -> 413 us
    ppermute x0 -> x4, waiting for transfers between devices: none -> 125 us  [the longest x1 56.3 us: fast_body(): lax.ppermute(pick_sum(dn_parts, 1 - (plane & 1), 1).astype(BF), 'dp', LIN...]
    ppermute x6 -> x3, starting transfers between devices: 99.2 us -> 15.9 us  [line_scatter_move(): right = lax.ppermute(sends[0], 'dp', [(i, i + 1) for i in range(step)])]
    ppermute x6 -> x3, waiting for transfers between devices: 60.4 us -> 26.4 us  [line_scatter_move(): right = lax.ppermute(sends[0], 'dp', [(i, i + 1) for i in range(step)])]
    ppermute x6 -> x3, starting transfers between devices: 25.7 us -> 5.05 us  [line_gather_move(): lax.ppermute(got[0], 'dp', [(i, i + 1) for i in range(step - 1, planes -...]
    ppermute x13, waiting for transfers between devices: 45 us -> 60.9 us  [send_second(): return lax.ppermute(x, 'sp', SECOND)]
    ppermute x11, waiting for transfers between devices: 30.2 us -> 41.3 us  [send_first(): return lax.ppermute(x, 'sp', FIRST)]
    unnamed x132 -> x142, local copies, waits for them, and re-layouts: 34.3 us -> 38.4 us
  transfers between devices with their start and end apart: 78 -> 70, of which waited for: 27 -> 30; matrix products, arithmetic and copies ran while one was open for 6% -> 7% of each run, Pallas kernels for 41% -> 39%
where the time goes in v5:
time: 1020 us; the launch traced here: 1010 us
  Pallas kernels  413 us (40%)
  waiting for transfers between devices  359 us (35%)
  starting transfers between devices  96.6 us (9%)
  other arithmetic  79.7 us (8%)
  local copies, waits for them, and re-layouts  49.2 us (5%)
  between operations  15.9 us (2%)
    pallas_call x4, Pallas kernels, attend_back(): pl.pallas_call(functools.partial(attend_back_kernel, heads=heads, start=s...  114 us
    pallas_call x4, Pallas kernels, ffn(): pl.pallas_call(functools.partial(ffn_kernel, cuts=cuts), in_specs=[hbm] *...  103 us
    ppermute x13, waiting for transfers between devices, send_second(): return lax.ppermute(x, 'sp', SECOND)  60.9 us
    ppermute x1, waiting for transfers between devices, fast_body(): lax.ppermute(pick_sum(dn_parts, 1 - (plane & 1), 1).astype(BF), 'dp', LIN...  56.3 us
    pallas_call x3, Pallas kernels, attend(): pl.pallas_call(functools.partial(attend_kernel, heads=heads, start=start,...  50.1 us
    ppermute x1, waiting for transfers between devices, fast_body(): dn_other = lax.ppermute(dn_pair, 'dp', LINE_NEAR)  46.4 us
    ppermute x11, waiting for transfers between devices, send_first(): return lax.ppermute(x, 'sp', FIRST)  41.3 us
    unnamed x142, local copies, waits for them, and re-layouts  38.4 us
  transfers between devices with their start and end apart: 70, of which 30 were waited for; matrix products, arithmetic and copies ran while one was open for 7% of the time, Pallas kernels for 39%

profile of v5, /device:TPU:0, one launch (start us, length us, event | category | flops | bytes accessed | tf_op | source)
XLA Modules:
  0.0 1013.8 jit_solution(2701160400506034428)
XLA Ops:
  27.8 12.1 %collective-permute-done.3.refs_1_.refs_9_ = bf16[256,2560]{1,0:T(8,128)(2,1)S(1)} collective-permute-done((bf16[256,2560]{1,0:T(8,128)(2,1)S(1)}, bf16[256,2560]{1,0:T(8,128)(2,1)S(1)}, u32[]{:S(2)}, u32[]{:S(2)}) %collective-permute-start.3) | collective-permute-done | bytes 1310752 | tf_op jit(solution)/shard_map/ppermute | solution.py:349
  42.5 7.5 fusion.16
  61.3 14.0 %collective-permute-done.7.refs_3_.refs_11_ = bf16[256,2560]{1,0:T(8,128)(2,1)S(1)} collective-permute-done((bf16[256,2560]{1,0:T(8,128)(2,1)S(1)}, bf16[256,2560]{1,0:T(8,128)(2,1)S(1)}, u32[]{:S(2)}, u32[]{:S(2)}) %collective-permute-start.7) | collective-permute-done | bytes 1310752 | tf_op jit(solution)/shard_map/ppermute | solution.py:353
  89.1 18.3 %project.1 = (bf16[8,512,384]{2,1,0:T(8,128)(2,1)}, bf16[512,2048]{1,0:T(8,128)(2,1)}, f32[512,1]{1,0:T(8,128)S(1)}) custom-call(s32[8]{0:T(128)S(1)} %stack.87.place_ref, bf16[512,2048]{1,0:T(8,128)(2,1)} %bitcast.138, f32[1,2048]{1,0:T(1,128)S(1)} %get-tuple-element.558.gain_ref, f32[512,128]{1,0:T(8,128)S(1)} %pad_maximum_fusion.4.cos_ref, ...), custom_call_target="tpu_custom_call" | custom-call | flops 1 | bytes 1 | tf_op jit(solution)/shard_map/project/pallas_call | solution.py:736
  108.1 5.7 collective-permute-done.10.refs_1_
  119.5 8.3 maximum_select_fusion.refs_3_
  127.8 27.7 %all-to-all-done = bf16[8,512,384]{2,1,0:T(8,128)(2,1)S(1)} async-done(((bf16[8,512,384]{2,1,0:T(8,128)(2,1)}), bf16[8,512,384]{2,1,0:T(8,128)(2,1)S(1)}, u32[]{:S(2)}, u32[]{:S(2)}) %all-to-all-start) | async-done | bytes 3145760 | tf_op jit(solution)/shard_map/all_to_all | solution.py:1304
  156.6 30.3 %attend.3 = (f32[4096,256]{1,0:T(8,128)}, bf16[8,512,256]{2,1,0:T(8,128)(2,1)S(1)}, f32[8,4,512]{2,1,0:T(4,128)S(1)}) custom-call(s32[1]{0:T(128)} %bitcast.14.zeros_ref, bf16[4096,384]{1,0:T(8,128)(2,1)S(1)} %bitcast.112, bf16[4096,384]{1,0:T(8,128)(2,1)S(1)} %bitcast.113), custom_call_target="tpu_custom_call" | custom-call | flops 1 | bytes 1 | tf_op jit(solution)/shard_map/attend/pallas_call | solution.py:1056
  193.1 11.3 %attend.4 = (f32[4096,256]{1,0:T(8,128)}, bf16[8,512,256]{2,1,0:T(8,128)(2,1)S(1)}, f32[8,4,512]{2,1,0:T(4,128)S(1)}) custom-call(s32[1]{0:T(128)} %bitcast.14.zeros_ref, bf16[4096,384]{1,0:T(8,128)(2,1)S(1)} %bitcast.114, bf16[4096,384]{1,0:T(8,128)(2,1)S(1)} %bitcast.115, ...), custom_call_target="tpu_custom_call", output_to_operand_aliasing={{0}: (3, {}), {1}: (4, {}), {2}: (5, {})} | custom-call | flops 1 | bytes 1 | tf_op jit(solution)/shard_map/attend/pallas_call | solution.py:1056
  205.7 22.6 %collective-permute-done.14.refs_3_ = bf16[256,2048]{1,0:T(8,128)(2,1)S(1)} collective-permute-done((bf16[256,2048]{1,0:T(8,128)(2,1)}, bf16[256,2048]{1,0:T(8,128)(2,1)S(1)}, u32[]{:S(2)}, u32[]{:S(2)}) %collective-permute-start.14) | collective-permute-done | bytes 1048608 | tf_op jit(solution)/shard_map/ppermute | solution.py:353
  233.2 8.4 attend.5
  256.3 6.1 join.1
  264.9 14.4 %all-to-all-done.2.attn_ref.keep_ref.give_ref = bf16[8,512,256]{2,1,0:T(8,128)(2,1)S(1)} async-done(((bf16[8,512,256]{2,1,0:T(8,128)(2,1)}), bf16[8,512,256]{2,1,0:T(8,128)(2,1)S(1)}, u32[]{:S(2)}, u32[]{:S(2)}) %all-to-all-start.2) | async-done | bytes 2097184 | tf_op jit(solution)/shard_map/all_to_all | solution.py:1322
  280.7 11.7 %out_proj.1 = (f32[512,2048]{1,0:T(8,128)}, f32[512,1]{1,0:T(8,128)}, bf16[512,2048]{1,0:T(8,128)(2,1)}) custom-call(s32[8]{0:T(128)} %copy-done.28, bf16[8,512,256]{2,1,0:T(8,128)(2,1)} %copy-done.1, bf16[512,2048]{1,0:T(8,128)(2,1)} %bitcast.139, f32[1,2048]{1,0:T(1,128)} %get-tuple-element.557.gain_ref, bf16[256,2048]{1,0:T(8,128)(2,1)} %refs_0_.1, ...), custom_call_target="tpu_custom_call" | custom-call | flops 1 | bytes 1 | tf_op jit(solution)/shard_map/out_proj/pallas_call | solution.py:790
  293.5 25.9 %ffn.4 = (bf16[512,1408]{1,0:T(8,128)(2,1)}, bf16[512,1408]{1,0:T(8,128)(2,1)}, bf16[512,1408]{1,0:T(8,128)(2,1)}, bf16[512,2048]{1,0:T(8,128)(2,1)}, bf16[512,2048]{1,0:T(8,128)(2,1)}) custom-call(bf16[512,2048]{1,0:T(8,128)(2,1)} %get-tuple-element.350.refs_0_.refs_4_, bf16[512,2048]{1,0:T(8,128)(2,1)} %multiply_bitcast_fusion.refs_1_.refs_4_.dy_ref, ...), custom_call_target="tpu_custom_call" | custom-call | flops 1 | bytes 1 | tf_op jit(solution)/shard_map/ffn/pallas_call | solution.py:597
  321.0 25.7 %ffn.5 = (bf16[512,1408]{1,0:T(8,128)(2,1)}, bf16[512,1408]{1,0:T(8,128)(2,1)}, bf16[512,1408]{1,0:T(8,128)(2,1)}, bf16[512,2048]{1,0:T(8,128)(2,1)}, bf16[512,2048]{1,0:T(8,128)(2,1)}) custom-call(bf16[512,2048]{1,0:T(8,128)(2,1)} %copy-done.32, bf16[512,2048]{1,0:T(8,128)(2,1)} %copy-done.40, bf16[2,2048,1408]{2,1,0:T(8,128)(2,1)} %bitcast.130, ...), custom_call_target="tpu_custom_call" | custom-call | flops 1 | bytes 1 | tf_op jit(solution)/shard_map/ffn/pallas_call | solution.py:597
  348.0 25.8 %ffn.6 = (bf16[512,1408]{1,0:T(8,128)(2,1)}, bf16[512,1408]{1,0:T(8,128)(2,1)}, bf16[512,1408]{1,0:T(8,128)(2,1)}, bf16[512,2048]{1,0:T(8,128)(2,1)}, bf16[512,2048]{1,0:T(8,128)(2,1)}) custom-call(bf16[512,2048]{1,0:T(8,128)(2,1)} %collective-permute-done.23.refs_0_.refs_2_.refs_6_, bf16[512,2048]{1,0:T(8,128)(2,1)} %copy-done.41, ...), custom_call_target="tpu_custom_call" | custom-call | flops 1 | bytes 1 | tf_op jit(solution)/shard_map/ffn/pallas_call | solution.py:597
  375.2 25.9 %ffn.7 = (bf16[512,1408]{1,0:T(8,128)(2,1)}, bf16[512,1408]{1,0:T(8,128)(2,1)}, bf16[512,1408]{1,0:T(8,128)(2,1)}, bf16[512,2048]{1,0:T(8,128)(2,1)}, bf16[512,2048]{1,0:T(8,128)(2,1)}) custom-call(bf16[512,2048]{1,0:T(8,128)(2,1)} %copy-done.33, bf16[512,2048]{1,0:T(8,128)(2,1)} %collective-permute-done.17.refs_1_.refs_7_, ...), custom_call_target="tpu_custom_call" | custom-call | flops 1 | bytes 1 | tf_op jit(solution)/shard_map/ffn/pallas_call | solution.py:597
  402.5 34.4 %grad_gu.1 = (bf16[4,4,64,2816]{3,2,1,0:T(8,128)(2,1)}, bf16[4,4,64,2816]{3,2,1,0:T(8,128)(2,1)}) custom-call(s32[1]{0:T(128)} %bitcast.20.core_ref, bf16[512,2048]{1,0:T(8,128)(2,1)} %get-tuple-element.350.refs_0_.refs_4_, bf16[512,2048]{1,0:T(8,128)(2,1)} %copy-done.32, bf16[512,2048]{1,0:T(8,128)(2,1)} %collective-permute-done.23.refs_0_.refs_2_.refs_6_, ...), custom_call_target="tpu_custom_call" | custom-call | flops 1 | bytes 1 | tf_op jit(solution)/shard_map/grad_gu/pallas_call | solution.py:638
  443.0 17.5 %grad_dn.1 = (bf16[704,2048]{1,0:T(8,128)(2,1)}, bf16[704,2048]{1,0:T(8,128)(2,1)}) custom-call(s32[1]{0:T(128)} %bitcast.20.core_ref, bf16[512,1408]{1,0:T(8,128)(2,1)} %get-tuple-element.399.refs_0_, bf16[512,1408]{1,0:T(8,128)(2,1)} %get-tuple-element.400.refs_1_, bf16[512,1408]{1,0:T(8,128)(2,1)} %get-tuple-element.401.refs_2_, ...), custom_call_target="tpu_custom_call" | custom-call | flops 1 | bytes 1 | tf_op jit(solution)/shard_map/grad_dn/pallas_call | solution.py:960
  460.5 8.0 collective-permute-done.27.passed_ref
  469.8 6.9 add_convert_fusion
  476.7 14.6 %resid_back.1 = (f32[512,2048]{1,0:T(8,128)}, bf16[512,2048]{1,0:T(8,128)(2,1)}, bf16[8,512,256]{2,1,0:T(8,128)(2,1)}) custom-call(s32[8]{0:T(128)} %copy-done.28, bf16[512,2048]{1,0:T(8,128)(2,1)} %get-tuple-element.348.db_ref, bf16[512,2048]{1,0:T(8,128)(2,1)} %copy-done.60, bf16[512,2048]{1,0:T(8,128)(2,1)} %copy-done.61, ...), custom_call_target="tpu_custom_call" | custom-call | flops 1 | bytes 1 | tf_op jit(solution)/shard_map/resid_back/pallas_call | solution.py:836
  498.9 6.2 grad_wo.1
  505.1 18.9 %all-to-all-done.3 = bf16[8,512,256]{2,1,0:T(8,128)(2,1)} async-done(((bf16[8,512,256]{2,1,0:T(8,128)(2,1)}), bf16[8,512,256]{2,1,0:T(8,128)(2,1)}, u32[]{:S(2)}, u32[]{:S(2)}) %all-to-all-start.3) | async-done | bytes 2097184 | tf_op jit(solution)/shard_map/all_to_all | solution.py:1368
  528.8 26.1 %attend_back.4 = (bf16[8,512,384]{2,1,0:T(8,128)(2,1)}, f32[256,4096]{1,0:T(8,128)}, f32[8,4,512]{2,1,0:T(4,128)}) custom-call(s32[1]{0:T(128)} %bitcast.14.zeros_ref, bf16[4096,384]{1,0:T(8,128)(2,1)} %bitcast.118, bf16[4096,384]{1,0:T(8,128)(2,1)} %bitcast.119, bf16[4096,256]{1,0:T(8,128)(2,1)} %bitcast.22.do_ref, f32[8,4,512]{2,1,0:T(4,128)} %copy-done.19, ...), custom_call_target="tpu_custom_call" | custom-call | flops 1 | bytes 1 | tf_op jit(solution)/shard_map/attend_back/pallas_call | solution.py:1197
  554.9 56.3 %collective-permute-done.32 = bf16[2,176,2048]{2,1,0:T(8,128)(2,1)S(1)} collective-permute-done((bf16[2,176,2048]{2,1,0:T(8,128)(2,1)S(1)}, bf16[2,176,2048]{2,1,0:T(8,128)(2,1)S(1)}, u32[]{:S(2)}, u32[]{:S(2)}) %collective-permute-start.32) | collective-permute-done | bytes 1441824 | tf_op jit(solution)/shard_map/ppermute | solution.py:1371
  617.0 21.2 %attend_back.5 = (bf16[8,512,384]{2,1,0:T(8,128)(2,1)}, f32[256,4096]{1,0:T(8,128)}, f32[8,4,512]{2,1,0:T(4,128)}) custom-call(s32[1]{0:T(128)} %bitcast.14.zeros_ref, bf16[4096,384]{1,0:T(8,128)(2,1)} %bitcast.120, bf16[4096,384]{1,0:T(8,128)(2,1)} %bitcast.121, bf16[4096,256]{1,0:T(8,128)(2,1)} %bitcast.22.do_ref, ...), custom_call_target="tpu_custom_call", output_to_operand_aliasing={{0}: (9, {})} | custom-call | flops 1 | bytes 1 | tf_op jit(solution)/shard_map/attend_back/pallas_call | solution.py:1197
  638.2 12.3 %collective-permute-done.34 = bf16[176,2048]{1,0:T(8,128)(2,1)S(1)} collective-permute-done((bf16[176,2048]{1,0:T(8,128)(2,1)}, bf16[176,2048]{1,0:T(8,128)(2,1)S(1)}, u32[]{:S(2)}, u32[]{:S(2)}) %collective-permute-start.34) | collective-permute-done | bytes 720928 | tf_op jit(solution)/shard_map/ppermute | solution.py:1390
  660.5 18.0 %attend_back.6 = (bf16[8,512,384]{2,1,0:T(8,128)(2,1)}, f32[256,4096]{1,0:T(8,128)}, f32[8,4,512]{2,1,0:T(4,128)}) custom-call(s32[1]{0:T(128)} %bitcast.14.zeros_ref, bf16[4096,384]{1,0:T(8,128)(2,1)} %bitcast.122, bf16[4096,384]{1,0:T(8,128)(2,1)} %bitcast.123, bf16[4096,256]{1,0:T(8,128)(2,1)} %bitcast.22.do_ref, ...), custom_call_target="tpu_custom_call", output_to_operand_aliasing={{0}: (9, {})} | custom-call | flops 1 | bytes 1 | tf_op jit(solution)/shard_map/attend_back/pallas_call | solution.py:1197
  678.6 10.0 collective-permute-done.37
  695.4 48.6 %attend_back.7 = (bf16[8,512,384]{2,1,0:T(8,128)(2,1)}, f32[256,4096]{1,0:T(8,128)}, f32[8,4,512]{2,1,0:T(4,128)}) custom-call(s32[1]{0:T(128)} %bitcast.14.zeros_ref, bf16[4096,384]{1,0:T(8,128)(2,1)} %bitcast.124, bf16[4096,384]{1,0:T(8,128)(2,1)} %bitcast.125, bf16[4096,256]{1,0:T(8,128)(2,1)} %bitcast.22.do_ref, ...), custom_call_target="tpu_custom_call", output_to_operand_aliasing={{0}: (9, {})} | custom-call | flops 1 | bytes 1 | tf_op jit(solution)/shard_map/attend_back/pallas_call | solution.py:1197
  746.4 46.4 %collective-permute-done.42 = bf16[2,176,2048]{2,1,0:T(8,128)(2,1)} collective-permute-done((bf16[2,176,2048]{2,1,0:T(8,128)(2,1)S(1)}, bf16[2,176,2048]{2,1,0:T(8,128)(2,1)}, u32[]{:S(2)}, u32[]{:S(2)}) %collective-permute-start.42) | collective-permute-done | bytes 1441824 | tf_op jit(solution)/shard_map/ppermute | solution.py:1415
  792.9 14.9 %collective-permute-done.44 = bf16[256,2048]{1,0:T(8,128)(2,1)} collective-permute-done((bf16[256,2048]{1,0:T(8,128)(2,1)S(1)}, bf16[256,2048]{1,0:T(8,128)(2,1)}, u32[]{:S(2)}, u32[]{:S(2)}) %collective-permute-start.44) | collective-permute-done | bytes 1048608 | tf_op jit(solution)/shard_map/ppermute | solution.py:353
  810.7 13.3 %grad_qkv.1 = bf16[4,64,3072]{2,1,0:T(8,128)(2,1)S(1)} custom-call(s32[8]{0:T(128)S(1)} %copy-done.29, bf16[512,2048]{1,0:T(8,128)(2,1)S(1)} %copy-done.21, bf16[512,2048]{1,0:T(8,128)(2,1)} %collective-permute-done.30.refs_1_, bf16[512,2048]{1,0:T(8,128)(2,1)} %collective-permute-done.33.refs_2_, bf16[512,2048]{1,0:T(8,128)(2,1)} %collective-permute-done.41.refs_3_, ...), custom_call_target="tpu_custom_call" | custom-call | flops 1 | bytes 1 | tf_op jit(solution)/shard_map/grad_qkv/pallas_call | solution.py:672
  828.6 12.0 %collective-permute-done.45 = bf16[64,5120]{1,0:T(8,128)(2,1)} collective-permute-done((bf16[64,5120]{1,0:T(8,128)(2,1)}, bf16[64,5120]{1,0:T(8,128)(2,1)}, u32[]{:S(2)}, u32[]{:S(2)}) %collective-permute-start.45) | collective-permute-done | bytes 655392 | tf_op jit(solution)/shard_map/ppermute | solution.py:409
  843.0 5.3 collective-permute-start.47
  863.6 8.5 collective-permute-start.49
  874.4 9.9 collective-permute-done.49
  896.6 19.5 %collective-permute-done.51 = bf16[512,2048]{1,0:T(8,128)(2,1)} collective-permute-done((bf16[512,2048]{1,0:T(8,128)(2,1)}, bf16[512,2048]{1,0:T(8,128)(2,1)}, u32[]{:S(2)}, u32[]{:S(2)}) %collective-permute-start.51) | collective-permute-done | bytes 2097184 | tf_op jit(solution)/shard_map/ppermute | solution.py:349
  919.8 14.6 %in_back.1 = bf16[512,2048]{1,0:T(8,128)(2,1)} custom-call(s32[8]{0:T(128)} %copy-done.28, bf16[8,512,384]{2,1,0:T(8,128)(2,1)} %all-to-all-done.5.back_ref, bf16[512,2048]{1,0:T(8,128)(2,1)} %bitcast.140, f32[512,1]{1,0:T(8,128)} %copy-done.23, f32[1,2048]{1,0:T(1,128)} %copy-done.27, f32[512,2048]{1,0:T(8,128)} %get-tuple-element.506.d_resid_ref, ...), custom_call_target="tpu_custom_call" | custom-call | flops 1 | bytes 1 | tf_op jit(solution)/shard_map/in_back/pallas_call | solution.py:889
  934.4 7.2 all-to-all-done.6
  953.4 7.0 collective-permute-done.53.refs_1_
  960.4 5.0 collective-permute-done.54.refs_4_
  973.0 6.5 spread.1
  979.6 4.9 collective-permute-done.56.refs_5_
  986.6 5.1 fusion.1
  991.7 9.6 collective-permute-done.58.refs_6_
  (323 shorter events, 207.4 us)
Async XLA Ops:
  22.3 17.7 %collective-permute-start.3 = (bf16[256,2560]{1,0:T(8,128)(2,1)S(1)}, bf16[256,2560]{1,0:T(8,128)(2,1)S(1)}, u32[]{:S(2)}, u32[]{:S(2)}) collective-permute-start(bf16[256,2560]{1,0:T(8,128)(2,1)S(1)} %concatenate.52.refs_0_.refs_8_), channel_id=1, source_target_pairs={{0,2},{1,5},{2,0},{3,7},{4,6},{5,1},{6,4},{7,3},{8,10},{9,13},{10,... | collective-permute-start | bytes 3932168 | tf_op jit(solution)/shard_map/ppermute | solution.py:349
  40.0 17.6 %collective-permute-start.4 = (bf16[256,2560]{1,0:T(8,128)(2,1)S(1)}, bf16[256,2560]{1,0:T(8,128)(2,1)S(1)}, u32[]{:S(2)}, u32[]{:S(2)}) collective-permute-start(bf16[256,2560]{1,0:T(8,128)(2,1)S(1)} %concatenate.52.refs_0_.refs_8_), channel_id=1, source_target_pairs={{0,4},{1,3},{2,6},{3,1},{4,0},{5,7},{6,2},{7,5},{8,12},{9,11},{10,... | collective-permute-start | bytes 3932168 | tf_op jit(solution)/shard_map/ppermute | solution.py:353
  57.6 17.7 %collective-permute-start.7 = (bf16[256,2560]{1,0:T(8,128)(2,1)S(1)}, bf16[256,2560]{1,0:T(8,128)(2,1)S(1)}, u32[]{:S(2)}, u32[]{:S(2)}) collective-permute-start(bf16[256,2560]{1,0:T(8,128)(2,1)S(1)} %collective-permute-done.3.refs_1_.refs_9_), channel_id=1, source_target_pairs={{0,4},{1,3},{2,6},{3,1},{4,0},{5,7},{6,2},{7,5},{8,12},{9,11},{10,... | collective-permute-start | bytes 3932168 | tf_op jit(solution)/shard_map/ppermute | solution.py:353
  79.5 34.3 %all-to-all-start.1 = ((bf16[4,64,2816]{2,1,0:T(8,128)(2,1)}), bf16[4,64,2816]{2,1,0:T(8,128)(2,1)}, u32[]{:S(2)}, u32[]{:S(2)}) async-start(bf16[4,64,2816]{2,1,0:T(8,128)(2,1)} %pad_maximum_fusion.2), calls=%async_computation.1 | async-start | bytes 2883584 | tf_op jit(solution)/shard_map/all_to_all | solution.py:1295
  83.8 146.1 %all-gather.5.cloned.1.call-start = ((), (), s32[]{:S(2)}) async-start(), calls=%async_computation.9 | async-start | bytes 7208960 | tf_op jit(solution)/shard_map/all_gather | solution.py:1299
  84.3 29.4 %collective-permute-start.10 = (bf16[256,2048]{1,0:T(8,128)(2,1)}, bf16[256,2048]{1,0:T(8,128)(2,1)}, u32[]{:S(2)}, u32[]{:S(2)}) collective-permute-start(bf16[256,2048]{1,0:T(8,128)(2,1)} %refs_0_.1), channel_id=1, source_target_pairs={{0,2},{1,5},{2,0},{3,7},{4,6},{5,1},{6,4},{7,3},{8,10},{9,13},{10,... | collective-permute-start | bytes 3145736 | tf_op jit(solution)/shard_map/ppermute | solution.py:349
  114.0 41.5 %all-to-all-start = ((bf16[8,512,384]{2,1,0:T(8,128)(2,1)}), bf16[8,512,384]{2,1,0:T(8,128)(2,1)S(1)}, u32[]{:S(2)}, u32[]{:S(2)}) async-start(bf16[8,512,384]{2,1,0:T(8,128)(2,1)} %get-tuple-element.297), calls=%async_computation | async-start | bytes 6291456 | tf_op jit(solution)/shard_map/all_to_all | solution.py:1304
  155.5 35.5 %collective-permute-start.13 = (bf16[512,2048]{1,0:T(8,128)(2,1)}, bf16[512,2048]{1,0:T(8,128)(2,1)S(1)}, u32[]{:S(2)}, u32[]{:S(2)}) collective-permute-start(bf16[512,2048]{1,0:T(8,128)(2,1)} %multiply_bitcast_fusion.refs_1_.refs_4_.dy_ref), channel_id=1, source_target_pairs={{0,2},{1,5},{2,0},{3,7},{4,6},{5,1},{6,4},{7,3},{8,10},{9,13},{10,... | collective-permute-start | bytes 6291464 | tf_op jit(solution)/shard_map/ppermute | solution.py:349
  156.0 31.0 %collective-permute-start.12 = (bf16[256,2048]{1,0:T(8,128)(2,1)}, bf16[256,2048]{1,0:T(8,128)(2,1)S(1)}, u32[]{:S(2)}, u32[]{:S(2)}) collective-permute-start(bf16[256,2048]{1,0:T(8,128)(2,1)} %refs_0_.1), channel_id=1, source_target_pairs={{0,4},{1,3},{2,6},{3,1},{4,0},{5,7},{6,2},{7,5},{8,12},{9,11},{10,... | collective-permute-start | bytes 3145736 | tf_op jit(solution)/shard_map/ppermute | solution.py:353
  191.0 37.3 %collective-permute-start.15 = (bf16[512,2048]{1,0:T(8,128)(2,1)S(1)}, bf16[512,2048]{1,0:T(8,128)(2,1)S(1)}, u32[]{:S(2)}, u32[]{:S(2)}) collective-permute-start(bf16[512,2048]{1,0:T(8,128)(2,1)S(1)} %copy-done.30), channel_id=1, source_target_pairs={{0,4},{1,3},{2,6},{3,1},{4,0},{5,7},{6,2},{7,5},{8,12},{9,11},{10,... | collective-permute-start | bytes 6291464 | tf_op jit(solution)/shard_map/ppermute | solution.py:353
  192.7 35.6 %collective-permute-start.14 = (bf16[256,2048]{1,0:T(8,128)(2,1)}, bf16[256,2048]{1,0:T(8,128)(2,1)S(1)}, u32[]{:S(2)}, u32[]{:S(2)}) collective-permute-start(bf16[256,2048]{1,0:T(8,128)(2,1)} %collective-permute-done.10.refs_1_), channel_id=1, source_target_pairs={{0,4},{1,3},{2,6},{3,1},{4,0},{5,7},{6,2},{7,5},{8,12},{9,11},{10,... | collective-permute-start | bytes 3145736 | tf_op jit(solution)/shard_map/ppermute | solution.py:353
  229.9 35.0 %collective-permute-start.17 = (bf16[512,2048]{1,0:T(8,128)(2,1)}, bf16[512,2048]{1,0:T(8,128)(2,1)}, u32[]{:S(2)}, u32[]{:S(2)}) collective-permute-start(bf16[512,2048]{1,0:T(8,128)(2,1)} %copy-done.40), channel_id=1, source_target_pairs={{0,4},{1,3},{2,6},{3,1},{4,0},{5,7},{6,2},{7,5},{8,12},{9,11},{10,... | collective-permute-start | bytes 6291464 | tf_op jit(solution)/shard_map/ppermute | solution.py:353
  246.1 33.2 %all-to-all-start.2 = ((bf16[8,512,256]{2,1,0:T(8,128)(2,1)}), bf16[8,512,256]{2,1,0:T(8,128)(2,1)S(1)}, u32[]{:S(2)}, u32[]{:S(2)}) async-start(bf16[8,512,256]{2,1,0:T(8,128)(2,1)} %copy-done.6), calls=%async_computation.2 | async-start | bytes 4194304 | tf_op jit(solution)/shard_map/all_to_all | solution.py:1322
  249.8 400.7 %reduce-scatter.2.cloned.1.call-start = ((), (), s32[]{:S(2)}) async-start(), calls=%async_computation.8 | async-start | bytes 7208960 | tf_op jit(solution)/shard_map/reduce_scatter | solution.py:1359
  292.4 27.1 %collective-permute-start.22 = (bf16[512,2048]{1,0:T(8,128)(2,1)}, bf16[512,2048]{1,0:T(8,128)(2,1)S(1)}, u32[]{:S(2)}, u32[]{:S(2)}) collective-permute-start(bf16[512,2048]{1,0:T(8,128)(2,1)} %get-tuple-element.350.refs_0_.refs_4_), channel_id=1, source_target_pairs={{0,2},{1,5},{2,0},{3,7},{4,6},{5,1},{6,4},{7,3},{8,10},{9,13},{10,... | collective-permute-start | bytes 6291464 | tf_op jit(solution)/shard_map/ppermute | solution.py:349
  319.5 27.2 %collective-permute-start.23 = (bf16[512,2048]{1,0:T(8,128)(2,1)S(1)}, bf16[512,2048]{1,0:T(8,128)(2,1)}, u32[]{:S(2)}, u32[]{:S(2)}) collective-permute-start(bf16[512,2048]{1,0:T(8,128)(2,1)S(1)} %copy-done.31), channel_id=1, source_target_pairs={{0,4},{1,3},{2,6},{3,1},{4,0},{5,7},{6,2},{7,5},{8,12},{9,11},{10,... | collective-permute-start | bytes 6291464 | tf_op jit(solution)/shard_map/ppermute | solution.py:353
  346.7 27.1 %collective-permute-start.24 = (bf16[512,2048]{1,0:T(8,128)(2,1)}, bf16[512,2048]{1,0:T(8,128)(2,1)S(1)}, u32[]{:S(2)}, u32[]{:S(2)}) collective-permute-start(bf16[512,2048]{1,0:T(8,128)(2,1)} %copy-done.32), channel_id=1, source_target_pairs={{0,4},{1,3},{2,6},{3,1},{4,0},{5,7},{6,2},{7,5},{8,12},{9,11},{10,... | collective-permute-start | bytes 6291464 | tf_op jit(solution)/shard_map/ppermute | solution.py:353
  373.8 27.3 %collective-permute-start.25 = (bf16[512,2048]{1,0:T(8,128)(2,1)}, bf16[512,2048]{1,0:T(8,128)(2,1)S(1)}, u32[]{:S(2)}, u32[]{:S(2)}) collective-permute-start(bf16[512,2048]{1,0:T(8,128)(2,1)} %get-tuple-element.365), channel_id=1, source_target_pairs={{0,2},{1,5},{2,0},{3,7},{4,6},{5,1},{6,4},{7,3},{8,10},{9,13},{10,... | collective-permute-start | bytes 6291464 | tf_op jit(solution)/shard_map/ppermute | solution.py:349
  401.2 35.8 %collective-permute-start.26 = (bf16[512,2048]{1,0:T(8,128)(2,1)}, bf16[512,2048]{1,0:T(8,128)(2,1)S(1)}, u32[]{:S(2)}, u32[]{:S(2)}) collective-permute-start(bf16[512,2048]{1,0:T(8,128)(2,1)} %get-tuple-element.374), channel_id=1, source_target_pairs={{0,2},{1,5},{2,0},{3,7},{4,6},{5,1},{6,4},{7,3},{8,10},{9,13},{10,... | collective-permute-start | bytes 6291464 | tf_op jit(solution)/shard_map/ppermute | solution.py:349
  442.2 26.3 %collective-permute-start.28 = (bf16[4,4,64,2816]{3,2,1,0:T(8,128)(2,1)}, bf16[4,4,64,2816]{3,2,1,0:T(8,128)(2,1)}, u32[]{:S(2)}, u32[]{:S(2)}) collective-permute-start(bf16[4,4,64,2816]{3,2,1,0:T(8,128)(2,1)} %get-tuple-element.398), channel_id=1, source_target_pairs={{0,1},{1,0},{2,3},{3,2},{4,5},{5,4},{6,7},{7,6},{8,9},{9,8},{10,11... | collective-permute-start | bytes 17301512 | tf_op jit(solution)/shard_map/ppermute | solution.py:357
  442.2 26.2 %collective-permute-start.27 = (bf16[512,2048]{1,0:T(8,128)(2,1)}, bf16[512,2048]{1,0:T(8,128)(2,1)S(1)}, u32[]{:S(2)}, u32[]{:S(2)}) collective-permute-start(bf16[512,2048]{1,0:T(8,128)(2,1)} %add_convert_fusion.3), channel_id=1, source_target_pairs={{0,4},{1,3},{2,6},{3,1},{4,0},{5,7},{6,2},{7,5},{8,12},{9,11},{10,... | collective-permute-start | bytes 6291464 | tf_op jit(solution)/shard_map/ppermute | solution.py:353
  492.8 31.1 %all-to-all-start.3 = ((bf16[8,512,256]{2,1,0:T(8,128)(2,1)}), bf16[8,512,256]{2,1,0:T(8,128)(2,1)}, u32[]{:S(2)}, u32[]{:S(2)}) async-start(bf16[8,512,256]{2,1,0:T(8,128)(2,1)} %get-tuple-element.414), calls=%async_computation.3 | async-start | bytes 4194304 | tf_op jit(solution)/shard_map/all_to_all | solution.py:1368
  524.0 87.2 %collective-permute-start.31 = (bf16[4,256,2048]{2,1,0:T(8,128)(2,1)}, bf16[4,256,2048]{2,1,0:T(8,128)(2,1)}, u32[]{:S(2)}, u32[]{:S(2)}) collective-permute-start(bf16[4,256,2048]{2,1,0:T(8,128)(2,1)} %get-tuple-element.421), channel_id=1, source_target_pairs={{0,1},{1,0},{2,3},{3,2},{4,5},{5,4},{6,7},{7,6},{8,9},{9,8},{10,11... | collective-permute-start | bytes 12582920 | tf_op jit(solution)/shard_map/ppermute | solution.py:357
  524.0 87.2 %collective-permute-start.30 = (bf16[512,2048]{1,0:T(8,128)(2,1)}, bf16[512,2048]{1,0:T(8,128)(2,1)}, u32[]{:S(2)}, u32[]{:S(2)}) collective-permute-start(bf16[512,2048]{1,0:T(8,128)(2,1)} %get-tuple-element.435.refs_0_), channel_id=1, source_target_pairs={{0,2},{1,5},{2,0},{3,7},{4,6},{5,1},{6,4},{7,3},{8,10},{9,13},{10,... | collective-permute-start | bytes 6291464 | tf_op jit(solution)/shard_map/ppermute | solution.py:349
  527.0 84.2 %collective-permute-start.32 = (bf16[2,176,2048]{2,1,0:T(8,128)(2,1)S(1)}, bf16[2,176,2048]{2,1,0:T(8,128)(2,1)S(1)}, u32[]{:S(2)}, u32[]{:S(2)}) collective-permute-start(bf16[2,176,2048]{2,1,0:T(8,128)(2,1)S(1)} %fusion.5), channel_id=1, source_target_pairs={{0,8},{8,0},{16,24},{24,16},{1,9},{9,1},{17,25},{25,17},{2,10},{10... | collective-permute-start | bytes 4325384 | tf_op jit(solution)/shard_map/ppermute | solution.py:1371
  615.0 35.6 %collective-permute-start.33 = (bf16[512,2048]{1,0:T(8,128)(2,1)S(1)}, bf16[512,2048]{1,0:T(8,128)(2,1)}, u32[]{:S(2)}, u32[]{:S(2)}) collective-permute-start(bf16[512,2048]{1,0:T(8,128)(2,1)S(1)} %copy-done.20), channel_id=1, source_target_pairs={{0,4},{1,3},{2,6},{3,1},{4,0},{5,7},{6,2},{7,5},{8,12},{9,11},{10,... | collective-permute-start | bytes 6291464 | tf_op jit(solution)/shard_map/ppermute | solution.py:353
  616.4 34.1 %collective-permute-start.35 = (bf16[512,2048]{1,0:T(8,128)(2,1)S(1)}, bf16[512,2048]{1,0:T(8,128)(2,1)}, u32[]{:S(2)}, u32[]{:S(2)}) collective-permute-start(bf16[512,2048]{1,0:T(8,128)(2,1)S(1)} %copy-done.20), channel_id=1, source_target_pairs={{0,1},{1,0},{2,3},{3,2},{4,5},{5,4},{6,7},{7,6},{8,9},{9,8},{10,11... | collective-permute-start | bytes 6291464 | tf_op jit(solution)/shard_map/ppermute | solution.py:357
  616.4 34.1 %collective-permute-start.36 = (bf16[512,2048]{1,0:T(8,128)(2,1)}, bf16[512,2048]{1,0:T(8,128)(2,1)}, u32[]{:S(2)}, u32[]{:S(2)}) collective-permute-start(bf16[512,2048]{1,0:T(8,128)(2,1)} %collective-permute-done.30.refs_1_), channel_id=1, source_target_pairs={{0,1},{1,0},{2,3},{3,2},{4,5},{5,4},{6,7},{7,6},{8,9},{9,8},{10,11... | collective-permute-start | bytes 6291464 | tf_op jit(solution)/shard_map/ppermute | solution.py:357
  617.0 33.6 %collective-permute-start.34 = (bf16[176,2048]{1,0:T(8,128)(2,1)}, bf16[176,2048]{1,0:T(8,128)(2,1)S(1)}, u32[]{:S(2)}, u32[]{:S(2)}) collective-permute-start(bf16[176,2048]{1,0:T(8,128)(2,1)} %fusion.15), channel_id=1, source_target_pairs={{0,16},{8,24},{16,0},{24,8},{1,17},{9,25},{17,1},{25,9},{2,18},{10... | collective-permute-start | bytes 2162696 | tf_op jit(solution)/shard_map/ppermute | solution.py:1390
  652.1 36.5 %collective-permute-start.38 = (bf16[512,2048]{1,0:T(8,128)(2,1)}, bf16[512,2048]{1,0:T(8,128)(2,1)}, u32[]{:S(2)}, u32[]{:S(2)}) collective-permute-start(bf16[512,2048]{1,0:T(8,128)(2,1)} %collective-permute-done.33.refs_2_), channel_id=1, source_target_pairs={{0,1},{1,0},{2,3},{3,2},{4,5},{5,4},{6,7},{7,6},{8,9},{9,8},{10,11... | collective-permute-start | bytes 6291464 | tf_op jit(solution)/shard_map/ppermute | solution.py:357
  652.2 36.4 %all-to-all-start.4 = ((bf16[4,64,2816]{2,1,0:T(8,128)(2,1)}), bf16[4,64,2816]{2,1,0:T(8,128)(2,1)S(1)}, u32[]{:S(2)}, u32[]{:S(2)}) async-start(bf16[4,64,2816]{2,1,0:T(8,128)(2,1)} %bitcast.153), calls=%async_computation.5 | async-start | bytes 2883584 | tf_op jit(solution)/shard_map/all_to_all | solution.py:1401
  655.8 236.7 %all-gather.7.cloned.1.call-start = ((), (), s32[]{:S(2)}) async-start(), calls=%async_computation.10 | async-start | bytes 7208960 | tf_op jit(solution)/shard_map/all_gather | solution.py:1411
  656.0 32.6 %collective-permute-start.37 = (bf16[176,2048]{1,0:T(8,128)(2,1)S(1)}, bf16[176,2048]{1,0:T(8,128)(2,1)S(1)}, u32[]{:S(2)}, u32[]{:S(2)}) collective-permute-start(bf16[176,2048]{1,0:T(8,128)(2,1)S(1)} %fusion.6), channel_id=1, source_target_pairs={{0,16},{8,24},{16,0},{24,8},{1,17},{9,25},{17,1},{25,9},{2,18},{10... | collective-permute-start | bytes 2162696 | tf_op jit(solution)/shard_map/ppermute | solution.py:1400
  691.6 101.2 %collective-permute-start.41 = (bf16[512,2048]{1,0:T(8,128)(2,1)}, bf16[512,2048]{1,0:T(8,128)(2,1)}, u32[]{:S(2)}, u32[]{:S(2)}) collective-permute-start(bf16[512,2048]{1,0:T(8,128)(2,1)} %collective-permute-done.30.refs_1_), channel_id=1, source_target_pairs={{0,4},{1,3},{2,6},{3,1},{4,0},{5,7},{6,2},{7,5},{8,12},{9,11},{10,... | collective-permute-start | bytes 6291464 | tf_op jit(solution)/shard_map/ppermute | solution.py:353
  693.4 50.6 %collective-permute-start.40 = (bf16[256,2048]{1,0:T(8,128)(2,1)}, bf16[256,2048]{1,0:T(8,128)(2,1)}, u32[]{:S(2)}, u32[]{:S(2)}) collective-permute-start(bf16[256,2048]{1,0:T(8,128)(2,1)} %get-tuple-element.475), channel_id=1, source_target_pairs={{0,2},{1,5},{2,0},{3,7},{4,6},{5,1},{6,4},{7,3},{8,10},{9,13},{10,... | collective-permute-start | bytes 3145736 | tf_op jit(solution)/shard_map/ppermute | solution.py:349
  694.8 98.0 %collective-permute-start.42 = (bf16[2,176,2048]{2,1,0:T(8,128)(2,1)S(1)}, bf16[2,176,2048]{2,1,0:T(8,128)(2,1)}, u32[]{:S(2)}, u32[]{:S(2)}) collective-permute-start(bf16[2,176,2048]{2,1,0:T(8,128)(2,1)S(1)} %maximum_select_fusion.2), channel_id=1, source_target_pairs={{0,8},{8,0},{16,24},{24,16},{1,9},{9,1},{17,25},{25,17},{2,10},{10... | collective-permute-start | bytes 4325384 | tf_op jit(solution)/shard_map/ppermute | solution.py:1415
  694.8 51.6 %collective-permute-start.39 = (bf16[256,2048]{1,0:T(8,128)(2,1)}, bf16[256,2048]{1,0:T(8,128)(2,1)}, u32[]{:S(2)}, u32[]{:S(2)}) collective-permute-start(bf16[256,2048]{1,0:T(8,128)(2,1)} %get-tuple-element.474), channel_id=1, source_target_pairs={{0,2},{1,5},{2,0},{3,7},{4,6},{5,1},{6,4},{7,3},{8,10},{9,13},{10,... | collective-permute-start | bytes 3145736 | tf_op jit(solution)/shard_map/ppermute | solution.py:349
  792.8 17.8 %collective-permute-start.43 = (bf16[512,2048]{1,0:T(8,128)(2,1)}, bf16[512,2048]{1,0:T(8,128)(2,1)}, u32[]{:S(2)}, u32[]{:S(2)}) collective-permute-start(bf16[512,2048]{1,0:T(8,128)(2,1)} %collective-permute-done.41.refs_3_), channel_id=1, source_target_pairs={{0,1},{1,0},{2,3},{3,2},{4,5},{5,4},{6,7},{7,6},{8,9},{9,8},{10,11... | collective-permute-start | bytes 6291464 | tf_op jit(solution)/shard_map/ppermute | solution.py:357
  843.0 17.9 %collective-permute-start.47 = (bf16[64,5120]{1,0:T(8,128)(2,1)}, bf16[64,5120]{1,0:T(8,128)(2,1)}, u32[]{:S(2)}, u32[]{:S(2)}) collective-permute-start(bf16[64,5120]{1,0:T(8,128)(2,1)} %get-tuple-element.493), channel_id=1, source_target_pairs={{0,8},{8,16},{1,9},{9,17},{2,10},{10,18},{3,11},{11,19},{4,12},{12... | collective-permute-start | bytes 1966088 | tf_op jit(solution)/shard_map/ppermute | solution.py:409
  849.8 42.7 %all-to-all-start.5 = ((bf16[8,512,384]{2,1,0:T(8,128)(2,1)}), bf16[8,512,384]{2,1,0:T(8,128)(2,1)}, u32[]{:S(2)}, u32[]{:S(2)}) async-start(bf16[8,512,384]{2,1,0:T(8,128)(2,1)} %get-tuple-element.481.refs_8_), calls=%async_computation.6 | async-start | bytes 6291456 | tf_op jit(solution)/shard_map/all_to_all | solution.py:1422
  854.5 61.6 %collective-permute-start.51 = (bf16[512,2048]{1,0:T(8,128)(2,1)}, bf16[512,2048]{1,0:T(8,128)(2,1)}, u32[]{:S(2)}, u32[]{:S(2)}) collective-permute-start(bf16[512,2048]{1,0:T(8,128)(2,1)} %get-tuple-element.486), channel_id=1, source_target_pairs={{0,2},{1,5},{2,0},{3,7},{4,6},{5,1},{6,4},{7,3},{8,10},{9,13},{10,... | collective-permute-start | bytes 6291464 | tf_op jit(solution)/shard_map/ppermute | solution.py:349
  863.6 20.8 %collective-permute-start.49 = (bf16[64,5120]{1,0:T(8,128)(2,1)}, bf16[64,5120]{1,0:T(8,128)(2,1)S(1)}, u32[]{:S(2)}, u32[]{:S(2)}) collective-permute-start(bf16[64,5120]{1,0:T(8,128)(2,1)} %get-tuple-element.497), channel_id=1, source_target_pairs={{0,8},{8,16},{16,24},{1,9},{9,17},{17,25},{2,10},{10,18},{18,26},{... | collective-permute-start | bytes 1966088 | tf_op jit(solution)/shard_map/ppermute | solution.py:409
  873.4 69.3 %collective-permute-start.52 = (bf16[512,2048]{1,0:T(8,128)(2,1)}, bf16[512,2048]{1,0:T(8,128)(2,1)}, u32[]{:S(2)}, u32[]{:S(2)}) collective-permute-start(bf16[512,2048]{1,0:T(8,128)(2,1)} %get-tuple-element.492), channel_id=1, source_target_pairs={{0,2},{1,5},{2,0},{3,7},{4,6},{5,1},{6,4},{7,3},{8,10},{9,13},{10,... | collective-permute-start | bytes 6291464 | tf_op jit(solution)/shard_map/ppermute | solution.py:349
  892.5 49.1 %all-to-all-start.6 = ((bf16[8,64,384]{2,1,0:T(8,128)(2,1)}), bf16[8,64,384]{2,1,0:T(8,128)(2,1)}, u32[]{:S(2)}, u32[]{:S(2)}) async-start(bf16[8,64,384]{2,1,0:T(8,128)(2,1)} %bitcast.111), calls=%async_computation.7 | async-start | bytes 786432 | tf_op jit(solution)/shard_map/all_to_all | solution.py:1441
  942.7 43.8 %collective-permute-start.59 = (bf16[512,2048]{1,0:T(8,128)(2,1)}, bf16[512,2048]{1,0:T(8,128)(2,1)}, u32[]{:S(2)}, u32[]{:S(2)}) collective-permute-start(bf16[512,2048]{1,0:T(8,128)(2,1)} %add_convert_fusion.2), channel_id=1, source_target_pairs={{0,4},{1,3},{2,6},{3,1},{4,0},{5,7},{6,2},{7,5},{8,12},{9,11},{10,... | collective-permute-start | bytes 6291464 | tf_op jit(solution)/shard_map/ppermute | solution.py:353
  943.3 17.1 %collective-permute-start.53 = (bf16[64,5120]{1,0:T(8,128)(2,1)S(1)}, bf16[64,5120]{1,0:T(8,128)(2,1)S(1)}, u32[]{:S(2)}, u32[]{:S(2)}) collective-permute-start(bf16[64,5120]{1,0:T(8,128)(2,1)S(1)} %pad_maximum_fusion.3.refs_0_), channel_id=1, source_target_pairs={{0,8},{8,16},{16,24},{1,9},{9,17},{17,25},{2,10},{10,18},{18,26},{... | collective-permute-start | bytes 1966088 | tf_op jit(solution)/shard_map/ppermute | solution.py:421
  946.9 18.6 %collective-permute-start.54 = (bf16[64,5120]{1,0:T(8,128)(2,1)S(1)}, bf16[64,5120]{1,0:T(8,128)(2,1)S(1)}, u32[]{:S(2)}, u32[]{:S(2)}) collective-permute-start(bf16[64,5120]{1,0:T(8,128)(2,1)S(1)} %pad_maximum_fusion.3.refs_0_), channel_id=1, source_target_pairs={{8,0},{16,8},{24,16},{9,1},{17,9},{25,17},{10,2},{18,10},{26,18},{... | collective-permute-start | bytes 1966088 | tf_op jit(solution)/shard_map/ppermute | solution.py:422
  966.1 18.3 %collective-permute-start.56 = (bf16[64,5120]{1,0:T(8,128)(2,1)S(1)}, bf16[64,5120]{1,0:T(8,128)(2,1)S(1)}, u32[]{:S(2)}, u32[]{:S(2)}) collective-permute-start(bf16[64,5120]{1,0:T(8,128)(2,1)S(1)} %collective-permute-done.54.refs_4_), channel_id=1, source_target_pairs={{8,0},{16,8},{9,1},{17,9},{10,2},{18,10},{11,3},{19,11},{12,4},{20... | collective-permute-start | bytes 1966088 | tf_op jit(solution)/shard_map/ppermute | solution.py:422
  (94 other events, 1064.0 us)
Sparse Core Ops, SparseCore 0:
  113.9 107.2 all-gather.4
  476.8 134.4 reduce-scatter.1
  695.6 125.3 all-gather.6

commit v6 on v5

--- a/solution.py
+++ b/solution.py
@@ -1353,7 +1353,7 @@
     db_passed = send_second(db_pass)
     gu_got = send_sibling(gu_give)
     dn_keep, dn_give = grad_dn(core, hid_rows, [dy, dy_first, dy_second, dy_far])
-    db_passed, gu_got, dn_keep, dn_give = fence(db_passed, gu_got, dn_keep, dn_give)
+    gu_got, dn_keep, dn_give = fence(gu_got, dn_keep, dn_give)
     gu_sum = (gu_keep.astype(F32) + gu_got.astype(F32)).astype(BF)
     gu_sum, db_passed, dn_give = fence(gu_sum, db_passed, dn_give)
     gu_z = lax.psum_scatter(
@@ -1366,9 +1366,6 @@
     )
     d_send, d_branch, dn_got = fence(d_send, d_branch, dn_got)
     d_heads = lax.all_to_all(d_send, "sp", 0, 0, tiled=True).reshape(length, share)
-    dn_parts = [part.reshape(2, 2, dn_keep.shape[0] // planes, width) for part in (dn_keep, dn_got)]
-    dn_own = pick_sum(dn_parts, plane & 1, 1)
-    dn_move = lax.ppermute(pick_sum(dn_parts, 1 - (plane & 1), 1).astype(BF), "dp", LINE_NEAR)
     wo_keep, wo_give = grad_wo(core, attn_tok, d_branch)
     d_heads, wo_keep, wo_give, normed = fence(d_heads, wo_keep, wo_give, normed)
 
@@ -1379,45 +1376,42 @@
     wo_got = send_sibling(wo_give)
     a_first = send_first(normed)
     bwd = back_call(d_heads, turns[0], turns[1], out=out_heads)
-    d_heads, a_first, wo_got, normed, dn_move, *bwd = fence(d_heads, a_first, wo_got, normed, dn_move, *bwd)
-
-    dn_own = dn_own + dn_move.astype(F32)
-    far_side = plane // 2
-    dn_move = pick(dn_own, 1 - far_side).astype(BF)
-    d_heads, normed, a_first, dn_move = fence(d_heads, normed, a_first, dn_move)
+    d_heads, a_first, wo_got, normed, *bwd = fence(d_heads, a_first, wo_got, normed, *bwd)
     a_second = send_second(normed)
     a_theirs = [send_sibling(normed), send_sibling(a_first)]
-    dn_move = lax.ppermute(dn_move, "dp", LINE_FAR)
     bwd = back_call(d_heads, turns[1], turns[2], before=bwd)
+    dn_parts = [part.reshape(2, 2, dn_keep.shape[0] // planes, width) for part in (dn_keep, dn_got)]
+    dn_move = pick_sum(dn_parts, 1 - (plane & 1), 1).astype(BF)
     d_heads, gu_z, a_second, dn_move, *moves = fence(d_heads, gu_z, a_second, dn_move, *a_theirs, *bwd)
     a_theirs, bwd = moves[:2], moves[2:]
 
     def wo_part(place):
         return pick(wo_keep, place).astype(F32) + pick(wo_got, place).astype(F32)
 
-    dn_z = (pick(dn_own, far_side) + dn_move.astype(F32)).astype(BF)
-    d_heads, dn_z, gu_z, a_second = fence(d_heads, dn_z, gu_z, a_second)
-    dn_move = lax.ppermute(dn_z, "dp", LINE_FAR)
+    dn_move = lax.ppermute(dn_move, "dp", LINE_NEAR)
     gu_z = lax.all_to_all(gu_z, "sp", 0, 0, axis_index_groups=SAME_CORE, tiled=True)
     a_theirs.append(send_sibling(a_second))
     bwd = back_call(d_heads, turns[2], turns[3], before=bwd)
     d_heads, gu_z, a_first, dn_move, *moves = fence(d_heads, gu_z, a_first, dn_move, *a_theirs, *bwd)
     a_theirs, bwd = moves[:3], moves[3:]
 
-    dn_pair = jnp.where(far_side == 0, jnp.stack([dn_z, dn_move]), jnp.stack([dn_move, dn_z]))
+    dn_own = pick_sum(dn_parts, plane & 1, 1) + dn_move.astype(F32)
+    dn_move = pick(dn_own, 1 - plane // 2).astype(BF)
     wo_first = wo_part(chip ^ (first_mask // 2)).astype(BF)
     wo_far = wo_part(chip ^ 3).astype(BF)
-    d_heads, gu_z, a_first, wo_first, wo_far, dn_pair = fence(d_heads, gu_z, a_first, wo_first, wo_far, dn_pair)
+    d_heads, gu_z, a_first, wo_first, wo_far, dn_move = fence(d_heads, gu_z, a_first, wo_first, wo_far, dn_move)
     gu_all = lax.all_gather(gu_z, "dp", axis=0, tiled=False)
     a_far = send_second(a_first)
     wo_far = send_first(wo_far)
     wo_first = send_first(wo_first)
-    dn_other = lax.ppermute(dn_pair, "dp", LINE_NEAR)
+    dn_move = lax.ppermute(dn_move, "dp", LINE_FAR)
     bwd = back_call(d_heads, turns[3], turns[4], before=bwd)
     wo_pass = (wo_part(chip ^ (second_mask // 2)) + wo_far.astype(F32)).astype(BF)
-    dp_heads, wo_first, wo_pass, a_far, dn_other = fence(bwd[0], wo_first, wo_pass, a_far, dn_other)
+    dn_z = (pick(dn_own, plane // 2) + dn_move.astype(F32)).astype(BF)
+    dp_heads, wo_first, wo_pass, a_far, dn_z = fence(bwd[0], wo_first, wo_pass, a_far, dn_z)
 
     wo_passed = send_second(wo_pass)
+    dn_all = lax.all_gather(dn_z, "dp", axis=0, tiled=False)
     a_theirs.append(send_sibling(a_far))
     back = lax.all_to_all(dp_heads, "sp", 0, 0, tiled=True)
     grad_wq = grad_qkv(places, [normed, a_first, a_second, a_far] + list(a_theirs), dp_heads, planes)
@@ -1431,34 +1425,35 @@
         y_far, y_first, *moves = fence(y_far, y_first, *moves)
         moves = line_scatter_move(moves, step)
         if step == 1:
+            back, *moves = fence(back, *moves)
+        elif step == 2:
             y_got_far = send_first(y_far)
-        elif step == 2:
+        elif step == 3:
             y_got_first = send_first(y_first)
         moves = fence(*moves)
     last_z = line_scatter_end(last_parts, moves, 0)
     wq_z = last_z[:, :split].reshape(quarter, devices, split // devices).transpose(1, 0, 2)
-    wq_z, wo_z, back, gu_all = fence(wq_z, last_z[:, split:], back, gu_all)
+    wq_z, wo_z, gu_all, y_got_far = fence(wq_z, last_z[:, split:], gu_all, y_got_far)
     wq_z = lax.all_to_all(wq_z, "sp", 0, 0, tiled=True)
     grad_tokens = in_back(places, back, x_bf, inv_one, attn_gain, d_resid, qkv_parts).reshape(tokens.shape)
     y_pass = (second[4].astype(F32) + y_got_far.astype(F32)).astype(BF)
     last_z = jnp.concatenate([wq_z.transpose(1, 0, 2).reshape(quarter, split), wo_z], axis=1)
-    last_z, grad_tokens, y_pass, y_got_first = fence(last_z, grad_tokens, y_pass, y_got_first)
+    last_z, grad_tokens, y_pass = fence(last_z, grad_tokens, y_pass)
     y_passed = send_second(y_pass)
     last_steps = [(last_z, last_z)]
     outs = []
     for step in range(1, planes):
         last_steps.append(line_gather_move(last_steps[-1], step))
         if step == 1:
-            low, high = jnp.stack([dn_pair, dn_other], axis=1), jnp.stack([dn_other, dn_pair], axis=1)
-            outs.append(jnp.where((plane & 1) == 0, low, high).astype(F32).reshape(w_down.shape))
-        elif step == 2:
             outs += spread(gu_all, w_gate_up, g_mlp.astype(F32).reshape(share, 1))
         if step == planes - 1:
             y_sum = own[4].astype(F32) + y_got_first.astype(F32) + y_passed.astype(F32)
             outs.append((residual + y_sum).astype(BF).reshape(tokens.shape))
+            break
         moves = fence(*last_steps[-1], *outs)
         last_steps[-1], outs = tuple(moves[:2]), list(moves[2:])
-    grad_w_down, grad_w_gate_up, grad_g_mlp, output = outs
+    grad_w_gate_up, grad_g_mlp, output = outs
+    grad_w_down = dn_all.astype(F32).reshape(w_down.shape)
     grad_w_qkv, grad_g_attn, grad_w_out = spread_last(last_steps, w_qkv, g_attn.astype(F32).reshape(share, 1), width)
     return (
         output,

time: 1020 us -> 961 us (0.942)
  waiting for transfers between devices: 359 us -> 230 us
  starting transfers between devices: 96.6 us -> 157 us
  Pallas kernels: 413 us -> 424 us
    ppermute x3 -> x1, waiting for transfers between devices: 113 us -> 4.64 us  [fast_body(): dn_move = lax.ppermute(dn_move, 'dp', LINE_NEAR)]
    ppermute x11, starting transfers between devices: 12.8 us -> 41.1 us  [send_first(): return lax.ppermute(x, 'sp', FIRST)]
    ppermute x11, waiting for transfers between devices: 41.3 us -> 16.8 us  [send_first(): return lax.ppermute(x, 'sp', FIRST)]
    ppermute x3, waiting for transfers between devices: 26.4 us -> 6.4 us  [line_scatter_move(): right = lax.ppermute(sends[0], 'dp', [(i, i + 1) for i in range(step)])]
    ppermute x1, starting transfers between devices: 0.01 us -> 16.5 us  [fast_body(): dn_move = lax.ppermute(dn_move, 'dp', LINE_FAR)]
    all_to_all x1, waiting for transfers between devices: 7.2 us -> 20.7 us  [fast_body(): wq_z = lax.all_to_all(wq_z, 'sp', 0, 0, tiled=True)]
    ppermute x3, waiting for transfers between devices: 19.5 us -> 31.6 us  [line_gather_move(): lax.ppermute(got[1], 'dp', [(i + 1, i) for i in range(planes - step)])]
    ppermute x1, waiting for transfers between devices: 12.3 us -> 24.4 us  [fast_body(): dn_move = lax.ppermute(dn_move, 'dp', LINE_FAR)]
  transfers between devices with their start and end apart: 70 -> 69, of which waited for: 30 -> 23; matrix products, arithmetic and copies ran while one was open for 7% -> 8% of each run, Pallas kernels for 39% -> 43%
where the time goes in v6:
time: 961 us; the launch traced here: 955 us
  Pallas kernels  424 us (44%)
  waiting for transfers between devices  230 us (24%)
  starting transfers between devices  157 us (16%)
  other arithmetic  83.3 us (9%)
  local copies, waits for them, and re-layouts  44.1 us (5%)
  between operations  15.6 us (2%)
    pallas_call x4, Pallas kernels, attend_back(): pl.pallas_call(functools.partial(attend_back_kernel, heads=heads, start=s...  120 us
    pallas_call x4, Pallas kernels, ffn(): pl.pallas_call(functools.partial(ffn_kernel, cuts=cuts), in_specs=[hbm] *...  103 us
    pallas_call x3, Pallas kernels, attend(): pl.pallas_call(functools.partial(attend_kernel, heads=heads, start=start,...  53 us
    ppermute x13, waiting for transfers between devices, send_second(): return lax.ppermute(x, 'sp', SECOND)  52.2 us
    ppermute x11, starting transfers between devices, send_first(): return lax.ppermute(x, 'sp', FIRST)  41.1 us
    unnamed x122, local copies, waits for them, and re-layouts  37.3 us
    pallas_call x1, Pallas kernels, grad_gu(): pl.pallas_call(functools.partial(grad_gu_kernel, count=count), grid_spec=...  34.5 us
    ppermute x3, waiting for transfers between devices, line_gather_move(): lax.ppermute(got[1], 'dp', [(i + 1, i) for i in range(planes - step)])  31.6 us
  transfers between devices with their start and end apart: 69, of which 23 were waited for; matrix products, arithmetic and copies ran while one was open for 8% of the time, Pallas kernels for 43%

profile of v6, /device:TPU:0, one launch (start us, length us, event | category | flops | bytes accessed | tf_op | source)
XLA Modules:
  0.0 954.5 jit_solution(2730922964566379990)
XLA Ops:
  27.8 12.1 %collective-permute-done.3.refs_1_.refs_9_ = bf16[256,2560]{1,0:T(8,128)(2,1)S(1)} collective-permute-done((bf16[256,2560]{1,0:T(8,128)(2,1)S(1)}, bf16[256,2560]{1,0:T(8,128)(2,1)S(1)}, u32[]{:S(2)}, u32[]{:S(2)}) %collective-permute-start.3) | collective-permute-done | bytes 1310752 | tf_op jit(solution)/shard_map/ppermute | solution.py:349
  42.5 7.5 fusion.15
  61.3 14.0 %collective-permute-done.7.refs_3_.refs_11_ = bf16[256,2560]{1,0:T(8,128)(2,1)S(1)} collective-permute-done((bf16[256,2560]{1,0:T(8,128)(2,1)S(1)}, bf16[256,2560]{1,0:T(8,128)(2,1)S(1)}, u32[]{:S(2)}, u32[]{:S(2)}) %collective-permute-start.7) | collective-permute-done | bytes 1310752 | tf_op jit(solution)/shard_map/ppermute | solution.py:353
  83.8 9.8 %all-gather.7.cloned.1.call-start = ((), (), s32[]{:S(2)}) async-start(), calls=%async_computation.9 | async-start | bytes 7208960 | tf_op jit(solution)/shard_map/all_gather | solution.py:1299
  98.4 18.3 %project.1 = (bf16[8,512,384]{2,1,0:T(8,128)(2,1)}, bf16[512,2048]{1,0:T(8,128)(2,1)}, f32[512,1]{1,0:T(8,128)S(1)}) custom-call(s32[8]{0:T(128)S(1)} %stack.59.place_ref, bf16[512,2048]{1,0:T(8,128)(2,1)} %bitcast.137, f32[1,2048]{1,0:T(1,128)S(1)} %get-tuple-element.534.gain_ref, f32[512,128]{1,0:T(8,128)S(1)} %pad_maximum_fusion.4.cos_ref, ...), custom_call_target="tpu_custom_call" | custom-call | flops 1 | bytes 1 | tf_op jit(solution)/shard_map/project/pallas_call | solution.py:736
  123.1 8.3 maximum_select_fusion.refs_3_
  131.4 27.6 %all-to-all-done = bf16[8,512,384]{2,1,0:T(8,128)(2,1)S(1)} async-done(((bf16[8,512,384]{2,1,0:T(8,128)(2,1)}), bf16[8,512,384]{2,1,0:T(8,128)(2,1)S(1)}, u32[]{:S(2)}, u32[]{:S(2)}) %all-to-all-start) | async-done | bytes 3145760 | tf_op jit(solution)/shard_map/all_to_all | solution.py:1304
  160.2 29.7 %attend.3 = (f32[4096,256]{1,0:T(8,128)}, bf16[8,512,256]{2,1,0:T(8,128)(2,1)S(1)}, f32[8,4,512]{2,1,0:T(4,128)S(1)}) custom-call(s32[1]{0:T(128)} %bitcast.14.zeros_ref, bf16[4096,384]{1,0:T(8,128)(2,1)S(1)} %bitcast.111, bf16[4096,384]{1,0:T(8,128)(2,1)S(1)} %bitcast.112), custom_call_target="tpu_custom_call" | custom-call | flops 1 | bytes 1 | tf_op jit(solution)/shard_map/attend/pallas_call | solution.py:1056
  196.6 16.2 %attend.4 = (f32[4096,256]{1,0:T(8,128)}, bf16[8,512,256]{2,1,0:T(8,128)(2,1)S(1)}, f32[8,4,512]{2,1,0:T(4,128)S(1)}) custom-call(s32[1]{0:T(128)} %bitcast.14.zeros_ref, bf16[4096,384]{1,0:T(8,128)(2,1)S(1)} %bitcast.113, bf16[4096,384]{1,0:T(8,128)(2,1)S(1)} %bitcast.114, ...), custom_call_target="tpu_custom_call", output_to_operand_aliasing={{0}: (3, {}), {1}: (4, {}), {2}: (5, {})} | custom-call | flops 1 | bytes 1 | tf_op jit(solution)/shard_map/attend/pallas_call | solution.py:1056
  214.1 17.7 %collective-permute-done.14.refs_3_ = bf16[256,2048]{1,0:T(8,128)(2,1)S(1)} collective-permute-done((bf16[256,2048]{1,0:T(8,128)(2,1)}, bf16[256,2048]{1,0:T(8,128)(2,1)S(1)}, u32[]{:S(2)}, u32[]{:S(2)}) %collective-permute-start.14) | collective-permute-done | bytes 1048608 | tf_op jit(solution)/shard_map/ppermute | solution.py:353
  236.8 7.1 attend.5
  258.5 6.1 join.1
  267.7 15.2 %all-to-all-done.2.attn_ref.keep_ref.give_ref = bf16[8,512,256]{2,1,0:T(8,128)(2,1)S(1)} async-done(((bf16[8,512,256]{2,1,0:T(8,128)(2,1)}), bf16[8,512,256]{2,1,0:T(8,128)(2,1)S(1)}, u32[]{:S(2)}, u32[]{:S(2)}) %all-to-all-start.2) | async-done | bytes 2097184 | tf_op jit(solution)/shard_map/all_to_all | solution.py:1322
  284.3 11.9 %out_proj.1 = (f32[512,2048]{1,0:T(8,128)}, f32[512,1]{1,0:T(8,128)}, bf16[512,2048]{1,0:T(8,128)(2,1)}) custom-call(s32[8]{0:T(128)} %copy-done.25, bf16[8,512,256]{2,1,0:T(8,128)(2,1)} %copy-done.1, bf16[512,2048]{1,0:T(8,128)(2,1)} %bitcast.138, f32[1,2048]{1,0:T(1,128)} %get-tuple-element.533.gain_ref, bf16[256,2048]{1,0:T(8,128)(2,1)} %refs_0_.1, ...), custom_call_target="tpu_custom_call" | custom-call | flops 1 | bytes 1 | tf_op jit(solution)/shard_map/out_proj/pallas_call | solution.py:790
  297.3 25.7 %ffn.4 = (bf16[512,1408]{1,0:T(8,128)(2,1)}, bf16[512,1408]{1,0:T(8,128)(2,1)}, bf16[512,1408]{1,0:T(8,128)(2,1)}, bf16[512,2048]{1,0:T(8,128)(2,1)}, bf16[512,2048]{1,0:T(8,128)(2,1)}) custom-call(bf16[512,2048]{1,0:T(8,128)(2,1)} %get-tuple-element.339.refs_0_.refs_4_, bf16[512,2048]{1,0:T(8,128)(2,1)} %multiply_bitcast_fusion.refs_1_.refs_4_.dy_ref, ...), custom_call_target="tpu_custom_call" | custom-call | flops 1 | bytes 1 | tf_op jit(solution)/shard_map/ffn/pallas_call | solution.py:597
  324.5 25.8 %ffn.5 = (bf16[512,1408]{1,0:T(8,128)(2,1)}, bf16[512,1408]{1,0:T(8,128)(2,1)}, bf16[512,1408]{1,0:T(8,128)(2,1)}, bf16[512,2048]{1,0:T(8,128)(2,1)}, bf16[512,2048]{1,0:T(8,128)(2,1)}) custom-call(bf16[512,2048]{1,0:T(8,128)(2,1)} %copy-done.29, bf16[512,2048]{1,0:T(8,128)(2,1)} %copy-done.35, bf16[2,2048,1408]{2,1,0:T(8,128)(2,1)} %bitcast.129, ...), custom_call_target="tpu_custom_call" | custom-call | flops 1 | bytes 1 | tf_op jit(solution)/shard_map/ffn/pallas_call | solution.py:597
  351.6 26.0 %ffn.6 = (bf16[512,1408]{1,0:T(8,128)(2,1)}, bf16[512,1408]{1,0:T(8,128)(2,1)}, bf16[512,1408]{1,0:T(8,128)(2,1)}, bf16[512,2048]{1,0:T(8,128)(2,1)}, bf16[512,2048]{1,0:T(8,128)(2,1)}) custom-call(bf16[512,2048]{1,0:T(8,128)(2,1)} %collective-permute-done.23.refs_0_.refs_2_.refs_6_, bf16[512,2048]{1,0:T(8,128)(2,1)} %copy-done.36, ...), custom_call_target="tpu_custom_call" | custom-call | flops 1 | bytes 1 | tf_op jit(solution)/shard_map/ffn/pallas_call | solution.py:597
  378.9 25.7 %ffn.7 = (bf16[512,1408]{1,0:T(8,128)(2,1)}, bf16[512,1408]{1,0:T(8,128)(2,1)}, bf16[512,1408]{1,0:T(8,128)(2,1)}, bf16[512,2048]{1,0:T(8,128)(2,1)}, bf16[512,2048]{1,0:T(8,128)(2,1)}) custom-call(bf16[512,2048]{1,0:T(8,128)(2,1)} %copy-done.30, bf16[512,2048]{1,0:T(8,128)(2,1)} %collective-permute-done.17.refs_1_.refs_7_, ...), custom_call_target="tpu_custom_call" | custom-call | flops 1 | bytes 1 | tf_op jit(solution)/shard_map/ffn/pallas_call | solution.py:597
  406.0 34.5 %grad_gu.1 = (bf16[4,4,64,2816]{3,2,1,0:T(8,128)(2,1)}, bf16[4,4,64,2816]{3,2,1,0:T(8,128)(2,1)}) custom-call(s32[1]{0:T(128)} %bitcast.20.core_ref, bf16[512,2048]{1,0:T(8,128)(2,1)} %get-tuple-element.339.refs_0_.refs_4_, bf16[512,2048]{1,0:T(8,128)(2,1)} %copy-done.29, bf16[512,2048]{1,0:T(8,128)(2,1)} %collective-permute-done.23.refs_0_.refs_2_.refs_6_, ...), custom_call_target="tpu_custom_call" | custom-call | flops 1 | bytes 1 | tf_op jit(solution)/shard_map/grad_gu/pallas_call | solution.py:638
  446.5 17.5 %grad_dn.1 = (bf16[704,2048]{1,0:T(8,128)(2,1)}, bf16[704,2048]{1,0:T(8,128)(2,1)}) custom-call(s32[1]{0:T(128)} %bitcast.20.core_ref, bf16[512,1408]{1,0:T(8,128)(2,1)} %get-tuple-element.390.refs_0_, bf16[512,1408]{1,0:T(8,128)(2,1)} %get-tuple-element.391.refs_1_, bf16[512,1408]{1,0:T(8,128)(2,1)} %get-tuple-element.392.refs_2_, ...), custom_call_target="tpu_custom_call" | custom-call | flops 1 | bytes 1 | tf_op jit(solution)/shard_map/grad_dn/pallas_call | solution.py:960
  464.1 6.9 add_convert_fusion
  473.3 14.8 %resid_back.1 = (f32[512,2048]{1,0:T(8,128)}, bf16[512,2048]{1,0:T(8,128)(2,1)}, bf16[8,512,256]{2,1,0:T(8,128)(2,1)}) custom-call(s32[8]{0:T(128)} %copy-done.25, bf16[512,2048]{1,0:T(8,128)(2,1)} %get-tuple-element.358.db_ref, bf16[512,2048]{1,0:T(8,128)(2,1)} %copy-done.51, bf16[512,2048]{1,0:T(8,128)(2,1)} %copy-done.52, ...), custom_call_target="tpu_custom_call" | custom-call | flops 1 | bytes 1 | tf_op jit(solution)/shard_map/resid_back/pallas_call | solution.py:836
  495.8 6.1 grad_wo.1
  501.9 18.9 %all-to-all-done.3 = bf16[8,512,256]{2,1,0:T(8,128)(2,1)} async-done(((bf16[8,512,256]{2,1,0:T(8,128)(2,1)}), bf16[8,512,256]{2,1,0:T(8,128)(2,1)}, u32[]{:S(2)}, u32[]{:S(2)}) %all-to-all-start.3) | async-done | bytes 2097184 | tf_op jit(solution)/shard_map/all_to_all | solution.py:1368
  521.4 28.8 %attend_back.4 = (bf16[8,512,384]{2,1,0:T(8,128)(2,1)}, f32[256,4096]{1,0:T(8,128)}, f32[8,4,512]{2,1,0:T(4,128)}) custom-call(s32[1]{0:T(128)} %bitcast.14.zeros_ref, bf16[4096,384]{1,0:T(8,128)(2,1)} %bitcast.117, bf16[4096,384]{1,0:T(8,128)(2,1)} %bitcast.118, bf16[4096,256]{1,0:T(8,128)(2,1)} %bitcast.22.do_ref, f32[8,4,512]{2,1,0:T(4,128)} %copy-done.19, ...), custom_call_target="tpu_custom_call" | custom-call | flops 1 | bytes 1 | tf_op jit(solution)/shard_map/attend_back/pallas_call | solution.py:1197
  555.0 24.2 %attend_back.5 = (bf16[8,512,384]{2,1,0:T(8,128)(2,1)}, f32[256,4096]{1,0:T(8,128)}, f32[8,4,512]{2,1,0:T(4,128)}) custom-call(s32[1]{0:T(128)} %bitcast.14.zeros_ref, bf16[4096,384]{1,0:T(8,128)(2,1)} %bitcast.119, bf16[4096,384]{1,0:T(8,128)(2,1)} %bitcast.120, bf16[4096,256]{1,0:T(8,128)(2,1)} %bitcast.22.do_ref, ...), custom_call_target="tpu_custom_call", output_to_operand_aliasing={{0}: (9, {})} | custom-call | flops 1 | bytes 1 | tf_op jit(solution)/shard_map/attend_back/pallas_call | solution.py:1197
  587.6 21.3 %attend_back.6 = (bf16[8,512,384]{2,1,0:T(8,128)(2,1)}, f32[256,4096]{1,0:T(8,128)}, f32[8,4,512]{2,1,0:T(4,128)}) custom-call(s32[1]{0:T(128)} %bitcast.14.zeros_ref, bf16[4096,384]{1,0:T(8,128)(2,1)} %bitcast.121, bf16[4096,384]{1,0:T(8,128)(2,1)} %bitcast.122, bf16[4096,256]{1,0:T(8,128)(2,1)} %bitcast.22.do_ref, ...), custom_call_target="tpu_custom_call", output_to_operand_aliasing={{0}: (9, {})} | custom-call | flops 1 | bytes 1 | tf_op jit(solution)/shard_map/attend_back/pallas_call | solution.py:1197
  608.9 4.6 collective-permute-done.35
  620.2 16.5 %collective-permute-start.40 = (bf16[176,2048]{1,0:T(8,128)(2,1)}, bf16[176,2048]{1,0:T(8,128)(2,1)}, u32[]{:S(2)}, u32[]{:S(2)}) collective-permute-start(bf16[176,2048]{1,0:T(8,128)(2,1)} %fusion.14), channel_id=1, source_target_pairs={{0,16},{8,24},{16,0},{24,8},{1,17},{9,25},{17,1},{25,9},{2,18},{10... | collective-permute-start | bytes 2162696 | tf_op jit(solution)/shard_map/ppermute | solution.py:1407
  638.8 45.5 %attend_back.7 = (bf16[8,512,384]{2,1,0:T(8,128)(2,1)}, f32[256,4096]{1,0:T(8,128)}, f32[8,4,512]{2,1,0:T(4,128)}) custom-call(s32[1]{0:T(128)} %bitcast.14.zeros_ref, bf16[4096,384]{1,0:T(8,128)(2,1)} %bitcast.123, bf16[4096,384]{1,0:T(8,128)(2,1)} %bitcast.124, bf16[4096,256]{1,0:T(8,128)(2,1)} %bitcast.22.do_ref, ...), custom_call_target="tpu_custom_call", output_to_operand_aliasing={{0}: (9, {})} | custom-call | flops 1 | bytes 1 | tf_op jit(solution)/shard_map/attend_back/pallas_call | solution.py:1197
  684.4 24.4 %collective-permute-done.40 = bf16[176,2048]{1,0:T(8,128)(2,1)} collective-permute-done((bf16[176,2048]{1,0:T(8,128)(2,1)}, bf16[176,2048]{1,0:T(8,128)(2,1)}, u32[]{:S(2)}, u32[]{:S(2)}) %collective-permute-start.40) | collective-permute-done | bytes 720928 | tf_op jit(solution)/shard_map/ppermute | solution.py:1407
  719.3 17.4 %collective-permute-done.42 = bf16[256,2048]{1,0:T(8,128)(2,1)} collective-permute-done((bf16[256,2048]{1,0:T(8,128)(2,1)S(1)}, bf16[256,2048]{1,0:T(8,128)(2,1)}, u32[]{:S(2)}, u32[]{:S(2)}) %collective-permute-start.42) | collective-permute-done | bytes 1048608 | tf_op jit(solution)/shard_map/ppermute | solution.py:353
  739.6 13.3 %grad_qkv.1 = bf16[4,64,3072]{2,1,0:T(8,128)(2,1)S(1)} custom-call(s32[8]{0:T(128)S(1)} %copy-done.26, bf16[512,2048]{1,0:T(8,128)(2,1)S(1)} %copy-done.21, bf16[512,2048]{1,0:T(8,128)(2,1)} %collective-permute-done.30.refs_1_, bf16[512,2048]{1,0:T(8,128)(2,1)} %collective-permute-done.32.refs_2_, bf16[512,2048]{1,0:T(8,128)(2,1)} %collective-permute-done.39.refs_3_, ...), custom_call_target="tpu_custom_call" | custom-call | flops 1 | bytes 1 | tf_op jit(solution)/shard_map/grad_qkv/pallas_call | solution.py:672
  753.9 12.7 %collective-permute-start.43 = (bf16[64,5120]{1,0:T(8,128)(2,1)}, bf16[64,5120]{1,0:T(8,128)(2,1)}, u32[]{:S(2)}, u32[]{:S(2)}) collective-permute-start(bf16[64,5120]{1,0:T(8,128)(2,1)} %get-tuple-element.467), channel_id=1, source_target_pairs={{0,8},{1,9},{2,10},{3,11},{4,12},{5,13},{6,14},{7,15}} | collective-permute-start | bytes 1966088 | tf_op jit(solution)/shard_map/ppermute | solution.py:409
  768.1 6.4 collective-permute-done.43
  776.9 5.2 collective-permute-start.45
  783.6 14.1 %collective-permute-start.50 = (bf16[512,2048]{1,0:T(8,128)(2,1)}, bf16[512,2048]{1,0:T(8,128)(2,1)}, u32[]{:S(2)}, u32[]{:S(2)}) collective-permute-start(bf16[512,2048]{1,0:T(8,128)(2,1)} %get-tuple-element.473), channel_id=1, source_target_pairs={{0,2},{1,5},{2,0},{3,7},{4,6},{5,1},{6,4},{7,3},{8,10},{9,13},{10,... | collective-permute-start | bytes 6291464 | tf_op jit(solution)/shard_map/ppermute | solution.py:349
  803.8 14.5 %in_back.1 = bf16[512,2048]{1,0:T(8,128)(2,1)} custom-call(s32[8]{0:T(128)} %copy-done.25, bf16[8,512,384]{2,1,0:T(8,128)(2,1)} %all-to-all-done.5.back_ref, bf16[512,2048]{1,0:T(8,128)(2,1)} %bitcast.139, f32[512,1]{1,0:T(8,128)} %copy-done.23, f32[1,2048]{1,0:T(1,128)} %copy-done.24, f32[512,2048]{1,0:T(8,128)} %get-tuple-element.489.d_resid_ref, ...), custom_call_target="tpu_custom_call" | custom-call | flops 1 | bytes 1 | tf_op jit(solution)/shard_map/in_back/pallas_call | solution.py:889
  818.3 17.2 %collective-permute-start.47 = (bf16[512,2048]{1,0:T(8,128)(2,1)}, bf16[512,2048]{1,0:T(8,128)(2,1)}, u32[]{:S(2)}, u32[]{:S(2)}) collective-permute-start(bf16[512,2048]{1,0:T(8,128)(2,1)} %get-tuple-element.479), channel_id=1, source_target_pairs={{0,2},{1,5},{2,0},{3,7},{4,6},{5,1},{6,4},{7,3},{8,10},{9,13},{10,... | collective-permute-start | bytes 6291464 | tf_op jit(solution)/shard_map/ppermute | solution.py:349
  837.7 5.9 all-to-all-start.6
  847.3 20.7 %all-to-all-done.6 = bf16[8,64,384]{2,1,0:T(8,128)(2,1)S(1)} async-done(((bf16[8,64,384]{2,1,0:T(8,128)(2,1)}), bf16[8,64,384]{2,1,0:T(8,128)(2,1)S(1)}, u32[]{:S(2)}, u32[]{:S(2)}) %all-to-all-start.6) | async-done | bytes 393248 | tf_op jit(solution)/shard_map/all_to_all | solution.py:1437
  868.4 4.6 collective-permute-start.52
  879.8 6.5 spread.1
  886.3 6.1 collective-permute-done.52.refs_1_
  896.9 19.8 %collective-permute-done.55.refs_5_ = bf16[64,5120]{1,0:T(8,128)(2,1)} collective-permute-done((bf16[64,5120]{1,0:T(8,128)(2,1)S(1)}, bf16[64,5120]{1,0:T(8,128)(2,1)}, u32[]{:S(2)}, u32[]{:S(2)}) %collective-permute-start.55) | collective-permute-done | bytes 655392 | tf_op jit(solution)/shard_map/ppermute | solution.py:422
  919.9 5.2 reshape.191
  925.8 10.1 %collective-permute-done.57.refs_6_ = bf16[64,5120]{1,0:T(8,128)(2,1)} collective-permute-done((bf16[64,5120]{1,0:T(8,128)(2,1)}, bf16[64,5120]{1,0:T(8,128)(2,1)}, u32[]{:S(2)}, u32[]{:S(2)}) %collective-permute-start.57) | collective-permute-done | bytes 655392 | tf_op jit(solution)/shard_map/ppermute | solution.py:422
  940.8 7.0 fusion
  (299 shorter events, 183.4 us)
Async XLA Ops:
  79.5 37.9 %all-to-all-start.1 = ((bf16[4,64,2816]{2,1,0:T(8,128)(2,1)}), bf16[4,64,2816]{2,1,0:T(8,128)(2,1)}, u32[]{:S(2)}, u32[]{:S(2)}) async-start(bf16[4,64,2816]{2,1,0:T(8,128)(2,1)} %pad_maximum_fusion.2), calls=%async_computation.1 | async-start | bytes 2883584 | tf_op jit(solution)/shard_map/all_to_all | solution.py:1295
  83.8 149.7 %all-gather.7.cloned.1.call-start = ((), (), s32[]{:S(2)}) async-start(), calls=%async_computation.9 | async-start | bytes 7208960 | tf_op jit(solution)/shard_map/all_gather | solution.py:1299
  93.6 23.8 %collective-permute-start.10 = (bf16[256,2048]{1,0:T(8,128)(2,1)}, bf16[256,2048]{1,0:T(8,128)(2,1)}, u32[]{:S(2)}, u32[]{:S(2)}) collective-permute-start(bf16[256,2048]{1,0:T(8,128)(2,1)} %refs_0_.1), channel_id=1, source_target_pairs={{0,2},{1,5},{2,0},{3,7},{4,6},{5,1},{6,4},{7,3},{8,10},{9,13},{10,... | collective-permute-start | bytes 3145736 | tf_op jit(solution)/shard_map/ppermute | solution.py:349
  117.5 41.5 %all-to-all-start = ((bf16[8,512,384]{2,1,0:T(8,128)(2,1)}), bf16[8,512,384]{2,1,0:T(8,128)(2,1)S(1)}, u32[]{:S(2)}, u32[]{:S(2)}) async-start(bf16[8,512,384]{2,1,0:T(8,128)(2,1)} %get-tuple-element.285), calls=%async_computation | async-start | bytes 6291456 | tf_op jit(solution)/shard_map/all_to_all | solution.py:1304
  159.0 35.5 %collective-permute-start.13 = (bf16[512,2048]{1,0:T(8,128)(2,1)}, bf16[512,2048]{1,0:T(8,128)(2,1)S(1)}, u32[]{:S(2)}, u32[]{:S(2)}) collective-permute-start(bf16[512,2048]{1,0:T(8,128)(2,1)} %multiply_bitcast_fusion.refs_1_.refs_4_.dy_ref), channel_id=1, source_target_pairs={{0,2},{1,5},{2,0},{3,7},{4,6},{5,1},{6,4},{7,3},{8,10},{9,13},{10,... | collective-permute-start | bytes 6291464 | tf_op jit(solution)/shard_map/ppermute | solution.py:349
  159.5 30.4 %collective-permute-start.12 = (bf16[256,2048]{1,0:T(8,128)(2,1)}, bf16[256,2048]{1,0:T(8,128)(2,1)S(1)}, u32[]{:S(2)}, u32[]{:S(2)}) collective-permute-start(bf16[256,2048]{1,0:T(8,128)(2,1)} %refs_0_.1), channel_id=1, source_target_pairs={{0,4},{1,3},{2,6},{3,1},{4,0},{5,7},{6,2},{7,5},{8,12},{9,11},{10,... | collective-permute-start | bytes 3145736 | tf_op jit(solution)/shard_map/ppermute | solution.py:353
  194.5 37.3 %collective-permute-start.15 = (bf16[512,2048]{1,0:T(8,128)(2,1)S(1)}, bf16[512,2048]{1,0:T(8,128)(2,1)S(1)}, u32[]{:S(2)}, u32[]{:S(2)}) collective-permute-start(bf16[512,2048]{1,0:T(8,128)(2,1)S(1)} %copy-done.27), channel_id=1, source_target_pairs={{0,4},{1,3},{2,6},{3,1},{4,0},{5,7},{6,2},{7,5},{8,12},{9,11},{10,... | collective-permute-start | bytes 6291464 | tf_op jit(solution)/shard_map/ppermute | solution.py:353
  196.3 35.6 %collective-permute-start.14 = (bf16[256,2048]{1,0:T(8,128)(2,1)}, bf16[256,2048]{1,0:T(8,128)(2,1)S(1)}, u32[]{:S(2)}, u32[]{:S(2)}) collective-permute-start(bf16[256,2048]{1,0:T(8,128)(2,1)} %collective-permute-done.10.refs_1_), channel_id=1, source_target_pairs={{0,4},{1,3},{2,6},{3,1},{4,0},{5,7},{6,2},{7,5},{8,12},{9,11},{10,... | collective-permute-start | bytes 3145736 | tf_op jit(solution)/shard_map/ppermute | solution.py:353
  233.5 34.2 %collective-permute-start.17 = (bf16[512,2048]{1,0:T(8,128)(2,1)}, bf16[512,2048]{1,0:T(8,128)(2,1)}, u32[]{:S(2)}, u32[]{:S(2)}) collective-permute-start(bf16[512,2048]{1,0:T(8,128)(2,1)} %copy-done.35), channel_id=1, source_target_pairs={{0,4},{1,3},{2,6},{3,1},{4,0},{5,7},{6,2},{7,5},{8,12},{9,11},{10,... | collective-permute-start | bytes 6291464 | tf_op jit(solution)/shard_map/ppermute | solution.py:353
  248.3 34.6 %all-to-all-start.2 = ((bf16[8,512,256]{2,1,0:T(8,128)(2,1)}), bf16[8,512,256]{2,1,0:T(8,128)(2,1)S(1)}, u32[]{:S(2)}, u32[]{:S(2)}) async-start(bf16[8,512,256]{2,1,0:T(8,128)(2,1)} %copy-done.6), calls=%async_computation.2 | async-start | bytes 4194304 | tf_op jit(solution)/shard_map/all_to_all | solution.py:1322
  252.1 327.1 %reduce-scatter.2.cloned.1.call-start = ((), (), s32[]{:S(2)}) async-start(), calls=%async_computation.8 | async-start | bytes 7208960 | tf_op jit(solution)/shard_map/reduce_scatter | solution.py:1359
  296.2 26.8 %collective-permute-start.22 = (bf16[512,2048]{1,0:T(8,128)(2,1)}, bf16[512,2048]{1,0:T(8,128)(2,1)S(1)}, u32[]{:S(2)}, u32[]{:S(2)}) collective-permute-start(bf16[512,2048]{1,0:T(8,128)(2,1)} %get-tuple-element.339.refs_0_.refs_4_), channel_id=1, source_target_pairs={{0,2},{1,5},{2,0},{3,7},{4,6},{5,1},{6,4},{7,3},{8,10},{9,13},{10,... | collective-permute-start | bytes 6291464 | tf_op jit(solution)/shard_map/ppermute | solution.py:349
  323.0 27.2 %collective-permute-start.23 = (bf16[512,2048]{1,0:T(8,128)(2,1)S(1)}, bf16[512,2048]{1,0:T(8,128)(2,1)}, u32[]{:S(2)}, u32[]{:S(2)}) collective-permute-start(bf16[512,2048]{1,0:T(8,128)(2,1)S(1)} %copy-done.28), channel_id=1, source_target_pairs={{0,4},{1,3},{2,6},{3,1},{4,0},{5,7},{6,2},{7,5},{8,12},{9,11},{10,... | collective-permute-start | bytes 6291464 | tf_op jit(solution)/shard_map/ppermute | solution.py:353
  350.3 27.3 %collective-permute-start.24 = (bf16[512,2048]{1,0:T(8,128)(2,1)}, bf16[512,2048]{1,0:T(8,128)(2,1)S(1)}, u32[]{:S(2)}, u32[]{:S(2)}) collective-permute-start(bf16[512,2048]{1,0:T(8,128)(2,1)} %copy-done.29), channel_id=1, source_target_pairs={{0,4},{1,3},{2,6},{3,1},{4,0},{5,7},{6,2},{7,5},{8,12},{9,11},{10,... | collective-permute-start | bytes 6291464 | tf_op jit(solution)/shard_map/ppermute | solution.py:353
  377.6 27.1 %collective-permute-start.25 = (bf16[512,2048]{1,0:T(8,128)(2,1)}, bf16[512,2048]{1,0:T(8,128)(2,1)S(1)}, u32[]{:S(2)}, u32[]{:S(2)}) collective-permute-start(bf16[512,2048]{1,0:T(8,128)(2,1)} %get-tuple-element.359), channel_id=1, source_target_pairs={{0,2},{1,5},{2,0},{3,7},{4,6},{5,1},{6,4},{7,3},{8,10},{9,13},{10,... | collective-permute-start | bytes 6291464 | tf_op jit(solution)/shard_map/ppermute | solution.py:349
  404.6 35.8 %collective-permute-start.26 = (bf16[512,2048]{1,0:T(8,128)(2,1)}, bf16[512,2048]{1,0:T(8,128)(2,1)S(1)}, u32[]{:S(2)}, u32[]{:S(2)}) collective-permute-start(bf16[512,2048]{1,0:T(8,128)(2,1)} %get-tuple-element.366), channel_id=1, source_target_pairs={{0,2},{1,5},{2,0},{3,7},{4,6},{5,1},{6,4},{7,3},{8,10},{9,13},{10,... | collective-permute-start | bytes 6291464 | tf_op jit(solution)/shard_map/ppermute | solution.py:349
  445.7 18.3 %collective-permute-start.27 = (bf16[4,4,64,2816]{3,2,1,0:T(8,128)(2,1)}, bf16[4,4,64,2816]{3,2,1,0:T(8,128)(2,1)}, u32[]{:S(2)}, u32[]{:S(2)}) collective-permute-start(bf16[4,4,64,2816]{3,2,1,0:T(8,128)(2,1)} %get-tuple-element.389), channel_id=1, source_target_pairs={{0,1},{1,0},{2,3},{3,2},{4,5},{5,4},{6,7},{7,6},{8,9},{9,8},{10,11... | collective-permute-start | bytes 17301512 | tf_op jit(solution)/shard_map/ppermute | solution.py:357
  445.7 26.2 %collective-permute-start.28 = (bf16[512,2048]{1,0:T(8,128)(2,1)}, bf16[512,2048]{1,0:T(8,128)(2,1)S(1)}, u32[]{:S(2)}, u32[]{:S(2)}) collective-permute-start(bf16[512,2048]{1,0:T(8,128)(2,1)} %add_convert_fusion.3), channel_id=1, source_target_pairs={{0,4},{1,3},{2,6},{3,1},{4,0},{5,7},{6,2},{7,5},{8,12},{9,11},{10,... | collective-permute-start | bytes 6291464 | tf_op jit(solution)/shard_map/ppermute | solution.py:353
  489.7 31.2 %all-to-all-start.3 = ((bf16[8,512,256]{2,1,0:T(8,128)(2,1)}), bf16[8,512,256]{2,1,0:T(8,128)(2,1)}, u32[]{:S(2)}, u32[]{:S(2)}) async-start(bf16[8,512,256]{2,1,0:T(8,128)(2,1)} %get-tuple-element.404), calls=%async_computation.3 | async-start | bytes 4194304 | tf_op jit(solution)/shard_map/all_to_all | solution.py:1368
  520.8 29.4 %collective-permute-start.31 = (bf16[4,256,2048]{2,1,0:T(8,128)(2,1)}, bf16[4,256,2048]{2,1,0:T(8,128)(2,1)}, u32[]{:S(2)}, u32[]{:S(2)}) collective-permute-start(bf16[4,256,2048]{2,1,0:T(8,128)(2,1)} %get-tuple-element.411), channel_id=1, source_target_pairs={{0,1},{1,0},{2,3},{3,2},{4,5},{5,4},{6,7},{7,6},{8,9},{9,8},{10,11... | collective-permute-start | bytes 12582920 | tf_op jit(solution)/shard_map/ppermute | solution.py:357
  520.8 29.4 %collective-permute-start.30 = (bf16[512,2048]{1,0:T(8,128)(2,1)}, bf16[512,2048]{1,0:T(8,128)(2,1)}, u32[]{:S(2)}, u32[]{:S(2)}) collective-permute-start(bf16[512,2048]{1,0:T(8,128)(2,1)} %get-tuple-element.419.refs_0_), channel_id=1, source_target_pairs={{0,2},{1,5},{2,0},{3,7},{4,6},{5,1},{6,4},{7,3},{8,10},{9,13},{10,... | collective-permute-start | bytes 6291464 | tf_op jit(solution)/shard_map/ppermute | solution.py:349
  550.3 28.9 %collective-permute-start.32 = (bf16[512,2048]{1,0:T(8,128)(2,1)S(1)}, bf16[512,2048]{1,0:T(8,128)(2,1)}, u32[]{:S(2)}, u32[]{:S(2)}) collective-permute-start(bf16[512,2048]{1,0:T(8,128)(2,1)S(1)} %copy-done.20), channel_id=1, source_target_pairs={{0,4},{1,3},{2,6},{3,1},{4,0},{5,7},{6,2},{7,5},{8,12},{9,11},{10,... | collective-permute-start | bytes 6291464 | tf_op jit(solution)/shard_map/ppermute | solution.py:353
  550.9 28.2 %collective-permute-start.33 = (bf16[512,2048]{1,0:T(8,128)(2,1)S(1)}, bf16[512,2048]{1,0:T(8,128)(2,1)}, u32[]{:S(2)}, u32[]{:S(2)}) collective-permute-start(bf16[512,2048]{1,0:T(8,128)(2,1)S(1)} %copy-done.20), channel_id=1, source_target_pairs={{0,1},{1,0},{2,3},{3,2},{4,5},{5,4},{6,7},{7,6},{8,9},{9,8},{10,11... | collective-permute-start | bytes 6291464 | tf_op jit(solution)/shard_map/ppermute | solution.py:357
  550.9 28.2 %collective-permute-start.34 = (bf16[512,2048]{1,0:T(8,128)(2,1)}, bf16[512,2048]{1,0:T(8,128)(2,1)}, u32[]{:S(2)}, u32[]{:S(2)}) collective-permute-start(bf16[512,2048]{1,0:T(8,128)(2,1)} %collective-permute-done.30.refs_1_), channel_id=1, source_target_pairs={{0,1},{1,0},{2,3},{3,2},{4,5},{5,4},{6,7},{7,6},{8,9},{9,8},{10,11... | collective-permute-start | bytes 6291464 | tf_op jit(solution)/shard_map/ppermute | solution.py:357
  579.2 34.4 %collective-permute-start.36 = (bf16[512,2048]{1,0:T(8,128)(2,1)}, bf16[512,2048]{1,0:T(8,128)(2,1)S(1)}, u32[]{:S(2)}, u32[]{:S(2)}) collective-permute-start(bf16[512,2048]{1,0:T(8,128)(2,1)} %collective-permute-done.32.refs_2_), channel_id=1, source_target_pairs={{0,1},{1,0},{2,3},{3,2},{4,5},{5,4},{6,7},{7,6},{8,9},{9,8},{10,11... | collective-permute-start | bytes 6291464 | tf_op jit(solution)/shard_map/ppermute | solution.py:357
  579.2 34.3 %collective-permute-start.35 = (bf16[2,176,2048]{2,1,0:T(8,128)(2,1)}, bf16[2,176,2048]{2,1,0:T(8,128)(2,1)}, u32[]{:S(2)}, u32[]{:S(2)}) collective-permute-start(bf16[2,176,2048]{2,1,0:T(8,128)(2,1)} %fusion.4), channel_id=1, source_target_pairs={{0,8},{8,0},{16,24},{24,16},{1,9},{9,1},{17,25},{25,17},{2,10},{10... | collective-permute-start | bytes 4325384 | tf_op jit(solution)/shard_map/ppermute | solution.py:1391
  579.3 29.6 %all-to-all-start.4 = ((bf16[4,64,2816]{2,1,0:T(8,128)(2,1)}), bf16[4,64,2816]{2,1,0:T(8,128)(2,1)S(1)}, u32[]{:S(2)}, u32[]{:S(2)}) async-start(bf16[4,64,2816]{2,1,0:T(8,128)(2,1)} %bitcast.150), calls=%async_computation.5 | async-start | bytes 2883584 | tf_op jit(solution)/shard_map/all_to_all | solution.py:1392
  582.9 254.8 %all-gather.9.cloned.1.call-start = ((), (), s32[]{:S(2)}) async-start(), calls=%async_computation.10 | async-start | bytes 7208960 | tf_op jit(solution)/shard_map/all_gather | solution.py:1403
  618.8 94.5 %collective-permute-start.39 = (bf16[512,2048]{1,0:T(8,128)(2,1)}, bf16[512,2048]{1,0:T(8,128)(2,1)}, u32[]{:S(2)}, u32[]{:S(2)}) collective-permute-start(bf16[512,2048]{1,0:T(8,128)(2,1)} %collective-permute-done.30.refs_1_), channel_id=1, source_target_pairs={{0,4},{1,3},{2,6},{3,1},{4,0},{5,7},{6,2},{7,5},{8,12},{9,11},{10,... | collective-permute-start | bytes 6291464 | tf_op jit(solution)/shard_map/ppermute | solution.py:353
  620.2 88.6 %collective-permute-start.40 = (bf16[176,2048]{1,0:T(8,128)(2,1)}, bf16[176,2048]{1,0:T(8,128)(2,1)}, u32[]{:S(2)}, u32[]{:S(2)}) collective-permute-start(bf16[176,2048]{1,0:T(8,128)(2,1)} %fusion.14), channel_id=1, source_target_pairs={{0,16},{8,24},{16,0},{24,8},{1,17},{9,25},{17,1},{25,9},{2,18},{10... | collective-permute-start | bytes 2162696 | tf_op jit(solution)/shard_map/ppermute | solution.py:1407
  636.7 74.2 %collective-permute-start.38 = (bf16[256,2048]{1,0:T(8,128)(2,1)}, bf16[256,2048]{1,0:T(8,128)(2,1)}, u32[]{:S(2)}, u32[]{:S(2)}) collective-permute-start(bf16[256,2048]{1,0:T(8,128)(2,1)} %get-tuple-element.456), channel_id=1, source_target_pairs={{0,2},{1,5},{2,0},{3,7},{4,6},{5,1},{6,4},{7,3},{8,10},{9,13},{10,... | collective-permute-start | bytes 3145736 | tf_op jit(solution)/shard_map/ppermute | solution.py:349
  638.3 75.0 %collective-permute-start.37 = (bf16[256,2048]{1,0:T(8,128)(2,1)}, bf16[256,2048]{1,0:T(8,128)(2,1)}, u32[]{:S(2)}, u32[]{:S(2)}) collective-permute-start(bf16[256,2048]{1,0:T(8,128)(2,1)} %get-tuple-element.455), channel_id=1, source_target_pairs={{0,2},{1,5},{2,0},{3,7},{4,6},{5,1},{6,4},{7,3},{8,10},{9,13},{10,... | collective-permute-start | bytes 3145736 | tf_op jit(solution)/shard_map/ppermute | solution.py:349
  713.3 26.2 %collective-permute-start.41 = (bf16[512,2048]{1,0:T(8,128)(2,1)}, bf16[512,2048]{1,0:T(8,128)(2,1)}, u32[]{:S(2)}, u32[]{:S(2)}) collective-permute-start(bf16[512,2048]{1,0:T(8,128)(2,1)} %collective-permute-done.39.refs_3_), channel_id=1, source_target_pairs={{0,1},{1,0},{2,3},{3,2},{4,5},{5,4},{6,7},{7,6},{8,9},{9,8},{10,11... | collective-permute-start | bytes 6291464 | tf_op jit(solution)/shard_map/ppermute | solution.py:357
  713.4 23.3 %collective-permute-start.42 = (bf16[256,2048]{1,0:T(8,128)(2,1)S(1)}, bf16[256,2048]{1,0:T(8,128)(2,1)}, u32[]{:S(2)}, u32[]{:S(2)}) collective-permute-start(bf16[256,2048]{1,0:T(8,128)(2,1)S(1)} %fusion.3), channel_id=1, source_target_pairs={{0,4},{1,3},{2,6},{3,1},{4,0},{5,7},{6,2},{7,5},{8,12},{9,11},{10,... | collective-permute-start | bytes 3145736 | tf_op jit(solution)/shard_map/ppermute | solution.py:353
  714.6 59.9 %all-to-all-start.5 = ((bf16[8,512,384]{2,1,0:T(8,128)(2,1)}), bf16[8,512,384]{2,1,0:T(8,128)(2,1)}, u32[]{:S(2)}, u32[]{:S(2)}) async-start(bf16[8,512,384]{2,1,0:T(8,128)(2,1)} %get-tuple-element.462.refs_8_), calls=%async_computation.6 | async-start | bytes 6291456 | tf_op jit(solution)/shard_map/all_to_all | solution.py:1416
  719.0 200.8 %all-gather.11.cloned.1.call-start = ((), (), s32[]{:S(2)}) async-start(), calls=%async_computation.11 | async-start | bytes 3604480 | tf_op jit(solution)/shard_map/all_gather | solution.py:1414
  753.9 20.6 %collective-permute-start.43 = (bf16[64,5120]{1,0:T(8,128)(2,1)}, bf16[64,5120]{1,0:T(8,128)(2,1)}, u32[]{:S(2)}, u32[]{:S(2)}) collective-permute-start(bf16[64,5120]{1,0:T(8,128)(2,1)} %get-tuple-element.467), channel_id=1, source_target_pairs={{0,8},{1,9},{2,10},{3,11},{4,12},{5,13},{6,14},{7,15}} | collective-permute-start | bytes 1966088 | tf_op jit(solution)/shard_map/ppermute | solution.py:409
  776.9 20.8 %collective-permute-start.45 = (bf16[64,5120]{1,0:T(8,128)(2,1)}, bf16[64,5120]{1,0:T(8,128)(2,1)}, u32[]{:S(2)}, u32[]{:S(2)}) collective-permute-start(bf16[64,5120]{1,0:T(8,128)(2,1)} %get-tuple-element.475), channel_id=1, source_target_pairs={{0,8},{8,16},{1,9},{9,17},{2,10},{10,18},{3,11},{11,19},{4,12},{12... | collective-permute-start | bytes 1966088 | tf_op jit(solution)/shard_map/ppermute | solution.py:409
  783.6 54.1 %collective-permute-start.50 = (bf16[512,2048]{1,0:T(8,128)(2,1)}, bf16[512,2048]{1,0:T(8,128)(2,1)}, u32[]{:S(2)}, u32[]{:S(2)}) collective-permute-start(bf16[512,2048]{1,0:T(8,128)(2,1)} %get-tuple-element.473), channel_id=1, source_target_pairs={{0,2},{1,5},{2,0},{3,7},{4,6},{5,1},{6,4},{7,3},{8,10},{9,13},{10,... | collective-permute-start | bytes 6291464 | tf_op jit(solution)/shard_map/ppermute | solution.py:349
  800.4 35.1 %collective-permute-start.48 = (bf16[64,5120]{1,0:T(8,128)(2,1)}, bf16[64,5120]{1,0:T(8,128)(2,1)S(1)}, u32[]{:S(2)}, u32[]{:S(2)}) collective-permute-start(bf16[64,5120]{1,0:T(8,128)(2,1)} %get-tuple-element.480), channel_id=1, source_target_pairs={{0,8},{8,16},{16,24},{1,9},{9,17},{17,25},{2,10},{10,18},{18,26},{... | collective-permute-start | bytes 1966088 | tf_op jit(solution)/shard_map/ppermute | solution.py:409
  802.5 33.0 %collective-permute-start.49 = (bf16[64,5120]{1,0:T(8,128)(2,1)}, bf16[64,5120]{1,0:T(8,128)(2,1)}, u32[]{:S(2)}, u32[]{:S(2)}) collective-permute-start(bf16[64,5120]{1,0:T(8,128)(2,1)} %get-tuple-element.481), channel_id=1, source_target_pairs={{24,16},{16,8},{8,0},{25,17},{17,9},{9,1},{26,18},{18,10},{10,2},{... | collective-permute-start | bytes 1966088 | tf_op jit(solution)/shard_map/ppermute | solution.py:410
  818.3 122.5 %collective-permute-start.47 = (bf16[512,2048]{1,0:T(8,128)(2,1)}, bf16[512,2048]{1,0:T(8,128)(2,1)}, u32[]{:S(2)}, u32[]{:S(2)}) collective-permute-start(bf16[512,2048]{1,0:T(8,128)(2,1)} %get-tuple-element.479), channel_id=1, source_target_pairs={{0,2},{1,5},{2,0},{3,7},{4,6},{5,1},{6,4},{7,3},{8,10},{9,13},{10,... | collective-permute-start | bytes 6291464 | tf_op jit(solution)/shard_map/ppermute | solution.py:349
  837.7 30.3 %all-to-all-start.6 = ((bf16[8,64,384]{2,1,0:T(8,128)(2,1)}), bf16[8,64,384]{2,1,0:T(8,128)(2,1)S(1)}, u32[]{:S(2)}, u32[]{:S(2)}) async-start(bf16[8,64,384]{2,1,0:T(8,128)(2,1)} %bitcast.110), calls=%async_computation.7 | async-start | bytes 786432 | tf_op jit(solution)/shard_map/all_to_all | solution.py:1437
  868.1 72.7 %collective-permute-start.51 = (bf16[512,2048]{1,0:T(8,128)(2,1)}, bf16[512,2048]{1,0:T(8,128)(2,1)}, u32[]{:S(2)}, u32[]{:S(2)}) collective-permute-start(bf16[512,2048]{1,0:T(8,128)(2,1)} %add_convert_fusion.2), channel_id=1, source_target_pairs={{0,4},{1,3},{2,6},{3,1},{4,0},{5,7},{6,2},{7,5},{8,12},{9,11},{10,... | collective-permute-start | bytes 6291464 | tf_op jit(solution)/shard_map/ppermute | solution.py:353
  868.4 24.0 %collective-permute-start.52 = (bf16[64,5120]{1,0:T(8,128)(2,1)S(1)}, bf16[64,5120]{1,0:T(8,128)(2,1)S(1)}, u32[]{:S(2)}, u32[]{:S(2)}) collective-permute-start(bf16[64,5120]{1,0:T(8,128)(2,1)S(1)} %pad_maximum_fusion.3.refs_0_), channel_id=1, source_target_pairs={{0,8},{8,16},{16,24},{1,9},{9,17},{17,25},{2,10},{10,18},{18,26},{... | collective-permute-start | bytes 1966088 | tf_op jit(solution)/shard_map/ppermute | solution.py:421
  873.0 21.1 %collective-permute-start.53 = (bf16[64,5120]{1,0:T(8,128)(2,1)S(1)}, bf16[64,5120]{1,0:T(8,128)(2,1)S(1)}, u32[]{:S(2)}, u32[]{:S(2)}) collective-permute-start(bf16[64,5120]{1,0:T(8,128)(2,1)S(1)} %pad_maximum_fusion.3.refs_0_), channel_id=1, source_target_pairs={{8,0},{16,8},{24,16},{9,1},{17,9},{25,17},{10,2},{18,10},{26,18},{... | collective-permute-start | bytes 1966088 | tf_op jit(solution)/shard_map/ppermute | solution.py:422
  895.6 21.1 %collective-permute-start.55 = (bf16[64,5120]{1,0:T(8,128)(2,1)S(1)}, bf16[64,5120]{1,0:T(8,128)(2,1)}, u32[]{:S(2)}, u32[]{:S(2)}) collective-permute-start(bf16[64,5120]{1,0:T(8,128)(2,1)S(1)} %collective-permute-done.53.refs_4_), channel_id=1, source_target_pairs={{8,0},{16,8},{9,1},{17,9},{10,2},{18,10},{11,3},{19,11},{12,4},{20... | collective-permute-start | bytes 1966088 | tf_op jit(solution)/shard_map/ppermute | solution.py:422
  918.2 17.7 %collective-permute-start.57 = (bf16[64,5120]{1,0:T(8,128)(2,1)}, bf16[64,5120]{1,0:T(8,128)(2,1)}, u32[]{:S(2)}, u32[]{:S(2)}) collective-permute-start(bf16[64,5120]{1,0:T(8,128)(2,1)} %collective-permute-done.55.refs_5_), channel_id=1, source_target_pairs={{8,0},{9,1},{10,2},{11,3},{12,4},{13,5},{14,6},{15,7}} | collective-permute-start | bytes 1966088 | tf_op jit(solution)/shard_map/ppermute | solution.py:422
  (82 other events, 950.7 us)
Sparse Core Ops, SparseCore 0:
  117.6 107.0 all-gather.6
  472.1 104.9 reduce-scatter.1
  636.9 124.6 all-gather.8
  803.9 81.0 all-gather.10

commit v7 on v6

--- a/solution.py
+++ b/solution.py
@@ -1407,14 +1407,13 @@
     dn_move = lax.ppermute(dn_move, "dp", LINE_FAR)
     bwd = back_call(d_heads, turns[3], turns[4], before=bwd)
     wo_pass = (wo_part(chip ^ (second_mask // 2)) + wo_far.astype(F32)).astype(BF)
-    dn_z = (pick(dn_own, plane // 2) + dn_move.astype(F32)).astype(BF)
-    dp_heads, wo_first, wo_pass, a_far, dn_z = fence(bwd[0], wo_first, wo_pass, a_far, dn_z)
+    dp_heads, wo_first, wo_pass, a_far, dn_move = fence(bwd[0], wo_first, wo_pass, a_far, dn_move)
 
     wo_passed = send_second(wo_pass)
-    dn_all = lax.all_gather(dn_z, "dp", axis=0, tiled=False)
     a_theirs.append(send_sibling(a_far))
     back = lax.all_to_all(dp_heads, "sp", 0, 0, tiled=True)
     grad_wq = grad_qkv(places, [normed, a_first, a_second, a_far] + list(a_theirs), dp_heads, planes)
+    wo_passed, grad_wq = fence(wo_passed, grad_wq)
     wo_rows = (wo_part(chip) + wo_first.astype(F32) + wo_passed.astype(F32)).astype(BF)
     split = grad_wq.shape[2]
     last_parts = [jnp.concatenate([grad_wq, wo_rows.reshape(planes, quarter, width)], axis=2)]
@@ -1425,20 +1424,23 @@
         y_far, y_first, *moves = fence(y_far, y_first, *moves)
         moves = line_scatter_move(moves, step)
         if step == 1:
+            dn_z = (pick(dn_own, plane // 2) + dn_move.astype(F32)).astype(BF)
+            dn_all = lax.all_gather(dn_z, "dp", axis=0, tiled=False)
+        elif step == 2:
             back, *moves = fence(back, *moves)
-        elif step == 2:
+        elif step == 3:
+            y_far, back = fence(y_far, back)
             y_got_far = send_first(y_far)
-        elif step == 3:
-            y_got_first = send_first(y_first)
         moves = fence(*moves)
     last_z = line_scatter_end(last_parts, moves, 0)
     wq_z = last_z[:, :split].reshape(quarter, devices, split // devices).transpose(1, 0, 2)
-    wq_z, wo_z, gu_all, y_got_far = fence(wq_z, last_z[:, split:], gu_all, y_got_far)
+    wq_z, wo_z, gu_all = fence(wq_z, last_z[:, split:], gu_all)
     wq_z = lax.all_to_all(wq_z, "sp", 0, 0, tiled=True)
     grad_tokens = in_back(places, back, x_bf, inv_one, attn_gain, d_resid, qkv_parts).reshape(tokens.shape)
     y_pass = (second[4].astype(F32) + y_got_far.astype(F32)).astype(BF)
     last_z = jnp.concatenate([wq_z.transpose(1, 0, 2).reshape(quarter, split), wo_z], axis=1)
-    last_z, grad_tokens, y_pass = fence(last_z, grad_tokens, y_pass)
+    last_z, grad_tokens, y_pass, y_first = fence(last_z, grad_tokens, y_pass, y_first)
+    y_got_first = send_first(y_first)
     y_passed = send_second(y_pass)
     last_steps = [(last_z, last_z)]
     outs = []
@@ -1446,14 +1448,15 @@
         last_steps.append(line_gather_move(last_steps[-1], step))
         if step == 1:
             outs += spread(gu_all, w_gate_up, g_mlp.astype(F32).reshape(share, 1))
+        elif step == 2:
+            outs.append(dn_all.astype(F32).reshape(w_down.shape))
         if step == planes - 1:
             y_sum = own[4].astype(F32) + y_got_first.astype(F32) + y_passed.astype(F32)
             outs.append((residual + y_sum).astype(BF).reshape(tokens.shape))
             break
         moves = fence(*last_steps[-1], *outs)
         last_steps[-1], outs = tuple(moves[:2]), list(moves[2:])
-    grad_w_gate_up, grad_g_mlp, output = outs
-    grad_w_down = dn_all.astype(F32).reshape(w_down.shape)
+    grad_w_gate_up, grad_g_mlp, grad_w_down, output = outs
     grad_w_qkv, grad_g_attn, grad_w_out = spread_last(last_steps, w_qkv, g_attn.astype(F32).reshape(share, 1), width)
     return (
         output,

time: 961 us -> 941 us (0.979)
  starting transfers between devices: 157 us -> 126 us
  waiting for transfers between devices: 230 us -> 247 us
    ppermute x11, starting transfers between devices: 41.1 us -> 10.5 us  [send_first(): return lax.ppermute(x, 'sp', FIRST)]
    ppermute x3, waiting for transfers between devices: 6.4 us -> 31.5 us  [line_scatter_move(): right = lax.ppermute(sends[0], 'dp', [(i, i + 1) for i in range(step)])]
    ppermute x1, starting transfers between devices: 0.07 us -> 19.8 us  [fast_body(): dn_move = lax.ppermute(dn_move, 'dp', LINE_NEAR)]
    ppermute x1, starting transfers between devices: 16.5 us -> 0.01 us  [fast_body(): dn_move = lax.ppermute(dn_move, 'dp', LINE_FAR)]
    all_to_all x1, waiting for transfers between devices: 20.7 us -> 4.56 us  [fast_body(): wq_z = lax.all_to_all(wq_z, 'sp', 0, 0, tiled=True)]
    ppermute x13, waiting for transfers between devices: 52.2 us -> 39.5 us  [send_second(): return lax.ppermute(x, 'sp', SECOND)]
    ppermute x3, waiting for transfers between devices: 0.01 us -> 11.7 us  [line_scatter_move(): lax.ppermute(sends[1], 'dp', [(planes - 1 - i, planes - 2 - i) for i in r...]
    unnamed x122 -> x126, local copies, waits for them, and re-layouts: 37.3 us -> 39.4 us
  transfers between devices with their start and end apart: 69 -> 69, of which waited for: 23 -> 26; matrix products, arithmetic and copies ran while one was open for 8% -> 8% of each run, Pallas kernels for 43% -> 43%
where the time goes in v7:
time: 941 us; the launch traced here: 934 us
  Pallas kernels  416 us (44%)
  waiting for transfers between devices  247 us (26%)
  starting transfers between devices  126 us (13%)
  other arithmetic  83.2 us (9%)
  local copies, waits for them, and re-layouts  46.2 us (5%)
  between operations  15.6 us (2%)
    pallas_call x4, Pallas kernels, attend_back(): pl.pallas_call(functools.partial(attend_back_kernel, heads=heads, start=s...  114 us
    pallas_call x4, Pallas kernels, ffn(): pl.pallas_call(functools.partial(ffn_kernel, cuts=cuts), in_specs=[hbm] *...  103 us
    pallas_call x3, Pallas kernels, attend(): pl.pallas_call(functools.partial(attend_kernel, heads=heads, start=start,...  50.1 us
    ppermute x13, waiting for transfers between devices, send_second(): return lax.ppermute(x, 'sp', SECOND)  39.5 us
    unnamed x126, local copies, waits for them, and re-layouts  39.4 us
    pallas_call x1, Pallas kernels, grad_gu(): pl.pallas_call(functools.partial(grad_gu_kernel, count=count), grid_spec=...  34.5 us
    ppermute x3, waiting for transfers between devices, line_gather_move(): lax.ppermute(got[1], 'dp', [(i + 1, i) for i in range(planes - step)])  32.5 us
    ppermute x3, waiting for transfers between devices, line_scatter_move(): right = lax.ppermute(sends[0], 'dp', [(i, i + 1) for i in range(step)])  31.5 us
  transfers between devices with their start and end apart: 69, of which 26 were waited for; matrix products, arithmetic and copies ran while one was open for 8% of the time, Pallas kernels for 43%

profile of v7, /device:TPU:0, one launch (start us, length us, event | category | flops | bytes accessed | tf_op | source)
XLA Modules:
  0.0 933.5 jit_solution(5083078916529325632)
XLA Ops:
  27.8 12.1 %collective-permute-done.3.refs_1_.refs_9_ = bf16[256,2560]{1,0:T(8,128)(2,1)S(1)} collective-permute-done((bf16[256,2560]{1,0:T(8,128)(2,1)S(1)}, bf16[256,2560]{1,0:T(8,128)(2,1)S(1)}, u32[]{:S(2)}, u32[]{:S(2)}) %collective-permute-start.3) | collective-permute-done | bytes 1310752 | tf_op jit(solution)/shard_map/ppermute | solution.py:349
  42.5 7.5 fusion.15
  61.3 14.0 %collective-permute-done.7.refs_3_.refs_11_ = bf16[256,2560]{1,0:T(8,128)(2,1)S(1)} collective-permute-done((bf16[256,2560]{1,0:T(8,128)(2,1)S(1)}, bf16[256,2560]{1,0:T(8,128)(2,1)S(1)}, u32[]{:S(2)}, u32[]{:S(2)}) %collective-permute-start.7) | collective-permute-done | bytes 1310752 | tf_op jit(solution)/shard_map/ppermute | solution.py:353
  83.8 9.8 %all-gather.7.cloned.1.call-start = ((), (), s32[]{:S(2)}) async-start(), calls=%async_computation.9 | async-start | bytes 7208960 | tf_op jit(solution)/shard_map/all_gather | solution.py:1299
  98.4 18.3 %project.1 = (bf16[8,512,384]{2,1,0:T(8,128)(2,1)}, bf16[512,2048]{1,0:T(8,128)(2,1)}, f32[512,1]{1,0:T(8,128)S(1)}) custom-call(s32[8]{0:T(128)S(1)} %stack.59.place_ref, bf16[512,2048]{1,0:T(8,128)(2,1)} %bitcast.137, f32[1,2048]{1,0:T(1,128)S(1)} %get-tuple-element.546.gain_ref, f32[512,128]{1,0:T(8,128)S(1)} %pad_maximum_fusion.4.cos_ref, ...), custom_call_target="tpu_custom_call" | custom-call | flops 1 | bytes 1 | tf_op jit(solution)/shard_map/project/pallas_call | solution.py:736
  123.2 8.3 maximum_select_fusion.refs_3_
  131.4 27.6 %all-to-all-done = bf16[8,512,384]{2,1,0:T(8,128)(2,1)S(1)} async-done(((bf16[8,512,384]{2,1,0:T(8,128)(2,1)}), bf16[8,512,384]{2,1,0:T(8,128)(2,1)S(1)}, u32[]{:S(2)}, u32[]{:S(2)}) %all-to-all-start) | async-done | bytes 3145760 | tf_op jit(solution)/shard_map/all_to_all | solution.py:1304
  160.2 26.0 %attend.3 = (f32[4096,256]{1,0:T(8,128)}, bf16[8,512,256]{2,1,0:T(8,128)(2,1)S(1)}, f32[8,4,512]{2,1,0:T(4,128)S(1)}) custom-call(s32[1]{0:T(128)} %bitcast.14.zeros_ref, bf16[4096,384]{1,0:T(8,128)(2,1)S(1)} %bitcast.111, bf16[4096,384]{1,0:T(8,128)(2,1)S(1)} %bitcast.112), custom_call_target="tpu_custom_call" | custom-call | flops 1 | bytes 1 | tf_op jit(solution)/shard_map/attend/pallas_call | solution.py:1056
  186.2 8.3 collective-permute-done.13.refs_1_.refs_5_
  196.6 14.2 %attend.4 = (f32[4096,256]{1,0:T(8,128)}, bf16[8,512,256]{2,1,0:T(8,128)(2,1)S(1)}, f32[8,4,512]{2,1,0:T(4,128)S(1)}) custom-call(s32[1]{0:T(128)} %bitcast.14.zeros_ref, bf16[4096,384]{1,0:T(8,128)(2,1)S(1)} %bitcast.113, bf16[4096,384]{1,0:T(8,128)(2,1)S(1)} %bitcast.114, ...), custom_call_target="tpu_custom_call", output_to_operand_aliasing={{0}: (3, {}), {1}: (4, {}), {2}: (5, {})} | custom-call | flops 1 | bytes 1 | tf_op jit(solution)/shard_map/attend/pallas_call | solution.py:1056
  212.1 19.8 %collective-permute-done.14.refs_3_ = bf16[256,2048]{1,0:T(8,128)(2,1)S(1)} collective-permute-done((bf16[256,2048]{1,0:T(8,128)(2,1)}, bf16[256,2048]{1,0:T(8,128)(2,1)S(1)}, u32[]{:S(2)}, u32[]{:S(2)}) %collective-permute-start.14) | collective-permute-done | bytes 1048608 | tf_op jit(solution)/shard_map/ppermute | solution.py:353
  236.8 9.9 %attend.5 = (f32[4096,256]{1,0:T(8,128)}, bf16[8,512,256]{2,1,0:T(8,128)(2,1)S(1)}, f32[8,4,512]{2,1,0:T(4,128)S(1)}) custom-call(s32[1]{0:T(128)} %bitcast.14.zeros_ref, bf16[4096,384]{1,0:T(8,128)(2,1)S(1)} %bitcast.115, bf16[4096,384]{1,0:T(8,128)(2,1)S(1)} %bitcast.116, ...), custom_call_target="tpu_custom_call", output_to_operand_aliasing={{0}: (3, {}), {1}: (4, {}), {2}: (5, {})} | custom-call | flops 1 | bytes 1 | tf_op jit(solution)/shard_map/attend/pallas_call | solution.py:1056
  261.4 6.1 join.1
  270.1 12.9 %all-to-all-done.2.attn_ref.keep_ref.give_ref = bf16[8,512,256]{2,1,0:T(8,128)(2,1)S(1)} async-done(((bf16[8,512,256]{2,1,0:T(8,128)(2,1)}), bf16[8,512,256]{2,1,0:T(8,128)(2,1)S(1)}, u32[]{:S(2)}, u32[]{:S(2)}) %all-to-all-start.2) | async-done | bytes 2097184 | tf_op jit(solution)/shard_map/all_to_all | solution.py:1322
  284.3 11.9 %out_proj.1 = (f32[512,2048]{1,0:T(8,128)}, f32[512,1]{1,0:T(8,128)}, bf16[512,2048]{1,0:T(8,128)(2,1)}) custom-call(s32[8]{0:T(128)} %copy-done.25, bf16[8,512,256]{2,1,0:T(8,128)(2,1)} %copy-done.1, bf16[512,2048]{1,0:T(8,128)(2,1)} %bitcast.138, f32[1,2048]{1,0:T(1,128)} %get-tuple-element.545.gain_ref, bf16[256,2048]{1,0:T(8,128)(2,1)} %refs_0_.1, ...), custom_call_target="tpu_custom_call" | custom-call | flops 1 | bytes 1 | tf_op jit(solution)/shard_map/out_proj/pallas_call | solution.py:790
  297.3 25.7 %ffn.4 = (bf16[512,1408]{1,0:T(8,128)(2,1)}, bf16[512,1408]{1,0:T(8,128)(2,1)}, bf16[512,1408]{1,0:T(8,128)(2,1)}, bf16[512,2048]{1,0:T(8,128)(2,1)}, bf16[512,2048]{1,0:T(8,128)(2,1)}) custom-call(bf16[512,2048]{1,0:T(8,128)(2,1)} %get-tuple-element.346.refs_0_.refs_4_, bf16[512,2048]{1,0:T(8,128)(2,1)} %multiply_bitcast_fusion.refs_1_.refs_4_.dy_ref, ...), custom_call_target="tpu_custom_call" | custom-call | flops 1 | bytes 1 | tf_op jit(solution)/shard_map/ffn/pallas_call | solution.py:597
  324.5 25.8 %ffn.5 = (bf16[512,1408]{1,0:T(8,128)(2,1)}, bf16[512,1408]{1,0:T(8,128)(2,1)}, bf16[512,1408]{1,0:T(8,128)(2,1)}, bf16[512,2048]{1,0:T(8,128)(2,1)}, bf16[512,2048]{1,0:T(8,128)(2,1)}) custom-call(bf16[512,2048]{1,0:T(8,128)(2,1)} %copy-done.29, bf16[512,2048]{1,0:T(8,128)(2,1)} %copy-done.37, bf16[2,2048,1408]{2,1,0:T(8,128)(2,1)} %bitcast.129, ...), custom_call_target="tpu_custom_call" | custom-call | flops 1 | bytes 1 | tf_op jit(solution)/shard_map/ffn/pallas_call | solution.py:597
  351.6 26.0 %ffn.6 = (bf16[512,1408]{1,0:T(8,128)(2,1)}, bf16[512,1408]{1,0:T(8,128)(2,1)}, bf16[512,1408]{1,0:T(8,128)(2,1)}, bf16[512,2048]{1,0:T(8,128)(2,1)}, bf16[512,2048]{1,0:T(8,128)(2,1)}) custom-call(bf16[512,2048]{1,0:T(8,128)(2,1)} %collective-permute-done.23.refs_0_.refs_2_.refs_6_, bf16[512,2048]{1,0:T(8,128)(2,1)} %copy-done.38, ...), custom_call_target="tpu_custom_call" | custom-call | flops 1 | bytes 1 | tf_op jit(solution)/shard_map/ffn/pallas_call | solution.py:597
  379.0 25.7 %ffn.7 = (bf16[512,1408]{1,0:T(8,128)(2,1)}, bf16[512,1408]{1,0:T(8,128)(2,1)}, bf16[512,1408]{1,0:T(8,128)(2,1)}, bf16[512,2048]{1,0:T(8,128)(2,1)}, bf16[512,2048]{1,0:T(8,128)(2,1)}) custom-call(bf16[512,2048]{1,0:T(8,128)(2,1)} %copy-done.30, bf16[512,2048]{1,0:T(8,128)(2,1)} %collective-permute-done.17.refs_1_.refs_7_, ...), custom_call_target="tpu_custom_call" | custom-call | flops 1 | bytes 1 | tf_op jit(solution)/shard_map/ffn/pallas_call | solution.py:597
  406.0 34.5 %grad_gu.1 = (bf16[4,4,64,2816]{3,2,1,0:T(8,128)(2,1)}, bf16[4,4,64,2816]{3,2,1,0:T(8,128)(2,1)}) custom-call(s32[1]{0:T(128)} %bitcast.20.core_ref, bf16[512,2048]{1,0:T(8,128)(2,1)} %get-tuple-element.346.refs_0_.refs_4_, bf16[512,2048]{1,0:T(8,128)(2,1)} %copy-done.29, bf16[512,2048]{1,0:T(8,128)(2,1)} %collective-permute-done.23.refs_0_.refs_2_.refs_6_, ...), custom_call_target="tpu_custom_call" | custom-call | flops 1 | bytes 1 | tf_op jit(solution)/shard_map/grad_gu/pallas_call | solution.py:638
  446.6 17.5 %grad_dn.1 = (bf16[704,2048]{1,0:T(8,128)(2,1)}, bf16[704,2048]{1,0:T(8,128)(2,1)}) custom-call(s32[1]{0:T(128)} %bitcast.20.core_ref, bf16[512,1408]{1,0:T(8,128)(2,1)} %get-tuple-element.394.refs_0_, bf16[512,1408]{1,0:T(8,128)(2,1)} %get-tuple-element.395.refs_1_, bf16[512,1408]{1,0:T(8,128)(2,1)} %get-tuple-element.396.refs_2_, ...), custom_call_target="tpu_custom_call" | custom-call | flops 1 | bytes 1 | tf_op jit(solution)/shard_map/grad_dn/pallas_call | solution.py:960
  464.2 6.9 add_convert_fusion
  473.4 15.8 %resid_back.1 = (f32[512,2048]{1,0:T(8,128)}, bf16[512,2048]{1,0:T(8,128)(2,1)}, bf16[8,512,256]{2,1,0:T(8,128)(2,1)}) custom-call(s32[8]{0:T(128)} %copy-done.25, bf16[512,2048]{1,0:T(8,128)(2,1)} %get-tuple-element.344.db_ref, bf16[512,2048]{1,0:T(8,128)(2,1)} %copy-done.53, bf16[512,2048]{1,0:T(8,128)(2,1)} %copy-done.54, ...), custom_call_target="tpu_custom_call" | custom-call | flops 1 | bytes 1 | tf_op jit(solution)/shard_map/resid_back/pallas_call | solution.py:836
  496.8 6.2 grad_wo.1
  503.0 18.9 %all-to-all-done.3 = bf16[8,512,256]{2,1,0:T(8,128)(2,1)} async-done(((bf16[8,512,256]{2,1,0:T(8,128)(2,1)}), bf16[8,512,256]{2,1,0:T(8,128)(2,1)}, u32[]{:S(2)}, u32[]{:S(2)}) %all-to-all-start.3) | async-done | bytes 2097184 | tf_op jit(solution)/shard_map/all_to_all | solution.py:1368
  522.5 23.1 %attend_back.4 = (bf16[8,512,384]{2,1,0:T(8,128)(2,1)}, f32[256,4096]{1,0:T(8,128)}, f32[8,4,512]{2,1,0:T(4,128)}) custom-call(s32[1]{0:T(128)} %bitcast.14.zeros_ref, bf16[4096,384]{1,0:T(8,128)(2,1)} %bitcast.117, bf16[4096,384]{1,0:T(8,128)(2,1)} %bitcast.118, bf16[4096,256]{1,0:T(8,128)(2,1)} %bitcast.22.do_ref, f32[8,4,512]{2,1,0:T(4,128)} %copy-done.19, ...), custom_call_target="tpu_custom_call" | custom-call | flops 1 | bytes 1 | tf_op jit(solution)/shard_map/attend_back/pallas_call | solution.py:1197
  552.8 18.5 %attend_back.5 = (bf16[8,512,384]{2,1,0:T(8,128)(2,1)}, f32[256,4096]{1,0:T(8,128)}, f32[8,4,512]{2,1,0:T(4,128)}) custom-call(s32[1]{0:T(128)} %bitcast.14.zeros_ref, bf16[4096,384]{1,0:T(8,128)(2,1)} %bitcast.119, bf16[4096,384]{1,0:T(8,128)(2,1)} %bitcast.120, bf16[4096,256]{1,0:T(8,128)(2,1)} %bitcast.22.do_ref, ...), custom_call_target="tpu_custom_call", output_to_operand_aliasing={{0}: (9, {})} | custom-call | flops 1 | bytes 1 | tf_op jit(solution)/shard_map/attend_back/pallas_call | solution.py:1197
  575.2 19.8 %collective-permute-start.35 = (bf16[2,176,2048]{2,1,0:T(8,128)(2,1)}, bf16[2,176,2048]{2,1,0:T(8,128)(2,1)}, u32[]{:S(2)}, u32[]{:S(2)}) collective-permute-start(bf16[2,176,2048]{2,1,0:T(8,128)(2,1)} %fusion.4), channel_id=1, source_target_pairs={{0,8},{8,0},{16,24},{24,16},{1,9},{9,1},{17,25},{25,17},{2,10},{10... | collective-permute-start | bytes 4325384 | tf_op jit(solution)/shard_map/ppermute | solution.py:1391
  603.2 15.6 %attend_back.6 = (bf16[8,512,384]{2,1,0:T(8,128)(2,1)}, f32[256,4096]{1,0:T(8,128)}, f32[8,4,512]{2,1,0:T(4,128)}) custom-call(s32[1]{0:T(128)} %bitcast.14.zeros_ref, bf16[4096,384]{1,0:T(8,128)(2,1)} %bitcast.121, bf16[4096,384]{1,0:T(8,128)(2,1)} %bitcast.122, bf16[4096,256]{1,0:T(8,128)(2,1)} %bitcast.22.do_ref, ...), custom_call_target="tpu_custom_call", output_to_operand_aliasing={{0}: (9, {})} | custom-call | flops 1 | bytes 1 | tf_op jit(solution)/shard_map/attend_back/pallas_call | solution.py:1197
  618.8 8.6 collective-permute-done.35
  637.2 56.9 %attend_back.7 = (bf16[8,512,384]{2,1,0:T(8,128)(2,1)}, f32[256,4096]{1,0:T(8,128)}, f32[8,4,512]{2,1,0:T(4,128)}) custom-call(s32[1]{0:T(128)} %bitcast.14.zeros_ref, bf16[4096,384]{1,0:T(8,128)(2,1)} %bitcast.123, bf16[4096,384]{1,0:T(8,128)(2,1)} %bitcast.124, bf16[4096,256]{1,0:T(8,128)(2,1)} %bitcast.22.do_ref, ...), custom_call_target="tpu_custom_call", output_to_operand_aliasing={{0}: (9, {})} | custom-call | flops 1 | bytes 1 | tf_op jit(solution)/shard_map/attend_back/pallas_call | solution.py:1197
  696.2 15.8 %collective-permute-done.40 = bf16[176,2048]{1,0:T(8,128)(2,1)S(1)} collective-permute-done((bf16[176,2048]{1,0:T(8,128)(2,1)}, bf16[176,2048]{1,0:T(8,128)(2,1)S(1)}, u32[]{:S(2)}, u32[]{:S(2)}) %collective-permute-start.40) | collective-permute-done | bytes 720928 | tf_op jit(solution)/shard_map/ppermute | solution.py:1407
  712.7 8.1 all-to-all-start.5
  722.6 13.4 %grad_qkv.1 = bf16[4,64,3072]{2,1,0:T(8,128)(2,1)S(1)} custom-call(s32[8]{0:T(128)S(1)} %copy-done.26, bf16[512,2048]{1,0:T(8,128)(2,1)S(1)} %copy-done.21, bf16[512,2048]{1,0:T(8,128)(2,1)} %collective-permute-done.30.refs_1_, bf16[512,2048]{1,0:T(8,128)(2,1)} %collective-permute-done.32.refs_2_, bf16[512,2048]{1,0:T(8,128)(2,1)} %collective-permute-done.39.refs_3_, ...), custom_call_target="tpu_custom_call" | custom-call | flops 1 | bytes 1 | tf_op jit(solution)/shard_map/grad_qkv/pallas_call | solution.py:672
  740.0 5.8 collective-permute-start.43
  747.3 20.1 %collective-permute-done.43 = bf16[64,5120]{1,0:T(8,128)(2,1)} collective-permute-done((bf16[64,5120]{1,0:T(8,128)(2,1)}, bf16[64,5120]{1,0:T(8,128)(2,1)}, u32[]{:S(2)}, u32[]{:S(2)}) %collective-permute-start.43) | collective-permute-done | bytes 655392 | tf_op jit(solution)/shard_map/ppermute | solution.py:409
  770.0 5.2 collective-permute-start.45
  776.7 11.4 %collective-permute-done.45 = bf16[64,5120]{1,0:T(8,128)(2,1)} collective-permute-done((bf16[64,5120]{1,0:T(8,128)(2,1)}, bf16[64,5120]{1,0:T(8,128)(2,1)}, u32[]{:S(2)}, u32[]{:S(2)}) %collective-permute-start.45) | collective-permute-done | bytes 655392 | tf_op jit(solution)/shard_map/ppermute | solution.py:409
  790.8 7.3 collective-permute-start.47
  800.6 14.5 %in_back.1 = bf16[512,2048]{1,0:T(8,128)(2,1)} custom-call(s32[8]{0:T(128)} %copy-done.25, bf16[8,512,384]{2,1,0:T(8,128)(2,1)} %all-to-all-done.5.back_ref, bf16[512,2048]{1,0:T(8,128)(2,1)} %bitcast.139, f32[512,1]{1,0:T(8,128)} %copy-done.23, f32[1,2048]{1,0:T(1,128)} %copy-done.24, f32[512,2048]{1,0:T(8,128)} %get-tuple-element.498.d_resid_ref, ...), custom_call_target="tpu_custom_call" | custom-call | flops 1 | bytes 1 | tf_op jit(solution)/shard_map/in_back/pallas_call | solution.py:889
  815.1 11.7 %collective-permute-done.48 = bf16[64,5120]{1,0:T(8,128)(2,1)} collective-permute-done((bf16[64,5120]{1,0:T(8,128)(2,1)}, bf16[64,5120]{1,0:T(8,128)(2,1)}, u32[]{:S(2)}, u32[]{:S(2)}) %collective-permute-start.48) | collective-permute-done | bytes 655392 | tf_op jit(solution)/shard_map/ppermute | solution.py:410
  850.4 6.5 spread.1
  857.0 13.5 %collective-permute-done.52.refs_1_ = bf16[64,5120]{1,0:T(8,128)(2,1)S(1)} collective-permute-done((bf16[64,5120]{1,0:T(8,128)(2,1)S(1)}, bf16[64,5120]{1,0:T(8,128)(2,1)S(1)}, u32[]{:S(2)}, u32[]{:S(2)}) %collective-permute-start.52) | collective-permute-done | bytes 655392 | tf_op jit(solution)/shard_map/ppermute | solution.py:421
  870.5 4.6 collective-permute-done.53.refs_4_
  878.1 5.1 reshape.191
  883.2 12.2 %collective-permute-done.55.refs_5_ = bf16[64,5120]{1,0:T(8,128)(2,1)} collective-permute-done((bf16[64,5120]{1,0:T(8,128)(2,1)S(1)}, bf16[64,5120]{1,0:T(8,128)(2,1)}, u32[]{:S(2)}, u32[]{:S(2)}) %collective-permute-start.55) | collective-permute-done | bytes 655392 | tf_op jit(solution)/shard_map/ppermute | solution.py:422
  899.2 15.6 %collective-permute-done.57.refs_6_ = bf16[64,5120]{1,0:T(8,128)(2,1)} collective-permute-done((bf16[64,5120]{1,0:T(8,128)(2,1)}, bf16[64,5120]{1,0:T(8,128)(2,1)}, u32[]{:S(2)}, u32[]{:S(2)}) %collective-permute-start.57) | collective-permute-done | bytes 655392 | tf_op jit(solution)/shard_map/ppermute | solution.py:422
  919.8 7.0 fusion
  (303 shorter events, 188.3 us)
Async XLA Ops:
  57.6 17.7 %collective-permute-start.7 = (bf16[256,2560]{1,0:T(8,128)(2,1)S(1)}, bf16[256,2560]{1,0:T(8,128)(2,1)S(1)}, u32[]{:S(2)}, u32[]{:S(2)}) collective-permute-start(bf16[256,2560]{1,0:T(8,128)(2,1)S(1)} %collective-permute-done.3.refs_1_.refs_9_), channel_id=1, source_target_pairs={{0,4},{1,3},{2,6},{3,1},{4,0},{5,7},{6,2},{7,5},{8,12},{9,11},{10,... | collective-permute-start | bytes 3932168 | tf_op jit(solution)/shard_map/ppermute | solution.py:353
  79.5 38.0 %all-to-all-start.1 = ((bf16[4,64,2816]{2,1,0:T(8,128)(2,1)}), bf16[4,64,2816]{2,1,0:T(8,128)(2,1)}, u32[]{:S(2)}, u32[]{:S(2)}) async-start(bf16[4,64,2816]{2,1,0:T(8,128)(2,1)} %pad_maximum_fusion.2), calls=%async_computation.1 | async-start | bytes 2883584 | tf_op jit(solution)/shard_map/all_to_all | solution.py:1295
  83.8 149.7 %all-gather.7.cloned.1.call-start = ((), (), s32[]{:S(2)}) async-start(), calls=%async_computation.9 | async-start | bytes 7208960 | tf_op jit(solution)/shard_map/all_gather | solution.py:1299
  93.6 23.8 %collective-permute-start.10 = (bf16[256,2048]{1,0:T(8,128)(2,1)}, bf16[256,2048]{1,0:T(8,128)(2,1)}, u32[]{:S(2)}, u32[]{:S(2)}) collective-permute-start(bf16[256,2048]{1,0:T(8,128)(2,1)} %refs_0_.1), channel_id=1, source_target_pairs={{0,2},{1,5},{2,0},{3,7},{4,6},{5,1},{6,4},{7,3},{8,10},{9,13},{10,... | collective-permute-start | bytes 3145736 | tf_op jit(solution)/shard_map/ppermute | solution.py:349
  117.5 41.5 %all-to-all-start = ((bf16[8,512,384]{2,1,0:T(8,128)(2,1)}), bf16[8,512,384]{2,1,0:T(8,128)(2,1)S(1)}, u32[]{:S(2)}, u32[]{:S(2)}) async-start(bf16[8,512,384]{2,1,0:T(8,128)(2,1)} %get-tuple-element.291), calls=%async_computation | async-start | bytes 6291456 | tf_op jit(solution)/shard_map/all_to_all | solution.py:1304
  159.0 35.5 %collective-permute-start.13 = (bf16[512,2048]{1,0:T(8,128)(2,1)}, bf16[512,2048]{1,0:T(8,128)(2,1)S(1)}, u32[]{:S(2)}, u32[]{:S(2)}) collective-permute-start(bf16[512,2048]{1,0:T(8,128)(2,1)} %multiply_bitcast_fusion.refs_1_.refs_4_.dy_ref), channel_id=1, source_target_pairs={{0,2},{1,5},{2,0},{3,7},{4,6},{5,1},{6,4},{7,3},{8,10},{9,13},{10,... | collective-permute-start | bytes 6291464 | tf_op jit(solution)/shard_map/ppermute | solution.py:349
  159.5 26.7 %collective-permute-start.12 = (bf16[256,2048]{1,0:T(8,128)(2,1)}, bf16[256,2048]{1,0:T(8,128)(2,1)S(1)}, u32[]{:S(2)}, u32[]{:S(2)}) collective-permute-start(bf16[256,2048]{1,0:T(8,128)(2,1)} %refs_0_.1), channel_id=1, source_target_pairs={{0,4},{1,3},{2,6},{3,1},{4,0},{5,7},{6,2},{7,5},{8,12},{9,11},{10,... | collective-permute-start | bytes 3145736 | tf_op jit(solution)/shard_map/ppermute | solution.py:353
  194.5 37.3 %collective-permute-start.15 = (bf16[512,2048]{1,0:T(8,128)(2,1)S(1)}, bf16[512,2048]{1,0:T(8,128)(2,1)S(1)}, u32[]{:S(2)}, u32[]{:S(2)}) collective-permute-start(bf16[512,2048]{1,0:T(8,128)(2,1)S(1)} %copy-done.27), channel_id=1, source_target_pairs={{0,4},{1,3},{2,6},{3,1},{4,0},{5,7},{6,2},{7,5},{8,12},{9,11},{10,... | collective-permute-start | bytes 6291464 | tf_op jit(solution)/shard_map/ppermute | solution.py:353
  196.3 35.6 %collective-permute-start.14 = (bf16[256,2048]{1,0:T(8,128)(2,1)}, bf16[256,2048]{1,0:T(8,128)(2,1)S(1)}, u32[]{:S(2)}, u32[]{:S(2)}) collective-permute-start(bf16[256,2048]{1,0:T(8,128)(2,1)} %collective-permute-done.10.refs_1_), channel_id=1, source_target_pairs={{0,4},{1,3},{2,6},{3,1},{4,0},{5,7},{6,2},{7,5},{8,12},{9,11},{10,... | collective-permute-start | bytes 3145736 | tf_op jit(solution)/shard_map/ppermute | solution.py:353
  233.5 36.5 %collective-permute-start.17 = (bf16[512,2048]{1,0:T(8,128)(2,1)}, bf16[512,2048]{1,0:T(8,128)(2,1)}, u32[]{:S(2)}, u32[]{:S(2)}) collective-permute-start(bf16[512,2048]{1,0:T(8,128)(2,1)} %copy-done.37), channel_id=1, source_target_pairs={{0,4},{1,3},{2,6},{3,1},{4,0},{5,7},{6,2},{7,5},{8,12},{9,11},{10,... | collective-permute-start | bytes 6291464 | tf_op jit(solution)/shard_map/ppermute | solution.py:353
  251.2 31.8 %all-to-all-start.2 = ((bf16[8,512,256]{2,1,0:T(8,128)(2,1)}), bf16[8,512,256]{2,1,0:T(8,128)(2,1)S(1)}, u32[]{:S(2)}, u32[]{:S(2)}) async-start(bf16[8,512,256]{2,1,0:T(8,128)(2,1)} %copy-done.6), calls=%async_computation.2 | async-start | bytes 4194304 | tf_op jit(solution)/shard_map/all_to_all | solution.py:1322
  254.9 320.2 %reduce-scatter.2.cloned.1.call-start = ((), (), s32[]{:S(2)}) async-start(), calls=%async_computation.8 | async-start | bytes 7208960 | tf_op jit(solution)/shard_map/reduce_scatter | solution.py:1359
  296.2 26.8 %collective-permute-start.22 = (bf16[512,2048]{1,0:T(8,128)(2,1)}, bf16[512,2048]{1,0:T(8,128)(2,1)S(1)}, u32[]{:S(2)}, u32[]{:S(2)}) collective-permute-start(bf16[512,2048]{1,0:T(8,128)(2,1)} %get-tuple-element.346.refs_0_.refs_4_), channel_id=1, source_target_pairs={{0,2},{1,5},{2,0},{3,7},{4,6},{5,1},{6,4},{7,3},{8,10},{9,13},{10,... | collective-permute-start | bytes 6291464 | tf_op jit(solution)/shard_map/ppermute | solution.py:349
  323.1 27.2 %collective-permute-start.23 = (bf16[512,2048]{1,0:T(8,128)(2,1)S(1)}, bf16[512,2048]{1,0:T(8,128)(2,1)}, u32[]{:S(2)}, u32[]{:S(2)}) collective-permute-start(bf16[512,2048]{1,0:T(8,128)(2,1)S(1)} %copy-done.28), channel_id=1, source_target_pairs={{0,4},{1,3},{2,6},{3,1},{4,0},{5,7},{6,2},{7,5},{8,12},{9,11},{10,... | collective-permute-start | bytes 6291464 | tf_op jit(solution)/shard_map/ppermute | solution.py:353
  350.3 27.3 %collective-permute-start.24 = (bf16[512,2048]{1,0:T(8,128)(2,1)}, bf16[512,2048]{1,0:T(8,128)(2,1)S(1)}, u32[]{:S(2)}, u32[]{:S(2)}) collective-permute-start(bf16[512,2048]{1,0:T(8,128)(2,1)} %copy-done.29), channel_id=1, source_target_pairs={{0,4},{1,3},{2,6},{3,1},{4,0},{5,7},{6,2},{7,5},{8,12},{9,11},{10,... | collective-permute-start | bytes 6291464 | tf_op jit(solution)/shard_map/ppermute | solution.py:353
  377.6 27.1 %collective-permute-start.25 = (bf16[512,2048]{1,0:T(8,128)(2,1)}, bf16[512,2048]{1,0:T(8,128)(2,1)S(1)}, u32[]{:S(2)}, u32[]{:S(2)}) collective-permute-start(bf16[512,2048]{1,0:T(8,128)(2,1)} %get-tuple-element.361), channel_id=1, source_target_pairs={{0,2},{1,5},{2,0},{3,7},{4,6},{5,1},{6,4},{7,3},{8,10},{9,13},{10,... | collective-permute-start | bytes 6291464 | tf_op jit(solution)/shard_map/ppermute | solution.py:349
  404.7 35.8 %collective-permute-start.26 = (bf16[512,2048]{1,0:T(8,128)(2,1)}, bf16[512,2048]{1,0:T(8,128)(2,1)S(1)}, u32[]{:S(2)}, u32[]{:S(2)}) collective-permute-start(bf16[512,2048]{1,0:T(8,128)(2,1)} %get-tuple-element.370), channel_id=1, source_target_pairs={{0,2},{1,5},{2,0},{3,7},{4,6},{5,1},{6,4},{7,3},{8,10},{9,13},{10,... | collective-permute-start | bytes 6291464 | tf_op jit(solution)/shard_map/ppermute | solution.py:349
  445.8 18.3 %collective-permute-start.27 = (bf16[4,4,64,2816]{3,2,1,0:T(8,128)(2,1)}, bf16[4,4,64,2816]{3,2,1,0:T(8,128)(2,1)}, u32[]{:S(2)}, u32[]{:S(2)}) collective-permute-start(bf16[4,4,64,2816]{3,2,1,0:T(8,128)(2,1)} %get-tuple-element.393), channel_id=1, source_target_pairs={{0,1},{1,0},{2,3},{3,2},{4,5},{5,4},{6,7},{7,6},{8,9},{9,8},{10,11... | collective-permute-start | bytes 17301512 | tf_op jit(solution)/shard_map/ppermute | solution.py:357
  445.8 26.2 %collective-permute-start.28 = (bf16[512,2048]{1,0:T(8,128)(2,1)}, bf16[512,2048]{1,0:T(8,128)(2,1)S(1)}, u32[]{:S(2)}, u32[]{:S(2)}) collective-permute-start(bf16[512,2048]{1,0:T(8,128)(2,1)} %add_convert_fusion.3), channel_id=1, source_target_pairs={{0,4},{1,3},{2,6},{3,1},{4,0},{5,7},{6,2},{7,5},{8,12},{9,11},{10,... | collective-permute-start | bytes 6291464 | tf_op jit(solution)/shard_map/ppermute | solution.py:353
  490.8 31.1 %all-to-all-start.3 = ((bf16[8,512,256]{2,1,0:T(8,128)(2,1)}), bf16[8,512,256]{2,1,0:T(8,128)(2,1)}, u32[]{:S(2)}, u32[]{:S(2)}) async-start(bf16[8,512,256]{2,1,0:T(8,128)(2,1)} %get-tuple-element.408), calls=%async_computation.3 | async-start | bytes 4194304 | tf_op jit(solution)/shard_map/all_to_all | solution.py:1368
  521.9 26.4 %collective-permute-start.31 = (bf16[4,256,2048]{2,1,0:T(8,128)(2,1)}, bf16[4,256,2048]{2,1,0:T(8,128)(2,1)}, u32[]{:S(2)}, u32[]{:S(2)}) collective-permute-start(bf16[4,256,2048]{2,1,0:T(8,128)(2,1)} %get-tuple-element.415), channel_id=1, source_target_pairs={{0,1},{1,0},{2,3},{3,2},{4,5},{5,4},{6,7},{7,6},{8,9},{9,8},{10,11... | collective-permute-start | bytes 12582920 | tf_op jit(solution)/shard_map/ppermute | solution.py:357
  521.9 26.4 %collective-permute-start.30 = (bf16[512,2048]{1,0:T(8,128)(2,1)}, bf16[512,2048]{1,0:T(8,128)(2,1)}, u32[]{:S(2)}, u32[]{:S(2)}) collective-permute-start(bf16[512,2048]{1,0:T(8,128)(2,1)} %get-tuple-element.425.refs_0_), channel_id=1, source_target_pairs={{0,2},{1,5},{2,0},{3,7},{4,6},{5,1},{6,4},{7,3},{8,10},{9,13},{10,... | collective-permute-start | bytes 6291464 | tf_op jit(solution)/shard_map/ppermute | solution.py:349
  548.3 26.1 %collective-permute-start.32 = (bf16[512,2048]{1,0:T(8,128)(2,1)S(1)}, bf16[512,2048]{1,0:T(8,128)(2,1)}, u32[]{:S(2)}, u32[]{:S(2)}) collective-permute-start(bf16[512,2048]{1,0:T(8,128)(2,1)S(1)} %copy-done.20), channel_id=1, source_target_pairs={{0,4},{1,3},{2,6},{3,1},{4,0},{5,7},{6,2},{7,5},{8,12},{9,11},{10,... | collective-permute-start | bytes 6291464 | tf_op jit(solution)/shard_map/ppermute | solution.py:353
  548.8 25.6 %collective-permute-start.33 = (bf16[512,2048]{1,0:T(8,128)(2,1)S(1)}, bf16[512,2048]{1,0:T(8,128)(2,1)}, u32[]{:S(2)}, u32[]{:S(2)}) collective-permute-start(bf16[512,2048]{1,0:T(8,128)(2,1)S(1)} %copy-done.20), channel_id=1, source_target_pairs={{0,1},{1,0},{2,3},{3,2},{4,5},{5,4},{6,7},{7,6},{8,9},{9,8},{10,11... | collective-permute-start | bytes 6291464 | tf_op jit(solution)/shard_map/ppermute | solution.py:357
  548.8 25.6 %collective-permute-start.34 = (bf16[512,2048]{1,0:T(8,128)(2,1)}, bf16[512,2048]{1,0:T(8,128)(2,1)}, u32[]{:S(2)}, u32[]{:S(2)}) collective-permute-start(bf16[512,2048]{1,0:T(8,128)(2,1)} %collective-permute-done.30.refs_1_), channel_id=1, source_target_pairs={{0,1},{1,0},{2,3},{3,2},{4,5},{5,4},{6,7},{7,6},{8,9},{9,8},{10,11... | collective-permute-start | bytes 6291464 | tf_op jit(solution)/shard_map/ppermute | solution.py:357
  575.2 52.3 %collective-permute-start.36 = (bf16[512,2048]{1,0:T(8,128)(2,1)}, bf16[512,2048]{1,0:T(8,128)(2,1)S(1)}, u32[]{:S(2)}, u32[]{:S(2)}) collective-permute-start(bf16[512,2048]{1,0:T(8,128)(2,1)} %collective-permute-done.32.refs_2_), channel_id=1, source_target_pairs={{0,1},{1,0},{2,3},{3,2},{4,5},{5,4},{6,7},{7,6},{8,9},{9,8},{10,11... | collective-permute-start | bytes 6291464 | tf_op jit(solution)/shard_map/ppermute | solution.py:357
  575.2 52.3 %collective-permute-start.35 = (bf16[2,176,2048]{2,1,0:T(8,128)(2,1)}, bf16[2,176,2048]{2,1,0:T(8,128)(2,1)}, u32[]{:S(2)}, u32[]{:S(2)}) collective-permute-start(bf16[2,176,2048]{2,1,0:T(8,128)(2,1)} %fusion.4), channel_id=1, source_target_pairs={{0,8},{8,0},{16,24},{24,16},{1,9},{9,1},{17,25},{25,17},{2,10},{10... | collective-permute-start | bytes 4325384 | tf_op jit(solution)/shard_map/ppermute | solution.py:1391
  594.9 23.9 %all-to-all-start.4 = ((bf16[4,64,2816]{2,1,0:T(8,128)(2,1)}), bf16[4,64,2816]{2,1,0:T(8,128)(2,1)S(1)}, u32[]{:S(2)}, u32[]{:S(2)}) async-start(bf16[4,64,2816]{2,1,0:T(8,128)(2,1)} %bitcast.150), calls=%async_computation.5 | async-start | bytes 2883584 | tf_op jit(solution)/shard_map/all_to_all | solution.py:1392
  598.5 230.7 %all-gather.9.cloned.1.call-start = ((), (), s32[]{:S(2)}) async-start(), calls=%async_computation.10 | async-start | bytes 7208960 | tf_op jit(solution)/shard_map/all_gather | solution.py:1403
  633.7 78.3 %collective-permute-start.39 = (bf16[512,2048]{1,0:T(8,128)(2,1)}, bf16[512,2048]{1,0:T(8,128)(2,1)}, u32[]{:S(2)}, u32[]{:S(2)}) collective-permute-start(bf16[512,2048]{1,0:T(8,128)(2,1)} %collective-permute-done.30.refs_1_), channel_id=1, source_target_pairs={{0,4},{1,3},{2,6},{3,1},{4,0},{5,7},{6,2},{7,5},{8,12},{9,11},{10,... | collective-permute-start | bytes 6291464 | tf_op jit(solution)/shard_map/ppermute | solution.py:353
  635.1 59.0 %collective-permute-start.38 = (bf16[256,2048]{1,0:T(8,128)(2,1)}, bf16[256,2048]{1,0:T(8,128)(2,1)S(1)}, u32[]{:S(2)}, u32[]{:S(2)}) collective-permute-start(bf16[256,2048]{1,0:T(8,128)(2,1)} %get-tuple-element.459), channel_id=1, source_target_pairs={{0,2},{1,5},{2,0},{3,7},{4,6},{5,1},{6,4},{7,3},{8,10},{9,13},{10,... | collective-permute-start | bytes 3145736 | tf_op jit(solution)/shard_map/ppermute | solution.py:349
  636.6 75.4 %collective-permute-start.37 = (bf16[256,2048]{1,0:T(8,128)(2,1)}, bf16[256,2048]{1,0:T(8,128)(2,1)}, u32[]{:S(2)}, u32[]{:S(2)}) collective-permute-start(bf16[256,2048]{1,0:T(8,128)(2,1)} %get-tuple-element.458), channel_id=1, source_target_pairs={{0,2},{1,5},{2,0},{3,7},{4,6},{5,1},{6,4},{7,3},{8,10},{9,13},{10,... | collective-permute-start | bytes 3145736 | tf_op jit(solution)/shard_map/ppermute | solution.py:349
  637.2 74.8 %collective-permute-start.40 = (bf16[176,2048]{1,0:T(8,128)(2,1)}, bf16[176,2048]{1,0:T(8,128)(2,1)S(1)}, u32[]{:S(2)}, u32[]{:S(2)}) collective-permute-start(bf16[176,2048]{1,0:T(8,128)(2,1)} %fusion.14), channel_id=1, source_target_pairs={{0,16},{8,24},{16,0},{24,8},{1,17},{9,25},{17,1},{25,9},{2,18},{10... | collective-permute-start | bytes 2162696 | tf_op jit(solution)/shard_map/ppermute | solution.py:1407
  712.0 23.9 %collective-permute-start.41 = (bf16[256,2048]{1,0:T(8,128)(2,1)S(1)}, bf16[256,2048]{1,0:T(8,128)(2,1)}, u32[]{:S(2)}, u32[]{:S(2)}) collective-permute-start(bf16[256,2048]{1,0:T(8,128)(2,1)S(1)} %fusion.3), channel_id=1, source_target_pairs={{0,4},{1,3},{2,6},{3,1},{4,0},{5,7},{6,2},{7,5},{8,12},{9,11},{10,... | collective-permute-start | bytes 3145736 | tf_op jit(solution)/shard_map/ppermute | solution.py:353
  712.7 64.1 %all-to-all-start.5 = ((bf16[8,512,384]{2,1,0:T(8,128)(2,1)}), bf16[8,512,384]{2,1,0:T(8,128)(2,1)}, u32[]{:S(2)}, u32[]{:S(2)}) async-start(bf16[8,512,384]{2,1,0:T(8,128)(2,1)} %get-tuple-element.467.refs_8_), calls=%async_computation.6 | async-start | bytes 6291456 | tf_op jit(solution)/shard_map/all_to_all | solution.py:1414
  720.7 157.3 %all-gather.11.cloned.1.call-start = ((), (), s32[]{:S(2)}) async-start(), calls=%async_computation.11 | async-start | bytes 3604480 | tf_op jit(solution)/shard_map/all_gather | solution.py:1428
  740.0 27.4 %collective-permute-start.43 = (bf16[64,5120]{1,0:T(8,128)(2,1)}, bf16[64,5120]{1,0:T(8,128)(2,1)}, u32[]{:S(2)}, u32[]{:S(2)}) collective-permute-start(bf16[64,5120]{1,0:T(8,128)(2,1)} %get-tuple-element.475), channel_id=1, source_target_pairs={{0,8},{1,9},{2,10},{3,11},{4,12},{5,13},{6,14},{7,15}} | collective-permute-start | bytes 1966088 | tf_op jit(solution)/shard_map/ppermute | solution.py:409
  745.7 21.6 %collective-permute-start.44 = (bf16[64,5120]{1,0:T(8,128)(2,1)}, bf16[64,5120]{1,0:T(8,128)(2,1)}, u32[]{:S(2)}, u32[]{:S(2)}) collective-permute-start(bf16[64,5120]{1,0:T(8,128)(2,1)} %get-tuple-element.476), channel_id=1, source_target_pairs={{24,16},{25,17},{26,18},{27,19},{28,20},{29,21},{30,22},{31,23}} | collective-permute-start | bytes 1966088 | tf_op jit(solution)/shard_map/ppermute | solution.py:410
  770.0 18.2 %collective-permute-start.45 = (bf16[64,5120]{1,0:T(8,128)(2,1)}, bf16[64,5120]{1,0:T(8,128)(2,1)}, u32[]{:S(2)}, u32[]{:S(2)}) collective-permute-start(bf16[64,5120]{1,0:T(8,128)(2,1)} %get-tuple-element.481), channel_id=1, source_target_pairs={{0,8},{8,16},{1,9},{9,17},{2,10},{10,18},{3,11},{11,19},{4,12},{12... | collective-permute-start | bytes 1966088 | tf_op jit(solution)/shard_map/ppermute | solution.py:409
  790.8 24.3 %collective-permute-start.47 = (bf16[64,5120]{1,0:T(8,128)(2,1)}, bf16[64,5120]{1,0:T(8,128)(2,1)}, u32[]{:S(2)}, u32[]{:S(2)}) collective-permute-start(bf16[64,5120]{1,0:T(8,128)(2,1)} %get-tuple-element.487), channel_id=1, source_target_pairs={{0,8},{8,16},{16,24},{1,9},{9,17},{17,25},{2,10},{10,18},{18,26},{... | collective-permute-start | bytes 1966088 | tf_op jit(solution)/shard_map/ppermute | solution.py:409
  798.1 28.7 %collective-permute-start.48 = (bf16[64,5120]{1,0:T(8,128)(2,1)}, bf16[64,5120]{1,0:T(8,128)(2,1)}, u32[]{:S(2)}, u32[]{:S(2)}) collective-permute-start(bf16[64,5120]{1,0:T(8,128)(2,1)} %get-tuple-element.488), channel_id=1, source_target_pairs={{24,16},{16,8},{8,0},{25,17},{17,9},{9,1},{26,18},{18,10},{10,2},{... | collective-permute-start | bytes 1966088 | tf_op jit(solution)/shard_map/ppermute | solution.py:410
  799.4 33.2 %collective-permute-start.49 = (bf16[512,2048]{1,0:T(8,128)(2,1)}, bf16[512,2048]{1,0:T(8,128)(2,1)}, u32[]{:S(2)}, u32[]{:S(2)}) collective-permute-start(bf16[512,2048]{1,0:T(8,128)(2,1)} %get-tuple-element.500), channel_id=1, source_target_pairs={{0,2},{1,5},{2,0},{3,7},{4,6},{5,1},{6,4},{7,3},{8,10},{9,13},{10,... | collective-permute-start | bytes 6291464 | tf_op jit(solution)/shard_map/ppermute | solution.py:349
  841.0 78.8 %collective-permute-start.50 = (bf16[512,2048]{1,0:T(8,128)(2,1)}, bf16[512,2048]{1,0:T(8,128)(2,1)}, u32[]{:S(2)}, u32[]{:S(2)}) collective-permute-start(bf16[512,2048]{1,0:T(8,128)(2,1)} %get-tuple-element.502), channel_id=1, source_target_pairs={{0,2},{1,5},{2,0},{3,7},{4,6},{5,1},{6,4},{7,3},{8,10},{9,13},{10,... | collective-permute-start | bytes 6291464 | tf_op jit(solution)/shard_map/ppermute | solution.py:349
  841.6 78.2 %collective-permute-start.51 = (bf16[512,2048]{1,0:T(8,128)(2,1)}, bf16[512,2048]{1,0:T(8,128)(2,1)}, u32[]{:S(2)}, u32[]{:S(2)}) collective-permute-start(bf16[512,2048]{1,0:T(8,128)(2,1)} %add_convert_fusion.2), channel_id=1, source_target_pairs={{0,4},{1,3},{2,6},{3,1},{4,0},{5,7},{6,2},{7,5},{8,12},{9,11},{10,... | collective-permute-start | bytes 6291464 | tf_op jit(solution)/shard_map/ppermute | solution.py:353
  842.2 28.3 %collective-permute-start.52 = (bf16[64,5120]{1,0:T(8,128)(2,1)S(1)}, bf16[64,5120]{1,0:T(8,128)(2,1)S(1)}, u32[]{:S(2)}, u32[]{:S(2)}) collective-permute-start(bf16[64,5120]{1,0:T(8,128)(2,1)S(1)} %pad_maximum_fusion.3.refs_0_), channel_id=1, source_target_pairs={{0,8},{8,16},{16,24},{1,9},{9,17},{17,25},{2,10},{10,18},{18,26},{... | collective-permute-start | bytes 1966088 | tf_op jit(solution)/shard_map/ppermute | solution.py:421
  843.6 31.5 %collective-permute-start.53 = (bf16[64,5120]{1,0:T(8,128)(2,1)S(1)}, bf16[64,5120]{1,0:T(8,128)(2,1)S(1)}, u32[]{:S(2)}, u32[]{:S(2)}) collective-permute-start(bf16[64,5120]{1,0:T(8,128)(2,1)S(1)} %pad_maximum_fusion.3.refs_0_), channel_id=1, source_target_pairs={{8,0},{16,8},{24,16},{9,1},{17,9},{25,17},{10,2},{18,10},{26,18},{... | collective-permute-start | bytes 1966088 | tf_op jit(solution)/shard_map/ppermute | solution.py:422
  876.8 18.6 %collective-permute-start.55 = (bf16[64,5120]{1,0:T(8,128)(2,1)S(1)}, bf16[64,5120]{1,0:T(8,128)(2,1)}, u32[]{:S(2)}, u32[]{:S(2)}) collective-permute-start(bf16[64,5120]{1,0:T(8,128)(2,1)S(1)} %collective-permute-done.53.refs_4_), channel_id=1, source_target_pairs={{8,0},{16,8},{9,1},{17,9},{10,2},{18,10},{11,3},{19,11},{12,4},{20... | collective-permute-start | bytes 1966088 | tf_op jit(solution)/shard_map/ppermute | solution.py:422
  896.9 18.0 %collective-permute-start.57 = (bf16[64,5120]{1,0:T(8,128)(2,1)}, bf16[64,5120]{1,0:T(8,128)(2,1)}, u32[]{:S(2)}, u32[]{:S(2)}) collective-permute-start(bf16[64,5120]{1,0:T(8,128)(2,1)} %collective-permute-done.55.refs_5_), channel_id=1, source_target_pairs={{8,0},{9,1},{10,2},{11,3},{12,4},{13,5},{14,6},{15,7}} | collective-permute-start | bytes 1966088 | tf_op jit(solution)/shard_map/ppermute | solution.py:422
  (84 other events, 935.7 us)
Sparse Core Ops, SparseCore 0:
  117.6 107.0 all-gather.6
  472.2 102.8 reduce-scatter.1
  636.7 127.4 all-gather.8
  800.7 69.0 all-gather.10

commit v8 on v7

--- a/solution.py
+++ b/solution.py
@@ -341,8 +341,6 @@
 SECOND = swap_pairs(4, 2)
 SIBLING = swap_pairs(1, 1)
 SAME_CORE = [[0, 2, 4, 6], [1, 3, 5, 7]]
-LINE_NEAR = [(z, z ^ 1) for z in range(4)]
-LINE_FAR = [(z, z ^ 2) for z in range(4)]
 
 
 def send_first(x):
@@ -1372,42 +1370,38 @@
     def back_call(heads, start, stop, **kwargs):
         return attend_back(zeros_one, qkv_heads, heads, lse, cos_all, sin_all, start, stop, **kwargs)
 
-    turns = (0, blocks // 8, blocks // 4, (3 * blocks) // 8, blocks)
+    turns = (0, blocks // 4, (3 * blocks) // 8, blocks)
     wo_got = send_sibling(wo_give)
     a_first = send_first(normed)
+    a_second = send_second(normed)
+    a_theirs = [send_sibling(normed)]
+    dn_sum = (dn_keep.astype(F32) + dn_got.astype(F32)).astype(BF)
     bwd = back_call(d_heads, turns[0], turns[1], out=out_heads)
-    d_heads, a_first, wo_got, normed, *bwd = fence(d_heads, a_first, wo_got, normed, *bwd)
-    a_second = send_second(normed)
-    a_theirs = [send_sibling(normed), send_sibling(a_first)]
-    bwd = back_call(d_heads, turns[1], turns[2], before=bwd)
-    dn_parts = [part.reshape(2, 2, dn_keep.shape[0] // planes, width) for part in (dn_keep, dn_got)]
-    dn_move = pick_sum(dn_parts, 1 - (plane & 1), 1).astype(BF)
-    d_heads, gu_z, a_second, dn_move, *moves = fence(d_heads, gu_z, a_second, dn_move, *a_theirs, *bwd)
-    a_theirs, bwd = moves[:2], moves[2:]
+    d_heads, a_first, a_second, wo_got, gu_z, dn_sum, *moves = fence(
+        d_heads, a_first, a_second, wo_got, gu_z, dn_sum, *a_theirs, *bwd
+    )
+    a_theirs, bwd = moves[:1], moves[1:]
 
     def wo_part(place):
         return pick(wo_keep, place).astype(F32) + pick(wo_got, place).astype(F32)
 
-    dn_move = lax.ppermute(dn_move, "dp", LINE_NEAR)
+    dn_z = lax.psum_scatter(dn_sum, "dp", scatter_dimension=0, tiled=True)
     gu_z = lax.all_to_all(gu_z, "sp", 0, 0, axis_index_groups=SAME_CORE, tiled=True)
-    a_theirs.append(send_sibling(a_second))
-    bwd = back_call(d_heads, turns[2], turns[3], before=bwd)
-    d_heads, gu_z, a_first, dn_move, *moves = fence(d_heads, gu_z, a_first, dn_move, *a_theirs, *bwd)
+    a_theirs += [send_sibling(a_first), send_sibling(a_second)]
+    bwd = back_call(d_heads, turns[1], turns[2], before=bwd)
+    d_heads, gu_z, a_first, *moves = fence(d_heads, gu_z, a_first, *a_theirs, *bwd)
     a_theirs, bwd = moves[:3], moves[3:]
 
-    dn_own = pick_sum(dn_parts, plane & 1, 1) + dn_move.astype(F32)
-    dn_move = pick(dn_own, 1 - plane // 2).astype(BF)
     wo_first = wo_part(chip ^ (first_mask // 2)).astype(BF)
     wo_far = wo_part(chip ^ 3).astype(BF)
-    d_heads, gu_z, a_first, wo_first, wo_far, dn_move = fence(d_heads, gu_z, a_first, wo_first, wo_far, dn_move)
+    d_heads, gu_z, a_first, wo_first, wo_far = fence(d_heads, gu_z, a_first, wo_first, wo_far)
     gu_all = lax.all_gather(gu_z, "dp", axis=0, tiled=False)
     a_far = send_second(a_first)
     wo_far = send_first(wo_far)
     wo_first = send_first(wo_first)
-    dn_move = lax.ppermute(dn_move, "dp", LINE_FAR)
-    bwd = back_call(d_heads, turns[3], turns[4], before=bwd)
+    bwd = back_call(d_heads, turns[2], turns[3], before=bwd)
     wo_pass = (wo_part(chip ^ (second_mask // 2)) + wo_far.astype(F32)).astype(BF)
-    dp_heads, wo_first, wo_pass, a_far, dn_move = fence(bwd[0], wo_first, wo_pass, a_far, dn_move)
+    dp_heads, wo_first, wo_pass, a_far = fence(bwd[0], wo_first, wo_pass, a_far)
 
     wo_passed = send_second(wo_pass)
     a_theirs.append(send_sibling(a_far))
@@ -1424,7 +1418,6 @@
         y_far, y_first, *moves = fence(y_far, y_first, *moves)
         moves = line_scatter_move(moves, step)
         if step == 1:
-            dn_z = (pick(dn_own, plane // 2) + dn_move.astype(F32)).astype(BF)
             dn_all = lax.all_gather(dn_z, "dp", axis=0, tiled=False)
         elif step == 2:
             back, *moves = fence(back, *moves)
@@ -1445,6 +1438,9 @@
     last_steps = [(last_z, last_z)]
     outs = []
     for step in range(1, planes):
+        if step == planes - 1:
+            y_got_first, y_passed, *moves = fence(y_got_first, y_passed, *last_steps[-1])
+            last_steps[-1] = tuple(moves)
         last_steps.append(line_gather_move(last_steps[-1], step))
         if step == 1:
             outs += spread(gu_all, w_gate_up, g_mlp.astype(F32).reshape(share, 1))
@@ -1453,7 +1449,6 @@
         if step == planes - 1:
             y_sum = own[4].astype(F32) + y_got_first.astype(F32) + y_passed.astype(F32)
             outs.append((residual + y_sum).astype(BF).reshape(tokens.shape))
-            break
         moves = fence(*last_steps[-1], *outs)
         last_steps[-1], outs = tuple(moves[:2]), list(moves[2:])
     grad_w_gate_up, grad_g_mlp, grad_w_down, output = outs

time: 941 us -> 918 us (0.976)
  Pallas kernels: 416 us -> 404 us
  starting transfers between devices: 126 us -> 114 us
    ppermute x2 -> x0, waiting for transfers between devices: 24.4 us -> none  [the longest x1 15.8 us: fast_body(): dn_move = lax.ppermute(dn_move, 'dp', LINE_FAR)]
    ppermute x3, waiting for transfers between devices: 31.5 us -> 52.7 us  [line_scatter_move(): right = lax.ppermute(sends[0], 'dp', [(i, i + 1) for i in range(step)])]
    ppermute x2 -> x0, starting transfers between devices: 19.8 us -> none  [the longest x1 19.8 us: fast_body(): dn_move = lax.ppermute(dn_move, 'dp', LINE_NEAR)]
    ppermute x3, starting transfers between devices: 18.3 us -> 28.9 us  [line_scatter_move(): right = lax.ppermute(sends[0], 'dp', [(i, i + 1) for i in range(step)])]
    all_gather x1, starting transfers between devices: 9.79 us -> 0.21 us  [fast_body(): lax.all_gather(after(gu_part, qkv_send), 'dp', axis=0, tiled=False)]
    pallas_call x4 -> x3, Pallas kernels: 114 us -> 105 us  [attend_back(): pl.pallas_call(functools.partial(attend_back_kernel, heads=heads, start=s...]
    unnamed x126 -> x120, local copies, waits for them, and re-layouts: 39.4 us -> 40 us
  transfers between devices with their start and end apart: 69 -> 68, of which waited for: 26 -> 26; matrix products, arithmetic and copies ran while one was open for 8% -> 8% of each run, Pallas kernels for 43% -> 43%
where the time goes in v8:
time: 918 us; the launch traced here: 908 us
  Pallas kernels  404 us (44%)
  waiting for transfers between devices  249 us (27%)
  starting transfers between devices  114 us (12%)
  other arithmetic  79.7 us (9%)
  local copies, waits for them, and re-layouts  45.8 us (5%)
  between operations  15.8 us (2%)
    pallas_call x3, Pallas kernels, attend_back(): pl.pallas_call(functools.partial(attend_back_kernel, heads=heads, start=s...  105 us
    pallas_call x4, Pallas kernels, ffn(): pl.pallas_call(functools.partial(ffn_kernel, cuts=cuts), in_specs=[hbm] *...  103 us
    ppermute x3, waiting for transfers between devices, line_scatter_move(): right = lax.ppermute(sends[0], 'dp', [(i, i + 1) for i in range(step)])  52.7 us
    pallas_call x3, Pallas kernels, attend(): pl.pallas_call(functools.partial(attend_kernel, heads=heads, start=start,...  50.1 us
    ppermute x13, waiting for transfers between devices, send_second(): return lax.ppermute(x, 'sp', SECOND)  42 us
    unnamed x120, local copies, waits for them, and re-layouts  40 us
    pallas_call x1, Pallas kernels, grad_gu(): pl.pallas_call(functools.partial(grad_gu_kernel, count=count), grid_spec=...  34.5 us
    ppermute x3, starting transfers between devices, line_scatter_move(): right = lax.ppermute(sends[0], 'dp', [(i, i + 1) for i in range(step)])  28.9 us
  transfers between devices with their start and end apart: 68, of which 26 were waited for; matrix products, arithmetic and copies ran while one was open for 8% of the time, Pallas kernels for 43%

profile of v8, /device:TPU:0, one launch (start us, length us, event | category | flops | bytes accessed | tf_op | source)
XLA Modules:
  0.0 907.9 jit_solution(2953324964502208480)
XLA Ops:
  27.8 12.1 %collective-permute-done.3.refs_1_.refs_9_ = bf16[256,2560]{1,0:T(8,128)(2,1)S(1)} collective-permute-done((bf16[256,2560]{1,0:T(8,128)(2,1)S(1)}, bf16[256,2560]{1,0:T(8,128)(2,1)S(1)}, u32[]{:S(2)}, u32[]{:S(2)}) %collective-permute-start.3) | collective-permute-done | bytes 1310752 | tf_op jit(solution)/shard_map/ppermute | solution.py:347
  42.5 7.5 fusion.12
  61.2 14.0 %collective-permute-done.7.refs_3_.refs_11_ = bf16[256,2560]{1,0:T(8,128)(2,1)S(1)} collective-permute-done((bf16[256,2560]{1,0:T(8,128)(2,1)S(1)}, bf16[256,2560]{1,0:T(8,128)(2,1)S(1)}, u32[]{:S(2)}, u32[]{:S(2)}) %collective-permute-start.7) | collective-permute-done | bytes 1310752 | tf_op jit(solution)/shard_map/ppermute | solution.py:351
  88.8 18.3 %project.1 = (bf16[8,512,384]{2,1,0:T(8,128)(2,1)}, bf16[512,2048]{1,0:T(8,128)(2,1)}, f32[512,1]{1,0:T(8,128)S(1)}) custom-call(s32[8]{0:T(128)S(1)} %stack.67.place_ref, bf16[512,2048]{1,0:T(8,128)(2,1)} %bitcast.115, f32[1,2048]{1,0:T(1,128)S(1)} %get-tuple-element.542.gain_ref, f32[512,128]{1,0:T(8,128)S(1)} %pad_maximum_fusion.4.cos_ref, ...), custom_call_target="tpu_custom_call" | custom-call | flops 1 | bytes 1 | tf_op jit(solution)/shard_map/project/pallas_call | solution.py:734
  107.8 5.9 collective-permute-done.10.refs_1_
  119.5 8.3 maximum_select_fusion.refs_3_
  127.8 27.7 %all-to-all-done = bf16[8,512,384]{2,1,0:T(8,128)(2,1)S(1)} async-done(((bf16[8,512,384]{2,1,0:T(8,128)(2,1)}), bf16[8,512,384]{2,1,0:T(8,128)(2,1)S(1)}, u32[]{:S(2)}, u32[]{:S(2)}) %all-to-all-start) | async-done | bytes 3145760 | tf_op jit(solution)/shard_map/all_to_all | solution.py:1302
  156.6 30.3 %attend.3 = (f32[4096,256]{1,0:T(8,128)}, bf16[8,512,256]{2,1,0:T(8,128)(2,1)S(1)}, f32[8,4,512]{2,1,0:T(4,128)S(1)}) custom-call(s32[1]{0:T(128)} %bitcast.6.zeros_ref, bf16[4096,384]{1,0:T(8,128)(2,1)S(1)} %bitcast.91, bf16[4096,384]{1,0:T(8,128)(2,1)S(1)} %bitcast.92), custom_call_target="tpu_custom_call" | custom-call | flops 1 | bytes 1 | tf_op jit(solution)/shard_map/attend/pallas_call | solution.py:1054
  193.0 11.3 %attend.4 = (f32[4096,256]{1,0:T(8,128)}, bf16[8,512,256]{2,1,0:T(8,128)(2,1)S(1)}, f32[8,4,512]{2,1,0:T(4,128)S(1)}) custom-call(s32[1]{0:T(128)} %bitcast.6.zeros_ref, bf16[4096,384]{1,0:T(8,128)(2,1)S(1)} %bitcast.93, bf16[4096,384]{1,0:T(8,128)(2,1)S(1)} %bitcast.94, ...), custom_call_target="tpu_custom_call", output_to_operand_aliasing={{0}: (3, {}), {1}: (4, {}), {2}: (5, {})} | custom-call | flops 1 | bytes 1 | tf_op jit(solution)/shard_map/attend/pallas_call | solution.py:1054
  205.7 22.6 %collective-permute-done.14.refs_3_ = bf16[256,2048]{1,0:T(8,128)(2,1)S(1)} collective-permute-done((bf16[256,2048]{1,0:T(8,128)(2,1)}, bf16[256,2048]{1,0:T(8,128)(2,1)S(1)}, u32[]{:S(2)}, u32[]{:S(2)}) %collective-permute-start.14) | collective-permute-done | bytes 1048608 | tf_op jit(solution)/shard_map/ppermute | solution.py:351
  233.3 8.5 attend.5
  256.4 6.1 join.1
  265.1 14.3 %all-to-all-done.2.attn_ref.keep_ref.give_ref = bf16[8,512,256]{2,1,0:T(8,128)(2,1)S(1)} async-done(((bf16[8,512,256]{2,1,0:T(8,128)(2,1)}), bf16[8,512,256]{2,1,0:T(8,128)(2,1)S(1)}, u32[]{:S(2)}, u32[]{:S(2)}) %all-to-all-start.2) | async-done | bytes 2097184 | tf_op jit(solution)/shard_map/all_to_all | solution.py:1320
  280.7 11.9 %out_proj.1 = (f32[512,2048]{1,0:T(8,128)}, f32[512,1]{1,0:T(8,128)}, bf16[512,2048]{1,0:T(8,128)(2,1)}) custom-call(s32[8]{0:T(128)} %copy-done.27, bf16[8,512,256]{2,1,0:T(8,128)(2,1)} %copy-done.1, bf16[512,2048]{1,0:T(8,128)(2,1)} %bitcast.116, f32[1,2048]{1,0:T(1,128)} %get-tuple-element.541.gain_ref, bf16[256,2048]{1,0:T(8,128)(2,1)} %refs_0_.1, ...), custom_call_target="tpu_custom_call" | custom-call | flops 1 | bytes 1 | tf_op jit(solution)/shard_map/out_proj/pallas_call | solution.py:788
  293.8 25.7 %ffn.4 = (bf16[512,1408]{1,0:T(8,128)(2,1)}, bf16[512,1408]{1,0:T(8,128)(2,1)}, bf16[512,1408]{1,0:T(8,128)(2,1)}, bf16[512,2048]{1,0:T(8,128)(2,1)}, bf16[512,2048]{1,0:T(8,128)(2,1)}) custom-call(bf16[512,2048]{1,0:T(8,128)(2,1)} %get-tuple-element.342.refs_0_.refs_4_, bf16[512,2048]{1,0:T(8,128)(2,1)} %multiply_bitcast_fusion.refs_1_.refs_4_.dy_ref, ...), custom_call_target="tpu_custom_call" | custom-call | flops 1 | bytes 1 | tf_op jit(solution)/shard_map/ffn/pallas_call | solution.py:595
  321.0 25.8 %ffn.5 = (bf16[512,1408]{1,0:T(8,128)(2,1)}, bf16[512,1408]{1,0:T(8,128)(2,1)}, bf16[512,1408]{1,0:T(8,128)(2,1)}, bf16[512,2048]{1,0:T(8,128)(2,1)}, bf16[512,2048]{1,0:T(8,128)(2,1)}) custom-call(bf16[512,2048]{1,0:T(8,128)(2,1)} %copy-done.31, bf16[512,2048]{1,0:T(8,128)(2,1)} %copy-done.38, bf16[2,2048,1408]{2,1,0:T(8,128)(2,1)} %bitcast.107, ...), custom_call_target="tpu_custom_call" | custom-call | flops 1 | bytes 1 | tf_op jit(solution)/shard_map/ffn/pallas_call | solution.py:595
  348.0 26.0 %ffn.6 = (bf16[512,1408]{1,0:T(8,128)(2,1)}, bf16[512,1408]{1,0:T(8,128)(2,1)}, bf16[512,1408]{1,0:T(8,128)(2,1)}, bf16[512,2048]{1,0:T(8,128)(2,1)}, bf16[512,2048]{1,0:T(8,128)(2,1)}) custom-call(bf16[512,2048]{1,0:T(8,128)(2,1)} %collective-permute-done.23.refs_0_.refs_2_.refs_6_, bf16[512,2048]{1,0:T(8,128)(2,1)} %copy-done.39, ...), custom_call_target="tpu_custom_call" | custom-call | flops 1 | bytes 1 | tf_op jit(solution)/shard_map/ffn/pallas_call | solution.py:595
  375.4 25.7 %ffn.7 = (bf16[512,1408]{1,0:T(8,128)(2,1)}, bf16[512,1408]{1,0:T(8,128)(2,1)}, bf16[512,1408]{1,0:T(8,128)(2,1)}, bf16[512,2048]{1,0:T(8,128)(2,1)}, bf16[512,2048]{1,0:T(8,128)(2,1)}) custom-call(bf16[512,2048]{1,0:T(8,128)(2,1)} %copy-done.32, bf16[512,2048]{1,0:T(8,128)(2,1)} %collective-permute-done.17.refs_1_.refs_7_, ...), custom_call_target="tpu_custom_call" | custom-call | flops 1 | bytes 1 | tf_op jit(solution)/shard_map/ffn/pallas_call | solution.py:595
  402.5 34.5 %grad_gu.1 = (bf16[4,4,64,2816]{3,2,1,0:T(8,128)(2,1)}, bf16[4,4,64,2816]{3,2,1,0:T(8,128)(2,1)}) custom-call(s32[1]{0:T(128)} %bitcast.20.core_ref, bf16[512,2048]{1,0:T(8,128)(2,1)} %get-tuple-element.342.refs_0_.refs_4_, bf16[512,2048]{1,0:T(8,128)(2,1)} %copy-done.31, bf16[512,2048]{1,0:T(8,128)(2,1)} %collective-permute-done.23.refs_0_.refs_2_.refs_6_, ...), custom_call_target="tpu_custom_call" | custom-call | flops 1 | bytes 1 | tf_op jit(solution)/shard_map/grad_gu/pallas_call | solution.py:636
  443.0 17.6 %grad_dn.1 = (bf16[704,2048]{1,0:T(8,128)(2,1)}, bf16[704,2048]{1,0:T(8,128)(2,1)}) custom-call(s32[1]{0:T(128)} %bitcast.20.core_ref, bf16[512,1408]{1,0:T(8,128)(2,1)} %get-tuple-element.390.refs_0_, bf16[512,1408]{1,0:T(8,128)(2,1)} %get-tuple-element.391.refs_1_, bf16[512,1408]{1,0:T(8,128)(2,1)} %get-tuple-element.392.refs_2_, ...), custom_call_target="tpu_custom_call" | custom-call | flops 1 | bytes 1 | tf_op jit(solution)/shard_map/grad_dn/pallas_call | solution.py:958
  460.7 6.9 add_convert_fusion
  469.8 14.7 %resid_back.1 = (f32[512,2048]{1,0:T(8,128)}, bf16[512,2048]{1,0:T(8,128)(2,1)}, bf16[8,512,256]{2,1,0:T(8,128)(2,1)}) custom-call(s32[8]{0:T(128)} %copy-done.27, bf16[512,2048]{1,0:T(8,128)(2,1)} %get-tuple-element.340.db_ref, bf16[512,2048]{1,0:T(8,128)(2,1)} %copy-done.54, bf16[512,2048]{1,0:T(8,128)(2,1)} %copy-done.55, ...), custom_call_target="tpu_custom_call" | custom-call | flops 1 | bytes 1 | tf_op jit(solution)/shard_map/resid_back/pallas_call | solution.py:834
  486.0 4.5 all-to-all-start.3
  492.2 6.5 grad_wo.1
  498.7 18.4 %all-to-all-done.3 = bf16[8,512,256]{2,1,0:T(8,128)(2,1)} async-done(((bf16[8,512,256]{2,1,0:T(8,128)(2,1)}), bf16[8,512,256]{2,1,0:T(8,128)(2,1)}, u32[]{:S(2)}, u32[]{:S(2)}) %all-to-all-start.3) | async-done | bytes 2097184 | tf_op jit(solution)/shard_map/all_to_all | solution.py:1366
  518.3 5.7 add_convert_fusion.1
  524.0 38.0 %attend_back.3 = (bf16[8,512,384]{2,1,0:T(8,128)(2,1)}, f32[256,4096]{1,0:T(8,128)}, f32[8,4,512]{2,1,0:T(4,128)}) custom-call(s32[1]{0:T(128)} %bitcast.6.zeros_ref, bf16[4096,384]{1,0:T(8,128)(2,1)} %bitcast.97, bf16[4096,384]{1,0:T(8,128)(2,1)} %bitcast.98, bf16[4096,256]{1,0:T(8,128)(2,1)} %bitcast.22.do_ref, f32[8,4,512]{2,1,0:T(4,128)} %copy-done.23, ...), custom_call_target="tpu_custom_call" | custom-call | flops 1 | bytes 1 | tf_op jit(solution)/shard_map/attend_back/pallas_call | solution.py:1195
  565.7 6.9 reduce-scatter.3.cloned.1.call-done
  576.9 18.0 %attend_back.4 = (bf16[8,512,384]{2,1,0:T(8,128)(2,1)}, f32[256,4096]{1,0:T(8,128)}, f32[8,4,512]{2,1,0:T(4,128)}) custom-call(s32[1]{0:T(128)} %bitcast.6.zeros_ref, bf16[4096,384]{1,0:T(8,128)(2,1)} %bitcast.99, bf16[4096,384]{1,0:T(8,128)(2,1)} %bitcast.100, bf16[4096,256]{1,0:T(8,128)(2,1)} %bitcast.22.do_ref, ...), custom_call_target="tpu_custom_call", output_to_operand_aliasing={{0}: (9, {})} | custom-call | flops 1 | bytes 1 | tf_op jit(solution)/shard_map/attend_back/pallas_call | solution.py:1195
  594.9 4.5 fusion.11
  603.5 48.6 %attend_back.5 = (bf16[8,512,384]{2,1,0:T(8,128)(2,1)}, f32[256,4096]{1,0:T(8,128)}, f32[8,4,512]{2,1,0:T(4,128)}) custom-call(s32[1]{0:T(128)} %bitcast.6.zeros_ref, bf16[4096,384]{1,0:T(8,128)(2,1)} %bitcast.101, bf16[4096,384]{1,0:T(8,128)(2,1)} %bitcast.102, bf16[4096,256]{1,0:T(8,128)(2,1)} %bitcast.22.do_ref, ...), custom_call_target="tpu_custom_call", output_to_operand_aliasing={{0}: (9, {})} | custom-call | flops 1 | bytes 1 | tf_op jit(solution)/shard_map/attend_back/pallas_call | solution.py:1195
  655.1 4.6 all-to-all-start.5
  663.0 13.3 %grad_qkv.1 = bf16[4,64,3072]{2,1,0:T(8,128)(2,1)S(1)} custom-call(s32[8]{0:T(128)S(1)} %copy-done.28, bf16[512,2048]{1,0:T(8,128)(2,1)S(1)} %copy-done.19, bf16[512,2048]{1,0:T(8,128)(2,1)S(1)} %copy-done.21, bf16[512,2048]{1,0:T(8,128)(2,1)} %collective-permute-done.31.refs_2_, bf16[512,2048]{1,0:T(8,128)(2,1)} %collective-permute-done.38.refs_3_, ...), custom_call_target="tpu_custom_call" | custom-call | flops 1 | bytes 1 | tf_op jit(solution)/shard_map/grad_qkv/pallas_call | solution.py:670
  688.8 26.1 %collective-permute-done.41 = bf16[64,5120]{1,0:T(8,128)(2,1)} collective-permute-done((bf16[64,5120]{1,0:T(8,128)(2,1)}, bf16[64,5120]{1,0:T(8,128)(2,1)}, u32[]{:S(2)}, u32[]{:S(2)}) %collective-permute-start.41) | collective-permute-done | bytes 655392 | tf_op jit(solution)/shard_map/ppermute | solution.py:407
  717.4 5.2 collective-permute-start.43
  724.4 25.6 %collective-permute-done.43 = bf16[64,5120]{1,0:T(8,128)(2,1)} collective-permute-done((bf16[64,5120]{1,0:T(8,128)(2,1)}, bf16[64,5120]{1,0:T(8,128)(2,1)}, u32[]{:S(2)}, u32[]{:S(2)}) %collective-permute-start.43) | collective-permute-done | bytes 655392 | tf_op jit(solution)/shard_map/ppermute | solution.py:407
  752.7 6.0 collective-permute-start.47
  758.6 19.4 %collective-permute-start.45 = (bf16[64,5120]{1,0:T(8,128)(2,1)}, bf16[64,5120]{1,0:T(8,128)(2,1)S(1)}, u32[]{:S(2)}, u32[]{:S(2)}) collective-permute-start(bf16[64,5120]{1,0:T(8,128)(2,1)} %get-tuple-element.472), channel_id=1, source_target_pairs={{0,8},{8,16},{16,24},{1,9},{9,17},{17,25},{2,10},{10,18},{18,26},{... | collective-permute-start | bytes 1966088 | tf_op jit(solution)/shard_map/ppermute | solution.py:407
  779.4 14.5 %in_back.1 = bf16[512,2048]{1,0:T(8,128)(2,1)} custom-call(s32[8]{0:T(128)} %copy-done.27, bf16[8,512,384]{2,1,0:T(8,128)(2,1)} %all-to-all-done.5.back_ref, bf16[512,2048]{1,0:T(8,128)(2,1)} %bitcast.117, f32[512,1]{1,0:T(8,128)} %copy-done.24, f32[1,2048]{1,0:T(1,128)} %copy-done.26, f32[512,2048]{1,0:T(8,128)} %get-tuple-element.483.d_resid_ref, ...), custom_call_target="tpu_custom_call" | custom-call | flops 1 | bytes 1 | tf_op jit(solution)/shard_map/in_back/pallas_call | solution.py:887
  794.9 13.6 %collective-permute-done.46 = bf16[64,5120]{1,0:T(8,128)(2,1)} collective-permute-done((bf16[64,5120]{1,0:T(8,128)(2,1)}, bf16[64,5120]{1,0:T(8,128)(2,1)}, u32[]{:S(2)}, u32[]{:S(2)}) %collective-permute-start.46) | collective-permute-done | bytes 655392 | tf_op jit(solution)/shard_map/ppermute | solution.py:408
  817.8 4.6 all-to-all-done.6
  823.7 7.0 collective-permute-start.50
  837.4 6.5 spread.1
  843.9 9.8 %collective-permute-done.50.refs_1_ = bf16[64,5120]{1,0:T(8,128)(2,1)S(1)} collective-permute-done((bf16[64,5120]{1,0:T(8,128)(2,1)S(1)}, bf16[64,5120]{1,0:T(8,128)(2,1)S(1)}, u32[]{:S(2)}, u32[]{:S(2)}) %collective-permute-start.50) | collective-permute-done | bytes 655392 | tf_op jit(solution)/shard_map/ppermute | solution.py:419
  860.4 5.3 reshape.175
  865.6 12.4 %collective-permute-done.53.refs_5_ = bf16[64,5120]{1,0:T(8,128)(2,1)S(1)} collective-permute-done((bf16[64,5120]{1,0:T(8,128)(2,1)S(1)}, bf16[64,5120]{1,0:T(8,128)(2,1)S(1)}, u32[]{:S(2)}, u32[]{:S(2)}) %collective-permute-start.53) | collective-permute-done | bytes 655392 | tf_op jit(solution)/shard_map/ppermute | solution.py:420
  880.1 5.1 fusion
  885.2 10.3 %collective-permute-done.55.refs_6_ = bf16[64,5120]{1,0:T(8,128)(2,1)S(1)} collective-permute-done((bf16[64,5120]{1,0:T(8,128)(2,1)S(1)}, bf16[64,5120]{1,0:T(8,128)(2,1)S(1)}, u32[]{:S(2)}, u32[]{:S(2)}) %collective-permute-start.55) | collective-permute-done | bytes 655392 | tf_op jit(solution)/shard_map/ppermute | solution.py:420
  (292 shorter events, 176.0 us)
Async XLA Ops:
  22.3 17.7 %collective-permute-start.3 = (bf16[256,2560]{1,0:T(8,128)(2,1)S(1)}, bf16[256,2560]{1,0:T(8,128)(2,1)S(1)}, u32[]{:S(2)}, u32[]{:S(2)}) collective-permute-start(bf16[256,2560]{1,0:T(8,128)(2,1)S(1)} %concatenate.52.refs_0_.refs_8_), channel_id=1, source_target_pairs={{0,2},{1,5},{2,0},{3,7},{4,6},{5,1},{6,4},{7,3},{8,10},{9,13},{10,... | collective-permute-start | bytes 3932168 | tf_op jit(solution)/shard_map/ppermute | solution.py:347
  57.6 17.7 %collective-permute-start.7 = (bf16[256,2560]{1,0:T(8,128)(2,1)S(1)}, bf16[256,2560]{1,0:T(8,128)(2,1)S(1)}, u32[]{:S(2)}, u32[]{:S(2)}) collective-permute-start(bf16[256,2560]{1,0:T(8,128)(2,1)S(1)} %collective-permute-done.3.refs_1_.refs_9_), channel_id=1, source_target_pairs={{0,4},{1,3},{2,6},{3,1},{4,0},{5,7},{6,2},{7,5},{8,12},{9,11},{10,... | collective-permute-start | bytes 3932168 | tf_op jit(solution)/shard_map/ppermute | solution.py:351
  79.4 34.4 %all-to-all-start.1 = ((bf16[4,64,2816]{2,1,0:T(8,128)(2,1)}), bf16[4,64,2816]{2,1,0:T(8,128)(2,1)}, u32[]{:S(2)}, u32[]{:S(2)}) async-start(bf16[4,64,2816]{2,1,0:T(8,128)(2,1)} %pad_maximum_fusion.2), calls=%async_computation.1 | async-start | bytes 2883584 | tf_op jit(solution)/shard_map/all_to_all | solution.py:1293
  83.8 146.2 %all-gather.7.cloned.1.call-start = ((), (), s32[]{:S(2)}) async-start(), calls=%async_computation.11 | async-start | bytes 7208960 | tf_op jit(solution)/shard_map/all_gather | solution.py:1297
  84.0 29.8 %collective-permute-start.10 = (bf16[256,2048]{1,0:T(8,128)(2,1)}, bf16[256,2048]{1,0:T(8,128)(2,1)}, u32[]{:S(2)}, u32[]{:S(2)}) collective-permute-start(bf16[256,2048]{1,0:T(8,128)(2,1)} %refs_0_.1), channel_id=1, source_target_pairs={{0,2},{1,5},{2,0},{3,7},{4,6},{5,1},{6,4},{7,3},{8,10},{9,13},{10,... | collective-permute-start | bytes 3145736 | tf_op jit(solution)/shard_map/ppermute | solution.py:347
  114.0 41.5 %all-to-all-start = ((bf16[8,512,384]{2,1,0:T(8,128)(2,1)}), bf16[8,512,384]{2,1,0:T(8,128)(2,1)S(1)}, u32[]{:S(2)}, u32[]{:S(2)}) async-start(bf16[8,512,384]{2,1,0:T(8,128)(2,1)} %get-tuple-element.289), calls=%async_computation | async-start | bytes 6291456 | tf_op jit(solution)/shard_map/all_to_all | solution.py:1302
  155.5 35.5 %collective-permute-start.13 = (bf16[512,2048]{1,0:T(8,128)(2,1)}, bf16[512,2048]{1,0:T(8,128)(2,1)S(1)}, u32[]{:S(2)}, u32[]{:S(2)}) collective-permute-start(bf16[512,2048]{1,0:T(8,128)(2,1)} %multiply_bitcast_fusion.refs_1_.refs_4_.dy_ref), channel_id=1, source_target_pairs={{0,2},{1,5},{2,0},{3,7},{4,6},{5,1},{6,4},{7,3},{8,10},{9,13},{10,... | collective-permute-start | bytes 6291464 | tf_op jit(solution)/shard_map/ppermute | solution.py:347
  155.9 30.9 %collective-permute-start.12 = (bf16[256,2048]{1,0:T(8,128)(2,1)}, bf16[256,2048]{1,0:T(8,128)(2,1)S(1)}, u32[]{:S(2)}, u32[]{:S(2)}) collective-permute-start(bf16[256,2048]{1,0:T(8,128)(2,1)} %refs_0_.1), channel_id=1, source_target_pairs={{0,4},{1,3},{2,6},{3,1},{4,0},{5,7},{6,2},{7,5},{8,12},{9,11},{10,... | collective-permute-start | bytes 3145736 | tf_op jit(solution)/shard_map/ppermute | solution.py:351
  190.9 37.3 %collective-permute-start.15 = (bf16[512,2048]{1,0:T(8,128)(2,1)S(1)}, bf16[512,2048]{1,0:T(8,128)(2,1)S(1)}, u32[]{:S(2)}, u32[]{:S(2)}) collective-permute-start(bf16[512,2048]{1,0:T(8,128)(2,1)S(1)} %copy-done.29), channel_id=1, source_target_pairs={{0,4},{1,3},{2,6},{3,1},{4,0},{5,7},{6,2},{7,5},{8,12},{9,11},{10,... | collective-permute-start | bytes 6291464 | tf_op jit(solution)/shard_map/ppermute | solution.py:351
  192.7 35.6 %collective-permute-start.14 = (bf16[256,2048]{1,0:T(8,128)(2,1)}, bf16[256,2048]{1,0:T(8,128)(2,1)S(1)}, u32[]{:S(2)}, u32[]{:S(2)}) collective-permute-start(bf16[256,2048]{1,0:T(8,128)(2,1)} %collective-permute-done.10.refs_1_), channel_id=1, source_target_pairs={{0,4},{1,3},{2,6},{3,1},{4,0},{5,7},{6,2},{7,5},{8,12},{9,11},{10,... | collective-permute-start | bytes 3145736 | tf_op jit(solution)/shard_map/ppermute | solution.py:351
  230.0 35.1 %collective-permute-start.17 = (bf16[512,2048]{1,0:T(8,128)(2,1)}, bf16[512,2048]{1,0:T(8,128)(2,1)}, u32[]{:S(2)}, u32[]{:S(2)}) collective-permute-start(bf16[512,2048]{1,0:T(8,128)(2,1)} %copy-done.38), channel_id=1, source_target_pairs={{0,4},{1,3},{2,6},{3,1},{4,0},{5,7},{6,2},{7,5},{8,12},{9,11},{10,... | collective-permute-start | bytes 6291464 | tf_op jit(solution)/shard_map/ppermute | solution.py:351
  246.2 33.2 %all-to-all-start.2 = ((bf16[8,512,256]{2,1,0:T(8,128)(2,1)}), bf16[8,512,256]{2,1,0:T(8,128)(2,1)S(1)}, u32[]{:S(2)}, u32[]{:S(2)}) async-start(bf16[8,512,256]{2,1,0:T(8,128)(2,1)} %copy-done.6), calls=%async_computation.2 | async-start | bytes 4194304 | tf_op jit(solution)/shard_map/all_to_all | solution.py:1320
  249.9 322.7 %reduce-scatter.3.cloned.1.call-start = ((), (), s32[]{:S(2)}) async-start(), calls=%async_computation.9 | async-start | bytes 7208960 | tf_op jit(solution)/shard_map/reduce_scatter | solution.py:1357
  292.7 26.8 %collective-permute-start.22 = (bf16[512,2048]{1,0:T(8,128)(2,1)}, bf16[512,2048]{1,0:T(8,128)(2,1)S(1)}, u32[]{:S(2)}, u32[]{:S(2)}) collective-permute-start(bf16[512,2048]{1,0:T(8,128)(2,1)} %get-tuple-element.342.refs_0_.refs_4_), channel_id=1, source_target_pairs={{0,2},{1,5},{2,0},{3,7},{4,6},{5,1},{6,4},{7,3},{8,10},{9,13},{10,... | collective-permute-start | bytes 6291464 | tf_op jit(solution)/shard_map/ppermute | solution.py:347
  319.5 27.2 %collective-permute-start.23 = (bf16[512,2048]{1,0:T(8,128)(2,1)S(1)}, bf16[512,2048]{1,0:T(8,128)(2,1)}, u32[]{:S(2)}, u32[]{:S(2)}) collective-permute-start(bf16[512,2048]{1,0:T(8,128)(2,1)S(1)} %copy-done.30), channel_id=1, source_target_pairs={{0,4},{1,3},{2,6},{3,1},{4,0},{5,7},{6,2},{7,5},{8,12},{9,11},{10,... | collective-permute-start | bytes 6291464 | tf_op jit(solution)/shard_map/ppermute | solution.py:351
  346.7 27.3 %collective-permute-start.24 = (bf16[512,2048]{1,0:T(8,128)(2,1)}, bf16[512,2048]{1,0:T(8,128)(2,1)S(1)}, u32[]{:S(2)}, u32[]{:S(2)}) collective-permute-start(bf16[512,2048]{1,0:T(8,128)(2,1)} %copy-done.31), channel_id=1, source_target_pairs={{0,4},{1,3},{2,6},{3,1},{4,0},{5,7},{6,2},{7,5},{8,12},{9,11},{10,... | collective-permute-start | bytes 6291464 | tf_op jit(solution)/shard_map/ppermute | solution.py:351
  374.1 27.1 %collective-permute-start.25 = (bf16[512,2048]{1,0:T(8,128)(2,1)}, bf16[512,2048]{1,0:T(8,128)(2,1)S(1)}, u32[]{:S(2)}, u32[]{:S(2)}) collective-permute-start(bf16[512,2048]{1,0:T(8,128)(2,1)} %get-tuple-element.357), channel_id=1, source_target_pairs={{0,2},{1,5},{2,0},{3,7},{4,6},{5,1},{6,4},{7,3},{8,10},{9,13},{10,... | collective-permute-start | bytes 6291464 | tf_op jit(solution)/shard_map/ppermute | solution.py:347
  401.2 35.8 %collective-permute-start.26 = (bf16[512,2048]{1,0:T(8,128)(2,1)}, bf16[512,2048]{1,0:T(8,128)(2,1)S(1)}, u32[]{:S(2)}, u32[]{:S(2)}) collective-permute-start(bf16[512,2048]{1,0:T(8,128)(2,1)} %get-tuple-element.366), channel_id=1, source_target_pairs={{0,2},{1,5},{2,0},{3,7},{4,6},{5,1},{6,4},{7,3},{8,10},{9,13},{10,... | collective-permute-start | bytes 6291464 | tf_op jit(solution)/shard_map/ppermute | solution.py:347
  442.2 18.4 %collective-permute-start.27 = (bf16[4,4,64,2816]{3,2,1,0:T(8,128)(2,1)}, bf16[4,4,64,2816]{3,2,1,0:T(8,128)(2,1)}, u32[]{:S(2)}, u32[]{:S(2)}) collective-permute-start(bf16[4,4,64,2816]{3,2,1,0:T(8,128)(2,1)} %get-tuple-element.389), channel_id=1, source_target_pairs={{0,1},{1,0},{2,3},{3,2},{4,5},{5,4},{6,7},{7,6},{8,9},{9,8},{10,11... | collective-permute-start | bytes 17301512 | tf_op jit(solution)/shard_map/ppermute | solution.py:355
  442.2 26.2 %collective-permute-start.28 = (bf16[512,2048]{1,0:T(8,128)(2,1)}, bf16[512,2048]{1,0:T(8,128)(2,1)S(1)}, u32[]{:S(2)}, u32[]{:S(2)}) collective-permute-start(bf16[512,2048]{1,0:T(8,128)(2,1)} %add_convert_fusion.4), channel_id=1, source_target_pairs={{0,4},{1,3},{2,6},{3,1},{4,0},{5,7},{6,2},{7,5},{8,12},{9,11},{10,... | collective-permute-start | bytes 6291464 | tf_op jit(solution)/shard_map/ppermute | solution.py:351
  486.0 31.1 %all-to-all-start.3 = ((bf16[8,512,256]{2,1,0:T(8,128)(2,1)}), bf16[8,512,256]{2,1,0:T(8,128)(2,1)}, u32[]{:S(2)}, u32[]{:S(2)}) async-start(bf16[8,512,256]{2,1,0:T(8,128)(2,1)} %get-tuple-element.405), calls=%async_computation.3 | async-start | bytes 4194304 | tf_op jit(solution)/shard_map/all_to_all | solution.py:1366
  490.5 288.8 %reduce-scatter.5.cloned.1.call-start = ((), (), s32[]{:S(2)}) async-start(), calls=%async_computation.10 | async-start | bytes 3604480 | tf_op jit(solution)/shard_map/reduce_scatter | solution.py:1388
  517.2 48.5 %collective-permute-start.32 = (bf16[4,256,2048]{2,1,0:T(8,128)(2,1)}, bf16[4,256,2048]{2,1,0:T(8,128)(2,1)}, u32[]{:S(2)}, u32[]{:S(2)}) collective-permute-start(bf16[4,256,2048]{2,1,0:T(8,128)(2,1)} %get-tuple-element.412), channel_id=1, source_target_pairs={{0,1},{1,0},{2,3},{3,2},{4,5},{5,4},{6,7},{7,6},{8,9},{9,8},{10,11... | collective-permute-start | bytes 12582920 | tf_op jit(solution)/shard_map/ppermute | solution.py:355
  517.2 48.5 %collective-permute-start.30 = (bf16[512,2048]{1,0:T(8,128)(2,1)}, bf16[512,2048]{1,0:T(8,128)(2,1)S(1)}, u32[]{:S(2)}, u32[]{:S(2)}) collective-permute-start(bf16[512,2048]{1,0:T(8,128)(2,1)} %get-tuple-element.411.refs_0_), channel_id=1, source_target_pairs={{0,2},{1,5},{2,0},{3,7},{4,6},{5,1},{6,4},{7,3},{8,10},{9,13},{10,... | collective-permute-start | bytes 6291464 | tf_op jit(solution)/shard_map/ppermute | solution.py:347
  517.7 47.9 %collective-permute-start.31 = (bf16[512,2048]{1,0:T(8,128)(2,1)}, bf16[512,2048]{1,0:T(8,128)(2,1)}, u32[]{:S(2)}, u32[]{:S(2)}) collective-permute-start(bf16[512,2048]{1,0:T(8,128)(2,1)} %get-tuple-element.411.refs_0_), channel_id=1, source_target_pairs={{0,4},{1,3},{2,6},{3,1},{4,0},{5,7},{6,2},{7,5},{8,12},{9,11},{10,... | collective-permute-start | bytes 6291464 | tf_op jit(solution)/shard_map/ppermute | solution.py:351
  518.3 47.4 %collective-permute-start.33 = (bf16[512,2048]{1,0:T(8,128)(2,1)}, bf16[512,2048]{1,0:T(8,128)(2,1)}, u32[]{:S(2)}, u32[]{:S(2)}) collective-permute-start(bf16[512,2048]{1,0:T(8,128)(2,1)} %get-tuple-element.411.refs_0_), channel_id=1, source_target_pairs={{0,1},{1,0},{2,3},{3,2},{4,5},{5,4},{6,7},{7,6},{8,9},{9,8},{10,11... | collective-permute-start | bytes 6291464 | tf_op jit(solution)/shard_map/ppermute | solution.py:355
  572.6 26.7 %collective-permute-start.34 = (bf16[512,2048]{1,0:T(8,128)(2,1)S(1)}, bf16[512,2048]{1,0:T(8,128)(2,1)}, u32[]{:S(2)}, u32[]{:S(2)}) collective-permute-start(bf16[512,2048]{1,0:T(8,128)(2,1)S(1)} %collective-permute-done.30.refs_1_), channel_id=1, source_target_pairs={{0,1},{1,0},{2,3},{3,2},{4,5},{5,4},{6,7},{7,6},{8,9},{9,8},{10,11... | collective-permute-start | bytes 6291464 | tf_op jit(solution)/shard_map/ppermute | solution.py:355
  572.7 26.7 %collective-permute-start.35 = (bf16[512,2048]{1,0:T(8,128)(2,1)}, bf16[512,2048]{1,0:T(8,128)(2,1)}, u32[]{:S(2)}, u32[]{:S(2)}) collective-permute-start(bf16[512,2048]{1,0:T(8,128)(2,1)} %collective-permute-done.31.refs_2_), channel_id=1, source_target_pairs={{0,1},{1,0},{2,3},{3,2},{4,5},{5,4},{6,7},{7,6},{8,9},{9,8},{10,11... | collective-permute-start | bytes 6291464 | tf_op jit(solution)/shard_map/ppermute | solution.py:355
  573.2 26.1 %all-to-all-start.4 = ((bf16[4,64,2816]{2,1,0:T(8,128)(2,1)}), bf16[4,64,2816]{2,1,0:T(8,128)(2,1)S(1)}, u32[]{:S(2)}, u32[]{:S(2)}) async-start(bf16[4,64,2816]{2,1,0:T(8,128)(2,1)} %bitcast.124), calls=%async_computation.5 | async-start | bytes 2883584 | tf_op jit(solution)/shard_map/all_to_all | solution.py:1389
  576.9 233.8 %all-gather.9.cloned.1.call-start = ((), (), s32[]{:S(2)}) async-start(), calls=%async_computation.12 | async-start | bytes 7208960 | tf_op jit(solution)/shard_map/all_gather | solution.py:1398
  599.4 55.1 %collective-permute-start.38 = (bf16[512,2048]{1,0:T(8,128)(2,1)S(1)}, bf16[512,2048]{1,0:T(8,128)(2,1)}, u32[]{:S(2)}, u32[]{:S(2)}) collective-permute-start(bf16[512,2048]{1,0:T(8,128)(2,1)S(1)} %collective-permute-done.30.refs_1_), channel_id=1, source_target_pairs={{0,4},{1,3},{2,6},{3,1},{4,0},{5,7},{6,2},{7,5},{8,12},{9,11},{10,... | collective-permute-start | bytes 6291464 | tf_op jit(solution)/shard_map/ppermute | solution.py:351
  601.4 50.7 %collective-permute-start.37 = (bf16[256,2048]{1,0:T(8,128)(2,1)}, bf16[256,2048]{1,0:T(8,128)(2,1)}, u32[]{:S(2)}, u32[]{:S(2)}) collective-permute-start(bf16[256,2048]{1,0:T(8,128)(2,1)} %get-tuple-element.445), channel_id=1, source_target_pairs={{0,2},{1,5},{2,0},{3,7},{4,6},{5,1},{6,4},{7,3},{8,10},{9,13},{10,... | collective-permute-start | bytes 3145736 | tf_op jit(solution)/shard_map/ppermute | solution.py:347
  602.9 51.6 %collective-permute-start.36 = (bf16[256,2048]{1,0:T(8,128)(2,1)}, bf16[256,2048]{1,0:T(8,128)(2,1)}, u32[]{:S(2)}, u32[]{:S(2)}) collective-permute-start(bf16[256,2048]{1,0:T(8,128)(2,1)} %get-tuple-element.444), channel_id=1, source_target_pairs={{0,2},{1,5},{2,0},{3,7},{4,6},{5,1},{6,4},{7,3},{8,10},{9,13},{10,... | collective-permute-start | bytes 3145736 | tf_op jit(solution)/shard_map/ppermute | solution.py:347
  654.6 24.6 %collective-permute-start.39 = (bf16[256,2048]{1,0:T(8,128)(2,1)S(1)}, bf16[256,2048]{1,0:T(8,128)(2,1)}, u32[]{:S(2)}, u32[]{:S(2)}) collective-permute-start(bf16[256,2048]{1,0:T(8,128)(2,1)S(1)} %fusion.3), channel_id=1, source_target_pairs={{0,4},{1,3},{2,6},{3,1},{4,0},{5,7},{6,2},{7,5},{8,12},{9,11},{10,... | collective-permute-start | bytes 3145736 | tf_op jit(solution)/shard_map/ppermute | solution.py:351
  655.1 69.3 %all-to-all-start.5 = ((bf16[8,512,384]{2,1,0:T(8,128)(2,1)}), bf16[8,512,384]{2,1,0:T(8,128)(2,1)}, u32[]{:S(2)}, u32[]{:S(2)}) async-start(bf16[8,512,384]{2,1,0:T(8,128)(2,1)} %get-tuple-element.452.refs_8_), calls=%async_computation.6 | async-start | bytes 6291456 | tf_op jit(solution)/shard_map/all_to_all | solution.py:1408
  659.7 200.6 %all-gather.11.cloned.1.call-start = ((), (), s32[]{:S(2)}) async-start(), calls=%async_computation.13 | async-start | bytes 3604480 | tf_op jit(solution)/shard_map/all_gather | solution.py:1421
  683.1 31.9 %collective-permute-start.41 = (bf16[64,5120]{1,0:T(8,128)(2,1)}, bf16[64,5120]{1,0:T(8,128)(2,1)}, u32[]{:S(2)}, u32[]{:S(2)}) collective-permute-start(bf16[64,5120]{1,0:T(8,128)(2,1)} %get-tuple-element.460), channel_id=1, source_target_pairs={{0,8},{1,9},{2,10},{3,11},{4,12},{5,13},{6,14},{7,15}} | collective-permute-start | bytes 1966088 | tf_op jit(solution)/shard_map/ppermute | solution.py:407
  687.3 27.7 %collective-permute-start.42 = (bf16[64,5120]{1,0:T(8,128)(2,1)S(1)}, bf16[64,5120]{1,0:T(8,128)(2,1)}, u32[]{:S(2)}, u32[]{:S(2)}) collective-permute-start(bf16[64,5120]{1,0:T(8,128)(2,1)S(1)} %get-tuple-element.461), channel_id=1, source_target_pairs={{24,16},{25,17},{26,18},{27,19},{28,20},{29,21},{30,22},{31,23}} | collective-permute-start | bytes 1966088 | tf_op jit(solution)/shard_map/ppermute | solution.py:408
  717.4 32.6 %collective-permute-start.43 = (bf16[64,5120]{1,0:T(8,128)(2,1)}, bf16[64,5120]{1,0:T(8,128)(2,1)}, u32[]{:S(2)}, u32[]{:S(2)}) collective-permute-start(bf16[64,5120]{1,0:T(8,128)(2,1)} %get-tuple-element.466), channel_id=1, source_target_pairs={{0,8},{8,16},{1,9},{9,17},{2,10},{10,18},{3,11},{11,19},{4,12},{12... | collective-permute-start | bytes 1966088 | tf_op jit(solution)/shard_map/ppermute | solution.py:407
  722.6 27.4 %collective-permute-start.44 = (bf16[64,5120]{1,0:T(8,128)(2,1)S(1)}, bf16[64,5120]{1,0:T(8,128)(2,1)}, u32[]{:S(2)}, u32[]{:S(2)}) collective-permute-start(bf16[64,5120]{1,0:T(8,128)(2,1)S(1)} %get-tuple-element.467), channel_id=1, source_target_pairs={{24,16},{16,8},{25,17},{17,9},{26,18},{18,10},{27,19},{19,11},{28,... | collective-permute-start | bytes 1966088 | tf_op jit(solution)/shard_map/ppermute | solution.py:408
  752.7 61.5 %collective-permute-start.47 = (bf16[512,2048]{1,0:T(8,128)(2,1)}, bf16[512,2048]{1,0:T(8,128)(2,1)}, u32[]{:S(2)}, u32[]{:S(2)}) collective-permute-start(bf16[512,2048]{1,0:T(8,128)(2,1)} %get-tuple-element.485), channel_id=1, source_target_pairs={{0,2},{1,5},{2,0},{3,7},{4,6},{5,1},{6,4},{7,3},{8,10},{9,13},{10,... | collective-permute-start | bytes 6291464 | tf_op jit(solution)/shard_map/ppermute | solution.py:347
  758.6 36.2 %collective-permute-start.45 = (bf16[64,5120]{1,0:T(8,128)(2,1)}, bf16[64,5120]{1,0:T(8,128)(2,1)S(1)}, u32[]{:S(2)}, u32[]{:S(2)}) collective-permute-start(bf16[64,5120]{1,0:T(8,128)(2,1)} %get-tuple-element.472), channel_id=1, source_target_pairs={{0,8},{8,16},{16,24},{1,9},{9,17},{17,25},{2,10},{10,18},{18,26},{... | collective-permute-start | bytes 1966088 | tf_op jit(solution)/shard_map/ppermute | solution.py:407
  778.0 30.4 %collective-permute-start.46 = (bf16[64,5120]{1,0:T(8,128)(2,1)}, bf16[64,5120]{1,0:T(8,128)(2,1)}, u32[]{:S(2)}, u32[]{:S(2)}) collective-permute-start(bf16[64,5120]{1,0:T(8,128)(2,1)} %get-tuple-element.473), channel_id=1, source_target_pairs={{24,16},{16,8},{8,0},{25,17},{17,9},{9,1},{26,18},{18,10},{10,2},{... | collective-permute-start | bytes 1966088 | tf_op jit(solution)/shard_map/ppermute | solution.py:408
  822.5 55.5 %collective-permute-start.48 = (bf16[512,2048]{1,0:T(8,128)(2,1)}, bf16[512,2048]{1,0:T(8,128)(2,1)}, u32[]{:S(2)}, u32[]{:S(2)}) collective-permute-start(bf16[512,2048]{1,0:T(8,128)(2,1)} %get-tuple-element.487), channel_id=1, source_target_pairs={{0,2},{1,5},{2,0},{3,7},{4,6},{5,1},{6,4},{7,3},{8,10},{9,13},{10,... | collective-permute-start | bytes 6291464 | tf_op jit(solution)/shard_map/ppermute | solution.py:347
  823.1 54.9 %collective-permute-start.49 = (bf16[512,2048]{1,0:T(8,128)(2,1)}, bf16[512,2048]{1,0:T(8,128)(2,1)}, u32[]{:S(2)}, u32[]{:S(2)}) collective-permute-start(bf16[512,2048]{1,0:T(8,128)(2,1)} %add_convert_fusion.3), channel_id=1, source_target_pairs={{0,4},{1,3},{2,6},{3,1},{4,0},{5,7},{6,2},{7,5},{8,12},{9,11},{10,... | collective-permute-start | bytes 6291464 | tf_op jit(solution)/shard_map/ppermute | solution.py:351
  823.7 30.0 %collective-permute-start.50 = (bf16[64,5120]{1,0:T(8,128)(2,1)S(1)}, bf16[64,5120]{1,0:T(8,128)(2,1)S(1)}, u32[]{:S(2)}, u32[]{:S(2)}) collective-permute-start(bf16[64,5120]{1,0:T(8,128)(2,1)S(1)} %pad_maximum_fusion.3.refs_0_), channel_id=1, source_target_pairs={{0,8},{8,16},{16,24},{1,9},{9,17},{17,25},{2,10},{10,18},{18,26},{... | collective-permute-start | bytes 1966088 | tf_op jit(solution)/shard_map/ppermute | solution.py:419
  830.7 27.5 %collective-permute-start.51 = (bf16[64,5120]{1,0:T(8,128)(2,1)S(1)}, bf16[64,5120]{1,0:T(8,128)(2,1)S(1)}, u32[]{:S(2)}, u32[]{:S(2)}) collective-permute-start(bf16[64,5120]{1,0:T(8,128)(2,1)S(1)} %pad_maximum_fusion.3.refs_0_), channel_id=1, source_target_pairs={{8,0},{16,8},{24,16},{9,1},{17,9},{25,17},{10,2},{18,10},{26,18},{... | collective-permute-start | bytes 1966088 | tf_op jit(solution)/shard_map/ppermute | solution.py:420
  858.9 19.2 %collective-permute-start.53 = (bf16[64,5120]{1,0:T(8,128)(2,1)S(1)}, bf16[64,5120]{1,0:T(8,128)(2,1)S(1)}, u32[]{:S(2)}, u32[]{:S(2)}) collective-permute-start(bf16[64,5120]{1,0:T(8,128)(2,1)S(1)} %collective-permute-done.51.refs_4_), channel_id=1, source_target_pairs={{8,0},{16,8},{9,1},{17,9},{10,2},{18,10},{11,3},{19,11},{12,4},{20... | collective-permute-start | bytes 1966088 | tf_op jit(solution)/shard_map/ppermute | solution.py:420
  (80 other events, 841.7 us)
Sparse Core Ops, SparseCore 0:
  113.9 107.1 all-gather.6
  468.6 103.9 reduce-scatter.2
  574.9 63.3 reduce-scatter.4
  640.4 130.2 all-gather.8
  779.5 69.5 all-gather.10

commit v9 on v8

--- a/solution.py
+++ b/solution.py
@@ -1365,7 +1365,8 @@
     d_send, d_branch, dn_got = fence(d_send, d_branch, dn_got)
     d_heads = lax.all_to_all(d_send, "sp", 0, 0, tiled=True).reshape(length, share)
     wo_keep, wo_give = grad_wo(core, attn_tok, d_branch)
-    d_heads, wo_keep, wo_give, normed = fence(d_heads, wo_keep, wo_give, normed)
+    dn_sum = (dn_keep.astype(F32) + dn_got.astype(F32)).astype(BF)
+    d_heads, wo_keep, wo_give, normed, dn_sum = fence(d_heads, wo_keep, wo_give, normed, dn_sum)
 
     def back_call(heads, start, stop, **kwargs):
         return attend_back(zeros_one, qkv_heads, heads, lse, cos_all, sin_all, start, stop, **kwargs)
@@ -1375,7 +1376,6 @@
     a_first = send_first(normed)
     a_second = send_second(normed)
     a_theirs = [send_sibling(normed)]
-    dn_sum = (dn_keep.astype(F32) + dn_got.astype(F32)).astype(BF)
     bwd = back_call(d_heads, turns[0], turns[1], out=out_heads)
     d_heads, a_first, a_second, wo_got, gu_z, dn_sum, *moves = fence(
         d_heads, a_first, a_second, wo_got, gu_z, dn_sum, *a_theirs, *bwd
@@ -1401,7 +1401,7 @@
     wo_first = send_first(wo_first)
     bwd = back_call(d_heads, turns[2], turns[3], before=bwd)
     wo_pass = (wo_part(chip ^ (second_mask // 2)) + wo_far.astype(F32)).astype(BF)
-    dp_heads, wo_first, wo_pass, a_far = fence(bwd[0], wo_first, wo_pass, a_far)
+    dp_heads, wo_first, wo_pass, a_far, dn_z = fence(bwd[0], wo_first, wo_pass, a_far, dn_z)
 
     wo_passed = send_second(wo_pass)
     a_theirs.append(send_sibling(a_far))
@@ -1419,11 +1419,10 @@
         moves = line_scatter_move(moves, step)
         if step == 1:
             dn_all = lax.all_gather(dn_z, "dp", axis=0, tiled=False)
+            back, *moves = fence(back, *moves)
         elif step == 2:
-            back, *moves = fence(back, *moves)
-        elif step == 3:
-            y_far, back = fence(y_far, back)
             y_got_far = send_first(y_far)
+            y_got_far, gu_all, *moves = fence(y_got_far, gu_all, *moves)
         moves = fence(*moves)
     last_z = line_scatter_end(last_parts, moves, 0)
     wq_z = last_z[:, :split].reshape(quarter, devices, split // devices).transpose(1, 0, 2)

time: 918 us -> 914 us (level)
  waiting for transfers between devices: 249 us -> 230 us
  Pallas kernels: 404 us -> 414 us
    ppermute x3, waiting for transfers between devices: 52.7 us -> 36.7 us  [line_scatter_move(): right = lax.ppermute(sends[0], 'dp', [(i, i + 1) for i in range(step)])]
    ppermute x3, waiting for transfers between devices: 13.6 us -> 0.01 us  [line_scatter_move(): lax.ppermute(sends[1], 'dp', [(planes - 1 - i, planes - 2 - i) for i in r...]
    unnamed x120 -> x128, local copies, waits for them, and re-layouts: 40 us -> 41.4 us
  transfers between devices with their start and end apart: 68 -> 68, of which waited for: 26 -> 26; matrix products, arithmetic and copies ran while one was open for 8% -> 8% of each run, Pallas kernels for 43% -> 44%
where the time goes in v9:
time: 914 us; the launch traced here: 905 us
  Pallas kernels  414 us (45%)
  waiting for transfers between devices  230 us (25%)
  starting transfers between devices  121 us (13%)
  other arithmetic  76.8 us (8%)
  local copies, waits for them, and re-layouts  47.3 us (5%)
  between operations  15.8 us (2%)
    pallas_call x3, Pallas kernels, attend_back(): pl.pallas_call(functools.partial(attend_back_kernel, heads=heads, start=s...  110 us
    pallas_call x4, Pallas kernels, ffn(): pl.pallas_call(functools.partial(ffn_kernel, cuts=cuts), in_specs=[hbm] *...  103 us
    pallas_call x3, Pallas kernels, attend(): pl.pallas_call(functools.partial(attend_kernel, heads=heads, start=start,...  53 us
    unnamed x128, local copies, waits for them, and re-layouts  41.4 us
    ppermute x13, waiting for transfers between devices, send_second(): return lax.ppermute(x, 'sp', SECOND)  38.3 us
    ppermute x3, waiting for transfers between devices, line_scatter_move(): right = lax.ppermute(sends[0], 'dp', [(i, i + 1) for i in range(step)])  36.7 us
    ppermute x3, starting transfers between devices, line_scatter_move(): right = lax.ppermute(sends[0], 'dp', [(i, i + 1) for i in range(step)])  35.7 us
    pallas_call x1, Pallas kernels, grad_gu(): pl.pallas_call(functools.partial(grad_gu_kernel, count=count), grid_spec=...  34.5 us
  transfers between devices with their start and end apart: 68, of which 26 were waited for; matrix products, arithmetic and copies ran while one was open for 8% of the time, Pallas kernels for 44%

profile of v9, /device:TPU:0, one launch (start us, length us, event | category | flops | bytes accessed | tf_op | source)
XLA Modules:
  0.0 904.7 jit_solution(14472727149751511932)
XLA Ops:
  27.8 12.1 %collective-permute-done.3.refs_1_.refs_9_ = bf16[256,2560]{1,0:T(8,128)(2,1)S(1)} collective-permute-done((bf16[256,2560]{1,0:T(8,128)(2,1)S(1)}, bf16[256,2560]{1,0:T(8,128)(2,1)S(1)}, u32[]{:S(2)}, u32[]{:S(2)}) %collective-permute-start.3) | collective-permute-done | bytes 1310752 | tf_op jit(solution)/shard_map/ppermute | solution.py:347
  42.5 7.5 fusion.12
  61.2 14.0 %collective-permute-done.7.refs_3_.refs_11_ = bf16[256,2560]{1,0:T(8,128)(2,1)S(1)} collective-permute-done((bf16[256,2560]{1,0:T(8,128)(2,1)S(1)}, bf16[256,2560]{1,0:T(8,128)(2,1)S(1)}, u32[]{:S(2)}, u32[]{:S(2)}) %collective-permute-start.7) | collective-permute-done | bytes 1310752 | tf_op jit(solution)/shard_map/ppermute | solution.py:351
  88.8 18.3 %project.1 = (bf16[8,512,384]{2,1,0:T(8,128)(2,1)}, bf16[512,2048]{1,0:T(8,128)(2,1)}, f32[512,1]{1,0:T(8,128)S(1)}) custom-call(s32[8]{0:T(128)S(1)} %stack.67.place_ref, bf16[512,2048]{1,0:T(8,128)(2,1)} %bitcast.115, f32[1,2048]{1,0:T(1,128)S(1)} %get-tuple-element.548.gain_ref, f32[512,128]{1,0:T(8,128)S(1)} %pad_maximum_fusion.4.cos_ref, ...), custom_call_target="tpu_custom_call" | custom-call | flops 1 | bytes 1 | tf_op jit(solution)/shard_map/project/pallas_call | solution.py:734
  107.8 5.9 collective-permute-done.10.refs_1_
  119.5 8.3 maximum_select_fusion.refs_3_
  127.7 27.7 %all-to-all-done = bf16[8,512,384]{2,1,0:T(8,128)(2,1)S(1)} async-done(((bf16[8,512,384]{2,1,0:T(8,128)(2,1)}), bf16[8,512,384]{2,1,0:T(8,128)(2,1)S(1)}, u32[]{:S(2)}, u32[]{:S(2)}) %all-to-all-start) | async-done | bytes 3145760 | tf_op jit(solution)/shard_map/all_to_all | solution.py:1302
  156.6 29.7 %attend.3 = (f32[4096,256]{1,0:T(8,128)}, bf16[8,512,256]{2,1,0:T(8,128)(2,1)S(1)}, f32[8,4,512]{2,1,0:T(4,128)S(1)}) custom-call(s32[1]{0:T(128)} %bitcast.6.zeros_ref, bf16[4096,384]{1,0:T(8,128)(2,1)S(1)} %bitcast.91, bf16[4096,384]{1,0:T(8,128)(2,1)S(1)} %bitcast.92), custom_call_target="tpu_custom_call" | custom-call | flops 1 | bytes 1 | tf_op jit(solution)/shard_map/attend/pallas_call | solution.py:1054
  186.3 4.6 collective-permute-done.13.refs_1_.refs_5_
  193.0 16.2 %attend.4 = (f32[4096,256]{1,0:T(8,128)}, bf16[8,512,256]{2,1,0:T(8,128)(2,1)S(1)}, f32[8,4,512]{2,1,0:T(4,128)S(1)}) custom-call(s32[1]{0:T(128)} %bitcast.6.zeros_ref, bf16[4096,384]{1,0:T(8,128)(2,1)S(1)} %bitcast.93, bf16[4096,384]{1,0:T(8,128)(2,1)S(1)} %bitcast.94, ...), custom_call_target="tpu_custom_call", output_to_operand_aliasing={{0}: (3, {}), {1}: (4, {}), {2}: (5, {})} | custom-call | flops 1 | bytes 1 | tf_op jit(solution)/shard_map/attend/pallas_call | solution.py:1054
  210.5 17.7 %collective-permute-done.14.refs_3_ = bf16[256,2048]{1,0:T(8,128)(2,1)S(1)} collective-permute-done((bf16[256,2048]{1,0:T(8,128)(2,1)}, bf16[256,2048]{1,0:T(8,128)(2,1)S(1)}, u32[]{:S(2)}, u32[]{:S(2)}) %collective-permute-start.14) | collective-permute-done | bytes 1048608 | tf_op jit(solution)/shard_map/ppermute | solution.py:351
  233.2 7.0 attend.5
  254.9 6.1 join.1
  263.9 15.4 %all-to-all-done.2.attn_ref.keep_ref.give_ref = bf16[8,512,256]{2,1,0:T(8,128)(2,1)S(1)} async-done(((bf16[8,512,256]{2,1,0:T(8,128)(2,1)}), bf16[8,512,256]{2,1,0:T(8,128)(2,1)S(1)}, u32[]{:S(2)}, u32[]{:S(2)}) %all-to-all-start.2) | async-done | bytes 2097184 | tf_op jit(solution)/shard_map/all_to_all | solution.py:1320
  280.7 11.9 %out_proj.1 = (f32[512,2048]{1,0:T(8,128)}, f32[512,1]{1,0:T(8,128)}, bf16[512,2048]{1,0:T(8,128)(2,1)}) custom-call(s32[8]{0:T(128)} %copy-done.29, bf16[8,512,256]{2,1,0:T(8,128)(2,1)} %copy-done.1, bf16[512,2048]{1,0:T(8,128)(2,1)} %bitcast.116, f32[1,2048]{1,0:T(1,128)} %get-tuple-element.547.gain_ref, bf16[256,2048]{1,0:T(8,128)(2,1)} %refs_0_.1, ...), custom_call_target="tpu_custom_call" | custom-call | flops 1 | bytes 1 | tf_op jit(solution)/shard_map/out_proj/pallas_call | solution.py:788
  293.7 25.7 %ffn.4 = (bf16[512,1408]{1,0:T(8,128)(2,1)}, bf16[512,1408]{1,0:T(8,128)(2,1)}, bf16[512,1408]{1,0:T(8,128)(2,1)}, bf16[512,2048]{1,0:T(8,128)(2,1)}, bf16[512,2048]{1,0:T(8,128)(2,1)}) custom-call(bf16[512,2048]{1,0:T(8,128)(2,1)} %get-tuple-element.345.refs_0_.refs_4_, bf16[512,2048]{1,0:T(8,128)(2,1)} %multiply_bitcast_fusion.refs_1_.refs_4_.dy_ref, ...), custom_call_target="tpu_custom_call" | custom-call | flops 1 | bytes 1 | tf_op jit(solution)/shard_map/ffn/pallas_call | solution.py:595
  320.9 25.8 %ffn.5 = (bf16[512,1408]{1,0:T(8,128)(2,1)}, bf16[512,1408]{1,0:T(8,128)(2,1)}, bf16[512,1408]{1,0:T(8,128)(2,1)}, bf16[512,2048]{1,0:T(8,128)(2,1)}, bf16[512,2048]{1,0:T(8,128)(2,1)}) custom-call(bf16[512,2048]{1,0:T(8,128)(2,1)} %copy-done.33, bf16[512,2048]{1,0:T(8,128)(2,1)} %copy-done.40, bf16[2,2048,1408]{2,1,0:T(8,128)(2,1)} %bitcast.107, ...), custom_call_target="tpu_custom_call" | custom-call | flops 1 | bytes 1 | tf_op jit(solution)/shard_map/ffn/pallas_call | solution.py:595
  348.0 26.0 %ffn.6 = (bf16[512,1408]{1,0:T(8,128)(2,1)}, bf16[512,1408]{1,0:T(8,128)(2,1)}, bf16[512,1408]{1,0:T(8,128)(2,1)}, bf16[512,2048]{1,0:T(8,128)(2,1)}, bf16[512,2048]{1,0:T(8,128)(2,1)}) custom-call(bf16[512,2048]{1,0:T(8,128)(2,1)} %collective-permute-done.23.refs_0_.refs_2_.refs_6_, bf16[512,2048]{1,0:T(8,128)(2,1)} %copy-done.41, ...), custom_call_target="tpu_custom_call" | custom-call | flops 1 | bytes 1 | tf_op jit(solution)/shard_map/ffn/pallas_call | solution.py:595
  375.4 25.7 %ffn.7 = (bf16[512,1408]{1,0:T(8,128)(2,1)}, bf16[512,1408]{1,0:T(8,128)(2,1)}, bf16[512,1408]{1,0:T(8,128)(2,1)}, bf16[512,2048]{1,0:T(8,128)(2,1)}, bf16[512,2048]{1,0:T(8,128)(2,1)}) custom-call(bf16[512,2048]{1,0:T(8,128)(2,1)} %copy-done.34, bf16[512,2048]{1,0:T(8,128)(2,1)} %collective-permute-done.17.refs_1_.refs_7_, ...), custom_call_target="tpu_custom_call" | custom-call | flops 1 | bytes 1 | tf_op jit(solution)/shard_map/ffn/pallas_call | solution.py:595
  402.5 34.5 %grad_gu.1 = (bf16[4,4,64,2816]{3,2,1,0:T(8,128)(2,1)}, bf16[4,4,64,2816]{3,2,1,0:T(8,128)(2,1)}) custom-call(s32[1]{0:T(128)} %bitcast.20.core_ref, bf16[512,2048]{1,0:T(8,128)(2,1)} %get-tuple-element.345.refs_0_.refs_4_, bf16[512,2048]{1,0:T(8,128)(2,1)} %copy-done.33, bf16[512,2048]{1,0:T(8,128)(2,1)} %collective-permute-done.23.refs_0_.refs_2_.refs_6_, ...), custom_call_target="tpu_custom_call" | custom-call | flops 1 | bytes 1 | tf_op jit(solution)/shard_map/grad_gu/pallas_call | solution.py:636
  443.1 17.5 %grad_dn.1 = (bf16[704,2048]{1,0:T(8,128)(2,1)}, bf16[704,2048]{1,0:T(8,128)(2,1)}) custom-call(s32[1]{0:T(128)} %bitcast.20.core_ref, bf16[512,1408]{1,0:T(8,128)(2,1)} %get-tuple-element.393.refs_0_, bf16[512,1408]{1,0:T(8,128)(2,1)} %get-tuple-element.394.refs_1_, bf16[512,1408]{1,0:T(8,128)(2,1)} %get-tuple-element.395.refs_2_, ...), custom_call_target="tpu_custom_call" | custom-call | flops 1 | bytes 1 | tf_op jit(solution)/shard_map/grad_dn/pallas_call | solution.py:958
  460.6 6.9 add_convert_fusion
  469.8 15.4 %resid_back.1 = (f32[512,2048]{1,0:T(8,128)}, bf16[512,2048]{1,0:T(8,128)(2,1)}, bf16[8,512,256]{2,1,0:T(8,128)(2,1)}) custom-call(s32[8]{0:T(128)} %copy-done.29, bf16[512,2048]{1,0:T(8,128)(2,1)} %get-tuple-element.343.db_ref, bf16[512,2048]{1,0:T(8,128)(2,1)} %copy-done.58, bf16[512,2048]{1,0:T(8,128)(2,1)} %copy-done.59, ...), custom_call_target="tpu_custom_call" | custom-call | flops 1 | bytes 1 | tf_op jit(solution)/shard_map/resid_back/pallas_call | solution.py:834
  486.8 4.5 all-to-all-start.3
  493.0 6.6 grad_wo.1
  502.4 15.6 %all-to-all-done.3 = bf16[8,512,256]{2,1,0:T(8,128)(2,1)} async-done(((bf16[8,512,256]{2,1,0:T(8,128)(2,1)}), bf16[8,512,256]{2,1,0:T(8,128)(2,1)}, u32[]{:S(2)}, u32[]{:S(2)}) %all-to-all-start.3) | async-done | bytes 2097184 | tf_op jit(solution)/shard_map/all_to_all | solution.py:1366
  519.2 43.8 %attend_back.3 = (bf16[8,512,384]{2,1,0:T(8,128)(2,1)}, f32[256,4096]{1,0:T(8,128)}, f32[8,4,512]{2,1,0:T(4,128)}) custom-call(s32[1]{0:T(128)} %bitcast.6.zeros_ref, bf16[4096,384]{1,0:T(8,128)(2,1)} %bitcast.97, bf16[4096,384]{1,0:T(8,128)(2,1)} %bitcast.98, bf16[4096,256]{1,0:T(8,128)(2,1)} %bitcast.22.do_ref, f32[8,4,512]{2,1,0:T(4,128)} %copy-done.25, ...), custom_call_target="tpu_custom_call" | custom-call | flops 1 | bytes 1 | tf_op jit(solution)/shard_map/attend_back/pallas_call | solution.py:1195
  575.9 20.9 %attend_back.4 = (bf16[8,512,384]{2,1,0:T(8,128)(2,1)}, f32[256,4096]{1,0:T(8,128)}, f32[8,4,512]{2,1,0:T(4,128)}) custom-call(s32[1]{0:T(128)} %bitcast.6.zeros_ref, bf16[4096,384]{1,0:T(8,128)(2,1)} %bitcast.99, bf16[4096,384]{1,0:T(8,128)(2,1)} %bitcast.100, bf16[4096,256]{1,0:T(8,128)(2,1)} %bitcast.22.do_ref, ...), custom_call_target="tpu_custom_call", output_to_operand_aliasing={{0}: (9, {})} | custom-call | flops 1 | bytes 1 | tf_op jit(solution)/shard_map/attend_back/pallas_call | solution.py:1195
  596.8 4.5 fusion.11
  605.5 45.7 %attend_back.5 = (bf16[8,512,384]{2,1,0:T(8,128)(2,1)}, f32[256,4096]{1,0:T(8,128)}, f32[8,4,512]{2,1,0:T(4,128)}) custom-call(s32[1]{0:T(128)} %bitcast.6.zeros_ref, bf16[4096,384]{1,0:T(8,128)(2,1)} %bitcast.101, bf16[4096,384]{1,0:T(8,128)(2,1)} %bitcast.102, bf16[4096,256]{1,0:T(8,128)(2,1)} %bitcast.22.do_ref, ...), custom_call_target="tpu_custom_call", output_to_operand_aliasing={{0}: (9, {})} | custom-call | flops 1 | bytes 1 | tf_op jit(solution)/shard_map/attend_back/pallas_call | solution.py:1195
  654.3 4.4 all-to-all-start.5
  662.0 13.3 %grad_qkv.1 = bf16[4,64,3072]{2,1,0:T(8,128)(2,1)S(1)} custom-call(s32[8]{0:T(128)S(1)} %copy-done.30, bf16[512,2048]{1,0:T(8,128)(2,1)S(1)} %copy-done.20, bf16[512,2048]{1,0:T(8,128)(2,1)S(1)} %copy-done.23, bf16[512,2048]{1,0:T(8,128)(2,1)} %collective-permute-done.31.refs_2_, bf16[512,2048]{1,0:T(8,128)(2,1)} %collective-permute-done.38.refs_3_, ...), custom_call_target="tpu_custom_call" | custom-call | flops 1 | bytes 1 | tf_op jit(solution)/shard_map/grad_qkv/pallas_call | solution.py:670
  682.9 26.9 %collective-permute-start.41 = (bf16[64,5120]{1,0:T(8,128)(2,1)}, bf16[64,5120]{1,0:T(8,128)(2,1)}, u32[]{:S(2)}, u32[]{:S(2)}) collective-permute-start(bf16[64,5120]{1,0:T(8,128)(2,1)} %get-tuple-element.465), channel_id=1, source_target_pairs={{0,8},{1,9},{2,10},{3,11},{4,12},{5,13},{6,14},{7,15}} | collective-permute-start | bytes 1966088 | tf_op jit(solution)/shard_map/ppermute | solution.py:407
  711.3 26.1 %collective-permute-done.41 = bf16[64,5120]{1,0:T(8,128)(2,1)} collective-permute-done((bf16[64,5120]{1,0:T(8,128)(2,1)}, bf16[64,5120]{1,0:T(8,128)(2,1)}, u32[]{:S(2)}, u32[]{:S(2)}) %collective-permute-start.41) | collective-permute-done | bytes 655392 | tf_op jit(solution)/shard_map/ppermute | solution.py:407
  740.1 8.6 collective-permute-start.43
  748.7 4.4 collective-permute-start.44
  754.9 10.6 %collective-permute-done.44 = bf16[64,5120]{1,0:T(8,128)(2,1)S(1)} collective-permute-done((bf16[64,5120]{1,0:T(8,128)(2,1)}, bf16[64,5120]{1,0:T(8,128)(2,1)S(1)}, u32[]{:S(2)}, u32[]{:S(2)}) %collective-permute-start.44) | collective-permute-done | bytes 655392 | tf_op jit(solution)/shard_map/ppermute | solution.py:407
  765.4 7.6 collective-permute-done.43
  781.2 14.5 %in_back.1 = bf16[512,2048]{1,0:T(8,128)(2,1)} custom-call(s32[8]{0:T(128)} %copy-done.29, bf16[8,512,384]{2,1,0:T(8,128)(2,1)} %all-to-all-done.5.back_ref, bf16[512,2048]{1,0:T(8,128)(2,1)} %bitcast.117, f32[512,1]{1,0:T(8,128)} %copy-done.26, f32[1,2048]{1,0:T(1,128)} %copy-done.28, f32[512,2048]{1,0:T(8,128)} %get-tuple-element.489.d_resid_ref, ...), custom_call_target="tpu_custom_call" | custom-call | flops 1 | bytes 1 | tf_op jit(solution)/shard_map/in_back/pallas_call | solution.py:887
  805.6 4.6 all-to-all-done.6
  811.5 4.6 collective-permute-start.50
  822.9 6.5 spread.1
  829.5 15.3 %collective-permute-done.50.refs_1_ = bf16[64,5120]{1,0:T(8,128)(2,1)S(1)} collective-permute-done((bf16[64,5120]{1,0:T(8,128)(2,1)S(1)}, bf16[64,5120]{1,0:T(8,128)(2,1)S(1)}, u32[]{:S(2)}, u32[]{:S(2)}) %collective-permute-start.50) | collective-permute-done | bytes 655392 | tf_op jit(solution)/shard_map/ppermute | solution.py:419
  844.7 8.2 collective-permute-done.51.refs_4_
  855.2 5.3 reshape.175
  860.4 13.2 %collective-permute-done.53.refs_5_ = bf16[64,5120]{1,0:T(8,128)(2,1)S(1)} collective-permute-done((bf16[64,5120]{1,0:T(8,128)(2,1)S(1)}, bf16[64,5120]{1,0:T(8,128)(2,1)S(1)}, u32[]{:S(2)}, u32[]{:S(2)}) %collective-permute-start.53) | collective-permute-done | bytes 655392 | tf_op jit(solution)/shard_map/ppermute | solution.py:420
  875.7 5.1 fusion
  880.8 11.5 %collective-permute-done.55.refs_6_ = bf16[64,5120]{1,0:T(8,128)(2,1)S(1)} collective-permute-done((bf16[64,5120]{1,0:T(8,128)(2,1)S(1)}, bf16[64,5120]{1,0:T(8,128)(2,1)S(1)}, u32[]{:S(2)}, u32[]{:S(2)}) %collective-permute-start.55) | collective-permute-done | bytes 655392 | tf_op jit(solution)/shard_map/ppermute | solution.py:420
  (300 shorter events, 176.6 us)
Async XLA Ops:
  22.3 17.7 %collective-permute-start.3 = (bf16[256,2560]{1,0:T(8,128)(2,1)S(1)}, bf16[256,2560]{1,0:T(8,128)(2,1)S(1)}, u32[]{:S(2)}, u32[]{:S(2)}) collective-permute-start(bf16[256,2560]{1,0:T(8,128)(2,1)S(1)} %concatenate.52.refs_0_.refs_8_), channel_id=1, source_target_pairs={{0,2},{1,5},{2,0},{3,7},{4,6},{5,1},{6,4},{7,3},{8,10},{9,13},{10,... | collective-permute-start | bytes 3932168 | tf_op jit(solution)/shard_map/ppermute | solution.py:347
  40.0 17.6 %collective-permute-start.4 = (bf16[256,2560]{1,0:T(8,128)(2,1)S(1)}, bf16[256,2560]{1,0:T(8,128)(2,1)S(1)}, u32[]{:S(2)}, u32[]{:S(2)}) collective-permute-start(bf16[256,2560]{1,0:T(8,128)(2,1)S(1)} %concatenate.52.refs_0_.refs_8_), channel_id=1, source_target_pairs={{0,4},{1,3},{2,6},{3,1},{4,0},{5,7},{6,2},{7,5},{8,12},{9,11},{10,... | collective-permute-start | bytes 3932168 | tf_op jit(solution)/shard_map/ppermute | solution.py:351
  57.6 17.7 %collective-permute-start.7 = (bf16[256,2560]{1,0:T(8,128)(2,1)S(1)}, bf16[256,2560]{1,0:T(8,128)(2,1)S(1)}, u32[]{:S(2)}, u32[]{:S(2)}) collective-permute-start(bf16[256,2560]{1,0:T(8,128)(2,1)S(1)} %collective-permute-done.3.refs_1_.refs_9_), channel_id=1, source_target_pairs={{0,4},{1,3},{2,6},{3,1},{4,0},{5,7},{6,2},{7,5},{8,12},{9,11},{10,... | collective-permute-start | bytes 3932168 | tf_op jit(solution)/shard_map/ppermute | solution.py:351
  79.4 34.3 %all-to-all-start.1 = ((bf16[4,64,2816]{2,1,0:T(8,128)(2,1)}), bf16[4,64,2816]{2,1,0:T(8,128)(2,1)}, u32[]{:S(2)}, u32[]{:S(2)}) async-start(bf16[4,64,2816]{2,1,0:T(8,128)(2,1)} %pad_maximum_fusion.2), calls=%async_computation.1 | async-start | bytes 2883584 | tf_op jit(solution)/shard_map/all_to_all | solution.py:1293
  83.8 146.1 %all-gather.7.cloned.1.call-start = ((), (), s32[]{:S(2)}) async-start(), calls=%async_computation.11 | async-start | bytes 7208960 | tf_op jit(solution)/shard_map/all_gather | solution.py:1297
  84.0 29.7 %collective-permute-start.10 = (bf16[256,2048]{1,0:T(8,128)(2,1)}, bf16[256,2048]{1,0:T(8,128)(2,1)}, u32[]{:S(2)}, u32[]{:S(2)}) collective-permute-start(bf16[256,2048]{1,0:T(8,128)(2,1)} %refs_0_.1), channel_id=1, source_target_pairs={{0,2},{1,5},{2,0},{3,7},{4,6},{5,1},{6,4},{7,3},{8,10},{9,13},{10,... | collective-permute-start | bytes 3145736 | tf_op jit(solution)/shard_map/ppermute | solution.py:347
  114.0 41.5 %all-to-all-start = ((bf16[8,512,384]{2,1,0:T(8,128)(2,1)}), bf16[8,512,384]{2,1,0:T(8,128)(2,1)S(1)}, u32[]{:S(2)}, u32[]{:S(2)}) async-start(bf16[8,512,384]{2,1,0:T(8,128)(2,1)} %get-tuple-element.292), calls=%async_computation | async-start | bytes 6291456 | tf_op jit(solution)/shard_map/all_to_all | solution.py:1302
  155.4 35.5 %collective-permute-start.13 = (bf16[512,2048]{1,0:T(8,128)(2,1)}, bf16[512,2048]{1,0:T(8,128)(2,1)S(1)}, u32[]{:S(2)}, u32[]{:S(2)}) collective-permute-start(bf16[512,2048]{1,0:T(8,128)(2,1)} %multiply_bitcast_fusion.refs_1_.refs_4_.dy_ref), channel_id=1, source_target_pairs={{0,2},{1,5},{2,0},{3,7},{4,6},{5,1},{6,4},{7,3},{8,10},{9,13},{10,... | collective-permute-start | bytes 6291464 | tf_op jit(solution)/shard_map/ppermute | solution.py:347
  155.9 30.4 %collective-permute-start.12 = (bf16[256,2048]{1,0:T(8,128)(2,1)}, bf16[256,2048]{1,0:T(8,128)(2,1)S(1)}, u32[]{:S(2)}, u32[]{:S(2)}) collective-permute-start(bf16[256,2048]{1,0:T(8,128)(2,1)} %refs_0_.1), channel_id=1, source_target_pairs={{0,4},{1,3},{2,6},{3,1},{4,0},{5,7},{6,2},{7,5},{8,12},{9,11},{10,... | collective-permute-start | bytes 3145736 | tf_op jit(solution)/shard_map/ppermute | solution.py:351
  190.9 37.3 %collective-permute-start.15 = (bf16[512,2048]{1,0:T(8,128)(2,1)S(1)}, bf16[512,2048]{1,0:T(8,128)(2,1)S(1)}, u32[]{:S(2)}, u32[]{:S(2)}) collective-permute-start(bf16[512,2048]{1,0:T(8,128)(2,1)S(1)} %copy-done.31), channel_id=1, source_target_pairs={{0,4},{1,3},{2,6},{3,1},{4,0},{5,7},{6,2},{7,5},{8,12},{9,11},{10,... | collective-permute-start | bytes 6291464 | tf_op jit(solution)/shard_map/ppermute | solution.py:351
  192.7 35.6 %collective-permute-start.14 = (bf16[256,2048]{1,0:T(8,128)(2,1)}, bf16[256,2048]{1,0:T(8,128)(2,1)S(1)}, u32[]{:S(2)}, u32[]{:S(2)}) collective-permute-start(bf16[256,2048]{1,0:T(8,128)(2,1)} %collective-permute-done.10.refs_1_), channel_id=1, source_target_pairs={{0,4},{1,3},{2,6},{3,1},{4,0},{5,7},{6,2},{7,5},{8,12},{9,11},{10,... | collective-permute-start | bytes 3145736 | tf_op jit(solution)/shard_map/ppermute | solution.py:351
  229.9 34.0 %collective-permute-start.17 = (bf16[512,2048]{1,0:T(8,128)(2,1)}, bf16[512,2048]{1,0:T(8,128)(2,1)}, u32[]{:S(2)}, u32[]{:S(2)}) collective-permute-start(bf16[512,2048]{1,0:T(8,128)(2,1)} %copy-done.40), channel_id=1, source_target_pairs={{0,4},{1,3},{2,6},{3,1},{4,0},{5,7},{6,2},{7,5},{8,12},{9,11},{10,... | collective-permute-start | bytes 6291464 | tf_op jit(solution)/shard_map/ppermute | solution.py:351
  244.7 34.6 %all-to-all-start.2 = ((bf16[8,512,256]{2,1,0:T(8,128)(2,1)}), bf16[8,512,256]{2,1,0:T(8,128)(2,1)S(1)}, u32[]{:S(2)}, u32[]{:S(2)}) async-start(bf16[8,512,256]{2,1,0:T(8,128)(2,1)} %copy-done.6), calls=%async_computation.2 | async-start | bytes 4194304 | tf_op jit(solution)/shard_map/all_to_all | solution.py:1320
  248.5 323.2 %reduce-scatter.3.cloned.1.call-start = ((), (), s32[]{:S(2)}) async-start(), calls=%async_computation.9 | async-start | bytes 7208960 | tf_op jit(solution)/shard_map/reduce_scatter | solution.py:1357
  292.6 26.8 %collective-permute-start.22 = (bf16[512,2048]{1,0:T(8,128)(2,1)}, bf16[512,2048]{1,0:T(8,128)(2,1)S(1)}, u32[]{:S(2)}, u32[]{:S(2)}) collective-permute-start(bf16[512,2048]{1,0:T(8,128)(2,1)} %get-tuple-element.345.refs_0_.refs_4_), channel_id=1, source_target_pairs={{0,2},{1,5},{2,0},{3,7},{4,6},{5,1},{6,4},{7,3},{8,10},{9,13},{10,... | collective-permute-start | bytes 6291464 | tf_op jit(solution)/shard_map/ppermute | solution.py:347
  319.5 27.2 %collective-permute-start.23 = (bf16[512,2048]{1,0:T(8,128)(2,1)S(1)}, bf16[512,2048]{1,0:T(8,128)(2,1)}, u32[]{:S(2)}, u32[]{:S(2)}) collective-permute-start(bf16[512,2048]{1,0:T(8,128)(2,1)S(1)} %copy-done.32), channel_id=1, source_target_pairs={{0,4},{1,3},{2,6},{3,1},{4,0},{5,7},{6,2},{7,5},{8,12},{9,11},{10,... | collective-permute-start | bytes 6291464 | tf_op jit(solution)/shard_map/ppermute | solution.py:351
  346.7 27.3 %collective-permute-start.24 = (bf16[512,2048]{1,0:T(8,128)(2,1)}, bf16[512,2048]{1,0:T(8,128)(2,1)S(1)}, u32[]{:S(2)}, u32[]{:S(2)}) collective-permute-start(bf16[512,2048]{1,0:T(8,128)(2,1)} %copy-done.33), channel_id=1, source_target_pairs={{0,4},{1,3},{2,6},{3,1},{4,0},{5,7},{6,2},{7,5},{8,12},{9,11},{10,... | collective-permute-start | bytes 6291464 | tf_op jit(solution)/shard_map/ppermute | solution.py:351
  374.0 27.1 %collective-permute-start.25 = (bf16[512,2048]{1,0:T(8,128)(2,1)}, bf16[512,2048]{1,0:T(8,128)(2,1)S(1)}, u32[]{:S(2)}, u32[]{:S(2)}) collective-permute-start(bf16[512,2048]{1,0:T(8,128)(2,1)} %get-tuple-element.360), channel_id=1, source_target_pairs={{0,2},{1,5},{2,0},{3,7},{4,6},{5,1},{6,4},{7,3},{8,10},{9,13},{10,... | collective-permute-start | bytes 6291464 | tf_op jit(solution)/shard_map/ppermute | solution.py:347
  401.1 35.8 %collective-permute-start.26 = (bf16[512,2048]{1,0:T(8,128)(2,1)}, bf16[512,2048]{1,0:T(8,128)(2,1)S(1)}, u32[]{:S(2)}, u32[]{:S(2)}) collective-permute-start(bf16[512,2048]{1,0:T(8,128)(2,1)} %get-tuple-element.369), channel_id=1, source_target_pairs={{0,2},{1,5},{2,0},{3,7},{4,6},{5,1},{6,4},{7,3},{8,10},{9,13},{10,... | collective-permute-start | bytes 6291464 | tf_op jit(solution)/shard_map/ppermute | solution.py:347
  442.3 18.3 %collective-permute-start.27 = (bf16[4,4,64,2816]{3,2,1,0:T(8,128)(2,1)}, bf16[4,4,64,2816]{3,2,1,0:T(8,128)(2,1)}, u32[]{:S(2)}, u32[]{:S(2)}) collective-permute-start(bf16[4,4,64,2816]{3,2,1,0:T(8,128)(2,1)} %get-tuple-element.392), channel_id=1, source_target_pairs={{0,1},{1,0},{2,3},{3,2},{4,5},{5,4},{6,7},{7,6},{8,9},{9,8},{10,11... | collective-permute-start | bytes 17301512 | tf_op jit(solution)/shard_map/ppermute | solution.py:355
  442.3 26.2 %collective-permute-start.28 = (bf16[512,2048]{1,0:T(8,128)(2,1)}, bf16[512,2048]{1,0:T(8,128)(2,1)S(1)}, u32[]{:S(2)}, u32[]{:S(2)}) collective-permute-start(bf16[512,2048]{1,0:T(8,128)(2,1)} %add_convert_fusion.4), channel_id=1, source_target_pairs={{0,4},{1,3},{2,6},{3,1},{4,0},{5,7},{6,2},{7,5},{8,12},{9,11},{10,... | collective-permute-start | bytes 6291464 | tf_op jit(solution)/shard_map/ppermute | solution.py:351
  486.8 31.1 %all-to-all-start.3 = ((bf16[8,512,256]{2,1,0:T(8,128)(2,1)}), bf16[8,512,256]{2,1,0:T(8,128)(2,1)}, u32[]{:S(2)}, u32[]{:S(2)}) async-start(bf16[8,512,256]{2,1,0:T(8,128)(2,1)} %get-tuple-element.408), calls=%async_computation.3 | async-start | bytes 4194304 | tf_op jit(solution)/shard_map/all_to_all | solution.py:1366
  491.3 162.3 %reduce-scatter.5.cloned.1.call-start = ((), (), s32[]{:S(2)}) async-start(), calls=%async_computation.10 | async-start | bytes 3604480 | tf_op jit(solution)/shard_map/reduce_scatter | solution.py:1388
  518.0 49.6 %collective-permute-start.32 = (bf16[4,256,2048]{2,1,0:T(8,128)(2,1)}, bf16[4,256,2048]{2,1,0:T(8,128)(2,1)}, u32[]{:S(2)}, u32[]{:S(2)}) collective-permute-start(bf16[4,256,2048]{2,1,0:T(8,128)(2,1)} %get-tuple-element.417), channel_id=1, source_target_pairs={{0,1},{1,0},{2,3},{3,2},{4,5},{5,4},{6,7},{7,6},{8,9},{9,8},{10,11... | collective-permute-start | bytes 12582920 | tf_op jit(solution)/shard_map/ppermute | solution.py:355
  518.0 48.3 %collective-permute-start.30 = (bf16[512,2048]{1,0:T(8,128)(2,1)S(1)}, bf16[512,2048]{1,0:T(8,128)(2,1)S(1)}, u32[]{:S(2)}, u32[]{:S(2)}) collective-permute-start(bf16[512,2048]{1,0:T(8,128)(2,1)S(1)} %copy-done.19), channel_id=1, source_target_pairs={{0,2},{1,5},{2,0},{3,7},{4,6},{5,1},{6,4},{7,3},{8,10},{9,13},{10,... | collective-permute-start | bytes 6291464 | tf_op jit(solution)/shard_map/ppermute | solution.py:347
  518.6 47.7 %collective-permute-start.31 = (bf16[512,2048]{1,0:T(8,128)(2,1)S(1)}, bf16[512,2048]{1,0:T(8,128)(2,1)}, u32[]{:S(2)}, u32[]{:S(2)}) collective-permute-start(bf16[512,2048]{1,0:T(8,128)(2,1)S(1)} %copy-done.19), channel_id=1, source_target_pairs={{0,4},{1,3},{2,6},{3,1},{4,0},{5,7},{6,2},{7,5},{8,12},{9,11},{10,... | collective-permute-start | bytes 6291464 | tf_op jit(solution)/shard_map/ppermute | solution.py:351
  519.2 47.1 %collective-permute-start.33 = (bf16[512,2048]{1,0:T(8,128)(2,1)S(1)}, bf16[512,2048]{1,0:T(8,128)(2,1)}, u32[]{:S(2)}, u32[]{:S(2)}) collective-permute-start(bf16[512,2048]{1,0:T(8,128)(2,1)S(1)} %copy-done.19), channel_id=1, source_target_pairs={{0,1},{1,0},{2,3},{3,2},{4,5},{5,4},{6,7},{7,6},{8,9},{9,8},{10,11... | collective-permute-start | bytes 6291464 | tf_op jit(solution)/shard_map/ppermute | solution.py:355
  571.7 29.6 %collective-permute-start.34 = (bf16[512,2048]{1,0:T(8,128)(2,1)S(1)}, bf16[512,2048]{1,0:T(8,128)(2,1)}, u32[]{:S(2)}, u32[]{:S(2)}) collective-permute-start(bf16[512,2048]{1,0:T(8,128)(2,1)S(1)} %copy-done.22), channel_id=1, source_target_pairs={{0,1},{1,0},{2,3},{3,2},{4,5},{5,4},{6,7},{7,6},{8,9},{9,8},{10,11... | collective-permute-start | bytes 6291464 | tf_op jit(solution)/shard_map/ppermute | solution.py:355
  571.8 29.5 %collective-permute-start.35 = (bf16[512,2048]{1,0:T(8,128)(2,1)}, bf16[512,2048]{1,0:T(8,128)(2,1)}, u32[]{:S(2)}, u32[]{:S(2)}) collective-permute-start(bf16[512,2048]{1,0:T(8,128)(2,1)} %collective-permute-done.31.refs_2_), channel_id=1, source_target_pairs={{0,1},{1,0},{2,3},{3,2},{4,5},{5,4},{6,7},{7,6},{8,9},{9,8},{10,11... | collective-permute-start | bytes 6291464 | tf_op jit(solution)/shard_map/ppermute | solution.py:355
  572.3 29.0 %all-to-all-start.4 = ((bf16[4,64,2816]{2,1,0:T(8,128)(2,1)}), bf16[4,64,2816]{2,1,0:T(8,128)(2,1)S(1)}, u32[]{:S(2)}, u32[]{:S(2)}) async-start(bf16[4,64,2816]{2,1,0:T(8,128)(2,1)} %bitcast.124), calls=%async_computation.5 | async-start | bytes 2883584 | tf_op jit(solution)/shard_map/all_to_all | solution.py:1389
  575.9 197.1 %all-gather.9.cloned.1.call-start = ((), (), s32[]{:S(2)}) async-start(), calls=%async_computation.12 | async-start | bytes 7208960 | tf_op jit(solution)/shard_map/all_gather | solution.py:1398
  601.3 52.3 %collective-permute-start.38 = (bf16[512,2048]{1,0:T(8,128)(2,1)S(1)}, bf16[512,2048]{1,0:T(8,128)(2,1)}, u32[]{:S(2)}, u32[]{:S(2)}) collective-permute-start(bf16[512,2048]{1,0:T(8,128)(2,1)S(1)} %copy-done.22), channel_id=1, source_target_pairs={{0,4},{1,3},{2,6},{3,1},{4,0},{5,7},{6,2},{7,5},{8,12},{9,11},{10,... | collective-permute-start | bytes 6291464 | tf_op jit(solution)/shard_map/ppermute | solution.py:351
  603.4 47.8 %collective-permute-start.37 = (bf16[256,2048]{1,0:T(8,128)(2,1)}, bf16[256,2048]{1,0:T(8,128)(2,1)}, u32[]{:S(2)}, u32[]{:S(2)}) collective-permute-start(bf16[256,2048]{1,0:T(8,128)(2,1)} %get-tuple-element.449), channel_id=1, source_target_pairs={{0,2},{1,5},{2,0},{3,7},{4,6},{5,1},{6,4},{7,3},{8,10},{9,13},{10,... | collective-permute-start | bytes 3145736 | tf_op jit(solution)/shard_map/ppermute | solution.py:347
  604.9 48.8 %collective-permute-start.36 = (bf16[256,2048]{1,0:T(8,128)(2,1)}, bf16[256,2048]{1,0:T(8,128)(2,1)}, u32[]{:S(2)}, u32[]{:S(2)}) collective-permute-start(bf16[256,2048]{1,0:T(8,128)(2,1)} %get-tuple-element.448), channel_id=1, source_target_pairs={{0,2},{1,5},{2,0},{3,7},{4,6},{5,1},{6,4},{7,3},{8,10},{9,13},{10,... | collective-permute-start | bytes 3145736 | tf_op jit(solution)/shard_map/ppermute | solution.py:347
  653.8 25.3 %collective-permute-start.39 = (bf16[256,2048]{1,0:T(8,128)(2,1)S(1)}, bf16[256,2048]{1,0:T(8,128)(2,1)}, u32[]{:S(2)}, u32[]{:S(2)}) collective-permute-start(bf16[256,2048]{1,0:T(8,128)(2,1)S(1)} %fusion.3), channel_id=1, source_target_pairs={{0,4},{1,3},{2,6},{3,1},{4,0},{5,7},{6,2},{7,5},{8,12},{9,11},{10,... | collective-permute-start | bytes 3145736 | tf_op jit(solution)/shard_map/ppermute | solution.py:351
  654.3 83.2 %all-to-all-start.5 = ((bf16[8,512,384]{2,1,0:T(8,128)(2,1)}), bf16[8,512,384]{2,1,0:T(8,128)(2,1)}, u32[]{:S(2)}, u32[]{:S(2)}) async-start(bf16[8,512,384]{2,1,0:T(8,128)(2,1)} %get-tuple-element.457.refs_8_), calls=%async_computation.7 | async-start | bytes 6291456 | tf_op jit(solution)/shard_map/all_to_all | solution.py:1408
  658.7 196.4 %all-gather.11.cloned.1.call-start = ((), (), s32[]{:S(2)}) async-start(), calls=%async_computation.13 | async-start | bytes 3604480 | tf_op jit(solution)/shard_map/all_gather | solution.py:1421
  682.9 54.5 %collective-permute-start.41 = (bf16[64,5120]{1,0:T(8,128)(2,1)}, bf16[64,5120]{1,0:T(8,128)(2,1)}, u32[]{:S(2)}, u32[]{:S(2)}) collective-permute-start(bf16[64,5120]{1,0:T(8,128)(2,1)} %get-tuple-element.465), channel_id=1, source_target_pairs={{0,8},{1,9},{2,10},{3,11},{4,12},{5,13},{6,14},{7,15}} | collective-permute-start | bytes 1966088 | tf_op jit(solution)/shard_map/ppermute | solution.py:407
  709.8 27.6 %collective-permute-start.42 = (bf16[64,5120]{1,0:T(8,128)(2,1)S(1)}, bf16[64,5120]{1,0:T(8,128)(2,1)}, u32[]{:S(2)}, u32[]{:S(2)}) collective-permute-start(bf16[64,5120]{1,0:T(8,128)(2,1)S(1)} %get-tuple-element.466), channel_id=1, source_target_pairs={{24,16},{25,17},{26,18},{27,19},{28,20},{29,21},{30,22},{31,23}} | collective-permute-start | bytes 1966088 | tf_op jit(solution)/shard_map/ppermute | solution.py:408
  740.1 32.9 %collective-permute-start.43 = (bf16[512,2048]{1,0:T(8,128)(2,1)}, bf16[512,2048]{1,0:T(8,128)(2,1)}, u32[]{:S(2)}, u32[]{:S(2)}) collective-permute-start(bf16[512,2048]{1,0:T(8,128)(2,1)} %get-tuple-element.471), channel_id=1, source_target_pairs={{0,2},{1,5},{2,0},{3,7},{4,6},{5,1},{6,4},{7,3},{8,10},{9,13},{10,... | collective-permute-start | bytes 6291464 | tf_op jit(solution)/shard_map/ppermute | solution.py:347
  748.7 16.7 %collective-permute-start.44 = (bf16[64,5120]{1,0:T(8,128)(2,1)}, bf16[64,5120]{1,0:T(8,128)(2,1)S(1)}, u32[]{:S(2)}, u32[]{:S(2)}) collective-permute-start(bf16[64,5120]{1,0:T(8,128)(2,1)} %get-tuple-element.474), channel_id=1, source_target_pairs={{0,8},{8,16},{1,9},{9,17},{2,10},{10,18},{3,11},{11,19},{4,12},{12... | collective-permute-start | bytes 1966088 | tf_op jit(solution)/shard_map/ppermute | solution.py:407
  775.5 20.2 %collective-permute-start.46 = (bf16[64,5120]{1,0:T(8,128)(2,1)}, bf16[64,5120]{1,0:T(8,128)(2,1)S(1)}, u32[]{:S(2)}, u32[]{:S(2)}) collective-permute-start(bf16[64,5120]{1,0:T(8,128)(2,1)} %get-tuple-element.480), channel_id=1, source_target_pairs={{0,8},{8,16},{16,24},{1,9},{9,17},{17,25},{2,10},{10,18},{18,26},{... | collective-permute-start | bytes 1966088 | tf_op jit(solution)/shard_map/ppermute | solution.py:407
  810.4 63.3 %collective-permute-start.48 = (bf16[512,2048]{1,0:T(8,128)(2,1)}, bf16[512,2048]{1,0:T(8,128)(2,1)}, u32[]{:S(2)}, u32[]{:S(2)}) collective-permute-start(bf16[512,2048]{1,0:T(8,128)(2,1)} %get-tuple-element.493), channel_id=1, source_target_pairs={{0,2},{1,5},{2,0},{3,7},{4,6},{5,1},{6,4},{7,3},{8,10},{9,13},{10,... | collective-permute-start | bytes 6291464 | tf_op jit(solution)/shard_map/ppermute | solution.py:347
  811.0 62.7 %collective-permute-start.49 = (bf16[512,2048]{1,0:T(8,128)(2,1)}, bf16[512,2048]{1,0:T(8,128)(2,1)}, u32[]{:S(2)}, u32[]{:S(2)}) collective-permute-start(bf16[512,2048]{1,0:T(8,128)(2,1)} %add_convert_fusion.3), channel_id=1, source_target_pairs={{0,4},{1,3},{2,6},{3,1},{4,0},{5,7},{6,2},{7,5},{8,12},{9,11},{10,... | collective-permute-start | bytes 6291464 | tf_op jit(solution)/shard_map/ppermute | solution.py:351
  811.5 33.2 %collective-permute-start.50 = (bf16[64,5120]{1,0:T(8,128)(2,1)S(1)}, bf16[64,5120]{1,0:T(8,128)(2,1)S(1)}, u32[]{:S(2)}, u32[]{:S(2)}) collective-permute-start(bf16[64,5120]{1,0:T(8,128)(2,1)S(1)} %pad_maximum_fusion.3.refs_0_), channel_id=1, source_target_pairs={{0,8},{8,16},{16,24},{1,9},{9,17},{17,25},{2,10},{10,18},{18,26},{... | collective-permute-start | bytes 1966088 | tf_op jit(solution)/shard_map/ppermute | solution.py:419
  816.2 36.8 %collective-permute-start.51 = (bf16[64,5120]{1,0:T(8,128)(2,1)S(1)}, bf16[64,5120]{1,0:T(8,128)(2,1)S(1)}, u32[]{:S(2)}, u32[]{:S(2)}) collective-permute-start(bf16[64,5120]{1,0:T(8,128)(2,1)S(1)} %pad_maximum_fusion.3.refs_0_), channel_id=1, source_target_pairs={{8,0},{16,8},{24,16},{9,1},{17,9},{25,17},{10,2},{18,10},{26,18},{... | collective-permute-start | bytes 1966088 | tf_op jit(solution)/shard_map/ppermute | solution.py:420
  853.7 20.0 %collective-permute-start.53 = (bf16[64,5120]{1,0:T(8,128)(2,1)S(1)}, bf16[64,5120]{1,0:T(8,128)(2,1)S(1)}, u32[]{:S(2)}, u32[]{:S(2)}) collective-permute-start(bf16[64,5120]{1,0:T(8,128)(2,1)S(1)} %collective-permute-done.51.refs_4_), channel_id=1, source_target_pairs={{8,0},{16,8},{9,1},{17,9},{10,2},{18,10},{11,3},{19,11},{12,4},{20... | collective-permute-start | bytes 1966088 | tf_op jit(solution)/shard_map/ppermute | solution.py:420
  874.4 17.9 %collective-permute-start.55 = (bf16[64,5120]{1,0:T(8,128)(2,1)S(1)}, bf16[64,5120]{1,0:T(8,128)(2,1)S(1)}, u32[]{:S(2)}, u32[]{:S(2)}) collective-permute-start(bf16[64,5120]{1,0:T(8,128)(2,1)S(1)} %collective-permute-done.53.refs_5_), channel_id=1, source_target_pairs={{8,0},{9,1},{10,2},{11,3},{12,4},{13,5},{14,6},{15,7}} | collective-permute-start | bytes 1966088 | tf_op jit(solution)/shard_map/ppermute | solution.py:420
  (84 other events, 847.9 us)
Sparse Core Ops, SparseCore 0:
  113.9 107.2 all-gather.6
  468.7 102.9 reduce-scatter.2
  574.0 59.0 reduce-scatter.4
  635.0 120.8 all-gather.8
  781.3 69.8 all-gather.10

commit v10 on v9

--- a/solution.py
+++ b/solution.py
@@ -341,6 +341,8 @@
 SECOND = swap_pairs(4, 2)
 SIBLING = swap_pairs(1, 1)
 SAME_CORE = [[0, 2, 4, 6], [1, 3, 5, 7]]
+LINE_NEAR = [(z, z ^ 1) for z in range(4)]
+LINE_FAR = [(z, z ^ 2) for z in range(4)]
 
 
 def send_first(x):
@@ -1337,6 +1339,15 @@
 
     b_rows = [inner, b_first, b_second, b_far]
     db_got_far = send_first(db_far)
+    dn_keep, dn_give = grad_dn(core, hid_rows, [dy, dy_first, dy_second, dy_far])
+    dn_got = send_sibling(dn_give)
+    db_got_far, dn_keep, dn_got = fence(db_got_far, dn_keep, dn_got)
+    db_pass = (second[3].astype(F32) + db_got_far.astype(F32)).astype(BF)
+    dn_parts = [part.reshape(2, 2, dn_keep.shape[0] // planes, width) for part in (dn_keep, dn_got)]
+    dn_move = pick_sum(dn_parts, 1 - (plane & 1), 1).astype(BF)
+    db_pass, dn_move, *b_rows = fence(db_pass, dn_move, *b_rows)
+    db_passed = send_second(db_pass)
+    dn_move = lax.ppermute(dn_move, "dp", LINE_NEAR)
     gu_keep, gu_give = grad_gu(
         core,
         b_rows,
@@ -1345,63 +1356,57 @@
         share,
         planes,
     )
-    db_got_far, gu_keep, gu_give, *hid_rows = fence(db_got_far, gu_keep, gu_give, *hid_rows)
-    db_pass = (second[3].astype(F32) + db_got_far.astype(F32)).astype(BF)
-    db_pass, gu_give, *hid_rows = fence(db_pass, gu_give, *hid_rows)
-    db_passed = send_second(db_pass)
+    db_passed, gu_keep, gu_give, dn_move = fence(db_passed, gu_keep, gu_give, dn_move)
+    dn_own = pick_sum(dn_parts, plane & 1, 1) + dn_move.astype(F32)
+    dn_move = pick(dn_own, 1 - plane // 2).astype(BF)
+    db_passed, gu_give, dn_move = fence(db_passed, gu_give, dn_move)
     gu_got = send_sibling(gu_give)
-    dn_keep, dn_give = grad_dn(core, hid_rows, [dy, dy_first, dy_second, dy_far])
-    gu_got, dn_keep, dn_give = fence(gu_got, dn_keep, dn_give)
+    dn_move = lax.ppermute(dn_move, "dp", LINE_FAR)
+    d_resid, d_branch, d_send = resid_back(
+        places, own[3], db_got_first, db_passed, residual, inv_two, mlp_gain, dy, out_parts
+    )
+    d_send, d_branch, gu_got = fence(d_send, d_branch, gu_got)
+    d_heads = lax.all_to_all(d_send, "sp", 0, 0, tiled=True).reshape(length, share)
     gu_sum = (gu_keep.astype(F32) + gu_got.astype(F32)).astype(BF)
-    gu_sum, db_passed, dn_give = fence(gu_sum, db_passed, dn_give)
     gu_z = lax.psum_scatter(
         gu_sum.reshape(planes * CHIPS * quarter, 2 * hidden_chip), "dp", scatter_dimension=0, tiled=True
     )
     gu_z = gu_z.reshape(CHIPS, quarter, 2 * hidden_chip)
-    dn_got = send_sibling(dn_give)
-    d_resid, d_branch, d_send = resid_back(
-        places, own[3], db_got_first, db_passed, residual, inv_two, mlp_gain, dy, out_parts
-    )
-    d_send, d_branch, dn_got = fence(d_send, d_branch, dn_got)
-    d_heads = lax.all_to_all(d_send, "sp", 0, 0, tiled=True).reshape(length, share)
     wo_keep, wo_give = grad_wo(core, attn_tok, d_branch)
-    dn_sum = (dn_keep.astype(F32) + dn_got.astype(F32)).astype(BF)
-    d_heads, wo_keep, wo_give, normed, dn_sum = fence(d_heads, wo_keep, wo_give, normed, dn_sum)
+    d_heads, wo_keep, wo_give, normed, gu_sum = fence(d_heads, wo_keep, wo_give, normed, gu_sum)
 
     def back_call(heads, start, stop, **kwargs):
         return attend_back(zeros_one, qkv_heads, heads, lse, cos_all, sin_all, start, stop, **kwargs)
 
-    turns = (0, blocks // 4, (3 * blocks) // 8, blocks)
+    def wo_part(place):
+        return pick(wo_keep, place).astype(F32) + pick(wo_got, place).astype(F32)
+
+    turns = (0, (3 * blocks) // 8, blocks // 2, blocks)
     wo_got = send_sibling(wo_give)
     a_first = send_first(normed)
     a_second = send_second(normed)
-    a_theirs = [send_sibling(normed)]
     bwd = back_call(d_heads, turns[0], turns[1], out=out_heads)
-    d_heads, a_first, a_second, wo_got, gu_z, dn_sum, *moves = fence(
-        d_heads, a_first, a_second, wo_got, gu_z, dn_sum, *a_theirs, *bwd
-    )
-    a_theirs, bwd = moves[:1], moves[1:]
-
-    def wo_part(place):
-        return pick(wo_keep, place).astype(F32) + pick(wo_got, place).astype(F32)
-
-    dn_z = lax.psum_scatter(dn_sum, "dp", scatter_dimension=0, tiled=True)
+    d_heads, a_first, a_second, wo_got, dn_move, gu_z, normed, *bwd = fence(
+        d_heads, a_first, a_second, wo_got, dn_move, gu_z, normed, *bwd
+    )
+    dn_z = (pick(dn_own, plane // 2) + dn_move.astype(F32)).astype(BF)
+    dn_all = lax.all_gather(dn_z, "dp", axis=0, tiled=False)
+
     gu_z = lax.all_to_all(gu_z, "sp", 0, 0, axis_index_groups=SAME_CORE, tiled=True)
-    a_theirs += [send_sibling(a_first), send_sibling(a_second)]
+    a_theirs = [send_sibling(normed), send_sibling(a_first), send_sibling(a_second)]
     bwd = back_call(d_heads, turns[1], turns[2], before=bwd)
-    d_heads, gu_z, a_first, *moves = fence(d_heads, gu_z, a_first, *a_theirs, *bwd)
-    a_theirs, bwd = moves[:3], moves[3:]
-
     wo_first = wo_part(chip ^ (first_mask // 2)).astype(BF)
     wo_far = wo_part(chip ^ 3).astype(BF)
-    d_heads, gu_z, a_first, wo_first, wo_far = fence(d_heads, gu_z, a_first, wo_first, wo_far)
+    d_heads, gu_z, a_first, wo_first, wo_far, *moves = fence(d_heads, gu_z, a_first, wo_first, wo_far, *a_theirs, *bwd)
+    a_theirs, bwd = moves[:3], moves[3:]
+
     gu_all = lax.all_gather(gu_z, "dp", axis=0, tiled=False)
     a_far = send_second(a_first)
     wo_far = send_first(wo_far)
     wo_first = send_first(wo_first)
     bwd = back_call(d_heads, turns[2], turns[3], before=bwd)
     wo_pass = (wo_part(chip ^ (second_mask // 2)) + wo_far.astype(F32)).astype(BF)
-    dp_heads, wo_first, wo_pass, a_far, dn_z = fence(bwd[0], wo_first, wo_pass, a_far, dn_z)
+    dp_heads, wo_first, wo_pass, a_far, dn_all = fence(bwd[0], wo_first, wo_pass, a_far, dn_all)
 
     wo_passed = send_second(wo_pass)
     a_theirs.append(send_sibling(a_far))
@@ -1418,11 +1423,10 @@
         y_far, y_first, *moves = fence(y_far, y_first, *moves)
         moves = line_scatter_move(moves, step)
         if step == 1:
-            dn_all = lax.all_gather(dn_z, "dp", axis=0, tiled=False)
             back, *moves = fence(back, *moves)
         elif step == 2:
             y_got_far = send_first(y_far)
-            y_got_far, gu_all, *moves = fence(y_got_far, gu_all, *moves)
+            y_got_far, *moves = fence(y_got_far, *moves)
         moves = fence(*moves)
     last_z = line_scatter_end(last_parts, moves, 0)
     wq_z = last_z[:, :split].reshape(quarter, devices, split // devices).transpose(1, 0, 2)

time: 914 us -> 987 us (1.080)
  waiting for transfers between devices: 230 us -> 304 us
  starting transfers between devices: 121 us -> 134 us
  Pallas kernels: 414 us -> 404 us
    ppermute x0 -> x2, waiting for transfers between devices: none -> 27.1 us  [the longest x1 27.1 us: fast_body(): dn_move = lax.ppermute(dn_move, 'dp', LINE_FAR)]
    ppermute x3, waiting for transfers between devices: 36.7 us -> 57.9 us  [line_scatter_move(): right = lax.ppermute(sends[0], 'dp', [(i, i + 1) for i in range(step)])]
    ppermute x11, waiting for transfers between devices: 33.6 us -> 52 us  [send_first(): return lax.ppermute(x, 'sp', FIRST)]
    ppermute x3, waiting for transfers between devices: 15.3 us -> 0.02 us  [line_gather_move(): lax.ppermute(got[0], 'dp', [(i, i + 1) for i in range(step - 1, planes -...]
    all_gather x1, waiting for transfers between devices: 0.01 us -> 11.9 us  [fast_body(): gu_all = lax.all_gather(gu_z, 'dp', axis=0, tiled=False)]
    unnamed x128 -> x120, local copies, waits for them, and re-layouts: 41.4 us -> 37.5 us
  transfers between devices with their start and end apart: 68 -> 69, of which waited for: 26 -> 27; matrix products, arithmetic and copies ran while one was open for 8% -> 6% of each run, Pallas kernels for 44% -> 38%
where the time goes in v10:
time: 987 us; the launch traced here: 979 us
  Pallas kernels  404 us (41%)
  waiting for transfers between devices  304 us (31%)
  starting transfers between devices  134 us (14%)
  other arithmetic  78.4 us (8%)
  local copies, waits for them, and re-layouts  43.4 us (4%)
  between operations  15.6 us (2%)
    pallas_call x3, Pallas kernels, attend_back(): pl.pallas_call(functools.partial(attend_back_kernel, heads=heads, start=s...  104 us
    pallas_call x4, Pallas kernels, ffn(): pl.pallas_call(functools.partial(ffn_kernel, cuts=cuts), in_specs=[hbm] *...  103 us
    ppermute x3, waiting for transfers between devices, line_scatter_move(): right = lax.ppermute(sends[0], 'dp', [(i, i + 1) for i in range(step)])  57.9 us
    ppermute x11, waiting for transfers between devices, send_first(): return lax.ppermute(x, 'sp', FIRST)  52 us
    pallas_call x3, Pallas kernels, attend(): pl.pallas_call(functools.partial(attend_kernel, heads=heads, start=start,...  50.3 us
    ppermute x3, starting transfers between devices, line_scatter_move(): right = lax.ppermute(sends[0], 'dp', [(i, i + 1) for i in range(step)])  40.8 us
    ppermute x13, waiting for transfers between devices, send_second(): return lax.ppermute(x, 'sp', SECOND)  40.4 us
    unnamed x120, local copies, waits for them, and re-layouts  37.5 us
  transfers between devices with their start and end apart: 69, of which 27 were waited for; matrix products, arithmetic and copies ran while one was open for 6% of the time, Pallas kernels for 38%

profile of v10, /device:TPU:0, one launch (start us, length us, event | category | flops | bytes accessed | tf_op | source)
XLA Modules:
  0.0 979.2 jit_solution(2147737770033737409)
XLA Ops:
  27.8 12.1 %collective-permute-done.3.refs_1_.refs_9_ = bf16[256,2560]{1,0:T(8,128)(2,1)S(1)} collective-permute-done((bf16[256,2560]{1,0:T(8,128)(2,1)S(1)}, bf16[256,2560]{1,0:T(8,128)(2,1)S(1)}, u32[]{:S(2)}, u32[]{:S(2)}) %collective-permute-start.3) | collective-permute-done | bytes 1310752 | tf_op jit(solution)/shard_map/ppermute | solution.py:349
  42.5 7.5 fusion.15
  61.3 14.0 %collective-permute-done.7.refs_3_.refs_11_ = bf16[256,2560]{1,0:T(8,128)(2,1)S(1)} collective-permute-done((bf16[256,2560]{1,0:T(8,128)(2,1)S(1)}, bf16[256,2560]{1,0:T(8,128)(2,1)S(1)}, u32[]{:S(2)}, u32[]{:S(2)}) %collective-permute-start.7) | collective-permute-done | bytes 1310752 | tf_op jit(solution)/shard_map/ppermute | solution.py:353
  88.8 18.3 %project.1 = (bf16[8,512,384]{2,1,0:T(8,128)(2,1)}, bf16[512,2048]{1,0:T(8,128)(2,1)}, f32[512,1]{1,0:T(8,128)S(1)}) custom-call(s32[8]{0:T(128)S(1)} %stack.67.place_ref, bf16[512,2048]{1,0:T(8,128)(2,1)} %bitcast.135, f32[1,2048]{1,0:T(1,128)S(1)} %get-tuple-element.532.gain_ref, f32[512,128]{1,0:T(8,128)S(1)} %pad_maximum_fusion.4.cos_ref, ...), custom_call_target="tpu_custom_call" | custom-call | flops 1 | bytes 1 | tf_op jit(solution)/shard_map/project/pallas_call | solution.py:736
  107.8 5.9 collective-permute-done.10.refs_1_
  119.4 8.2 maximum_select_fusion.refs_3_
  127.7 27.7 %all-to-all-done = bf16[8,512,384]{2,1,0:T(8,128)(2,1)S(1)} async-done(((bf16[8,512,384]{2,1,0:T(8,128)(2,1)}), bf16[8,512,384]{2,1,0:T(8,128)(2,1)S(1)}, u32[]{:S(2)}, u32[]{:S(2)}) %all-to-all-start) | async-done | bytes 3145760 | tf_op jit(solution)/shard_map/all_to_all | solution.py:1304
  156.6 30.3 %attend.3 = (f32[4096,256]{1,0:T(8,128)}, bf16[8,512,256]{2,1,0:T(8,128)(2,1)S(1)}, f32[8,4,512]{2,1,0:T(4,128)S(1)}) custom-call(s32[1]{0:T(128)} %bitcast.6.zeros_ref, bf16[4096,384]{1,0:T(8,128)(2,1)S(1)} %bitcast.111, bf16[4096,384]{1,0:T(8,128)(2,1)S(1)} %bitcast.112), custom_call_target="tpu_custom_call" | custom-call | flops 1 | bytes 1 | tf_op jit(solution)/shard_map/attend/pallas_call | solution.py:1056
  193.0 11.3 %attend.4 = (f32[4096,256]{1,0:T(8,128)}, bf16[8,512,256]{2,1,0:T(8,128)(2,1)S(1)}, f32[8,4,512]{2,1,0:T(4,128)S(1)}) custom-call(s32[1]{0:T(128)} %bitcast.6.zeros_ref, bf16[4096,384]{1,0:T(8,128)(2,1)S(1)} %bitcast.113, bf16[4096,384]{1,0:T(8,128)(2,1)S(1)} %bitcast.114, ...), custom_call_target="tpu_custom_call", output_to_operand_aliasing={{0}: (3, {}), {1}: (4, {}), {2}: (5, {})} | custom-call | flops 1 | bytes 1 | tf_op jit(solution)/shard_map/attend/pallas_call | solution.py:1056
  205.6 22.6 %collective-permute-done.14.refs_3_ = bf16[256,2048]{1,0:T(8,128)(2,1)S(1)} collective-permute-done((bf16[256,2048]{1,0:T(8,128)(2,1)}, bf16[256,2048]{1,0:T(8,128)(2,1)S(1)}, u32[]{:S(2)}, u32[]{:S(2)}) %collective-permute-start.14) | collective-permute-done | bytes 1048608 | tf_op jit(solution)/shard_map/ppermute | solution.py:353
  233.2 8.6 attend.5
  256.5 6.1 join.1
  265.2 14.1 %all-to-all-done.2.attn_ref.keep_ref.give_ref = bf16[8,512,256]{2,1,0:T(8,128)(2,1)S(1)} async-done(((bf16[8,512,256]{2,1,0:T(8,128)(2,1)}), bf16[8,512,256]{2,1,0:T(8,128)(2,1)S(1)}, u32[]{:S(2)}, u32[]{:S(2)}) %all-to-all-start.2) | async-done | bytes 2097184 | tf_op jit(solution)/shard_map/all_to_all | solution.py:1322
  280.7 11.7 %out_proj.1 = (f32[512,2048]{1,0:T(8,128)}, f32[512,1]{1,0:T(8,128)}, bf16[512,2048]{1,0:T(8,128)(2,1)}) custom-call(s32[8]{0:T(128)} %copy-done.25, bf16[8,512,256]{2,1,0:T(8,128)(2,1)} %copy-done.1, bf16[512,2048]{1,0:T(8,128)(2,1)} %bitcast.136, f32[1,2048]{1,0:T(1,128)} %get-tuple-element.531.gain_ref, bf16[256,2048]{1,0:T(8,128)(2,1)} %refs_0_.1, ...), custom_call_target="tpu_custom_call" | custom-call | flops 1 | bytes 1 | tf_op jit(solution)/shard_map/out_proj/pallas_call | solution.py:790
  293.5 25.7 %ffn.4 = (bf16[512,1408]{1,0:T(8,128)(2,1)}, bf16[512,1408]{1,0:T(8,128)(2,1)}, bf16[512,1408]{1,0:T(8,128)(2,1)}, bf16[512,2048]{1,0:T(8,128)(2,1)}, bf16[512,2048]{1,0:T(8,128)(2,1)}) custom-call(bf16[512,2048]{1,0:T(8,128)(2,1)} %get-tuple-element.373.refs_0_.refs_4_, bf16[512,2048]{1,0:T(8,128)(2,1)} %multiply_bitcast_fusion.refs_1_.refs_4_.dy_ref, ...), custom_call_target="tpu_custom_call" | custom-call | flops 1 | bytes 1 | tf_op jit(solution)/shard_map/ffn/pallas_call | solution.py:597
  320.7 25.9 %ffn.5 = (bf16[512,1408]{1,0:T(8,128)(2,1)}, bf16[512,1408]{1,0:T(8,128)(2,1)}, bf16[512,1408]{1,0:T(8,128)(2,1)}, bf16[512,2048]{1,0:T(8,128)(2,1)}, bf16[512,2048]{1,0:T(8,128)(2,1)}) custom-call(bf16[512,2048]{1,0:T(8,128)(2,1)} %copy-done.29, bf16[512,2048]{1,0:T(8,128)(2,1)} %copy-done.37, bf16[2,2048,1408]{2,1,0:T(8,128)(2,1)} %bitcast.127, ...), custom_call_target="tpu_custom_call" | custom-call | flops 1 | bytes 1 | tf_op jit(solution)/shard_map/ffn/pallas_call | solution.py:597
  348.0 25.8 %ffn.6 = (bf16[512,1408]{1,0:T(8,128)(2,1)}, bf16[512,1408]{1,0:T(8,128)(2,1)}, bf16[512,1408]{1,0:T(8,128)(2,1)}, bf16[512,2048]{1,0:T(8,128)(2,1)}, bf16[512,2048]{1,0:T(8,128)(2,1)}) custom-call(bf16[512,2048]{1,0:T(8,128)(2,1)} %collective-permute-done.23.refs_0_.refs_2_.refs_6_, bf16[512,2048]{1,0:T(8,128)(2,1)} %copy-done.38, ...), custom_call_target="tpu_custom_call" | custom-call | flops 1 | bytes 1 | tf_op jit(solution)/shard_map/ffn/pallas_call | solution.py:597
  375.1 26.0 %ffn.7 = (bf16[512,1408]{1,0:T(8,128)(2,1)}, bf16[512,1408]{1,0:T(8,128)(2,1)}, bf16[512,1408]{1,0:T(8,128)(2,1)}, bf16[512,2048]{1,0:T(8,128)(2,1)}, bf16[512,2048]{1,0:T(8,128)(2,1)}) custom-call(bf16[512,2048]{1,0:T(8,128)(2,1)} %copy-done.30, bf16[512,2048]{1,0:T(8,128)(2,1)} %collective-permute-done.17.refs_1_.refs_7_, ...), custom_call_target="tpu_custom_call" | custom-call | flops 1 | bytes 1 | tf_op jit(solution)/shard_map/ffn/pallas_call | solution.py:597
  401.1 18.3 %grad_dn.1 = (bf16[704,2048]{1,0:T(8,128)(2,1)}, bf16[704,2048]{1,0:T(8,128)(2,1)}) custom-call(s32[1]{0:T(128)} %bitcast.20.core_ref, bf16[512,1408]{1,0:T(8,128)(2,1)} %get-tuple-element.363.refs_0_, bf16[512,1408]{1,0:T(8,128)(2,1)} %get-tuple-element.364.refs_1_, bf16[512,1408]{1,0:T(8,128)(2,1)} %get-tuple-element.365.refs_2_, ...), custom_call_target="tpu_custom_call" | custom-call | flops 1 | bytes 1 | tf_op jit(solution)/shard_map/grad_dn/pallas_call | solution.py:960
  420.4 25.5 %collective-permute-done.26 = bf16[512,2048]{1,0:T(8,128)(2,1)} collective-permute-done((bf16[512,2048]{1,0:T(8,128)(2,1)}, bf16[512,2048]{1,0:T(8,128)(2,1)}, u32[]{:S(2)}, u32[]{:S(2)}) %collective-permute-start.26) | collective-permute-done | bytes 2097184 | tf_op jit(solution)/shard_map/ppermute | solution.py:349
  447.6 4.7 add_convert_fusion.3
  456.5 34.2 %grad_gu.1 = (bf16[4,4,64,2816]{3,2,1,0:T(8,128)(2,1)}, bf16[4,4,64,2816]{3,2,1,0:T(8,128)(2,1)}) custom-call(s32[1]{0:T(128)} %bitcast.20.core_ref, bf16[512,2048]{1,0:T(8,128)(2,1)} %get-tuple-element.373.refs_0_.refs_4_, bf16[512,2048]{1,0:T(8,128)(2,1)} %copy-done.29, bf16[512,2048]{1,0:T(8,128)(2,1)} %collective-permute-done.23.refs_0_.refs_2_.refs_6_, ...), custom_call_target="tpu_custom_call" | custom-call | flops 1 | bytes 1 | tf_op jit(solution)/shard_map/grad_gu/pallas_call | solution.py:638
  494.9 14.9 %resid_back.1 = (f32[512,2048]{1,0:T(8,128)}, bf16[512,2048]{1,0:T(8,128)(2,1)}, bf16[8,512,256]{2,1,0:T(8,128)(2,1)}) custom-call(s32[8]{0:T(128)} %copy-done.25, bf16[512,2048]{1,0:T(8,128)(2,1)} %get-tuple-element.335.db_ref, bf16[512,2048]{1,0:T(8,128)(2,1)} %copy-done.55, bf16[512,2048]{1,0:T(8,128)(2,1)} %collective-permute-done.28.passed_ref, ...), custom_call_target="tpu_custom_call" | custom-call | flops 1 | bytes 1 | tf_op jit(solution)/shard_map/resid_back/pallas_call | solution.py:836
  509.8 6.9 add_convert_fusion
  522.9 6.4 grad_wo.1
  529.3 18.6 %all-to-all-done.3 = bf16[8,512,256]{2,1,0:T(8,128)(2,1)} async-done(((bf16[8,512,256]{2,1,0:T(8,128)(2,1)}), bf16[8,512,256]{2,1,0:T(8,128)(2,1)}, u32[]{:S(2)}, u32[]{:S(2)}) %all-to-all-start.3) | async-done | bytes 2097184 | tf_op jit(solution)/shard_map/all_to_all | solution.py:1369
  549.0 5.0 collective-permute-start.34
  554.1 47.9 %attend_back.3 = (bf16[8,512,384]{2,1,0:T(8,128)(2,1)}, f32[256,4096]{1,0:T(8,128)}, f32[8,4,512]{2,1,0:T(4,128)}) custom-call(s32[1]{0:T(128)} %bitcast.6.zeros_ref, bf16[4096,384]{1,0:T(8,128)(2,1)} %bitcast.117, bf16[4096,384]{1,0:T(8,128)(2,1)} %bitcast.118, bf16[4096,256]{1,0:T(8,128)(2,1)} %bitcast.27.do_ref, f32[8,4,512]{2,1,0:T(4,128)} %copy-done.22, ...), custom_call_target="tpu_custom_call" | custom-call | flops 1 | bytes 1 | tf_op jit(solution)/shard_map/attend_back/pallas_call | solution.py:1197
  602.0 27.1 %collective-permute-done.34 = bf16[176,2048]{1,0:T(8,128)(2,1)S(1)} collective-permute-done((bf16[176,2048]{1,0:T(8,128)(2,1)S(1)}, bf16[176,2048]{1,0:T(8,128)(2,1)S(1)}, u32[]{:S(2)}, u32[]{:S(2)}) %collective-permute-start.34) | collective-permute-done | bytes 720928 | tf_op jit(solution)/shard_map/ppermute | solution.py:1364
  629.1 13.8 %reduce-scatter.2.cloned.1.call-done = bf16[256,2816]{1,0:T(8,128)(2,1)} async-done(((bf16[1024,2816]{1,0:T(8,128)(2,1)}), bf16[256,2816]{1,0:T(8,128)(2,1)}) %reduce-scatter.2.cloned.1.call-update) | async-done | bytes 1441808 | tf_op jit(solution)/shard_map/reduce_scatter | solution.py:1371
  650.1 14.8 %attend_back.4 = (bf16[8,512,384]{2,1,0:T(8,128)(2,1)}, f32[256,4096]{1,0:T(8,128)}, f32[8,4,512]{2,1,0:T(4,128)}) custom-call(s32[1]{0:T(128)} %bitcast.6.zeros_ref, bf16[4096,384]{1,0:T(8,128)(2,1)} %bitcast.119, bf16[4096,384]{1,0:T(8,128)(2,1)} %bitcast.120, bf16[4096,256]{1,0:T(8,128)(2,1)} %bitcast.27.do_ref, ...), custom_call_target="tpu_custom_call", output_to_operand_aliasing={{0}: (9, {})} | custom-call | flops 1 | bytes 1 | tf_op jit(solution)/shard_map/attend_back/pallas_call | solution.py:1197
  673.5 41.0 %attend_back.5 = (bf16[8,512,384]{2,1,0:T(8,128)(2,1)}, f32[256,4096]{1,0:T(8,128)}, f32[8,4,512]{2,1,0:T(4,128)}) custom-call(s32[1]{0:T(128)} %bitcast.6.zeros_ref, bf16[4096,384]{1,0:T(8,128)(2,1)} %bitcast.121, bf16[4096,384]{1,0:T(8,128)(2,1)} %bitcast.122, bf16[4096,256]{1,0:T(8,128)(2,1)} %bitcast.27.do_ref, ...), custom_call_target="tpu_custom_call", output_to_operand_aliasing={{0}: (9, {})} | custom-call | flops 1 | bytes 1 | tf_op jit(solution)/shard_map/attend_back/pallas_call | solution.py:1197
  728.1 13.3 %grad_qkv.1 = bf16[4,64,3072]{2,1,0:T(8,128)(2,1)S(1)} custom-call(s32[8]{0:T(128)S(1)} %copy-done.26, bf16[512,2048]{1,0:T(8,128)(2,1)S(1)} %copy-done.20, bf16[512,2048]{1,0:T(8,128)(2,1)} %collective-permute-done.31.refs_1_, bf16[512,2048]{1,0:T(8,128)(2,1)} %collective-permute-done.32.refs_2_, bf16[512,2048]{1,0:T(8,128)(2,1)} %copy-done.52, ...), custom_call_target="tpu_custom_call" | custom-call | flops 1 | bytes 1 | tf_op jit(solution)/shard_map/grad_qkv/pallas_call | solution.py:672
  747.5 23.0 %collective-permute-start.43 = (bf16[64,5120]{1,0:T(8,128)(2,1)}, bf16[64,5120]{1,0:T(8,128)(2,1)}, u32[]{:S(2)}, u32[]{:S(2)}) collective-permute-start(bf16[64,5120]{1,0:T(8,128)(2,1)} %get-tuple-element.450), channel_id=1, source_target_pairs={{0,8},{1,9},{2,10},{3,11},{4,12},{5,13},{6,14},{7,15}} | collective-permute-start | bytes 1966088 | tf_op jit(solution)/shard_map/ppermute | solution.py:409
  771.9 26.1 %collective-permute-done.43 = bf16[64,5120]{1,0:T(8,128)(2,1)} collective-permute-done((bf16[64,5120]{1,0:T(8,128)(2,1)}, bf16[64,5120]{1,0:T(8,128)(2,1)}, u32[]{:S(2)}, u32[]{:S(2)}) %collective-permute-start.43) | collective-permute-done | bytes 655392 | tf_op jit(solution)/shard_map/ppermute | solution.py:409
  800.5 6.7 collective-permute-start.45
  807.3 5.2 collective-permute-start.46
  814.0 24.5 %collective-permute-done.46 = bf16[64,5120]{1,0:T(8,128)(2,1)} collective-permute-done((bf16[64,5120]{1,0:T(8,128)(2,1)}, bf16[64,5120]{1,0:T(8,128)(2,1)}, u32[]{:S(2)}, u32[]{:S(2)}) %collective-permute-start.46) | collective-permute-done | bytes 655392 | tf_op jit(solution)/shard_map/ppermute | solution.py:409
  841.2 12.6 %collective-permute-start.48 = (bf16[64,5120]{1,0:T(8,128)(2,1)}, bf16[64,5120]{1,0:T(8,128)(2,1)S(1)}, u32[]{:S(2)}, u32[]{:S(2)}) collective-permute-start(bf16[64,5120]{1,0:T(8,128)(2,1)} %get-tuple-element.464), channel_id=1, source_target_pairs={{0,8},{8,16},{16,24},{1,9},{9,17},{17,25},{2,10},{10,18},{18,26},{... | collective-permute-start | bytes 1966088 | tf_op jit(solution)/shard_map/ppermute | solution.py:409
  855.3 14.5 %in_back.1 = bf16[512,2048]{1,0:T(8,128)(2,1)} custom-call(s32[8]{0:T(128)} %copy-done.25, bf16[8,512,384]{2,1,0:T(8,128)(2,1)} %all-to-all-done.5.back_ref, bf16[512,2048]{1,0:T(8,128)(2,1)} %bitcast.137, f32[512,1]{1,0:T(8,128)} %copy-done.23, f32[1,2048]{1,0:T(1,128)} %copy-done.24, f32[512,2048]{1,0:T(8,128)} %get-tuple-element.473.d_resid_ref, ...), custom_call_target="tpu_custom_call" | custom-call | flops 1 | bytes 1 | tf_op jit(solution)/shard_map/in_back/pallas_call | solution.py:889
  869.8 7.2 collective-permute-done.48
  879.2 11.9 %all-gather.11.cloned.1.call-done = bf16[16,64,2816]{2,1,0:T(8,128)(2,1)} async-done(((bf16[4,64,2816]{2,1,0:T(8,128)(2,1)}), bf16[16,64,2816]{2,1,0:T(8,128)(2,1)}) %all-gather.11.cloned.1.call-update) | async-done | bytes 5767184 | tf_op jit(solution)/shard_map/all_gather | solution.py:1403
  904.6 4.7 collective-permute-start.52
  916.2 6.5 spread.1
  922.7 4.8 collective-permute-done.53.refs_4_
  933.1 13.5 %collective-permute-done.55.refs_5_ = bf16[64,5120]{1,0:T(8,128)(2,1)S(1)} collective-permute-done((bf16[64,5120]{1,0:T(8,128)(2,1)S(1)}, bf16[64,5120]{1,0:T(8,128)(2,1)S(1)}, u32[]{:S(2)}, u32[]{:S(2)}) %collective-permute-start.55) | collective-permute-done | bytes 655392 | tf_op jit(solution)/shard_map/ppermute | solution.py:422
  952.3 5.1 fusion
  957.5 11.0 %collective-permute-done.57.refs_6_ = bf16[64,5120]{1,0:T(8,128)(2,1)S(1)} collective-permute-done((bf16[64,5120]{1,0:T(8,128)(2,1)S(1)}, bf16[64,5120]{1,0:T(8,128)(2,1)S(1)}, u32[]{:S(2)}, u32[]{:S(2)}) %collective-permute-start.57) | collective-permute-done | bytes 655392 | tf_op jit(solution)/shard_map/ppermute | solution.py:422
  (296 shorter events, 191.6 us)
Async XLA Ops:
  57.6 17.7 %collective-permute-start.7 = (bf16[256,2560]{1,0:T(8,128)(2,1)S(1)}, bf16[256,2560]{1,0:T(8,128)(2,1)S(1)}, u32[]{:S(2)}, u32[]{:S(2)}) collective-permute-start(bf16[256,2560]{1,0:T(8,128)(2,1)S(1)} %collective-permute-done.3.refs_1_.refs_9_), channel_id=1, source_target_pairs={{0,4},{1,3},{2,6},{3,1},{4,0},{5,7},{6,2},{7,5},{8,12},{9,11},{10,... | collective-permute-start | bytes 3932168 | tf_op jit(solution)/shard_map/ppermute | solution.py:353
  79.4 34.3 %all-to-all-start.1 = ((bf16[4,64,2816]{2,1,0:T(8,128)(2,1)}), bf16[4,64,2816]{2,1,0:T(8,128)(2,1)}, u32[]{:S(2)}, u32[]{:S(2)}) async-start(bf16[4,64,2816]{2,1,0:T(8,128)(2,1)} %pad_maximum_fusion.2), calls=%async_computation.1 | async-start | bytes 2883584 | tf_op jit(solution)/shard_map/all_to_all | solution.py:1295
  83.8 146.1 %all-gather.7.cloned.1.call-start = ((), (), s32[]{:S(2)}) async-start(), calls=%async_computation.9 | async-start | bytes 7208960 | tf_op jit(solution)/shard_map/all_gather | solution.py:1299
  84.0 29.7 %collective-permute-start.10 = (bf16[256,2048]{1,0:T(8,128)(2,1)}, bf16[256,2048]{1,0:T(8,128)(2,1)}, u32[]{:S(2)}, u32[]{:S(2)}) collective-permute-start(bf16[256,2048]{1,0:T(8,128)(2,1)} %refs_0_.1), channel_id=1, source_target_pairs={{0,2},{1,5},{2,0},{3,7},{4,6},{5,1},{6,4},{7,3},{8,10},{9,13},{10,... | collective-permute-start | bytes 3145736 | tf_op jit(solution)/shard_map/ppermute | solution.py:349
  113.9 41.5 %all-to-all-start = ((bf16[8,512,384]{2,1,0:T(8,128)(2,1)}), bf16[8,512,384]{2,1,0:T(8,128)(2,1)S(1)}, u32[]{:S(2)}, u32[]{:S(2)}) async-start(bf16[8,512,384]{2,1,0:T(8,128)(2,1)} %get-tuple-element.284), calls=%async_computation | async-start | bytes 6291456 | tf_op jit(solution)/shard_map/all_to_all | solution.py:1304
  155.4 35.5 %collective-permute-start.13 = (bf16[512,2048]{1,0:T(8,128)(2,1)}, bf16[512,2048]{1,0:T(8,128)(2,1)S(1)}, u32[]{:S(2)}, u32[]{:S(2)}) collective-permute-start(bf16[512,2048]{1,0:T(8,128)(2,1)} %multiply_bitcast_fusion.refs_1_.refs_4_.dy_ref), channel_id=1, source_target_pairs={{0,2},{1,5},{2,0},{3,7},{4,6},{5,1},{6,4},{7,3},{8,10},{9,13},{10,... | collective-permute-start | bytes 6291464 | tf_op jit(solution)/shard_map/ppermute | solution.py:349
  155.9 31.0 %collective-permute-start.12 = (bf16[256,2048]{1,0:T(8,128)(2,1)}, bf16[256,2048]{1,0:T(8,128)(2,1)S(1)}, u32[]{:S(2)}, u32[]{:S(2)}) collective-permute-start(bf16[256,2048]{1,0:T(8,128)(2,1)} %refs_0_.1), channel_id=1, source_target_pairs={{0,4},{1,3},{2,6},{3,1},{4,0},{5,7},{6,2},{7,5},{8,12},{9,11},{10,... | collective-permute-start | bytes 3145736 | tf_op jit(solution)/shard_map/ppermute | solution.py:353
  190.9 37.3 %collective-permute-start.15 = (bf16[512,2048]{1,0:T(8,128)(2,1)S(1)}, bf16[512,2048]{1,0:T(8,128)(2,1)S(1)}, u32[]{:S(2)}, u32[]{:S(2)}) collective-permute-start(bf16[512,2048]{1,0:T(8,128)(2,1)S(1)} %copy-done.27), channel_id=1, source_target_pairs={{0,4},{1,3},{2,6},{3,1},{4,0},{5,7},{6,2},{7,5},{8,12},{9,11},{10,... | collective-permute-start | bytes 6291464 | tf_op jit(solution)/shard_map/ppermute | solution.py:353
  192.7 35.6 %collective-permute-start.14 = (bf16[256,2048]{1,0:T(8,128)(2,1)}, bf16[256,2048]{1,0:T(8,128)(2,1)S(1)}, u32[]{:S(2)}, u32[]{:S(2)}) collective-permute-start(bf16[256,2048]{1,0:T(8,128)(2,1)} %collective-permute-done.10.refs_1_), channel_id=1, source_target_pairs={{0,4},{1,3},{2,6},{3,1},{4,0},{5,7},{6,2},{7,5},{8,12},{9,11},{10,... | collective-permute-start | bytes 3145736 | tf_op jit(solution)/shard_map/ppermute | solution.py:353
  229.9 35.3 %collective-permute-start.17 = (bf16[512,2048]{1,0:T(8,128)(2,1)}, bf16[512,2048]{1,0:T(8,128)(2,1)}, u32[]{:S(2)}, u32[]{:S(2)}) collective-permute-start(bf16[512,2048]{1,0:T(8,128)(2,1)} %copy-done.37), channel_id=1, source_target_pairs={{0,4},{1,3},{2,6},{3,1},{4,0},{5,7},{6,2},{7,5},{8,12},{9,11},{10,... | collective-permute-start | bytes 6291464 | tf_op jit(solution)/shard_map/ppermute | solution.py:353
  246.3 33.0 %all-to-all-start.2 = ((bf16[8,512,256]{2,1,0:T(8,128)(2,1)}), bf16[8,512,256]{2,1,0:T(8,128)(2,1)S(1)}, u32[]{:S(2)}, u32[]{:S(2)}) async-start(bf16[8,512,256]{2,1,0:T(8,128)(2,1)} %copy-done.6), calls=%async_computation.2 | async-start | bytes 4194304 | tf_op jit(solution)/shard_map/all_to_all | solution.py:1322
  250.1 392.8 %reduce-scatter.2.cloned.1.call-start = ((), (), s32[]{:S(2)}) async-start(), calls=%async_computation.8 | async-start | bytes 7208960 | tf_op jit(solution)/shard_map/reduce_scatter | solution.py:1371
  292.4 26.8 %collective-permute-start.22 = (bf16[512,2048]{1,0:T(8,128)(2,1)}, bf16[512,2048]{1,0:T(8,128)(2,1)S(1)}, u32[]{:S(2)}, u32[]{:S(2)}) collective-permute-start(bf16[512,2048]{1,0:T(8,128)(2,1)} %get-tuple-element.373.refs_0_.refs_4_), channel_id=1, source_target_pairs={{0,2},{1,5},{2,0},{3,7},{4,6},{5,1},{6,4},{7,3},{8,10},{9,13},{10,... | collective-permute-start | bytes 6291464 | tf_op jit(solution)/shard_map/ppermute | solution.py:349
  319.3 27.4 %collective-permute-start.23 = (bf16[512,2048]{1,0:T(8,128)(2,1)S(1)}, bf16[512,2048]{1,0:T(8,128)(2,1)}, u32[]{:S(2)}, u32[]{:S(2)}) collective-permute-start(bf16[512,2048]{1,0:T(8,128)(2,1)S(1)} %copy-done.28), channel_id=1, source_target_pairs={{0,4},{1,3},{2,6},{3,1},{4,0},{5,7},{6,2},{7,5},{8,12},{9,11},{10,... | collective-permute-start | bytes 6291464 | tf_op jit(solution)/shard_map/ppermute | solution.py:353
  346.7 27.1 %collective-permute-start.24 = (bf16[512,2048]{1,0:T(8,128)(2,1)}, bf16[512,2048]{1,0:T(8,128)(2,1)S(1)}, u32[]{:S(2)}, u32[]{:S(2)}) collective-permute-start(bf16[512,2048]{1,0:T(8,128)(2,1)} %copy-done.29), channel_id=1, source_target_pairs={{0,4},{1,3},{2,6},{3,1},{4,0},{5,7},{6,2},{7,5},{8,12},{9,11},{10,... | collective-permute-start | bytes 6291464 | tf_op jit(solution)/shard_map/ppermute | solution.py:353
  373.9 27.3 %collective-permute-start.25 = (bf16[512,2048]{1,0:T(8,128)(2,1)}, bf16[512,2048]{1,0:T(8,128)(2,1)S(1)}, u32[]{:S(2)}, u32[]{:S(2)}) collective-permute-start(bf16[512,2048]{1,0:T(8,128)(2,1)} %get-tuple-element.352), channel_id=1, source_target_pairs={{0,2},{1,5},{2,0},{3,7},{4,6},{5,1},{6,4},{7,3},{8,10},{9,13},{10,... | collective-permute-start | bytes 6291464 | tf_op jit(solution)/shard_map/ppermute | solution.py:349
  419.5 26.5 %collective-permute-start.27 = (bf16[704,2048]{1,0:T(8,128)(2,1)}, bf16[704,2048]{1,0:T(8,128)(2,1)S(1)}, u32[]{:S(2)}, u32[]{:S(2)}) collective-permute-start(bf16[704,2048]{1,0:T(8,128)(2,1)} %get-tuple-element.368), channel_id=1, source_target_pairs={{0,1},{1,0},{2,3},{3,2},{4,5},{5,4},{6,7},{7,6},{8,9},{9,8},{10,11... | collective-permute-start | bytes 8650760 | tf_op jit(solution)/shard_map/ppermute | solution.py:357
  419.6 26.4 %collective-permute-start.26 = (bf16[512,2048]{1,0:T(8,128)(2,1)}, bf16[512,2048]{1,0:T(8,128)(2,1)}, u32[]{:S(2)}, u32[]{:S(2)}) collective-permute-start(bf16[512,2048]{1,0:T(8,128)(2,1)} %get-tuple-element.362), channel_id=1, source_target_pairs={{0,2},{1,5},{2,0},{3,7},{4,6},{5,1},{6,4},{7,3},{8,10},{9,13},{10,... | collective-permute-start | bytes 6291464 | tf_op jit(solution)/shard_map/ppermute | solution.py:349
  453.9 36.8 %collective-permute-start.28 = (bf16[512,2048]{1,0:T(8,128)(2,1)}, bf16[512,2048]{1,0:T(8,128)(2,1)}, u32[]{:S(2)}, u32[]{:S(2)}) collective-permute-start(bf16[512,2048]{1,0:T(8,128)(2,1)} %add_convert_fusion.3), channel_id=1, source_target_pairs={{0,4},{1,3},{2,6},{3,1},{4,0},{5,7},{6,2},{7,5},{8,12},{9,11},{10,... | collective-permute-start | bytes 6291464 | tf_op jit(solution)/shard_map/ppermute | solution.py:353
  454.7 36.0 %collective-permute-start.29 = (bf16[2,176,2048]{2,1,0:T(8,128)(2,1)}, bf16[2,176,2048]{2,1,0:T(8,128)(2,1)}, u32[]{:S(2)}, u32[]{:S(2)}) collective-permute-start(bf16[2,176,2048]{2,1,0:T(8,128)(2,1)} %fusion.4), channel_id=1, source_target_pairs={{0,8},{8,0},{16,24},{24,16},{1,9},{9,1},{17,25},{25,17},{2,10},{10... | collective-permute-start | bytes 4325384 | tf_op jit(solution)/shard_map/ppermute | solution.py:1350
  516.7 31.1 %all-to-all-start.3 = ((bf16[8,512,256]{2,1,0:T(8,128)(2,1)}), bf16[8,512,256]{2,1,0:T(8,128)(2,1)}, u32[]{:S(2)}, u32[]{:S(2)}) async-start(bf16[8,512,256]{2,1,0:T(8,128)(2,1)} %get-tuple-element.397), calls=%async_computation.3 | async-start | bytes 4194304 | tf_op jit(solution)/shard_map/all_to_all | solution.py:1369
  521.2 196.4 %all-gather.9.cloned.1.call-start = ((), (), s32[]{:S(2)}) async-start(), calls=%async_computation.10 | async-start | bytes 3604480 | tf_op jit(solution)/shard_map/all_gather | solution.py:1393
  547.9 81.2 %collective-permute-start.33 = (bf16[4,256,2048]{2,1,0:T(8,128)(2,1)}, bf16[4,256,2048]{2,1,0:T(8,128)(2,1)}, u32[]{:S(2)}, u32[]{:S(2)}) collective-permute-start(bf16[4,256,2048]{2,1,0:T(8,128)(2,1)} %get-tuple-element.406), channel_id=1, source_target_pairs={{0,1},{1,0},{2,3},{3,2},{4,5},{5,4},{6,7},{7,6},{8,9},{9,8},{10,11... | collective-permute-start | bytes 12582920 | tf_op jit(solution)/shard_map/ppermute | solution.py:357
  547.9 81.2 %collective-permute-start.31 = (bf16[512,2048]{1,0:T(8,128)(2,1)}, bf16[512,2048]{1,0:T(8,128)(2,1)}, u32[]{:S(2)}, u32[]{:S(2)}) collective-permute-start(bf16[512,2048]{1,0:T(8,128)(2,1)} %get-tuple-element.420.refs_0_), channel_id=1, source_target_pairs={{0,2},{1,5},{2,0},{3,7},{4,6},{5,1},{6,4},{7,3},{8,10},{9,13},{10,... | collective-permute-start | bytes 6291464 | tf_op jit(solution)/shard_map/ppermute | solution.py:349
  548.5 80.7 %collective-permute-start.32 = (bf16[512,2048]{1,0:T(8,128)(2,1)}, bf16[512,2048]{1,0:T(8,128)(2,1)}, u32[]{:S(2)}, u32[]{:S(2)}) collective-permute-start(bf16[512,2048]{1,0:T(8,128)(2,1)} %get-tuple-element.420.refs_0_), channel_id=1, source_target_pairs={{0,4},{1,3},{2,6},{3,1},{4,0},{5,7},{6,2},{7,5},{8,12},{9,11},{10,... | collective-permute-start | bytes 6291464 | tf_op jit(solution)/shard_map/ppermute | solution.py:353
  549.0 80.1 %collective-permute-start.34 = (bf16[176,2048]{1,0:T(8,128)(2,1)S(1)}, bf16[176,2048]{1,0:T(8,128)(2,1)S(1)}, u32[]{:S(2)}, u32[]{:S(2)}) collective-permute-start(bf16[176,2048]{1,0:T(8,128)(2,1)S(1)} %fusion.14), channel_id=1, source_target_pairs={{0,16},{8,24},{16,0},{24,8},{1,17},{9,25},{17,1},{25,9},{2,18},{10... | collective-permute-start | bytes 2162696 | tf_op jit(solution)/shard_map/ppermute | solution.py:1364
  645.4 24.0 %collective-permute-start.35 = (bf16[512,2048]{1,0:T(8,128)(2,1)S(1)}, bf16[512,2048]{1,0:T(8,128)(2,1)}, u32[]{:S(2)}, u32[]{:S(2)}) collective-permute-start(bf16[512,2048]{1,0:T(8,128)(2,1)S(1)} %copy-done.19), channel_id=1, source_target_pairs={{0,1},{1,0},{2,3},{3,2},{4,5},{5,4},{6,7},{7,6},{8,9},{9,8},{10,11... | collective-permute-start | bytes 6291464 | tf_op jit(solution)/shard_map/ppermute | solution.py:357
  645.4 23.9 %collective-permute-start.36 = (bf16[512,2048]{1,0:T(8,128)(2,1)}, bf16[512,2048]{1,0:T(8,128)(2,1)}, u32[]{:S(2)}, u32[]{:S(2)}) collective-permute-start(bf16[512,2048]{1,0:T(8,128)(2,1)} %collective-permute-done.31.refs_1_), channel_id=1, source_target_pairs={{0,1},{1,0},{2,3},{3,2},{4,5},{5,4},{6,7},{7,6},{8,9},{9,8},{10,11... | collective-permute-start | bytes 6291464 | tf_op jit(solution)/shard_map/ppermute | solution.py:357
  645.9 23.4 %collective-permute-start.37 = (bf16[512,2048]{1,0:T(8,128)(2,1)}, bf16[512,2048]{1,0:T(8,128)(2,1)}, u32[]{:S(2)}, u32[]{:S(2)}) collective-permute-start(bf16[512,2048]{1,0:T(8,128)(2,1)} %collective-permute-done.32.refs_2_), channel_id=1, source_target_pairs={{0,1},{1,0},{2,3},{3,2},{4,5},{5,4},{6,7},{7,6},{8,9},{9,8},{10,11... | collective-permute-start | bytes 6291464 | tf_op jit(solution)/shard_map/ppermute | solution.py:357
  646.0 23.3 %all-to-all-start.4 = ((bf16[4,64,2816]{2,1,0:T(8,128)(2,1)}), bf16[4,64,2816]{2,1,0:T(8,128)(2,1)S(1)}, u32[]{:S(2)}, u32[]{:S(2)}) async-start(bf16[4,64,2816]{2,1,0:T(8,128)(2,1)} %bitcast.149), calls=%async_computation.5 | async-start | bytes 2883584 | tf_op jit(solution)/shard_map/all_to_all | solution.py:1395
  669.4 48.2 %collective-permute-start.40 = (bf16[512,2048]{1,0:T(8,128)(2,1)}, bf16[512,2048]{1,0:T(8,128)(2,1)S(1)}, u32[]{:S(2)}, u32[]{:S(2)}) collective-permute-start(bf16[512,2048]{1,0:T(8,128)(2,1)} %collective-permute-done.31.refs_1_), channel_id=1, source_target_pairs={{0,4},{1,3},{2,6},{3,1},{4,0},{5,7},{6,2},{7,5},{8,12},{9,11},{10,... | collective-permute-start | bytes 6291464 | tf_op jit(solution)/shard_map/ppermute | solution.py:353
  671.5 43.1 %collective-permute-start.39 = (bf16[256,2048]{1,0:T(8,128)(2,1)}, bf16[256,2048]{1,0:T(8,128)(2,1)}, u32[]{:S(2)}, u32[]{:S(2)}) collective-permute-start(bf16[256,2048]{1,0:T(8,128)(2,1)} %get-tuple-element.434), channel_id=1, source_target_pairs={{0,2},{1,5},{2,0},{3,7},{4,6},{5,1},{6,4},{7,3},{8,10},{9,13},{10,... | collective-permute-start | bytes 3145736 | tf_op jit(solution)/shard_map/ppermute | solution.py:349
  672.9 44.7 %collective-permute-start.38 = (bf16[256,2048]{1,0:T(8,128)(2,1)}, bf16[256,2048]{1,0:T(8,128)(2,1)}, u32[]{:S(2)}, u32[]{:S(2)}) collective-permute-start(bf16[256,2048]{1,0:T(8,128)(2,1)} %get-tuple-element.433), channel_id=1, source_target_pairs={{0,2},{1,5},{2,0},{3,7},{4,6},{5,1},{6,4},{7,3},{8,10},{9,13},{10,... | collective-permute-start | bytes 3145736 | tf_op jit(solution)/shard_map/ppermute | solution.py:349
  719.4 24.2 %collective-permute-start.41 = (bf16[256,2048]{1,0:T(8,128)(2,1)S(1)}, bf16[256,2048]{1,0:T(8,128)(2,1)}, u32[]{:S(2)}, u32[]{:S(2)}) collective-permute-start(bf16[256,2048]{1,0:T(8,128)(2,1)S(1)} %fusion.3), channel_id=1, source_target_pairs={{0,4},{1,3},{2,6},{3,1},{4,0},{5,7},{6,2},{7,5},{8,12},{9,11},{10,... | collective-permute-start | bytes 3145736 | tf_op jit(solution)/shard_map/ppermute | solution.py:353
  721.4 76.6 %all-to-all-start.5 = ((bf16[8,512,384]{2,1,0:T(8,128)(2,1)}), bf16[8,512,384]{2,1,0:T(8,128)(2,1)}, u32[]{:S(2)}, u32[]{:S(2)}) async-start(bf16[8,512,384]{2,1,0:T(8,128)(2,1)} %get-tuple-element.442.refs_8_), calls=%async_computation.6 | async-start | bytes 6291456 | tf_op jit(solution)/shard_map/all_to_all | solution.py:1413
  725.9 165.2 %all-gather.11.cloned.1.call-start = ((), (), s32[]{:S(2)}) async-start(), calls=%async_computation.11 | async-start | bytes 7208960 | tf_op jit(solution)/shard_map/all_gather | solution.py:1403
  747.5 50.6 %collective-permute-start.43 = (bf16[64,5120]{1,0:T(8,128)(2,1)}, bf16[64,5120]{1,0:T(8,128)(2,1)}, u32[]{:S(2)}, u32[]{:S(2)}) collective-permute-start(bf16[64,5120]{1,0:T(8,128)(2,1)} %get-tuple-element.450), channel_id=1, source_target_pairs={{0,8},{1,9},{2,10},{3,11},{4,12},{5,13},{6,14},{7,15}} | collective-permute-start | bytes 1966088 | tf_op jit(solution)/shard_map/ppermute | solution.py:409
  770.4 27.6 %collective-permute-start.44 = (bf16[64,5120]{1,0:T(8,128)(2,1)S(1)}, bf16[64,5120]{1,0:T(8,128)(2,1)}, u32[]{:S(2)}, u32[]{:S(2)}) collective-permute-start(bf16[64,5120]{1,0:T(8,128)(2,1)S(1)} %get-tuple-element.451), channel_id=1, source_target_pairs={{24,16},{25,17},{26,18},{27,19},{28,20},{29,21},{30,22},{31,23}} | collective-permute-start | bytes 1966088 | tf_op jit(solution)/shard_map/ppermute | solution.py:410
  800.5 38.0 %collective-permute-start.45 = (bf16[512,2048]{1,0:T(8,128)(2,1)}, bf16[512,2048]{1,0:T(8,128)(2,1)}, u32[]{:S(2)}, u32[]{:S(2)}) collective-permute-start(bf16[512,2048]{1,0:T(8,128)(2,1)} %get-tuple-element.456), channel_id=1, source_target_pairs={{0,2},{1,5},{2,0},{3,7},{4,6},{5,1},{6,4},{7,3},{8,10},{9,13},{10,... | collective-permute-start | bytes 6291464 | tf_op jit(solution)/shard_map/ppermute | solution.py:349
  807.3 31.3 %collective-permute-start.46 = (bf16[64,5120]{1,0:T(8,128)(2,1)}, bf16[64,5120]{1,0:T(8,128)(2,1)}, u32[]{:S(2)}, u32[]{:S(2)}) collective-permute-start(bf16[64,5120]{1,0:T(8,128)(2,1)} %get-tuple-element.458), channel_id=1, source_target_pairs={{0,8},{8,16},{1,9},{9,17},{2,10},{10,18},{3,11},{11,19},{4,12},{12... | collective-permute-start | bytes 1966088 | tf_op jit(solution)/shard_map/ppermute | solution.py:409
  812.5 26.1 %collective-permute-start.47 = (bf16[64,5120]{1,0:T(8,128)(2,1)S(1)}, bf16[64,5120]{1,0:T(8,128)(2,1)}, u32[]{:S(2)}, u32[]{:S(2)}) collective-permute-start(bf16[64,5120]{1,0:T(8,128)(2,1)S(1)} %get-tuple-element.459), channel_id=1, source_target_pairs={{24,16},{16,8},{25,17},{17,9},{26,18},{18,10},{27,19},{19,11},{28,... | collective-permute-start | bytes 1966088 | tf_op jit(solution)/shard_map/ppermute | solution.py:410
  841.2 35.8 %collective-permute-start.48 = (bf16[64,5120]{1,0:T(8,128)(2,1)}, bf16[64,5120]{1,0:T(8,128)(2,1)S(1)}, u32[]{:S(2)}, u32[]{:S(2)}) collective-permute-start(bf16[64,5120]{1,0:T(8,128)(2,1)} %get-tuple-element.464), channel_id=1, source_target_pairs={{0,8},{8,16},{16,24},{1,9},{9,17},{17,25},{2,10},{10,18},{18,26},{... | collective-permute-start | bytes 1966088 | tf_op jit(solution)/shard_map/ppermute | solution.py:409
  853.8 23.2 %collective-permute-start.49 = (bf16[64,5120]{1,0:T(8,128)(2,1)}, bf16[64,5120]{1,0:T(8,128)(2,1)}, u32[]{:S(2)}, u32[]{:S(2)}) collective-permute-start(bf16[64,5120]{1,0:T(8,128)(2,1)} %get-tuple-element.465), channel_id=1, source_target_pairs={{24,16},{16,8},{8,0},{25,17},{17,9},{9,1},{26,18},{18,10},{10,2},{... | collective-permute-start | bytes 1966088 | tf_op jit(solution)/shard_map/ppermute | solution.py:410
  903.4 46.9 %collective-permute-start.50 = (bf16[512,2048]{1,0:T(8,128)(2,1)}, bf16[512,2048]{1,0:T(8,128)(2,1)}, u32[]{:S(2)}, u32[]{:S(2)}) collective-permute-start(bf16[512,2048]{1,0:T(8,128)(2,1)} %get-tuple-element.477), channel_id=1, source_target_pairs={{0,2},{1,5},{2,0},{3,7},{4,6},{5,1},{6,4},{7,3},{8,10},{9,13},{10,... | collective-permute-start | bytes 6291464 | tf_op jit(solution)/shard_map/ppermute | solution.py:349
  904.0 46.3 %collective-permute-start.51 = (bf16[512,2048]{1,0:T(8,128)(2,1)}, bf16[512,2048]{1,0:T(8,128)(2,1)}, u32[]{:S(2)}, u32[]{:S(2)}) collective-permute-start(bf16[512,2048]{1,0:T(8,128)(2,1)} %add_convert_fusion.2), channel_id=1, source_target_pairs={{0,4},{1,3},{2,6},{3,1},{4,0},{5,7},{6,2},{7,5},{8,12},{9,11},{10,... | collective-permute-start | bytes 6291464 | tf_op jit(solution)/shard_map/ppermute | solution.py:353
  904.6 18.1 %collective-permute-start.52 = (bf16[64,5120]{1,0:T(8,128)(2,1)S(1)}, bf16[64,5120]{1,0:T(8,128)(2,1)S(1)}, u32[]{:S(2)}, u32[]{:S(2)}) collective-permute-start(bf16[64,5120]{1,0:T(8,128)(2,1)S(1)} %pad_maximum_fusion.3.refs_0_), channel_id=1, source_target_pairs={{0,8},{8,16},{16,24},{1,9},{9,17},{17,25},{2,10},{10,18},{18,26},{... | collective-permute-start | bytes 1966088 | tf_op jit(solution)/shard_map/ppermute | solution.py:421
  909.3 18.2 %collective-permute-start.53 = (bf16[64,5120]{1,0:T(8,128)(2,1)S(1)}, bf16[64,5120]{1,0:T(8,128)(2,1)S(1)}, u32[]{:S(2)}, u32[]{:S(2)}) collective-permute-start(bf16[64,5120]{1,0:T(8,128)(2,1)S(1)} %pad_maximum_fusion.3.refs_0_), channel_id=1, source_target_pairs={{8,0},{16,8},{24,16},{9,1},{17,9},{25,17},{10,2},{18,10},{26,18},{... | collective-permute-start | bytes 1966088 | tf_op jit(solution)/shard_map/ppermute | solution.py:422
  928.3 18.3 %collective-permute-start.55 = (bf16[64,5120]{1,0:T(8,128)(2,1)S(1)}, bf16[64,5120]{1,0:T(8,128)(2,1)S(1)}, u32[]{:S(2)}, u32[]{:S(2)}) collective-permute-start(bf16[64,5120]{1,0:T(8,128)(2,1)S(1)} %collective-permute-done.53.refs_4_), channel_id=1, source_target_pairs={{8,0},{16,8},{9,1},{17,9},{10,2},{18,10},{11,3},{19,11},{12,4},{20... | collective-permute-start | bytes 1966088 | tf_op jit(solution)/shard_map/ppermute | solution.py:422
  (81 other events, 932.1 us)
Sparse Core Ops, SparseCore 0:
  113.9 107.2 all-gather.6
  516.9 126.0 reduce-scatter.1
  645.5 67.1 all-gather.8
  728.5 162.5 all-gather.10

commit v11 on v9

--- a/solution.py
+++ b/solution.py
@@ -1292,7 +1292,6 @@
     out_first = send_first(w_out)
     gu_part = lax.all_to_all(gu_send, "sp", 0, 0, axis_index_groups=SAME_CORE, tiled=True)
     qkv_send, normed, inv_one = project(places, x_bf, attn_gain, cos, sin, qkv_parts)
-    qkv_send, out_first = fence(qkv_send, out_first)
     gu_mine = lax.all_gather(after(gu_part, qkv_send), "dp", axis=0, tiled=False)
     gu_mine = lax.all_gather(after(gu_part, qkv_send), "dp", axis=0, tiled=False)
     down_theirs = send_sibling(w_down)

time: 914 us -> 922 us (level)
  waiting for transfers between devices: 230 us -> 250 us
  starting transfers between devices: 121 us -> 108 us
    all_to_all x1, waiting for transfers between devices: 27.7 us -> 0.01 us  [fast_body(): lax.all_to_all(qkv_send, 'sp', 0, 0, tiled=True)]
    ppermute x11, waiting for transfers between devices: 33.6 us -> 58.4 us  [send_first(): return lax.ppermute(x, 'sp', FIRST)]
    ppermute x3, starting transfers between devices: 35.7 us -> 18.8 us  [line_scatter_move(): right = lax.ppermute(sends[0], 'dp', [(i, i + 1) for i in range(step)])]
    ppermute x3, waiting for transfers between devices: 36.7 us -> 49.6 us  [line_scatter_move(): right = lax.ppermute(sends[0], 'dp', [(i, i + 1) for i in range(step)])]
  transfers between devices with their start and end apart: 68 -> 68, of which waited for: 26 -> 25; matrix products, arithmetic and copies ran while one was open for 8% -> 8% of each run, Pallas kernels for 44% -> 44%
where the time goes in v11:
time: 922 us; the launch traced here: 910 us
  Pallas kernels  413 us (45%)
  waiting for transfers between devices  250 us (27%)
  starting transfers between devices  108 us (12%)
  other arithmetic  76.7 us (8%)
  local copies, waits for them, and re-layouts  47 us (5%)
  between operations  15.8 us (2%)
    pallas_call x3, Pallas kernels, attend_back(): pl.pallas_call(functools.partial(attend_back_kernel, heads=heads, start=s...  110 us
    pallas_call x4, Pallas kernels, ffn(): pl.pallas_call(functools.partial(ffn_kernel, cuts=cuts), in_specs=[hbm] *...  103 us
    ppermute x11, waiting for transfers between devices, send_first(): return lax.ppermute(x, 'sp', FIRST)  58.4 us
    pallas_call x3, Pallas kernels, attend(): pl.pallas_call(functools.partial(attend_kernel, heads=heads, start=start,...  53 us
    ppermute x3, waiting for transfers between devices, line_scatter_move(): right = lax.ppermute(sends[0], 'dp', [(i, i + 1) for i in range(step)])  49.6 us
    unnamed x128, local copies, waits for them, and re-layouts  41.1 us
    ppermute x13, waiting for transfers between devices, send_second(): return lax.ppermute(x, 'sp', SECOND)  38.4 us
    pallas_call x1, Pallas kernels, grad_gu(): pl.pallas_call(functools.partial(grad_gu_kernel, count=count), grid_spec=...  34.5 us
  transfers between devices with their start and end apart: 68, of which 25 were waited for; matrix products, arithmetic and copies ran while one was open for 8% of the time, Pallas kernels for 44%

profile of v11, /device:TPU:0, one launch (start us, length us, event | category | flops | bytes accessed | tf_op | source)
XLA Modules:
  0.0 910.1 jit_solution(10921664118067142406)
XLA Ops:
  27.8 12.1 %collective-permute-done.3.refs_1_.refs_9_ = bf16[256,2560]{1,0:T(8,128)(2,1)S(1)} collective-permute-done((bf16[256,2560]{1,0:T(8,128)(2,1)S(1)}, bf16[256,2560]{1,0:T(8,128)(2,1)S(1)}, u32[]{:S(2)}, u32[]{:S(2)}) %collective-permute-start.3) | collective-permute-done | bytes 1310752 | tf_op jit(solution)/shard_map/ppermute | solution.py:347
  42.5 7.5 fusion.12
  61.2 14.0 %collective-permute-done.7.refs_3_.refs_11_ = bf16[256,2560]{1,0:T(8,128)(2,1)S(1)} collective-permute-done((bf16[256,2560]{1,0:T(8,128)(2,1)S(1)}, bf16[256,2560]{1,0:T(8,128)(2,1)S(1)}, u32[]{:S(2)}, u32[]{:S(2)}) %collective-permute-start.7) | collective-permute-done | bytes 1310752 | tf_op jit(solution)/shard_map/ppermute | solution.py:351
  86.6 18.3 %project.1 = (bf16[8,512,384]{2,1,0:T(8,128)(2,1)}, bf16[512,2048]{1,0:T(8,128)(2,1)}, f32[512,1]{1,0:T(8,128)S(1)}) custom-call(s32[8]{0:T(128)S(1)} %stack.67.place_ref, bf16[512,2048]{1,0:T(8,128)(2,1)} %bitcast.115, f32[1,2048]{1,0:T(1,128)S(1)} %get-tuple-element.544.gain_ref, f32[512,128]{1,0:T(8,128)S(1)} %pad_maximum_fusion.4.cos_ref, ...), custom_call_target="tpu_custom_call" | custom-call | flops 1 | bytes 1 | tf_op jit(solution)/shard_map/project/pallas_call | solution.py:734
  112.4 8.2 maximum_select_fusion.refs_3_
  120.5 38.1 %collective-permute-done.11.refs_1_ = bf16[256,2048]{1,0:T(8,128)(2,1)} collective-permute-done((bf16[256,2048]{1,0:T(8,128)(2,1)}, bf16[256,2048]{1,0:T(8,128)(2,1)}, u32[]{:S(2)}, u32[]{:S(2)}) %collective-permute-start.11) | collective-permute-done | bytes 1048608 | tf_op jit(solution)/shard_map/ppermute | solution.py:347
  160.6 29.7 %attend.3 = (f32[4096,256]{1,0:T(8,128)}, bf16[8,512,256]{2,1,0:T(8,128)(2,1)S(1)}, f32[8,4,512]{2,1,0:T(4,128)S(1)}) custom-call(s32[1]{0:T(128)} %bitcast.6.zeros_ref, bf16[4096,384]{1,0:T(8,128)(2,1)S(1)} %bitcast.91, bf16[4096,384]{1,0:T(8,128)(2,1)S(1)} %bitcast.92), custom_call_target="tpu_custom_call" | custom-call | flops 1 | bytes 1 | tf_op jit(solution)/shard_map/attend/pallas_call | solution.py:1054
  190.4 4.8 collective-permute-done.13.refs_1_.refs_5_
  197.3 16.2 %attend.4 = (f32[4096,256]{1,0:T(8,128)}, bf16[8,512,256]{2,1,0:T(8,128)(2,1)S(1)}, f32[8,4,512]{2,1,0:T(4,128)S(1)}) custom-call(s32[1]{0:T(128)} %bitcast.6.zeros_ref, bf16[4096,384]{1,0:T(8,128)(2,1)S(1)} %bitcast.93, bf16[4096,384]{1,0:T(8,128)(2,1)S(1)} %bitcast.94, ...), custom_call_target="tpu_custom_call", output_to_operand_aliasing={{0}: (3, {}), {1}: (4, {}), {2}: (5, {})} | custom-call | flops 1 | bytes 1 | tf_op jit(solution)/shard_map/attend/pallas_call | solution.py:1054
  214.8 17.7 %collective-permute-done.14.refs_3_ = bf16[256,2048]{1,0:T(8,128)(2,1)S(1)} collective-permute-done((bf16[256,2048]{1,0:T(8,128)(2,1)}, bf16[256,2048]{1,0:T(8,128)(2,1)S(1)}, u32[]{:S(2)}, u32[]{:S(2)}) %collective-permute-start.14) | collective-permute-done | bytes 1048608 | tf_op jit(solution)/shard_map/ppermute | solution.py:351
  237.5 7.0 attend.5
  259.2 6.1 join.1
  268.2 15.4 %all-to-all-done.2.attn_ref.keep_ref.give_ref = bf16[8,512,256]{2,1,0:T(8,128)(2,1)S(1)} async-done(((bf16[8,512,256]{2,1,0:T(8,128)(2,1)}), bf16[8,512,256]{2,1,0:T(8,128)(2,1)S(1)}, u32[]{:S(2)}, u32[]{:S(2)}) %all-to-all-start.2) | async-done | bytes 2097184 | tf_op jit(solution)/shard_map/all_to_all | solution.py:1319
  285.0 11.9 %out_proj.1 = (f32[512,2048]{1,0:T(8,128)}, f32[512,1]{1,0:T(8,128)}, bf16[512,2048]{1,0:T(8,128)(2,1)}) custom-call(s32[8]{0:T(128)} %copy-done.29, bf16[8,512,256]{2,1,0:T(8,128)(2,1)} %copy-done.1, bf16[512,2048]{1,0:T(8,128)(2,1)} %bitcast.116, f32[1,2048]{1,0:T(1,128)} %get-tuple-element.543.gain_ref, bf16[256,2048]{1,0:T(8,128)(2,1)} %refs_0_.1, ...), custom_call_target="tpu_custom_call" | custom-call | flops 1 | bytes 1 | tf_op jit(solution)/shard_map/out_proj/pallas_call | solution.py:788
  297.5 25.7 %ffn.4 = (bf16[512,1408]{1,0:T(8,128)(2,1)}, bf16[512,1408]{1,0:T(8,128)(2,1)}, bf16[512,1408]{1,0:T(8,128)(2,1)}, bf16[512,2048]{1,0:T(8,128)(2,1)}, bf16[512,2048]{1,0:T(8,128)(2,1)}) custom-call(bf16[512,2048]{1,0:T(8,128)(2,1)} %get-tuple-element.341.refs_0_.refs_4_, bf16[512,2048]{1,0:T(8,128)(2,1)} %multiply_bitcast_fusion.refs_1_.refs_4_.dy_ref, ...), custom_call_target="tpu_custom_call" | custom-call | flops 1 | bytes 1 | tf_op jit(solution)/shard_map/ffn/pallas_call | solution.py:595
  325.0 25.8 %ffn.5 = (bf16[512,1408]{1,0:T(8,128)(2,1)}, bf16[512,1408]{1,0:T(8,128)(2,1)}, bf16[512,1408]{1,0:T(8,128)(2,1)}, bf16[512,2048]{1,0:T(8,128)(2,1)}, bf16[512,2048]{1,0:T(8,128)(2,1)}) custom-call(bf16[512,2048]{1,0:T(8,128)(2,1)} %copy-done.33, bf16[512,2048]{1,0:T(8,128)(2,1)} %copy-done.40, bf16[2,2048,1408]{2,1,0:T(8,128)(2,1)} %bitcast.107, ...), custom_call_target="tpu_custom_call" | custom-call | flops 1 | bytes 1 | tf_op jit(solution)/shard_map/ffn/pallas_call | solution.py:595
  352.1 26.0 %ffn.6 = (bf16[512,1408]{1,0:T(8,128)(2,1)}, bf16[512,1408]{1,0:T(8,128)(2,1)}, bf16[512,1408]{1,0:T(8,128)(2,1)}, bf16[512,2048]{1,0:T(8,128)(2,1)}, bf16[512,2048]{1,0:T(8,128)(2,1)}) custom-call(bf16[512,2048]{1,0:T(8,128)(2,1)} %collective-permute-done.23.refs_0_.refs_2_.refs_6_, bf16[512,2048]{1,0:T(8,128)(2,1)} %copy-done.41, ...), custom_call_target="tpu_custom_call" | custom-call | flops 1 | bytes 1 | tf_op jit(solution)/shard_map/ffn/pallas_call | solution.py:595
  379.5 25.7 %ffn.7 = (bf16[512,1408]{1,0:T(8,128)(2,1)}, bf16[512,1408]{1,0:T(8,128)(2,1)}, bf16[512,1408]{1,0:T(8,128)(2,1)}, bf16[512,2048]{1,0:T(8,128)(2,1)}, bf16[512,2048]{1,0:T(8,128)(2,1)}) custom-call(bf16[512,2048]{1,0:T(8,128)(2,1)} %copy-done.34, bf16[512,2048]{1,0:T(8,128)(2,1)} %collective-permute-done.17.refs_1_.refs_7_, ...), custom_call_target="tpu_custom_call" | custom-call | flops 1 | bytes 1 | tf_op jit(solution)/shard_map/ffn/pallas_call | solution.py:595
  406.6 34.5 %grad_gu.1 = (bf16[4,4,64,2816]{3,2,1,0:T(8,128)(2,1)}, bf16[4,4,64,2816]{3,2,1,0:T(8,128)(2,1)}) custom-call(s32[1]{0:T(128)} %bitcast.20.core_ref, bf16[512,2048]{1,0:T(8,128)(2,1)} %get-tuple-element.341.refs_0_.refs_4_, bf16[512,2048]{1,0:T(8,128)(2,1)} %copy-done.33, bf16[512,2048]{1,0:T(8,128)(2,1)} %collective-permute-done.23.refs_0_.refs_2_.refs_6_, ...), custom_call_target="tpu_custom_call" | custom-call | flops 1 | bytes 1 | tf_op jit(solution)/shard_map/grad_gu/pallas_call | solution.py:636
  447.1 17.5 %grad_dn.1 = (bf16[704,2048]{1,0:T(8,128)(2,1)}, bf16[704,2048]{1,0:T(8,128)(2,1)}) custom-call(s32[1]{0:T(128)} %bitcast.20.core_ref, bf16[512,1408]{1,0:T(8,128)(2,1)} %get-tuple-element.389.refs_0_, bf16[512,1408]{1,0:T(8,128)(2,1)} %get-tuple-element.390.refs_1_, bf16[512,1408]{1,0:T(8,128)(2,1)} %get-tuple-element.391.refs_2_, ...), custom_call_target="tpu_custom_call" | custom-call | flops 1 | bytes 1 | tf_op jit(solution)/shard_map/grad_dn/pallas_call | solution.py:958
  464.7 6.9 add_convert_fusion
  473.9 14.3 %resid_back.1 = (f32[512,2048]{1,0:T(8,128)}, bf16[512,2048]{1,0:T(8,128)(2,1)}, bf16[8,512,256]{2,1,0:T(8,128)(2,1)}) custom-call(s32[8]{0:T(128)} %copy-done.29, bf16[512,2048]{1,0:T(8,128)(2,1)} %get-tuple-element.339.db_ref, bf16[512,2048]{1,0:T(8,128)(2,1)} %copy-done.58, bf16[512,2048]{1,0:T(8,128)(2,1)} %copy-done.59, ...), custom_call_target="tpu_custom_call" | custom-call | flops 1 | bytes 1 | tf_op jit(solution)/shard_map/resid_back/pallas_call | solution.py:834
  489.8 4.5 all-to-all-start.3
  496.0 6.6 grad_wo.1
  505.4 15.6 %all-to-all-done.3 = bf16[8,512,256]{2,1,0:T(8,128)(2,1)} async-done(((bf16[8,512,256]{2,1,0:T(8,128)(2,1)}), bf16[8,512,256]{2,1,0:T(8,128)(2,1)}, u32[]{:S(2)}, u32[]{:S(2)}) %all-to-all-start.3) | async-done | bytes 2097184 | tf_op jit(solution)/shard_map/all_to_all | solution.py:1365
  522.2 43.8 %attend_back.3 = (bf16[8,512,384]{2,1,0:T(8,128)(2,1)}, f32[256,4096]{1,0:T(8,128)}, f32[8,4,512]{2,1,0:T(4,128)}) custom-call(s32[1]{0:T(128)} %bitcast.6.zeros_ref, bf16[4096,384]{1,0:T(8,128)(2,1)} %bitcast.97, bf16[4096,384]{1,0:T(8,128)(2,1)} %bitcast.98, bf16[4096,256]{1,0:T(8,128)(2,1)} %bitcast.22.do_ref, f32[8,4,512]{2,1,0:T(4,128)} %copy-done.25, ...), custom_call_target="tpu_custom_call" | custom-call | flops 1 | bytes 1 | tf_op jit(solution)/shard_map/attend_back/pallas_call | solution.py:1195
  570.6 7.5 reduce-scatter.3.cloned.1.call-done
  582.4 20.9 %attend_back.4 = (bf16[8,512,384]{2,1,0:T(8,128)(2,1)}, f32[256,4096]{1,0:T(8,128)}, f32[8,4,512]{2,1,0:T(4,128)}) custom-call(s32[1]{0:T(128)} %bitcast.6.zeros_ref, bf16[4096,384]{1,0:T(8,128)(2,1)} %bitcast.99, bf16[4096,384]{1,0:T(8,128)(2,1)} %bitcast.100, bf16[4096,256]{1,0:T(8,128)(2,1)} %bitcast.22.do_ref, ...), custom_call_target="tpu_custom_call", output_to_operand_aliasing={{0}: (9, {})} | custom-call | flops 1 | bytes 1 | tf_op jit(solution)/shard_map/attend_back/pallas_call | solution.py:1195
  603.2 4.5 fusion.11
  611.9 45.7 %attend_back.5 = (bf16[8,512,384]{2,1,0:T(8,128)(2,1)}, f32[256,4096]{1,0:T(8,128)}, f32[8,4,512]{2,1,0:T(4,128)}) custom-call(s32[1]{0:T(128)} %bitcast.6.zeros_ref, bf16[4096,384]{1,0:T(8,128)(2,1)} %bitcast.101, bf16[4096,384]{1,0:T(8,128)(2,1)} %bitcast.102, bf16[4096,256]{1,0:T(8,128)(2,1)} %bitcast.22.do_ref, ...), custom_call_target="tpu_custom_call", output_to_operand_aliasing={{0}: (9, {})} | custom-call | flops 1 | bytes 1 | tf_op jit(solution)/shard_map/attend_back/pallas_call | solution.py:1195
  660.7 4.4 all-to-all-start.5
  668.4 13.3 %grad_qkv.1 = bf16[4,64,3072]{2,1,0:T(8,128)(2,1)S(1)} custom-call(s32[8]{0:T(128)S(1)} %copy-done.30, bf16[512,2048]{1,0:T(8,128)(2,1)S(1)} %copy-done.20, bf16[512,2048]{1,0:T(8,128)(2,1)S(1)} %copy-done.23, bf16[512,2048]{1,0:T(8,128)(2,1)} %collective-permute-done.31.refs_2_, bf16[512,2048]{1,0:T(8,128)(2,1)} %collective-permute-done.38.refs_3_, ...), custom_call_target="tpu_custom_call" | custom-call | flops 1 | bytes 1 | tf_op jit(solution)/shard_map/grad_qkv/pallas_call | solution.py:670
  689.4 9.8 %collective-permute-start.41 = (bf16[64,5120]{1,0:T(8,128)(2,1)}, bf16[64,5120]{1,0:T(8,128)(2,1)}, u32[]{:S(2)}, u32[]{:S(2)}) collective-permute-start(bf16[64,5120]{1,0:T(8,128)(2,1)} %get-tuple-element.461), channel_id=1, source_target_pairs={{0,8},{1,9},{2,10},{3,11},{4,12},{5,13},{6,14},{7,15}} | collective-permute-start | bytes 1966088 | tf_op jit(solution)/shard_map/ppermute | solution.py:407
  700.7 25.9 %collective-permute-done.41 = bf16[64,5120]{1,0:T(8,128)(2,1)} collective-permute-done((bf16[64,5120]{1,0:T(8,128)(2,1)}, bf16[64,5120]{1,0:T(8,128)(2,1)}, u32[]{:S(2)}, u32[]{:S(2)}) %collective-permute-start.41) | collective-permute-done | bytes 655392 | tf_op jit(solution)/shard_map/ppermute | solution.py:407
  729.2 8.7 collective-permute-start.43
  737.9 4.4 collective-permute-start.44
  744.1 23.7 %collective-permute-done.44 = bf16[64,5120]{1,0:T(8,128)(2,1)S(1)} collective-permute-done((bf16[64,5120]{1,0:T(8,128)(2,1)}, bf16[64,5120]{1,0:T(8,128)(2,1)S(1)}, u32[]{:S(2)}, u32[]{:S(2)}) %collective-permute-start.44) | collective-permute-done | bytes 655392 | tf_op jit(solution)/shard_map/ppermute | solution.py:407
  774.2 4.6 collective-permute-start.46
  780.1 14.5 %in_back.1 = bf16[512,2048]{1,0:T(8,128)(2,1)} custom-call(s32[8]{0:T(128)} %copy-done.29, bf16[8,512,384]{2,1,0:T(8,128)(2,1)} %all-to-all-done.5.back_ref, bf16[512,2048]{1,0:T(8,128)(2,1)} %bitcast.117, f32[512,1]{1,0:T(8,128)} %copy-done.26, f32[1,2048]{1,0:T(1,128)} %copy-done.28, f32[512,2048]{1,0:T(8,128)} %get-tuple-element.485.d_resid_ref, ...), custom_call_target="tpu_custom_call" | custom-call | flops 1 | bytes 1 | tf_op jit(solution)/shard_map/in_back/pallas_call | solution.py:887
  807.0 4.6 all-to-all-done.6
  812.9 7.3 collective-permute-start.50
  827.0 6.5 spread.1
  833.5 15.2 %collective-permute-done.50.refs_1_ = bf16[64,5120]{1,0:T(8,128)(2,1)S(1)} collective-permute-done((bf16[64,5120]{1,0:T(8,128)(2,1)S(1)}, bf16[64,5120]{1,0:T(8,128)(2,1)S(1)}, u32[]{:S(2)}, u32[]{:S(2)}) %collective-permute-start.50) | collective-permute-done | bytes 655392 | tf_op jit(solution)/shard_map/ppermute | solution.py:419
  848.7 10.1 %collective-permute-done.51.refs_4_ = bf16[64,5120]{1,0:T(8,128)(2,1)S(1)} collective-permute-done((bf16[64,5120]{1,0:T(8,128)(2,1)S(1)}, bf16[64,5120]{1,0:T(8,128)(2,1)S(1)}, u32[]{:S(2)}, u32[]{:S(2)}) %collective-permute-start.51) | collective-permute-done | bytes 655392 | tf_op jit(solution)/shard_map/ppermute | solution.py:420
  861.0 5.3 reshape.175
  866.3 13.0 %collective-permute-done.53.refs_5_ = bf16[64,5120]{1,0:T(8,128)(2,1)S(1)} collective-permute-done((bf16[64,5120]{1,0:T(8,128)(2,1)S(1)}, bf16[64,5120]{1,0:T(8,128)(2,1)S(1)}, u32[]{:S(2)}, u32[]{:S(2)}) %collective-permute-start.53) | collective-permute-done | bytes 655392 | tf_op jit(solution)/shard_map/ppermute | solution.py:420
  881.3 5.1 fusion
  886.5 11.2 %collective-permute-done.55.refs_6_ = bf16[64,5120]{1,0:T(8,128)(2,1)S(1)} collective-permute-done((bf16[64,5120]{1,0:T(8,128)(2,1)S(1)}, bf16[64,5120]{1,0:T(8,128)(2,1)S(1)}, u32[]{:S(2)}, u32[]{:S(2)}) %collective-permute-start.55) | collective-permute-done | bytes 655392 | tf_op jit(solution)/shard_map/ppermute | solution.py:420
  (300 shorter events, 174.0 us)
Async XLA Ops:
  57.6 17.7 %collective-permute-start.7 = (bf16[256,2560]{1,0:T(8,128)(2,1)S(1)}, bf16[256,2560]{1,0:T(8,128)(2,1)S(1)}, u32[]{:S(2)}, u32[]{:S(2)}) collective-permute-start(bf16[256,2560]{1,0:T(8,128)(2,1)S(1)} %collective-permute-done.3.refs_1_.refs_9_), channel_id=1, source_target_pairs={{0,4},{1,3},{2,6},{3,1},{4,0},{5,7},{6,2},{7,5},{8,12},{9,11},{10,... | collective-permute-start | bytes 3932168 | tf_op jit(solution)/shard_map/ppermute | solution.py:351
  79.4 26.2 %all-to-all-start.1 = ((bf16[4,64,2816]{2,1,0:T(8,128)(2,1)}), bf16[4,64,2816]{2,1,0:T(8,128)(2,1)}, u32[]{:S(2)}, u32[]{:S(2)}) async-start(bf16[4,64,2816]{2,1,0:T(8,128)(2,1)} %pad_maximum_fusion.2), calls=%async_computation.1 | async-start | bytes 2883584 | tf_op jit(solution)/shard_map/all_to_all | solution.py:1293
  83.8 150.4 %all-gather.7.cloned.1.call-start = ((), (), s32[]{:S(2)}) async-start(), calls=%async_computation.11 | async-start | bytes 7208960 | tf_op jit(solution)/shard_map/all_gather | solution.py:1296
  105.9 52.7 %all-to-all-start = ((bf16[8,512,384]{2,1,0:T(8,128)(2,1)}), bf16[8,512,384]{2,1,0:T(8,128)(2,1)S(1)}, u32[]{:S(2)}, u32[]{:S(2)}) async-start(bf16[8,512,384]{2,1,0:T(8,128)(2,1)} %get-tuple-element.288), calls=%async_computation | async-start | bytes 6291456 | tf_op jit(solution)/shard_map/all_to_all | solution.py:1301
  110.3 48.3 %collective-permute-start.11 = (bf16[256,2048]{1,0:T(8,128)(2,1)}, bf16[256,2048]{1,0:T(8,128)(2,1)}, u32[]{:S(2)}, u32[]{:S(2)}) collective-permute-start(bf16[256,2048]{1,0:T(8,128)(2,1)} %refs_0_.1), channel_id=1, source_target_pairs={{0,2},{1,5},{2,0},{3,7},{4,6},{5,1},{6,4},{7,3},{8,10},{9,13},{10,... | collective-permute-start | bytes 3145736 | tf_op jit(solution)/shard_map/ppermute | solution.py:347
  158.6 36.6 %collective-permute-start.13 = (bf16[512,2048]{1,0:T(8,128)(2,1)}, bf16[512,2048]{1,0:T(8,128)(2,1)S(1)}, u32[]{:S(2)}, u32[]{:S(2)}) collective-permute-start(bf16[512,2048]{1,0:T(8,128)(2,1)} %multiply_bitcast_fusion.refs_1_.refs_4_.dy_ref), channel_id=1, source_target_pairs={{0,2},{1,5},{2,0},{3,7},{4,6},{5,1},{6,4},{7,3},{8,10},{9,13},{10,... | collective-permute-start | bytes 6291464 | tf_op jit(solution)/shard_map/ppermute | solution.py:347
  159.0 31.4 %collective-permute-start.12 = (bf16[256,2048]{1,0:T(8,128)(2,1)}, bf16[256,2048]{1,0:T(8,128)(2,1)S(1)}, u32[]{:S(2)}, u32[]{:S(2)}) collective-permute-start(bf16[256,2048]{1,0:T(8,128)(2,1)} %refs_0_.1), channel_id=1, source_target_pairs={{0,4},{1,3},{2,6},{3,1},{4,0},{5,7},{6,2},{7,5},{8,12},{9,11},{10,... | collective-permute-start | bytes 3145736 | tf_op jit(solution)/shard_map/ppermute | solution.py:351
  195.2 37.3 %collective-permute-start.15 = (bf16[512,2048]{1,0:T(8,128)(2,1)S(1)}, bf16[512,2048]{1,0:T(8,128)(2,1)S(1)}, u32[]{:S(2)}, u32[]{:S(2)}) collective-permute-start(bf16[512,2048]{1,0:T(8,128)(2,1)S(1)} %copy-done.31), channel_id=1, source_target_pairs={{0,4},{1,3},{2,6},{3,1},{4,0},{5,7},{6,2},{7,5},{8,12},{9,11},{10,... | collective-permute-start | bytes 6291464 | tf_op jit(solution)/shard_map/ppermute | solution.py:351
  197.0 35.6 %collective-permute-start.14 = (bf16[256,2048]{1,0:T(8,128)(2,1)}, bf16[256,2048]{1,0:T(8,128)(2,1)S(1)}, u32[]{:S(2)}, u32[]{:S(2)}) collective-permute-start(bf16[256,2048]{1,0:T(8,128)(2,1)} %collective-permute-done.11.refs_1_), channel_id=1, source_target_pairs={{0,4},{1,3},{2,6},{3,1},{4,0},{5,7},{6,2},{7,5},{8,12},{9,11},{10,... | collective-permute-start | bytes 3145736 | tf_op jit(solution)/shard_map/ppermute | solution.py:351
  234.3 34.0 %collective-permute-start.17 = (bf16[512,2048]{1,0:T(8,128)(2,1)}, bf16[512,2048]{1,0:T(8,128)(2,1)}, u32[]{:S(2)}, u32[]{:S(2)}) collective-permute-start(bf16[512,2048]{1,0:T(8,128)(2,1)} %copy-done.40), channel_id=1, source_target_pairs={{0,4},{1,3},{2,6},{3,1},{4,0},{5,7},{6,2},{7,5},{8,12},{9,11},{10,... | collective-permute-start | bytes 6291464 | tf_op jit(solution)/shard_map/ppermute | solution.py:351
  249.0 34.6 %all-to-all-start.2 = ((bf16[8,512,256]{2,1,0:T(8,128)(2,1)}), bf16[8,512,256]{2,1,0:T(8,128)(2,1)S(1)}, u32[]{:S(2)}, u32[]{:S(2)}) async-start(bf16[8,512,256]{2,1,0:T(8,128)(2,1)} %copy-done.6), calls=%async_computation.2 | async-start | bytes 4194304 | tf_op jit(solution)/shard_map/all_to_all | solution.py:1319
  252.8 325.3 %reduce-scatter.3.cloned.1.call-start = ((), (), s32[]{:S(2)}) async-start(), calls=%async_computation.9 | async-start | bytes 7208960 | tf_op jit(solution)/shard_map/reduce_scatter | solution.py:1356
  296.9 26.3 %collective-permute-start.22 = (bf16[512,2048]{1,0:T(8,128)(2,1)}, bf16[512,2048]{1,0:T(8,128)(2,1)S(1)}, u32[]{:S(2)}, u32[]{:S(2)}) collective-permute-start(bf16[512,2048]{1,0:T(8,128)(2,1)} %get-tuple-element.341.refs_0_.refs_4_), channel_id=1, source_target_pairs={{0,2},{1,5},{2,0},{3,7},{4,6},{5,1},{6,4},{7,3},{8,10},{9,13},{10,... | collective-permute-start | bytes 6291464 | tf_op jit(solution)/shard_map/ppermute | solution.py:347
  323.3 27.5 %collective-permute-start.23 = (bf16[512,2048]{1,0:T(8,128)(2,1)S(1)}, bf16[512,2048]{1,0:T(8,128)(2,1)}, u32[]{:S(2)}, u32[]{:S(2)}) collective-permute-start(bf16[512,2048]{1,0:T(8,128)(2,1)S(1)} %copy-done.32), channel_id=1, source_target_pairs={{0,4},{1,3},{2,6},{3,1},{4,0},{5,7},{6,2},{7,5},{8,12},{9,11},{10,... | collective-permute-start | bytes 6291464 | tf_op jit(solution)/shard_map/ppermute | solution.py:351
  350.8 27.3 %collective-permute-start.24 = (bf16[512,2048]{1,0:T(8,128)(2,1)}, bf16[512,2048]{1,0:T(8,128)(2,1)S(1)}, u32[]{:S(2)}, u32[]{:S(2)}) collective-permute-start(bf16[512,2048]{1,0:T(8,128)(2,1)} %copy-done.33), channel_id=1, source_target_pairs={{0,4},{1,3},{2,6},{3,1},{4,0},{5,7},{6,2},{7,5},{8,12},{9,11},{10,... | collective-permute-start | bytes 6291464 | tf_op jit(solution)/shard_map/ppermute | solution.py:351
  378.1 27.1 %collective-permute-start.25 = (bf16[512,2048]{1,0:T(8,128)(2,1)}, bf16[512,2048]{1,0:T(8,128)(2,1)S(1)}, u32[]{:S(2)}, u32[]{:S(2)}) collective-permute-start(bf16[512,2048]{1,0:T(8,128)(2,1)} %get-tuple-element.356), channel_id=1, source_target_pairs={{0,2},{1,5},{2,0},{3,7},{4,6},{5,1},{6,4},{7,3},{8,10},{9,13},{10,... | collective-permute-start | bytes 6291464 | tf_op jit(solution)/shard_map/ppermute | solution.py:347
  405.2 35.8 %collective-permute-start.26 = (bf16[512,2048]{1,0:T(8,128)(2,1)}, bf16[512,2048]{1,0:T(8,128)(2,1)S(1)}, u32[]{:S(2)}, u32[]{:S(2)}) collective-permute-start(bf16[512,2048]{1,0:T(8,128)(2,1)} %get-tuple-element.365), channel_id=1, source_target_pairs={{0,2},{1,5},{2,0},{3,7},{4,6},{5,1},{6,4},{7,3},{8,10},{9,13},{10,... | collective-permute-start | bytes 6291464 | tf_op jit(solution)/shard_map/ppermute | solution.py:347
  446.3 18.3 %collective-permute-start.27 = (bf16[4,4,64,2816]{3,2,1,0:T(8,128)(2,1)}, bf16[4,4,64,2816]{3,2,1,0:T(8,128)(2,1)}, u32[]{:S(2)}, u32[]{:S(2)}) collective-permute-start(bf16[4,4,64,2816]{3,2,1,0:T(8,128)(2,1)} %get-tuple-element.388), channel_id=1, source_target_pairs={{0,1},{1,0},{2,3},{3,2},{4,5},{5,4},{6,7},{7,6},{8,9},{9,8},{10,11... | collective-permute-start | bytes 17301512 | tf_op jit(solution)/shard_map/ppermute | solution.py:355
  446.3 26.2 %collective-permute-start.28 = (bf16[512,2048]{1,0:T(8,128)(2,1)}, bf16[512,2048]{1,0:T(8,128)(2,1)S(1)}, u32[]{:S(2)}, u32[]{:S(2)}) collective-permute-start(bf16[512,2048]{1,0:T(8,128)(2,1)} %add_convert_fusion.4), channel_id=1, source_target_pairs={{0,4},{1,3},{2,6},{3,1},{4,0},{5,7},{6,2},{7,5},{8,12},{9,11},{10,... | collective-permute-start | bytes 6291464 | tf_op jit(solution)/shard_map/ppermute | solution.py:351
  489.8 31.1 %all-to-all-start.3 = ((bf16[8,512,256]{2,1,0:T(8,128)(2,1)}), bf16[8,512,256]{2,1,0:T(8,128)(2,1)}, u32[]{:S(2)}, u32[]{:S(2)}) async-start(bf16[8,512,256]{2,1,0:T(8,128)(2,1)} %get-tuple-element.404), calls=%async_computation.3 | async-start | bytes 4194304 | tf_op jit(solution)/shard_map/all_to_all | solution.py:1365
  494.3 165.8 %reduce-scatter.5.cloned.1.call-start = ((), (), s32[]{:S(2)}) async-start(), calls=%async_computation.10 | async-start | bytes 3604480 | tf_op jit(solution)/shard_map/reduce_scatter | solution.py:1387
  521.0 49.6 %collective-permute-start.32 = (bf16[4,256,2048]{2,1,0:T(8,128)(2,1)}, bf16[4,256,2048]{2,1,0:T(8,128)(2,1)}, u32[]{:S(2)}, u32[]{:S(2)}) collective-permute-start(bf16[4,256,2048]{2,1,0:T(8,128)(2,1)} %get-tuple-element.413), channel_id=1, source_target_pairs={{0,1},{1,0},{2,3},{3,2},{4,5},{5,4},{6,7},{7,6},{8,9},{9,8},{10,11... | collective-permute-start | bytes 12582920 | tf_op jit(solution)/shard_map/ppermute | solution.py:355
  521.0 48.3 %collective-permute-start.30 = (bf16[512,2048]{1,0:T(8,128)(2,1)S(1)}, bf16[512,2048]{1,0:T(8,128)(2,1)S(1)}, u32[]{:S(2)}, u32[]{:S(2)}) collective-permute-start(bf16[512,2048]{1,0:T(8,128)(2,1)S(1)} %copy-done.19), channel_id=1, source_target_pairs={{0,2},{1,5},{2,0},{3,7},{4,6},{5,1},{6,4},{7,3},{8,10},{9,13},{10,... | collective-permute-start | bytes 6291464 | tf_op jit(solution)/shard_map/ppermute | solution.py:347
  521.6 47.7 %collective-permute-start.31 = (bf16[512,2048]{1,0:T(8,128)(2,1)S(1)}, bf16[512,2048]{1,0:T(8,128)(2,1)}, u32[]{:S(2)}, u32[]{:S(2)}) collective-permute-start(bf16[512,2048]{1,0:T(8,128)(2,1)S(1)} %copy-done.19), channel_id=1, source_target_pairs={{0,4},{1,3},{2,6},{3,1},{4,0},{5,7},{6,2},{7,5},{8,12},{9,11},{10,... | collective-permute-start | bytes 6291464 | tf_op jit(solution)/shard_map/ppermute | solution.py:351
  522.1 47.2 %collective-permute-start.33 = (bf16[512,2048]{1,0:T(8,128)(2,1)S(1)}, bf16[512,2048]{1,0:T(8,128)(2,1)}, u32[]{:S(2)}, u32[]{:S(2)}) collective-permute-start(bf16[512,2048]{1,0:T(8,128)(2,1)S(1)} %copy-done.19), channel_id=1, source_target_pairs={{0,1},{1,0},{2,3},{3,2},{4,5},{5,4},{6,7},{7,6},{8,9},{9,8},{10,11... | collective-permute-start | bytes 6291464 | tf_op jit(solution)/shard_map/ppermute | solution.py:355
  578.2 29.6 %collective-permute-start.34 = (bf16[512,2048]{1,0:T(8,128)(2,1)S(1)}, bf16[512,2048]{1,0:T(8,128)(2,1)}, u32[]{:S(2)}, u32[]{:S(2)}) collective-permute-start(bf16[512,2048]{1,0:T(8,128)(2,1)S(1)} %copy-done.22), channel_id=1, source_target_pairs={{0,1},{1,0},{2,3},{3,2},{4,5},{5,4},{6,7},{7,6},{8,9},{9,8},{10,11... | collective-permute-start | bytes 6291464 | tf_op jit(solution)/shard_map/ppermute | solution.py:355
  578.2 29.5 %collective-permute-start.35 = (bf16[512,2048]{1,0:T(8,128)(2,1)}, bf16[512,2048]{1,0:T(8,128)(2,1)}, u32[]{:S(2)}, u32[]{:S(2)}) collective-permute-start(bf16[512,2048]{1,0:T(8,128)(2,1)} %collective-permute-done.31.refs_2_), channel_id=1, source_target_pairs={{0,1},{1,0},{2,3},{3,2},{4,5},{5,4},{6,7},{7,6},{8,9},{9,8},{10,11... | collective-permute-start | bytes 6291464 | tf_op jit(solution)/shard_map/ppermute | solution.py:355
  578.7 29.0 %all-to-all-start.4 = ((bf16[4,64,2816]{2,1,0:T(8,128)(2,1)}), bf16[4,64,2816]{2,1,0:T(8,128)(2,1)S(1)}, u32[]{:S(2)}, u32[]{:S(2)}) async-start(bf16[4,64,2816]{2,1,0:T(8,128)(2,1)} %bitcast.124), calls=%async_computation.5 | async-start | bytes 2883584 | tf_op jit(solution)/shard_map/all_to_all | solution.py:1388
  582.4 189.4 %all-gather.9.cloned.1.call-start = ((), (), s32[]{:S(2)}) async-start(), calls=%async_computation.12 | async-start | bytes 7208960 | tf_op jit(solution)/shard_map/all_gather | solution.py:1397
  607.8 52.3 %collective-permute-start.38 = (bf16[512,2048]{1,0:T(8,128)(2,1)S(1)}, bf16[512,2048]{1,0:T(8,128)(2,1)}, u32[]{:S(2)}, u32[]{:S(2)}) collective-permute-start(bf16[512,2048]{1,0:T(8,128)(2,1)S(1)} %copy-done.22), channel_id=1, source_target_pairs={{0,4},{1,3},{2,6},{3,1},{4,0},{5,7},{6,2},{7,5},{8,12},{9,11},{10,... | collective-permute-start | bytes 6291464 | tf_op jit(solution)/shard_map/ppermute | solution.py:351
  609.8 47.8 %collective-permute-start.37 = (bf16[256,2048]{1,0:T(8,128)(2,1)}, bf16[256,2048]{1,0:T(8,128)(2,1)}, u32[]{:S(2)}, u32[]{:S(2)}) collective-permute-start(bf16[256,2048]{1,0:T(8,128)(2,1)} %get-tuple-element.445), channel_id=1, source_target_pairs={{0,2},{1,5},{2,0},{3,7},{4,6},{5,1},{6,4},{7,3},{8,10},{9,13},{10,... | collective-permute-start | bytes 3145736 | tf_op jit(solution)/shard_map/ppermute | solution.py:347
  611.3 48.8 %collective-permute-start.36 = (bf16[256,2048]{1,0:T(8,128)(2,1)}, bf16[256,2048]{1,0:T(8,128)(2,1)}, u32[]{:S(2)}, u32[]{:S(2)}) collective-permute-start(bf16[256,2048]{1,0:T(8,128)(2,1)} %get-tuple-element.444), channel_id=1, source_target_pairs={{0,2},{1,5},{2,0},{3,7},{4,6},{5,1},{6,4},{7,3},{8,10},{9,13},{10,... | collective-permute-start | bytes 3145736 | tf_op jit(solution)/shard_map/ppermute | solution.py:347
  660.2 25.4 %collective-permute-start.39 = (bf16[256,2048]{1,0:T(8,128)(2,1)S(1)}, bf16[256,2048]{1,0:T(8,128)(2,1)}, u32[]{:S(2)}, u32[]{:S(2)}) collective-permute-start(bf16[256,2048]{1,0:T(8,128)(2,1)S(1)} %fusion.3), channel_id=1, source_target_pairs={{0,4},{1,3},{2,6},{3,1},{4,0},{5,7},{6,2},{7,5},{8,12},{9,11},{10,... | collective-permute-start | bytes 3145736 | tf_op jit(solution)/shard_map/ppermute | solution.py:351
  660.7 65.9 %all-to-all-start.5 = ((bf16[8,512,384]{2,1,0:T(8,128)(2,1)}), bf16[8,512,384]{2,1,0:T(8,128)(2,1)}, u32[]{:S(2)}, u32[]{:S(2)}) async-start(bf16[8,512,384]{2,1,0:T(8,128)(2,1)} %get-tuple-element.453.refs_8_), calls=%async_computation.7 | async-start | bytes 6291456 | tf_op jit(solution)/shard_map/all_to_all | solution.py:1407
  665.1 195.9 %all-gather.11.cloned.1.call-start = ((), (), s32[]{:S(2)}) async-start(), calls=%async_computation.13 | async-start | bytes 3604480 | tf_op jit(solution)/shard_map/all_gather | solution.py:1420
  689.4 37.2 %collective-permute-start.41 = (bf16[64,5120]{1,0:T(8,128)(2,1)}, bf16[64,5120]{1,0:T(8,128)(2,1)}, u32[]{:S(2)}, u32[]{:S(2)}) collective-permute-start(bf16[64,5120]{1,0:T(8,128)(2,1)} %get-tuple-element.461), channel_id=1, source_target_pairs={{0,8},{1,9},{2,10},{3,11},{4,12},{5,13},{6,14},{7,15}} | collective-permute-start | bytes 1966088 | tf_op jit(solution)/shard_map/ppermute | solution.py:407
  699.2 27.4 %collective-permute-start.42 = (bf16[64,5120]{1,0:T(8,128)(2,1)S(1)}, bf16[64,5120]{1,0:T(8,128)(2,1)}, u32[]{:S(2)}, u32[]{:S(2)}) collective-permute-start(bf16[64,5120]{1,0:T(8,128)(2,1)S(1)} %get-tuple-element.462), channel_id=1, source_target_pairs={{24,16},{25,17},{26,18},{27,19},{28,20},{29,21},{30,22},{31,23}} | collective-permute-start | bytes 1966088 | tf_op jit(solution)/shard_map/ppermute | solution.py:408
  729.2 38.6 %collective-permute-start.43 = (bf16[512,2048]{1,0:T(8,128)(2,1)}, bf16[512,2048]{1,0:T(8,128)(2,1)}, u32[]{:S(2)}, u32[]{:S(2)}) collective-permute-start(bf16[512,2048]{1,0:T(8,128)(2,1)} %get-tuple-element.467), channel_id=1, source_target_pairs={{0,2},{1,5},{2,0},{3,7},{4,6},{5,1},{6,4},{7,3},{8,10},{9,13},{10,... | collective-permute-start | bytes 6291464 | tf_op jit(solution)/shard_map/ppermute | solution.py:347
  737.9 29.8 %collective-permute-start.44 = (bf16[64,5120]{1,0:T(8,128)(2,1)}, bf16[64,5120]{1,0:T(8,128)(2,1)S(1)}, u32[]{:S(2)}, u32[]{:S(2)}) collective-permute-start(bf16[64,5120]{1,0:T(8,128)(2,1)} %get-tuple-element.470), channel_id=1, source_target_pairs={{0,8},{8,16},{1,9},{9,17},{2,10},{10,18},{3,11},{11,19},{4,12},{12... | collective-permute-start | bytes 1966088 | tf_op jit(solution)/shard_map/ppermute | solution.py:407
  742.4 25.4 %collective-permute-start.45 = (bf16[64,5120]{1,0:T(8,128)(2,1)}, bf16[64,5120]{1,0:T(8,128)(2,1)}, u32[]{:S(2)}, u32[]{:S(2)}) collective-permute-start(bf16[64,5120]{1,0:T(8,128)(2,1)} %get-tuple-element.471), channel_id=1, source_target_pairs={{24,16},{16,8},{25,17},{17,9},{26,18},{18,10},{27,19},{19,11},{28,... | collective-permute-start | bytes 1966088 | tf_op jit(solution)/shard_map/ppermute | solution.py:408
  774.2 20.4 %collective-permute-start.46 = (bf16[64,5120]{1,0:T(8,128)(2,1)}, bf16[64,5120]{1,0:T(8,128)(2,1)S(1)}, u32[]{:S(2)}, u32[]{:S(2)}) collective-permute-start(bf16[64,5120]{1,0:T(8,128)(2,1)} %get-tuple-element.476), channel_id=1, source_target_pairs={{0,8},{8,16},{16,24},{1,9},{9,17},{17,25},{2,10},{10,18},{18,26},{... | collective-permute-start | bytes 1966088 | tf_op jit(solution)/shard_map/ppermute | solution.py:407
  778.8 18.6 %collective-permute-start.47 = (bf16[64,5120]{1,0:T(8,128)(2,1)}, bf16[64,5120]{1,0:T(8,128)(2,1)}, u32[]{:S(2)}, u32[]{:S(2)}) collective-permute-start(bf16[64,5120]{1,0:T(8,128)(2,1)} %get-tuple-element.477), channel_id=1, source_target_pairs={{24,16},{16,8},{8,0},{25,17},{17,9},{9,1},{26,18},{18,10},{10,2},{... | collective-permute-start | bytes 1966088 | tf_op jit(solution)/shard_map/ppermute | solution.py:408
  811.7 67.6 %collective-permute-start.48 = (bf16[512,2048]{1,0:T(8,128)(2,1)}, bf16[512,2048]{1,0:T(8,128)(2,1)}, u32[]{:S(2)}, u32[]{:S(2)}) collective-permute-start(bf16[512,2048]{1,0:T(8,128)(2,1)} %get-tuple-element.489), channel_id=1, source_target_pairs={{0,2},{1,5},{2,0},{3,7},{4,6},{5,1},{6,4},{7,3},{8,10},{9,13},{10,... | collective-permute-start | bytes 6291464 | tf_op jit(solution)/shard_map/ppermute | solution.py:347
  812.3 67.0 %collective-permute-start.49 = (bf16[512,2048]{1,0:T(8,128)(2,1)}, bf16[512,2048]{1,0:T(8,128)(2,1)}, u32[]{:S(2)}, u32[]{:S(2)}) collective-permute-start(bf16[512,2048]{1,0:T(8,128)(2,1)} %add_convert_fusion.3), channel_id=1, source_target_pairs={{0,4},{1,3},{2,6},{3,1},{4,0},{5,7},{6,2},{7,5},{8,12},{9,11},{10,... | collective-permute-start | bytes 6291464 | tf_op jit(solution)/shard_map/ppermute | solution.py:351
  812.9 35.8 %collective-permute-start.50 = (bf16[64,5120]{1,0:T(8,128)(2,1)S(1)}, bf16[64,5120]{1,0:T(8,128)(2,1)S(1)}, u32[]{:S(2)}, u32[]{:S(2)}) collective-permute-start(bf16[64,5120]{1,0:T(8,128)(2,1)S(1)} %pad_maximum_fusion.3.refs_0_), channel_id=1, source_target_pairs={{0,8},{8,16},{16,24},{1,9},{9,17},{17,25},{2,10},{10,18},{18,26},{... | collective-permute-start | bytes 1966088 | tf_op jit(solution)/shard_map/ppermute | solution.py:419
  820.2 38.6 %collective-permute-start.51 = (bf16[64,5120]{1,0:T(8,128)(2,1)S(1)}, bf16[64,5120]{1,0:T(8,128)(2,1)S(1)}, u32[]{:S(2)}, u32[]{:S(2)}) collective-permute-start(bf16[64,5120]{1,0:T(8,128)(2,1)S(1)} %pad_maximum_fusion.3.refs_0_), channel_id=1, source_target_pairs={{8,0},{16,8},{24,16},{9,1},{17,9},{25,17},{10,2},{18,10},{26,18},{... | collective-permute-start | bytes 1966088 | tf_op jit(solution)/shard_map/ppermute | solution.py:420
  859.5 19.8 %collective-permute-start.53 = (bf16[64,5120]{1,0:T(8,128)(2,1)S(1)}, bf16[64,5120]{1,0:T(8,128)(2,1)S(1)}, u32[]{:S(2)}, u32[]{:S(2)}) collective-permute-start(bf16[64,5120]{1,0:T(8,128)(2,1)S(1)} %collective-permute-done.51.refs_4_), channel_id=1, source_target_pairs={{8,0},{16,8},{9,1},{17,9},{10,2},{18,10},{11,3},{19,11},{12,4},{20... | collective-permute-start | bytes 1966088 | tf_op jit(solution)/shard_map/ppermute | solution.py:420
  880.0 17.7 %collective-permute-start.55 = (bf16[64,5120]{1,0:T(8,128)(2,1)S(1)}, bf16[64,5120]{1,0:T(8,128)(2,1)S(1)}, u32[]{:S(2)}, u32[]{:S(2)}) collective-permute-start(bf16[64,5120]{1,0:T(8,128)(2,1)S(1)} %collective-permute-done.53.refs_5_), channel_id=1, source_target_pairs={{8,0},{9,1},{10,2},{11,3},{12,4},{13,5},{14,6},{15,7}} | collective-permute-start | bytes 1966088 | tf_op jit(solution)/shard_map/ppermute | solution.py:420
  (84 other events, 851.8 us)
Sparse Core Ops, SparseCore 0:
  105.8 108.7 all-gather.6
  472.7 105.3 reduce-scatter.2
  580.4 58.9 reduce-scatter.4
  641.4 130.3 all-gather.8
  780.3 76.7 all-gather.10
